TPU v7x, 32 devices: a whole 2x2x4 slice. The times are simulated.
32 devices in a mesh: sec: 2 (over x), band: 4 (over y, core), fld: 4 (over z).
Axes of the slice: x: 2, y: 2, z: 4, core: 2. Of those that a mesh axis runs over, the one named last changes fastest.
Arguments:
- grid: bfloat16 [4, 16, 160, 2688], P('fld', 'sec', 'band'), may hold values from -6 to 6
- legendre: bfloat16 [96, 160, 96], P(('band', 'fld'), None, 'sec'), may hold values from -0.5 to 0.5
- counts: int32 [4], replicated, may hold values from 1 to 1024, 2048 in all
- blocks: int32 [4096], P('band'), may hold values from 0 to 839
- interp: bfloat16 [4096, 128], P('band'), may hold values from -0.5 to 0.5
- source_weights: bfloat16 [64, 2048], replicated, may hold values from -0.75 to 0.75
- inverses: bfloat16 [64, 32, 32], replicated, may hold values from -1 to 1
Outputs:
- spectral: bfloat16 [96, 2, 4, 16, 96], P(('band', 'fld'), None, None, None, 'sec')
- heating: bfloat16 [16, 160, 2688], P(('sec', 'fld'), 'band')
Inputs may be any that keep to these rules, and one draw needn't show every extreme that they name: Band b has counts[b] live slots, slots 0 to counts[b] - 1; the counts sum to 2048 and the largest is 1024.
All inputs are finite; a program needn't handle non-finite values.
Results may differ from a plain program's by a relative error of at most 0.0085.
Values may be sent and summed in bfloat16 or wider, within the bound.
No kernel may reach another device: no remote copies, remote signals or barrier semaphores. Data moves between devices by JAX's collectives and lax.ppermute only.
A program may use at most 64 MiB of HBM per device.

v0:
```python
import math

import jax
import jax.numpy as jnp
from jax import lax
from jax.sharding import PartitionSpec as P


def dft_table(lon, waves):
    column = jnp.arange(2 * waves, dtype=jnp.int32)
    wave = column // 2
    part = column % 2
    place = jnp.arange(lon, dtype=jnp.int32)
    phase = place[:, None] * wave[None, :] % lon
    angle = phase.astype(jnp.float32) * (2.0 * math.pi / lon)
    values = jnp.where(part[None, :] == 0, jnp.cos(angle), -jnp.sin(angle))
    return (values * (1.0 / math.sqrt(lon))).astype(jnp.bfloat16)


def heat_rates(flux, count, start):
    levels = flux.shape[0] // 2
    width = flux.shape[1]
    upward = flux[:levels]
    downward = flux[levels:]
    empty = jnp.zeros((1, width), jnp.float32)
    up_next = jnp.concatenate([upward[1:], empty], axis=0)
    down_next = jnp.concatenate([downward[1:], empty], axis=0)
    heat = upward - up_next - (downward - down_next)
    slots = start + jnp.arange(width, dtype=jnp.int32)
    heat = jnp.where(slots[None, :] < count, heat, jnp.zeros_like(heat))
    return heat.astype(jnp.bfloat16)


def body(grid, legendre, counts, blocks, interp, source_weights, inverses):
    n_sec = lax.axis_size("sec")
    n_band = lax.axis_size("band")
    n_fld = lax.axis_size("fld")
    lev_s = grid.shape[1]
    lat_d = grid.shape[2]
    lon = grid.shape[3]
    wave_dev = legendre.shape[0]
    degrees = legendre.shape[2]
    waves = wave_dev * n_band * n_fld
    groups = n_sec * n_fld
    flat_rows = grid.reshape(lev_s * lat_d, lon)
    table = dft_table(lon, waves)
    coeffs = jnp.dot(flat_rows, table, preferred_element_type=jnp.float32).astype(jnp.bfloat16)
    coeffs = coeffs.reshape(1, 1, lev_s, lat_d, n_band, n_fld, 2 * wave_dev)
    moved = lax.all_to_all(
        lax.all_to_all(coeffs, "band", split_axis=4, concat_axis=0, tiled=True),
        "fld",
        split_axis=5,
        concat_axis=1,
        tiled=True,
    )
    moved = moved.reshape(n_band, n_fld, lev_s, lat_d, wave_dev, 2)
    levels_all = lax.all_gather(moved, "sec", axis=2, tiled=True)
    weights = legendre.reshape(wave_dev, n_band, lat_d, degrees)
    spectral = jnp.einsum(
        "bflakr,kban->krfln", levels_all, weights, preferred_element_type=jnp.float32
    )
    spectral = spectral.astype(jnp.bfloat16)
    slots_all = blocks.shape[0]
    width = interp.shape[1]
    nblocks = lat_d * lon // width
    patch = grid.reshape(lev_s, nblocks, width)
    block_ids = jnp.arange(nblocks, dtype=jnp.int32)
    selector = (blocks[:, None] == block_ids[None, :]).astype(jnp.bfloat16)
    picked = lax.dot_general(
        selector, patch, (((1,), (1,)), ((), ())), preferred_element_type=jnp.float32
    )
    picked = picked.astype(jnp.bfloat16)
    partial_state = jnp.einsum("jlk,jk->lj", picked, interp, preferred_element_type=jnp.float32)
    partial_state = partial_state.astype(jnp.bfloat16).reshape(1, lev_s, slots_all)
    columns = lax.all_to_all(partial_state, ("sec", "fld"), split_axis=2, concat_axis=0, tiled=True)
    per_dev = slots_all // groups
    state = columns.reshape(n_sec, n_fld, lev_s, per_dev)
    state = jnp.transpose(state, (1, 0, 2, 3)).reshape(n_fld * n_sec * lev_s, per_dev)
    gates = lax.dot_general(
        source_weights, state, (((0,), (0,)), ((), ())), preferred_element_type=jnp.float32
    )
    spec_bands = inverses.shape[0]
    flux_rows = inverses.shape[1]
    source = jax.nn.softplus(gates).astype(jnp.bfloat16).reshape(spec_bands, flux_rows, per_dev)
    flux = jnp.einsum("bpq,bqj->pj", inverses, source, preferred_element_type=jnp.float32)
    band_place = lax.axis_index("band")
    count = jnp.sum(
        jnp.where(jnp.arange(n_band, dtype=jnp.int32) == band_place, counts, jnp.zeros_like(counts))
    )
    group_place = lax.axis_index(("sec", "fld"))
    heat = heat_rates(flux, count, group_place * per_dev)
    returned = lax.all_to_all(heat, ("sec", "fld"), split_axis=0, concat_axis=1, tiled=True)
    spread = (
        jnp.transpose(returned.astype(jnp.float32))[:, :, None]
        * interp.astype(jnp.float32)[:, None, :]
    )
    spread_high = spread.astype(jnp.bfloat16)
    spread_low = (spread - spread_high.astype(jnp.float32)).astype(jnp.bfloat16)
    summed = lax.dot_general(
        selector, spread_high, (((0,), (0,)), ((), ())), preferred_element_type=jnp.float32
    )
    summed = summed + lax.dot_general(
        selector, spread_low, (((0,), (0,)), ((), ())), preferred_element_type=jnp.float32
    )
    heating = (
        jnp.transpose(summed, (1, 0, 2)).reshape(returned.shape[0], lat_d, lon).astype(jnp.bfloat16)
    )
    return (spectral, heating)


def solution(mesh):
    return jax.shard_map(
        body,
        mesh=mesh,
        in_specs=(
            P("fld", "sec", "band", None),
            P(("band", "fld"), None, "sec"),
            P(),
            P("band"),
            P("band", None),
            P(),
            P(),
        ),
        out_specs=(P(("band", "fld"), None, None, None, "sec"), P(("sec", "fld"), "band", None)),
        check_vma=False,
    )
```

profile of v0, /device:TPU:0, one launch (start us, length us, event | category | flops | bytes accessed | tf_op | source)
XLA Modules:
  0.0 80.8 jit_solution(8253120125578889802)
XLA Ops:
  0.7 3.6 %reshape.77 = bf16[8,840,128]{2,1,0:T(8,128)(2,1)S(1)} reshape(bf16[1,8,40,2688]{3,2,1,0:T(8,128)(2,1)} %param.7) | data formatting | bytes 3440640 | tf_op jit(solution)/shard_map/reshape | solution.py:66
  4.3 2.4 %fusion.14 = bf16[1024,8,128]{2,0,1:T(8,128)(2,1)S(1)} fusion(bf16[8,840,128]{2,1,0:T(8,128)(2,1)S(1)} %reshape.77, s32[1024]{0:T(1024)S(1)} %copy-done.5), kind=kOutput, calls=%fused_computation.17 | convolution fusion | flops 1763516416 | bytes 3821568 | tf_op jit(solution)/shard_map/dot_general | solution.py:69
  6.7 1.6 %fusion.12 = bf16[1024,1,8]{2,1,0:T(2,128)(2,1)S(1)} fusion(bf16[1024,8,128]{2,0,1:T(8,128)(2,1)S(1)} %fusion.14, bf16[1024,128,1]{1,0,2:T(8,128)(2,1)S(1)} %bitcast.110), kind=kOutput, calls=%fused_computation.15 | convolution fusion | flops 2097152 | bytes 2375680 | tf_op jit(solution)/shard_map/jlk,jk->lj/dot_general | solution.py:73
  9.5 2.3 %reduce = bf16[1024,8]{1,0:T(8,128)(2,1)S(1)} reduce(bf16[1024,1,8]{2,1,0:T(2,128)(2,1)S(1)} %bitcast.105, bf16[]{:T(256)} %broadcast.78), dimensions={1}, to_apply=%bitcast.86.reduce_sub_computation | reduce | bytes 32770
  11.8 0.9 %reshape.93 = bf16[8,2,512]{2,1,0:T(2,128)(2,1)} reshape(bf16[1024,8]{1,0:T(8,128)(2,1)S(1)} %reduce) | data formatting | bytes 32768
  12.6 7.3 %all-to-all-start.2 = ((bf16[8,2,512]{2,1,0:T(2,128)(2,1)}), bf16[8,2,512]{2,1,0:T(2,128)(2,1)S(1)}, u32[]{:S(2)}, u32[]{:S(2)}) async-start(bf16[8,2,512]{2,1,0:T(2,128)(2,1)} %reshape.93), calls=%async_computation.2 | async-start | bytes 32768 | tf_op jit(solution)/shard_map/all_to_all | solution.py:75
  20.6 12.3 %fusion.39 = bf16[320,192]{0,1:T(8,128)(2,1)S(1)} fusion(bf16[320,2688]{1,0:T(8,128)(2,1)S(1)} %bitcast.108, s32[192]{0:T(256)S(1)} %and_select_fusion, pred[192]{0:T(512)(128)(4,1)S(1)} %fusion.53), kind=kOutput, calls=%fused_computation.37 | convolution fusion | flops 337072128 | bytes 1844160 | tf_op jit(solution)/shard_map/dot_general | solution.py:47
  32.8 0.7 add_compare_fusion
  33.5 0.8 copy.53
  34.7 0.7 reshape.94
  35.7 0.7 fusion.41
  37.7 6.0 %all-to-all-start.3 = ((bf16[8,2,128]{2,1,0:T(2,128)(2,1)}), bf16[8,2,128]{2,1,0:T(2,128)(2,1)S(1)}, u32[]{:S(2)}, u32[]{:S(2)}) async-start(bf16[8,2,128]{2,1,0:T(2,128)(2,1)} %bitcast.30), calls=%async_computation.3 | async-start | bytes 8192 | tf_op jit(solution)/shard_map/all_to_all | solution.py:92
  43.8 1.2 %reshape.89 = bf16[4,2,7680]{2,1,0:T(2,128)(2,1)} reshape(bf16[4,1,1,4,12,8,40]{6,5,4,3,2,1,0:T(8,128)(2,1)S(1)} %bitcast_bitcast_fusion.2) | data formatting | bytes 245760
  45.2 4.9 %all-to-all-done.3 = bf16[8,2,128]{2,1,0:T(2,128)(2,1)S(1)} async-done(((bf16[8,2,128]{2,1,0:T(2,128)(2,1)}), bf16[8,2,128]{2,1,0:T(2,128)(2,1)S(1)}, u32[]{:S(2)}, u32[]{:S(2)}) %all-to-all-start.3) | async-done | bytes 4128 | tf_op jit(solution)/shard_map/all_to_all | solution.py:92
  50.1 3.3 %all-to-all-start = ((bf16[4,2,7680]{2,1,0:T(2,128)(2,1)}), bf16[4,2,7680]{2,1,0:T(2,128)(2,1)S(1)}, u32[]{:S(2)}, u32[]{:S(2)}) async-start(bf16[4,2,7680]{2,1,0:T(2,128)(2,1)} %reshape.89), calls=%async_computation | async-start | bytes 245760 | tf_op jit(solution)/shard_map/all_to_all | solution.py:50
  53.5 0.8 %fusion.1 = f32[840,2,128]{2,0,1:T(8,128)S(1)} fusion(s32[1024]{0:T(1024)S(1)} %copy-done.5, f32[1024,128]{1,0:T(8,128)S(1)} %convert_element_type.75, f32[1024,2]{0,1:T(2,128)S(1)} %convert_bitcast_fusion), kind=kOutput, calls=%fused_computation.3 | convolution fusion | flops 442572800 | bytes 1396736 | tf_op jit(solution)/shard_map/dot_general | solution.py:102
  54.3 3.6 %all-to-all-done = bf16[4,2,7680]{2,1,0:T(2,128)(2,1)S(1)} async-done(((bf16[4,2,7680]{2,1,0:T(2,128)(2,1)}), bf16[4,2,7680]{2,1,0:T(2,128)(2,1)S(1)}, u32[]{:S(2)}, u32[]{:S(2)}) %all-to-all-start) | async-done | bytes 122912 | tf_op jit(solution)/shard_map/all_to_all | solution.py:50
  58.6 1.2 %reshape.91 = bf16[4,2,7680]{2,1,0:T(2,128)(2,1)} reshape(bf16[4,1,1,4,12,8,40]{6,5,4,3,2,1,0:T(8,128)(2,1)S(1)} %copy_bitcast_fusion) | data formatting | bytes 245760
  59.8 3.3 %all-to-all-start.1 = ((bf16[4,2,7680]{2,1,0:T(2,128)(2,1)}), bf16[4,2,7680]{2,1,0:T(2,128)(2,1)S(1)}, u32[]{:S(2)}, u32[]{:S(2)}) async-start(bf16[4,2,7680]{2,1,0:T(2,128)(2,1)} %reshape.91), calls=%async_computation.1 | async-start | bytes 245760 | tf_op jit(solution)/shard_map/all_to_all | solution.py:49
  63.1 0.9 %fusion.33 = bf16[2,840,128]{2,1,0:T(8,128)(2,1)S(1)} fusion(f32[840,2,128]{2,0,1:T(8,128)S(1)} %fusion.1, s32[1024]{0:T(1024)S(1)} %copy-done.5, f32[1024,128]{1,0:T(8,128)S(1)} %convert_element_type.75, f32[1024,2]{0,1:T(2,128)S(1)} %convert_bitcast_fusion), kind=kOutput, calls=%fused_computation.32 | convolution fusion | flops 442216448 | bytes 1826816 | tf_op jit(solution)/shard_map/dot_general | solution.py:99
  64.0 1.2 %convert_element_type.81 = bf16[2,40,2688]{2,1,0:T(8,128)(2,1)} reshape(bf16[2,840,128]{2,1,0:T(8,128)(2,1)S(1)} %fusion.33) | data formatting | bytes 860160 | tf_op jit(solution)/shard_map/convert_element_type | solution.py:106
  65.2 3.8 %all-to-all-done.1 = bf16[4,2,7680]{2,1,0:T(2,128)(2,1)S(1)} async-done(((bf16[4,2,7680]{2,1,0:T(2,128)(2,1)}), bf16[4,2,7680]{2,1,0:T(2,128)(2,1)S(1)}, u32[]{:S(2)}, u32[]{:S(2)}) %all-to-all-start.1) | async-done | bytes 122912 | tf_op jit(solution)/shard_map/all_to_all | solution.py:49
  69.8 10.0 %all_gather.3 = bf16[4,4,16,40,6,2]{3,2,0,5,1,4:T(8,128)(2,1)S(1)} all-gather(bf16[4,4,8,40,6,2]{3,2,0,5,1,4:T(8,128)(2,1)S(1)} %copy.46), channel_id=1, replica_groups=mesh['sec'=2,'band'=4,'fld'=4] {'sec'}, dimensions={2}, use_global_device_ids=true | all-gather | bytes 368640 | tf_op jit(solution)/shard_map/all_gather | solution.py:57
  80.1 0.7 copy.54
  (40 shorter events, 5.6 us)
Async XLA Ops:
  0.6 35.0 %copy-start = (bf16[64,2048]{1,0:T(8,128)(2,1)S(1)}, bf16[64,2048]{1,0:T(8,128)(2,1)}, u32[]{:S(2)}) copy-start(bf16[64,2048]{1,0:T(8,128)(2,1)} %param.12) | copy-start | bytes 786436
  0.6 3.6 %copy-start.5 = (s32[1024]{0:T(1024)S(1)}, s32[1024]{0:T(1024)}, u32[]{:S(2)}) copy-start(s32[1024]{0:T(1024)} %param.10) | copy-start | bytes 12292
  4.3 2.4 %copy-start.3 = (bf16[1024,128]{1,0:T(8,128)(2,1)S(1)}, bf16[1024,128]{1,0:T(8,128)(2,1)}, u32[]{:S(2)}) copy-start(bf16[1024,128]{1,0:T(8,128)(2,1)} %param.11) | copy-start | bytes 786436
  8.3 11.6 %copy-start.6 = (s32[4]{0:T(128)S(1)}, s32[4]{0:T(128)}, u32[]{:S(2)}) copy-start(s32[4]{0:T(128)} %param.9) | copy-start | bytes 52
  8.3 12.3 %copy-start.1 = (bf16[1,8,40,2688]{3,2,1,0:T(8,128)(2,1)S(1)}, bf16[1,8,40,2688]{3,2,1,0:T(8,128)(2,1)}, u32[]{:S(2)}) copy-start(bf16[1,8,40,2688]{3,2,1,0:T(8,128)(2,1)} %param.7) | copy-start | bytes 5160964
  12.6 22.0 %all-to-all-start.2 = ((bf16[8,2,512]{2,1,0:T(2,128)(2,1)}), bf16[8,2,512]{2,1,0:T(2,128)(2,1)S(1)}, u32[]{:S(2)}, u32[]{:S(2)}) async-start(bf16[8,2,512]{2,1,0:T(2,128)(2,1)} %reshape.93), calls=%async_computation.2 | async-start | bytes 32768 | tf_op jit(solution)/shard_map/all_to_all | solution.py:75
  20.6 12.9 %copy-start.2 = (bf16[64,32,32]{0,2,1:T(8,128)(2,1)S(1)}, bf16[64,32,32]{0,2,1:T(8,128)(2,1)}, u32[]{:S(2)}) copy-start(bf16[64,32,32]{0,2,1:T(8,128)(2,1)} %param.13) | copy-start | bytes 393220
  36.4 8.6 %copy-start.4 = (bf16[6,160,48]{1,2,0:T(8,128)(2,1)S(1)}, bf16[6,160,48]{1,2,0:T(8,128)(2,1)}, u32[]{:S(2)}) copy-start(bf16[6,160,48]{1,2,0:T(8,128)(2,1)} %param.8) | copy-start | bytes 276484
  37.7 12.4 %all-to-all-start.3 = ((bf16[8,2,128]{2,1,0:T(2,128)(2,1)}), bf16[8,2,128]{2,1,0:T(2,128)(2,1)S(1)}, u32[]{:S(2)}, u32[]{:S(2)}) async-start(bf16[8,2,128]{2,1,0:T(2,128)(2,1)} %bitcast.30), calls=%async_computation.3 | async-start | bytes 8192 | tf_op jit(solution)/shard_map/all_to_all | solution.py:92
  50.1 7.8 %all-to-all-start = ((bf16[4,2,7680]{2,1,0:T(2,128)(2,1)}), bf16[4,2,7680]{2,1,0:T(2,128)(2,1)S(1)}, u32[]{:S(2)}, u32[]{:S(2)}) async-start(bf16[4,2,7680]{2,1,0:T(2,128)(2,1)} %reshape.89), calls=%async_computation | async-start | bytes 245760 | tf_op jit(solution)/shard_map/all_to_all | solution.py:50
  59.8 9.3 %all-to-all-start.1 = ((bf16[4,2,7680]{2,1,0:T(2,128)(2,1)}), bf16[4,2,7680]{2,1,0:T(2,128)(2,1)S(1)}, u32[]{:S(2)}, u32[]{:S(2)}) async-start(bf16[4,2,7680]{2,1,0:T(2,128)(2,1)} %reshape.91), calls=%async_computation.1 | async-start | bytes 245760 | tf_op jit(solution)/shard_map/all_to_all | solution.py:49
where the time goes:
time: 81.3 us; the launch traced here: 80.8 us
  starting transfers between devices  19.9 us (24%)
  matrix products  19.4 us (24%)
  local copies, waits for them, and re-layouts  14 us (17%)
  waiting for transfers between devices  12.4 us (15%)
  blocking collectives  10 us (12%)
  other arithmetic  4.24 us (5%)
  between operations  0.95 us (1%)
    dot_general x1, matrix products, body(): jnp.dot(flat_rows, table, preferred_element_type=jnp.float32)  12.3 us
    all_gather x1, blocking collectives, body(): levels_all = lax.all_gather(moved, 'sec', axis=2, tiled=True)  10 us
    unnamed x26, local copies, waits for them, and re-layouts  7.29 us
    all_to_all x1, starting transfers between devices, body(): lax.all_to_all(partial_state, ('sec', 'fld'), split_axis=2, concat_axis=0...  7.26 us
    all_to_all x1, starting transfers between devices, body(): lax.all_to_all(heat, ('sec', 'fld'), split_axis=0, concat_axis=1, tiled=T...  5.98 us
    all_to_all x1, waiting for transfers between devices, body(): lax.all_to_all(heat, ('sec', 'fld'), split_axis=0, concat_axis=1, tiled=T...  4.94 us
    all_to_all x1, waiting for transfers between devices, body(): lax.all_to_all(lax.all_to_all(coeffs, 'band', split_axis=4, concat_axis=0...  3.83 us
    all_to_all x1, waiting for transfers between devices, body(): lax.all_to_all(coeffs, 'band', split_axis=4, concat_axis=0, tiled=True)  3.64 us
  transfers between devices with their start and end apart: 4, of which 3 were waited for; matrix products, arithmetic and copies ran while one was open for 24% of the time, Pallas kernels for 0%

commit v1 on v0

v1 whole, which is shorter than its diff:
```python
import functools
import math

import jax
import jax.numpy as jnp
import numpy as np
from jax import lax
from jax.experimental import pallas as pl
from jax.experimental.pallas import tpu as pltpu
from jax.sharding import PartitionSpec as P

BF16 = jnp.bfloat16
F32 = jnp.float32
LANES = 128
THIRDS = 3
VMEM = pl.BlockSpec(memory_space=pltpu.VMEM)
SMEM = pl.BlockSpec(memory_space=pltpu.SMEM)
LIMIT = 40 * 1024 * 1024
NT = (((1,), (1,)), ((), ()))


def dft_table(lon, wave_dev, n_band, n_fld):
    values_dev = 2 * wave_dev
    rest = values_dev // THIRDS
    third, fld, band, low = np.meshgrid(
        np.arange(THIRDS), np.arange(n_fld), np.arange(n_band), np.arange(rest), indexing="ij"
    )
    value = third * rest + low
    wave = ((band * n_fld + fld) * wave_dev + value // 2).reshape(-1)
    part = (value % 2).reshape(-1)
    phase = np.arange(lon, dtype=np.int64)[:, None] * wave[None, :] % lon
    angle = phase * (2.0 * math.pi / lon)
    values = np.where(part[None, :] == 0, np.cos(angle), -np.sin(angle)) / math.sqrt(lon)
    return values.astype(np.float32).astype(BF16)


def dft_kernel(lev, lat, n_fld, place, grid, table, *refs):
    outs, (padded, rows) = refs[:n_fld], refs[n_fld:]
    coeffs = jnp.dot(grid[...], table[...], preferred_element_type=F32)
    group = coeffs.shape[1] // THIRDS
    padded[...] = jnp.zeros_like(padded)
    for level in range(lev):
        one = coeffs[level * lat : (level + 1) * lat]
        for third in range(THIRDS):
            padded[third * lat : (third + 1) * lat, :group] = one[
                :, third * group : (third + 1) * group
            ]
        rows[pl.ds(level, group, stride=lev), :] = jnp.transpose(padded[...])[:group]
    size = outs[0].shape[0]
    for shift in range(n_fld):
        start = pl.multiple_of((place[0] ^ shift) * size, size)
        outs[shift][...] = rows[pl.ds(start, size), :].astype(BF16)


def regroup_kernel(n_fld, n_band, place, *refs):
    pieces, outs = refs[:n_fld], refs[n_fld:]
    size = outs[0].shape[0] // n_fld
    for shift in range(n_band):
        start = pl.multiple_of((place[1] ^ shift) * size, size)
        for piece in range(n_fld):
            outs[shift][piece * size : (piece + 1) * size, :] = pieces[piece][pl.ds(start, size), :]


def spread_kernel(lat, n_band, legendre, out, wide):
    waves, degrees, _ = legendre.shape
    wide[...] = jnp.zeros_like(wide)
    lane = lax.broadcasted_iota(jnp.int32, (degrees, LANES), 1)
    for wave in range(waves):
        third, parity = wave // 2, wave % 2
        wide[:, : n_band * lat] = legendre[wave].astype(F32)
        place = third * lat
        live = (lane >= place) & (lane < place + lat)
        for band in range(n_band):
            base = band * lat // LANES * LANES
            moved = pltpu.roll(
                wide[:, base : base + 2 * LANES], (place - (band * lat - base)) % (2 * LANES), 1
            )
            out[band, parity, third * degrees : (third + 1) * degrees, :] = jnp.where(
                live, moved[:, :LANES], 0.0
            ).astype(BF16)


def legendre_kernel(n_sec, n_band, n_fld, lev, place, weights, *refs):
    pieces, out = refs[: n_sec * n_band], refs[n_sec * n_band]
    degrees = out.shape[4]
    size = pieces[0].shape[0] // n_fld
    half = size // 2
    first = place[2] == 0
    for parity in range(2):
        basis = jnp.concatenate(
            [weights[place[1] ^ shift, parity] for shift in range(n_band)], axis=1
        )
        left = jnp.concatenate(
            [
                jnp.concatenate(
                    [
                        pieces[sec * n_band + shift][
                            fld * size + parity * half : fld * size + (parity + 1) * half, :
                        ]
                        for shift in range(n_band)
                    ],
                    axis=1,
                )
                for sec in range(n_sec)
                for fld in range(n_fld)
            ],
            axis=0,
        )
        result = lax.dot_general(left, basis, NT, preferred_element_type=F32)
        for third in range(THIRDS):
            part = result[:, third * degrees : (third + 1) * degrees]
            for fld in range(n_fld):
                for real in range(2):
                    near = part[fld * half + real * lev : fld * half + (real + 1) * lev]
                    base = (n_fld + fld) * half + real * lev
                    far = part[base : base + lev]
                    levels = jnp.concatenate(
                        [jnp.where(first, near, far), jnp.where(first, far, near)], axis=0
                    )
                    out[2 * third + parity, real, place[0] ^ fld] = levels.astype(BF16)


def slot_rows(blocks, across, lat_pad):
    shift = 16
    factor = -(-(1 << shift) // across)
    lat = lax.shift_right_logical(blocks * factor, shift)
    return (blocks - lat * across) * lat_pad + lat


def pick_kernel(lat_pad, grid, blocks, interp, state, patch, column):
    lev, lat, lon = grid.shape
    across = lon // LANES
    slots = interp.shape[0]
    depth = patch.shape[0]
    for tile in range(across):
        patch[tile * lat_pad + lat : (tile + 1) * lat_pad, :] = jnp.zeros(
            (lat_pad - lat, lev * LANES), BF16
        )
        for level in range(lev):
            patch[
                tile * lat_pad : tile * lat_pad + lat, level * LANES : (level + 1) * LANES
            ] = grid[level, :, tile * LANES : (tile + 1) * LANES]
    if depth > across * lat_pad:
        patch[across * lat_pad :, :] = jnp.zeros((depth - across * lat_pad, lev * LANES), BF16)
    row = slot_rows(blocks[...], across, lat_pad)
    column[...] = jnp.transpose(jnp.broadcast_to(row, (LANES, slots)))
    chunk = 256
    lane = lax.broadcasted_iota(jnp.int32, (chunk, LANES), 1)
    for start in range(0, slots, chunk):
        mine = column[start : start + chunk, :]
        selector = jnp.concatenate(
            [
                jnp.where(mine == lane + base, 1.0, 0.0).astype(BF16)
                for base in range(0, depth, LANES)
            ],
            axis=1,
        )
        picked = jnp.dot(selector, patch[...], preferred_element_type=F32)
        weights = interp[start : start + chunk, :].astype(F32)
        total = jnp.zeros((chunk, LANES), F32)
        for level in range(lev):
            product = picked[:, level * LANES : (level + 1) * LANES] * weights
            total = jnp.where(lane == level, jnp.sum(product, axis=1, keepdims=True), total)
        state[:, start : start + chunk] = jnp.transpose(total)[:lev].astype(BF16)


def softplus(x):
    small = jnp.exp(-jnp.abs(x))
    tail = jnp.where(small < 2.0**-11, small, jnp.log(1.0 + small))
    return jnp.maximum(x, 0.0) + tail


def column_kernel(n_sec, n_fld, lat_pad, place, counts, weights, inverses, blocks, interp, *refs):
    pieces = refs[: n_sec * n_fld]
    out, state, flux_up, flux_down = refs[n_sec * n_fld :]
    lev = pieces[0].shape[0]
    slots = pieces[0].shape[1]
    for sec in range(n_sec):
        for fld in range(n_fld):
            row = ((place[0] ^ fld) * n_sec + (place[2] ^ sec)) * lev
            state[pl.ds(pl.multiple_of(row, lev), lev), :] = pieces[sec * n_fld + fld][...].astype(F32)
    column = state[...].astype(BF16)
    flux_rows = inverses.shape[0]
    flux = jnp.zeros((flux_rows, slots), F32)
    chunk = 256
    for start in range(0, weights.shape[0], chunk):
        gates = jnp.dot(weights[start : start + chunk, :], column, preferred_element_type=F32)
        source = softplus(gates).astype(BF16)
        flux = flux + jnp.dot(
            inverses[:, start : start + chunk], source, preferred_element_type=F32
        )
    levels = flux_rows // 2
    flux_up[:levels, :] = flux[:levels]
    flux_down[:levels, :] = flux[levels:]
    flux_up[levels:, :] = jnp.zeros((8, slots), F32)
    flux_down[levels:, :] = jnp.zeros((8, slots), F32)
    mine, lat, lon = out.shape
    across = lon // LANES
    live = lax.broadcasted_iota(jnp.int32, (1, slots), 1) < counts[place[1]]
    base = (place[2] * n_fld + place[0]) * mine
    heats = []
    for level in range(mine):
        at = base + level
        heat = (flux_up[pl.ds(at, 1), :] - flux_up[pl.ds(at + 1, 1), :]) - (
            flux_down[pl.ds(at, 1), :] - flux_down[pl.ds(at + 1, 1), :]
        )
        heats.append(jnp.where(live, heat, 0.0).astype(BF16).astype(F32))
    row = slot_rows(blocks[...], across, lat_pad)
    tiles = max(t for t in range(1, 8) if across % t == 0)
    height = tiles * lat_pad
    for first in range(0, across, tiles):
        match = row == lax.broadcasted_iota(jnp.int32, (height, slots), 0) + first * lat_pad
        for level in range(mine):
            left = jnp.where(match, heats[level], 0.0).astype(BF16)
            summed = jnp.dot(left, interp[...], preferred_element_type=F32).astype(BF16)
            for tile in range(tiles):
                out[level, :, (first + tile) * LANES : (first + tile + 1) * LANES] = summed[
                    tile * lat_pad : tile * lat_pad + lat
                ]


def call(kernel, outs, specs, scratch, args, flops, size, name):
    shapes = [jax.ShapeDtypeStruct(shape, dtype) for shape, dtype in outs]
    single = len(outs) == 1
    return pl.pallas_call(
        kernel,
        out_shape=shapes[0] if single else shapes,
        in_specs=specs,
        out_specs=VMEM if single else [VMEM] * len(outs),
        scratch_shapes=scratch,
        compiler_params=pltpu.CompilerParams(vmem_limit_bytes=LIMIT),
        cost_estimate=pl.CostEstimate(flops=flops, bytes_accessed=size, transcendentals=0),
        name=name,
    )(*args)


def exchange(value, axes, shifts):
    sizes = [lax.axis_size(axis) for axis in axes]
    pairs = []
    for i in range(math.prod(sizes)):
        at = np.unravel_index(i, sizes)
        to = tuple(int(a) ^ s for a, s in zip(at, shifts))
        pairs.append((i, int(np.ravel_multi_index(to, sizes))))
    return lax.ppermute(value, axes, pairs)


def body(grid, legendre, counts, blocks, interp, source_weights, inverses):
    n_sec = lax.axis_size("sec")
    n_band = lax.axis_size("band")
    n_fld = lax.axis_size("fld")
    lev, lat, lon = grid.shape[1:]
    wave_dev, _, degrees = legendre.shape
    slots = blocks.shape[0]
    across = lon // LANES
    lat_pad = -(-lat // 16) * 16
    rest = 2 * wave_dev // THIRDS
    piece = rest * lev
    place = jnp.stack([lax.axis_index("fld"), lax.axis_index("band"), lax.axis_index("sec")]).astype(
        jnp.int32
    )
    block_row = blocks.reshape(1, slots)

    table = jnp.asarray(dft_table(lon, wave_dev, n_band, n_fld))
    group = n_fld * n_band * rest
    padded_group = -(-group // LANES) * LANES
    sent = call(
        functools.partial(dft_kernel, lev, lat, n_fld),
        [((n_band * piece, LANES), BF16)] * n_fld,
        [SMEM, VMEM, VMEM],
        [pltpu.VMEM((LANES, padded_group), F32), pltpu.VMEM((group * lev, LANES), F32)],
        (place, grid.reshape(lev * lat, lon), table),
        2 * lev * lat * lon * THIRDS * group,
        2 * lon * (lev * lat + THIRDS * group),
        "fourier",
    )
    fields = [sent[0]] + [exchange(sent[d], ("fld",), (d,)) for d in range(1, n_fld)]

    depth = -(-across * lat_pad // LANES) * LANES
    state = call(
        functools.partial(pick_kernel, lat_pad),
        [((lev, slots), BF16)],
        [VMEM, VMEM, VMEM],
        [pltpu.VMEM((depth, lev * LANES), BF16), pltpu.VMEM((slots, LANES), jnp.int32)],
        (grid.reshape(lev, lat, lon), block_row, interp),
        2 * slots * depth * lev * LANES,
        2 * lev * lat * lon + 2 * slots * LANES,
        "pick",
    )
    columns = [
        state if sec == 0 and fld == 0 else exchange(state, ("sec", "fld"), (sec, fld))
        for sec in range(n_sec)
        for fld in range(n_fld)
    ]

    basis = call(
        functools.partial(spread_kernel, lat, n_band),
        [((n_band, 2, THIRDS * degrees, LANES), BF16)],
        [VMEM],
        [pltpu.VMEM((degrees, (n_band * lat // LANES + 2) * LANES), F32)],
        (jnp.swapaxes(legendre, 1, 2),),
        0,
        8 * wave_dev * degrees * n_band * LANES,
        "basis",
    )
    grouped = call(
        functools.partial(regroup_kernel, n_fld, n_band),
        [((n_fld * piece, LANES), BF16)] * n_band,
        [SMEM] + [VMEM] * n_fld,
        [],
        (place, *fields),
        0,
        4 * n_fld * n_band * piece * LANES,
        "regroup",
    )
    bands = [
        grouped[0] if sec == 0 and band == 0 else exchange(grouped[band], ("sec", "band"), (sec, band))
        for sec in range(n_sec)
        for band in range(n_band)
    ]

    spec_bands, flux_rows, _ = inverses.shape
    heating = call(
        functools.partial(column_kernel, n_sec, n_fld, lat_pad),
        [((n_sec * lev // (n_sec * n_fld), lat, lon), BF16)],
        [SMEM, SMEM] + [VMEM] * (4 + n_sec * n_fld),
        [
            pltpu.VMEM((n_sec * n_fld * lev, slots), F32),
            pltpu.VMEM((flux_rows // 2 + 8, slots), F32),
            pltpu.VMEM((flux_rows // 2 + 8, slots), F32),
        ],
        (
            place,
            counts,
            jnp.transpose(source_weights),
            jnp.transpose(inverses, (1, 0, 2)).reshape(flux_rows, spec_bands * flux_rows),
            block_row,
            interp,
            *columns,
        ),
        8 * slots * slots * 1024,
        2 * slots * slots,
        "columns",
    )

    spectral = call(
        functools.partial(legendre_kernel, n_sec, n_band, n_fld, lev),
        [((wave_dev, 2, n_fld, n_sec * lev, degrees), BF16)],
        [SMEM] + [VMEM] * (1 + n_sec * n_band),
        [],
        (place, basis, *bands),
        4 * n_sec * n_fld * piece * n_band * LANES * degrees * THIRDS,
        2 * n_sec * n_band * n_fld * piece * LANES,
        "legendre",
    )
    return (spectral, heating)


def solution(mesh):
    return jax.shard_map(
        body,
        mesh=mesh,
        in_specs=(
            P("fld", "sec", "band", None),
            P(("band", "fld"), None, "sec"),
            P(),
            P("band"),
            P("band", None),
            P(),
            P(),
        ),
        out_specs=(P(("band", "fld"), None, None, None, "sec"), P(("sec", "fld"), "band", None)),
        check_vma=False,
    )
```

time: 81.3 us -> 45.2 us (0.56)
  matrix products: 19.4 us -> 0 us
  Pallas kernels: 0 us -> 13.3 us
  local copies, waits for them, and re-layouts: 14 us -> 3.92 us
  blocking collectives: 10 us -> 0 us
  waiting for transfers between devices: 12.4 us -> 3.43 us
  other arithmetic: 4.24 us -> 0.08 us
  starting transfers between devices: 19.9 us -> 23.5 us
    ppermute x0 -> x17, starting transfers between devices: none -> 23.5 us  [exchange(): return lax.ppermute(value, axes, pairs)]
    all_to_all x4 -> x0, starting transfers between devices: 19.9 us -> none  [the longest x1 7.26 us: body(): lax.all_to_all(partial_state, ('sec', 'fld'), split_axis=2, concat_axis=0...]
    dot_general x8 -> x0, matrix products: 19.4 us -> none  [the longest x1 12.3 us: body(): jnp.dot(flat_rows, table, preferred_element_type=jnp.float32)]
    pallas_call x0 -> x6, Pallas kernels: none -> 13.3 us  [call(): pl.pallas_call(kernel, out_shape=shapes[0] if single else shapes, in_spec...]
    all_to_all x4 -> x0, waiting for transfers between devices: 12.4 us -> none  [the longest x1 4.94 us: body(): lax.all_to_all(heat, ('sec', 'fld'), split_axis=0, concat_axis=1, tiled=T...]
    all_gather x1 -> x0, blocking collectives: 10 us -> none  [body(): levels_all = lax.all_gather(moved, 'sec', axis=2, tiled=True)]
    unnamed x26 -> x19, local copies, waits for them, and re-layouts: 7.29 us -> 3.1 us
    reshape x6 -> x1, local copies, waits for them, and re-layouts: 4.62 us -> 0.54 us  [body(): jnp.transpose(inverses, (1, 0, 2))]
  transfers between devices with their start and end apart: 4 -> 17, of which waited for: 3 -> 3; matrix products, arithmetic and copies ran while one was open for 24% -> 2% of each run, Pallas kernels for 0% -> 23%
where the time goes in v1:
time: 45.2 us; the launch traced here: 45 us
  starting transfers between devices  23.5 us (52%)
  Pallas kernels  13.3 us (29%)
  local copies, waits for them, and re-layouts  3.92 us (9%)
  waiting for transfers between devices  3.43 us (8%)
  between operations  0.79 us (2%)
    ppermute x17, starting transfers between devices, exchange(): return lax.ppermute(value, axes, pairs)  23.5 us
    pallas_call x6, Pallas kernels, call(): pl.pallas_call(kernel, out_shape=shapes[0] if single else shapes, in_spec...  13.3 us
    ppermute x17, waiting for transfers between devices, exchange(): return lax.ppermute(value, axes, pairs)  3.43 us
    unnamed x19, local copies, waits for them, and re-layouts  3.1 us
  transfers between devices with their start and end apart: 17, of which 3 were waited for; matrix products, arithmetic and copies ran while one was open for 2% of the time, Pallas kernels for 23%

profile of v1, /device:TPU:0, one launch (start us, length us, event | category | flops | bytes accessed | tf_op | source)
XLA Modules:
  0.0 45.0 jit_solution(10895815521891512679)
XLA Ops:
  0.7 1.5 %copy-done = bf16[1,8,40,2688]{3,2,1,0:T(8,128)(2,1)S(1)} copy-done((bf16[1,8,40,2688]{3,2,1,0:T(8,128)(2,1)S(1)}, bf16[1,8,40,2688]{3,2,1,0:T(8,128)(2,1)}, u32[]{:S(2)}) %copy-start) | copy-done | bytes 1720344
  2.2 1.3 %copy-done.2 = bf16[2688,192]{1,0:T(8,128)(2,1)S(1)} copy-done((bf16[2688,192]{1,0:T(8,128)(2,1)S(1)}, bf16[2688,192]{1,0:T(8,128)(2,1)}, u32[]{:S(2)}) %copy-start.2) | copy-done | bytes 1032216
  3.5 1.4 %fourier.1 = (bf16[128,128]{1,0:T(8,128)(2,1)S(1)}, bf16[128,128]{1,0:T(8,128)(2,1)S(1)}, bf16[128,128]{1,0:T(8,128)(2,1)S(1)}, bf16[128,128]{1,0:T(8,128)(2,1)S(1)}) custom-call(s32[3]{0:T(128)S(1)} %pad_add_fusion.place, bf16[320,2688]{1,0:T(8,128)(2,1)S(1)} %bitcast.9, bf16[2688,192]{1,0:T(8,128)(2,1)S(1)} %copy-done.2), custom_call_target="tpu_custom_call" | custom-call | flops 330301440 | bytes 2752512 | tf_op jit(solution)/shard_map/fourier/pallas_call | solution.py:225
  5.0 3.1 %collective-permute-start = (bf16[128,128]{1,0:T(8,128)(2,1)S(1)}, bf16[128,128]{1,0:T(8,128)(2,1)S(1)}, u32[]{:S(2)}, u32[]{:S(2)}) collective-permute-start(bf16[128,128]{1,0:T(8,128)(2,1)S(1)} %get-tuple-element.11), channel_id=1, source_target_pairs={{0,1},{1,0},{2,3},{3,2},{4,5},{5,4},{6,7},{7,6},{8,9},{9,8},{10,11... | collective-permute-start | bytes 98312 | tf_op jit(solution)/shard_map/ppermute | solution.py:244
  8.1 2.6 %collective-permute-start.1 = (bf16[128,128]{1,0:T(8,128)(2,1)S(1)}, bf16[128,128]{1,0:T(8,128)(2,1)S(1)}, u32[]{:S(2)}, u32[]{:S(2)}) collective-permute-start(bf16[128,128]{1,0:T(8,128)(2,1)S(1)} %get-tuple-element.12), channel_id=1, source_target_pairs={{0,2},{1,3},{2,0},{3,1},{4,6},{5,7},{6,4},{7,5},{8,10},{9,11},{10,... | collective-permute-start | bytes 98312 | tf_op jit(solution)/shard_map/ppermute | solution.py:244
  10.7 2.7 %pick.1.refs_0_ = bf16[8,1024]{1,0:T(8,128)(2,1)S(1)} custom-call(bf16[8,40,2688]{2,1,0:T(8,128)(2,1)S(1)} %bitcast.10, s32[1,1024]{1,0:T(1,128)S(1)} %bitcast.13, bf16[1024,128]{1,0:T(8,128)(2,1)S(1)} %copy-done.4), custom_call_target="tpu_custom_call" | custom-call | flops 2147483648 | bytes 1982464 | tf_op jit(solution)/shard_map/pick/pallas_call | solution.py:225
  13.4 0.9 %collective-permute-start.10 = (bf16[8,1024]{1,0:T(8,128)(2,1)S(1)}, bf16[8,1024]{1,0:T(8,128)(2,1)S(1)}, u32[]{:S(2)}, u32[]{:S(2)}) collective-permute-start(bf16[8,1024]{1,0:T(8,128)(2,1)S(1)} %pick.1.refs_0_), channel_id=1, source_target_pairs={{0,1},{1,0},{2,3},{3,2},{16,17},{17,16},{18,19},{19,18},{4,5},{5,4... | collective-permute-start | bytes 49160 | tf_op jit(solution)/shard_map/ppermute | solution.py:244
  14.4 3.5 %collective-permute-start.11 = (bf16[8,1024]{1,0:T(8,128)(2,1)S(1)}, bf16[8,1024]{1,0:T(8,128)(2,1)S(1)}, u32[]{:S(2)}, u32[]{:S(2)}) collective-permute-start(bf16[8,1024]{1,0:T(8,128)(2,1)S(1)} %pick.1.refs_0_), channel_id=1, source_target_pairs={{0,2},{1,3},{2,0},{3,1},{16,18},{17,19},{18,16},{19,17},{4,6},{5,7... | collective-permute-start | bytes 49160 | tf_op jit(solution)/shard_map/ppermute | solution.py:244
  17.9 1.7 %collective-permute-start.13 = (bf16[8,1024]{1,0:T(8,128)(2,1)S(1)}, bf16[8,1024]{1,0:T(8,128)(2,1)S(1)}, u32[]{:S(2)}, u32[]{:S(2)}) collective-permute-start(bf16[8,1024]{1,0:T(8,128)(2,1)S(1)} %pick.1.refs_0_), channel_id=1, source_target_pairs={{0,16},{1,17},{2,18},{3,19},{16,0},{17,1},{18,2},{19,3},{4,20},{5,... | collective-permute-start | bytes 49160 | tf_op jit(solution)/shard_map/ppermute | solution.py:244
  19.6 0.6 %regroup.1 = (bf16[128,128]{1,0:T(8,128)(2,1)S(1)}, bf16[128,128]{1,0:T(8,128)(2,1)S(1)}, bf16[128,128]{1,0:T(8,128)(2,1)S(1)}, bf16[128,128]{1,0:T(8,128)(2,1)S(1)}) custom-call(s32[3]{0:T(128)S(1)} %pad_add_fusion.place, bf16[128,128]{1,0:T(8,128)(2,1)S(1)} %get-tuple-element.10.refs_0_, bf16[128,128]{1,0:T(8,128)(2,1)S(1)} %collective-permute-done.refs_1_, ...), custom_call_target="tpu_custom_call" | custom-call | bytes 262144 | tf_op jit(solution)/shard_map/regroup/pallas_call | solution.py:225
  20.2 1.6 %collective-permute-start.4 = (bf16[128,128]{1,0:T(8,128)(2,1)S(1)}, bf16[128,128]{1,0:T(8,128)(2,1)S(1)}, u32[]{:S(2)}, u32[]{:S(2)}) collective-permute-start(bf16[128,128]{1,0:T(8,128)(2,1)S(1)} %get-tuple-element.16), channel_id=1, source_target_pairs={{0,8},{4,12},{8,0},{12,4},{16,24},{20,28},{24,16},{28,20},{1,9},{5... | collective-permute-start | bytes 98312 | tf_op jit(solution)/shard_map/ppermute | solution.py:244
  21.8 0.3 collective-permute-start.14
  22.1 1.3 %collective-permute-done.12.refs_3_ = bf16[8,1024]{1,0:T(8,128)(2,1)S(1)} collective-permute-done((bf16[8,1024]{1,0:T(8,128)(2,1)S(1)}, bf16[8,1024]{1,0:T(8,128)(2,1)S(1)}, u32[]{:S(2)}, u32[]{:S(2)}) %collective-permute-start.12) | collective-permute-done | bytes 16416 | tf_op jit(solution)/shard_map/ppermute | solution.py:244
  23.4 3.5 %collective-permute-start.15 = (bf16[8,1024]{1,0:T(8,128)(2,1)S(1)}, bf16[8,1024]{1,0:T(8,128)(2,1)S(1)}, u32[]{:S(2)}, u32[]{:S(2)}) collective-permute-start(bf16[8,1024]{1,0:T(8,128)(2,1)S(1)} %pick.1.refs_0_), channel_id=1, source_target_pairs={{0,18},{1,19},{2,16},{3,17},{16,2},{17,3},{18,0},{19,1},{4,22},{5,... | collective-permute-start | bytes 49160 | tf_op jit(solution)/shard_map/ppermute | solution.py:244
  27.3 0.3 copy.13
  27.6 0.5 %reshape.17.inverses = bf16[32,2048]{1,0:T(8,128)(2,1)S(1)} reshape(bf16[32,64,32]{2,1,0:T(8,128)(2,1)S(1)} %copy.13) | data formatting | bytes 262144 | tf_op jit(solution)/shard_map/reshape | solution.py:335
  28.1 0.3 copy.12
  28.4 0.5 %collective-permute-start.7 = (bf16[128,128]{1,0:T(8,128)(2,1)S(1)}, bf16[128,128]{1,0:T(8,128)(2,1)S(1)}, u32[]{:S(2)}, u32[]{:S(2)}) collective-permute-start(bf16[128,128]{1,0:T(8,128)(2,1)S(1)} %get-tuple-element.15), channel_id=1, source_target_pairs={{0,20},{4,16},{8,28},{12,24},{16,4},{20,0},{24,12},{28,8},{1,21},{... | collective-permute-start | bytes 98312 | tf_op jit(solution)/shard_map/ppermute | solution.py:244
  29.1 2.3 %collective-permute-start.8 = (bf16[128,128]{1,0:T(8,128)(2,1)S(1)}, bf16[128,128]{1,0:T(8,128)(2,1)S(1)}, u32[]{:S(2)}, u32[]{:S(2)}) collective-permute-start(bf16[128,128]{1,0:T(8,128)(2,1)S(1)} %get-tuple-element.16), channel_id=1, source_target_pairs={{0,24},{4,28},{8,16},{12,20},{16,8},{20,12},{24,0},{28,4},{1,25},{... | collective-permute-start | bytes 98312 | tf_op jit(solution)/shard_map/ppermute | solution.py:244
  31.4 1.9 %collective-permute-done.16.refs_7_ = bf16[8,1024]{1,0:T(8,128)(2,1)S(1)} collective-permute-done((bf16[8,1024]{1,0:T(8,128)(2,1)S(1)}, bf16[8,1024]{1,0:T(8,128)(2,1)S(1)}, u32[]{:S(2)}, u32[]{:S(2)}) %collective-permute-start.16) | collective-permute-done | bytes 16416 | tf_op jit(solution)/shard_map/ppermute | solution.py:244
  33.3 1.8 %collective-permute-start.9 = (bf16[128,128]{1,0:T(8,128)(2,1)S(1)}, bf16[128,128]{1,0:T(8,128)(2,1)S(1)}, u32[]{:S(2)}, u32[]{:S(2)}) collective-permute-start(bf16[128,128]{1,0:T(8,128)(2,1)S(1)} %get-tuple-element.17), channel_id=1, source_target_pairs={{0,28},{4,24},{8,20},{12,16},{16,12},{20,8},{24,4},{28,0},{1,29},{... | collective-permute-start | bytes 98312 | tf_op jit(solution)/shard_map/ppermute | solution.py:244
  35.2 1.4 %collective-permute-start.6 = (bf16[128,128]{1,0:T(8,128)(2,1)S(1)}, bf16[128,128]{1,0:T(8,128)(2,1)S(1)}, u32[]{:S(2)}, u32[]{:S(2)}) collective-permute-start(bf16[128,128]{1,0:T(8,128)(2,1)S(1)} %get-tuple-element.14.refs_0_), channel_id=1, source_target_pairs={{0,16},{4,20},{8,24},{12,28},{16,0},{20,4},{24,8},{28,12},{1,17},{... | collective-permute-start | bytes 98312 | tf_op jit(solution)/shard_map/ppermute | solution.py:244
  36.5 6.9 %columns.1 = bf16[2,40,2688]{2,1,0:T(8,128)(2,1)} custom-call(s32[3]{0:T(128)S(1)} %pad_add_fusion.place, s32[4]{0:T(128)S(1)} %copy-done.6, bf16[2048,64]{1,0:T(8,128)(2,1)S(1)} %bitcast.11, bf16[32,2048]{1,0:T(8,128)(2,1)S(1)} %reshape.17.inverses, s32[1,1024]{1,0:T(1,128)S(1)} %bitcast.14, bf16[1024,128]{1,0:T(8,128)(2,1)S(1)} %copy-done.4, ...), custom_call_target="tpu_custom_call" | custom-call | flops 8589934592 | bytes 2097152 | tf_op jit(solution)/shard_map/columns/pallas_call | solution.py:225
  43.4 1.6 %legendre.1 = bf16[6,2,4,16,48]{4,3,2,1,0:T(8,128)(2,1)} custom-call(s32[3]{0:T(128)S(1)} %pad_add_fusion.place, bf16[4,2,144,128]{3,2,1,0:T(8,128)(2,1)S(1)} %basis.1.weights, bf16[128,128]{1,0:T(8,128)(2,1)S(1)} %get-tuple-element.14.refs_0_, bf16[128,128]{1,0:T(8,128)(2,1)S(1)} %collective-permute-done.3.refs_1_, ...), custom_call_target="tpu_custom_call" | custom-call | flops 75497472 | bytes 262144 | tf_op jit(solution)/shard_map/legendre/pallas_call | solution.py:225
  (38 shorter events, 0.8 us)
Async XLA Ops:
  0.6 10.0 %copy-start.5 = (s32[1024]{0:T(1024)S(1)}, s32[1024]{0:T(1024)}, u32[]{:S(2)}) copy-start(s32[1024]{0:T(1024)} %param.11) | copy-start | bytes 12292
  3.5 7.1 %copy-start.1 = (bf16[1,8,40,2688]{3,2,1,0:T(8,128)(2,1)S(1)}, bf16[1,8,40,2688]{3,2,1,0:T(8,128)(2,1)}, u32[]{:S(2)}) copy-start(bf16[1,8,40,2688]{3,2,1,0:T(8,128)(2,1)} %param.8) | copy-start | bytes 5160964
  3.5 7.1 %copy-start.4 = (bf16[1024,128]{1,0:T(8,128)(2,1)S(1)}, bf16[1024,128]{1,0:T(8,128)(2,1)}, u32[]{:S(2)}) copy-start(bf16[1024,128]{1,0:T(8,128)(2,1)} %interp.3) | copy-start | bytes 786436
  5.0 12.9 %collective-permute-start = (bf16[128,128]{1,0:T(8,128)(2,1)S(1)}, bf16[128,128]{1,0:T(8,128)(2,1)S(1)}, u32[]{:S(2)}, u32[]{:S(2)}) collective-permute-start(bf16[128,128]{1,0:T(8,128)(2,1)S(1)} %get-tuple-element.11), channel_id=1, source_target_pairs={{0,1},{1,0},{2,3},{3,2},{4,5},{5,4},{6,7},{7,6},{8,9},{9,8},{10,11... | collective-permute-start | bytes 98312 | tf_op jit(solution)/shard_map/ppermute | solution.py:244
  8.1 9.8 %collective-permute-start.1 = (bf16[128,128]{1,0:T(8,128)(2,1)S(1)}, bf16[128,128]{1,0:T(8,128)(2,1)S(1)}, u32[]{:S(2)}, u32[]{:S(2)}) collective-permute-start(bf16[128,128]{1,0:T(8,128)(2,1)S(1)} %get-tuple-element.12), channel_id=1, source_target_pairs={{0,2},{1,3},{2,0},{3,1},{4,6},{5,7},{6,4},{7,5},{8,10},{9,11},{10,... | collective-permute-start | bytes 98312 | tf_op jit(solution)/shard_map/ppermute | solution.py:244
  10.7 8.9 %collective-permute-start.2 = (bf16[128,128]{1,0:T(8,128)(2,1)S(1)}, bf16[128,128]{1,0:T(8,128)(2,1)S(1)}, u32[]{:S(2)}, u32[]{:S(2)}) collective-permute-start(bf16[128,128]{1,0:T(8,128)(2,1)S(1)} %get-tuple-element.13), channel_id=1, source_target_pairs={{0,3},{1,2},{2,1},{3,0},{4,7},{5,6},{6,5},{7,4},{8,11},{9,10},{10,... | collective-permute-start | bytes 98312 | tf_op jit(solution)/shard_map/ppermute | solution.py:244
  10.7 16.4 %copy-start.3 = (bf16[6,160,48]{1,2,0:T(8,128)(2,1)S(1)}, bf16[6,160,48]{1,2,0:T(8,128)(2,1)}, u32[]{:S(2)}) copy-start(bf16[6,160,48]{1,2,0:T(8,128)(2,1)} %param.9) | copy-start | bytes 276484
  10.7 16.6 %copy-start.7 = (bf16[64,32,32]{0,2,1:T(8,128)(2,1)S(1)}, bf16[64,32,32]{0,2,1:T(8,128)(2,1)}, u32[]{:S(2)}) copy-start(bf16[64,32,32]{0,2,1:T(8,128)(2,1)} %param.14) | copy-start | bytes 393220
  13.4 14.7 %copy-start.8 = (bf16[64,2048]{1,0:T(8,128)(2,1)S(1)}, bf16[64,2048]{1,0:T(8,128)(2,1)}, u32[]{:S(2)}) copy-start(bf16[64,2048]{1,0:T(8,128)(2,1)} %param.13) | copy-start | bytes 786436
  13.4 23.1 %copy-start.6 = (s32[4]{0:T(128)S(1)}, s32[4]{0:T(128)}, u32[]{:S(2)}) copy-start(s32[4]{0:T(128)} %counts.1) | copy-start | bytes 52
  13.4 6.8 %collective-permute-start.10 = (bf16[8,1024]{1,0:T(8,128)(2,1)S(1)}, bf16[8,1024]{1,0:T(8,128)(2,1)S(1)}, u32[]{:S(2)}, u32[]{:S(2)}) collective-permute-start(bf16[8,1024]{1,0:T(8,128)(2,1)S(1)} %pick.1.refs_0_), channel_id=1, source_target_pairs={{0,1},{1,0},{2,3},{3,2},{16,17},{17,16},{18,19},{19,18},{4,5},{5,4... | collective-permute-start | bytes 49160 | tf_op jit(solution)/shard_map/ppermute | solution.py:244
  14.4 7.5 %collective-permute-start.11 = (bf16[8,1024]{1,0:T(8,128)(2,1)S(1)}, bf16[8,1024]{1,0:T(8,128)(2,1)S(1)}, u32[]{:S(2)}, u32[]{:S(2)}) collective-permute-start(bf16[8,1024]{1,0:T(8,128)(2,1)S(1)} %pick.1.refs_0_), channel_id=1, source_target_pairs={{0,2},{1,3},{2,0},{3,1},{16,18},{17,19},{18,16},{19,17},{4,6},{5,7... | collective-permute-start | bytes 49160 | tf_op jit(solution)/shard_map/ppermute | solution.py:244
  17.9 5.5 %collective-permute-start.12 = (bf16[8,1024]{1,0:T(8,128)(2,1)S(1)}, bf16[8,1024]{1,0:T(8,128)(2,1)S(1)}, u32[]{:S(2)}, u32[]{:S(2)}) collective-permute-start(bf16[8,1024]{1,0:T(8,128)(2,1)S(1)} %pick.1.refs_0_), channel_id=1, source_target_pairs={{0,3},{1,2},{2,1},{3,0},{16,19},{17,18},{18,17},{19,16},{4,7},{5,6... | collective-permute-start | bytes 49160 | tf_op jit(solution)/shard_map/ppermute | solution.py:244
  17.9 9.0 %collective-permute-start.13 = (bf16[8,1024]{1,0:T(8,128)(2,1)S(1)}, bf16[8,1024]{1,0:T(8,128)(2,1)S(1)}, u32[]{:S(2)}, u32[]{:S(2)}) collective-permute-start(bf16[8,1024]{1,0:T(8,128)(2,1)S(1)} %pick.1.refs_0_), channel_id=1, source_target_pairs={{0,16},{1,17},{2,18},{3,19},{16,0},{17,1},{18,2},{19,3},{4,20},{5,... | collective-permute-start | bytes 49160 | tf_op jit(solution)/shard_map/ppermute | solution.py:244
  20.1 13.2 %collective-permute-start.3 = (bf16[128,128]{1,0:T(8,128)(2,1)S(1)}, bf16[128,128]{1,0:T(8,128)(2,1)S(1)}, u32[]{:S(2)}, u32[]{:S(2)}) collective-permute-start(bf16[128,128]{1,0:T(8,128)(2,1)S(1)} %get-tuple-element.15), channel_id=1, source_target_pairs={{0,4},{4,0},{8,12},{12,8},{16,20},{20,16},{24,28},{28,24},{1,5},{5... | collective-permute-start | bytes 98312 | tf_op jit(solution)/shard_map/ppermute | solution.py:244
  20.2 14.9 %collective-permute-start.4 = (bf16[128,128]{1,0:T(8,128)(2,1)S(1)}, bf16[128,128]{1,0:T(8,128)(2,1)S(1)}, u32[]{:S(2)}, u32[]{:S(2)}) collective-permute-start(bf16[128,128]{1,0:T(8,128)(2,1)S(1)} %get-tuple-element.16), channel_id=1, source_target_pairs={{0,8},{4,12},{8,0},{12,4},{16,24},{20,28},{24,16},{28,20},{1,9},{5... | collective-permute-start | bytes 98312 | tf_op jit(solution)/shard_map/ppermute | solution.py:244
  21.8 6.6 %collective-permute-start.14 = (bf16[8,1024]{1,0:T(8,128)(2,1)S(1)}, bf16[8,1024]{1,0:T(8,128)(2,1)S(1)}, u32[]{:S(2)}, u32[]{:S(2)}) collective-permute-start(bf16[8,1024]{1,0:T(8,128)(2,1)S(1)} %pick.1.refs_0_), channel_id=1, source_target_pairs={{0,17},{1,16},{2,19},{3,18},{16,1},{17,0},{18,3},{19,2},{4,21},{5,... | collective-permute-start | bytes 49160 | tf_op jit(solution)/shard_map/ppermute | solution.py:244
  23.4 5.7 %collective-permute-start.15 = (bf16[8,1024]{1,0:T(8,128)(2,1)S(1)}, bf16[8,1024]{1,0:T(8,128)(2,1)S(1)}, u32[]{:S(2)}, u32[]{:S(2)}) collective-permute-start(bf16[8,1024]{1,0:T(8,128)(2,1)S(1)} %pick.1.refs_0_), channel_id=1, source_target_pairs={{0,18},{1,19},{2,16},{3,17},{16,2},{17,3},{18,0},{19,1},{4,22},{5,... | collective-permute-start | bytes 49160 | tf_op jit(solution)/shard_map/ppermute | solution.py:244
  26.9 6.4 %collective-permute-start.16 = (bf16[8,1024]{1,0:T(8,128)(2,1)S(1)}, bf16[8,1024]{1,0:T(8,128)(2,1)S(1)}, u32[]{:S(2)}, u32[]{:S(2)}) collective-permute-start(bf16[8,1024]{1,0:T(8,128)(2,1)S(1)} %pick.1.refs_0_), channel_id=1, source_target_pairs={{0,19},{1,18},{2,17},{3,16},{16,3},{17,2},{18,1},{19,0},{4,23},{5,... | collective-permute-start | bytes 49160 | tf_op jit(solution)/shard_map/ppermute | solution.py:244
  28.4 15.0 %collective-permute-start.7 = (bf16[128,128]{1,0:T(8,128)(2,1)S(1)}, bf16[128,128]{1,0:T(8,128)(2,1)S(1)}, u32[]{:S(2)}, u32[]{:S(2)}) collective-permute-start(bf16[128,128]{1,0:T(8,128)(2,1)S(1)} %get-tuple-element.15), channel_id=1, source_target_pairs={{0,20},{4,16},{8,28},{12,24},{16,4},{20,0},{24,12},{28,8},{1,21},{... | collective-permute-start | bytes 98312 | tf_op jit(solution)/shard_map/ppermute | solution.py:244
  29.1 14.3 %collective-permute-start.8 = (bf16[128,128]{1,0:T(8,128)(2,1)S(1)}, bf16[128,128]{1,0:T(8,128)(2,1)S(1)}, u32[]{:S(2)}, u32[]{:S(2)}) collective-permute-start(bf16[128,128]{1,0:T(8,128)(2,1)S(1)} %get-tuple-element.16), channel_id=1, source_target_pairs={{0,24},{4,28},{8,16},{12,20},{16,8},{20,12},{24,0},{28,4},{1,25},{... | collective-permute-start | bytes 98312 | tf_op jit(solution)/shard_map/ppermute | solution.py:244
  33.3 10.1 %collective-permute-start.5 = (bf16[128,128]{1,0:T(8,128)(2,1)S(1)}, bf16[128,128]{1,0:T(8,128)(2,1)S(1)}, u32[]{:S(2)}, u32[]{:S(2)}) collective-permute-start(bf16[128,128]{1,0:T(8,128)(2,1)S(1)} %get-tuple-element.17), channel_id=1, source_target_pairs={{0,12},{4,8},{8,4},{12,0},{16,28},{20,24},{24,20},{28,16},{1,13},{... | collective-permute-start | bytes 98312 | tf_op jit(solution)/shard_map/ppermute | solution.py:244
  33.3 10.1 %collective-permute-start.9 = (bf16[128,128]{1,0:T(8,128)(2,1)S(1)}, bf16[128,128]{1,0:T(8,128)(2,1)S(1)}, u32[]{:S(2)}, u32[]{:S(2)}) collective-permute-start(bf16[128,128]{1,0:T(8,128)(2,1)S(1)} %get-tuple-element.17), channel_id=1, source_target_pairs={{0,28},{4,24},{8,20},{12,16},{16,12},{20,8},{24,4},{28,0},{1,29},{... | collective-permute-start | bytes 98312 | tf_op jit(solution)/shard_map/ppermute | solution.py:244
  35.2 8.3 %collective-permute-start.6 = (bf16[128,128]{1,0:T(8,128)(2,1)S(1)}, bf16[128,128]{1,0:T(8,128)(2,1)S(1)}, u32[]{:S(2)}, u32[]{:S(2)}) collective-permute-start(bf16[128,128]{1,0:T(8,128)(2,1)S(1)} %get-tuple-element.14.refs_0_), channel_id=1, source_target_pairs={{0,16},{4,20},{8,24},{12,28},{16,0},{20,4},{24,8},{28,12},{1,17},{... | collective-permute-start | bytes 98312 | tf_op jit(solution)/shard_map/ppermute | solution.py:244
  (2 other events, 2.8 us)

commit v2 on v1

--- a/solution.py
+++ b/solution.py
@@ -22,8 +22,8 @@
 def dft_table(lon, wave_dev, n_band, n_fld):
     values_dev = 2 * wave_dev
     rest = values_dev // THIRDS
-    third, fld, band, low = np.meshgrid(
-        np.arange(THIRDS), np.arange(n_fld), np.arange(n_band), np.arange(rest), indexing="ij"
+    third, band, fld, low = np.meshgrid(
+        np.arange(THIRDS), np.arange(n_band), np.arange(n_fld), np.arange(rest), indexing="ij"
     )
     value = third * rest + low
     wave = ((band * n_fld + fld) * wave_dev + value // 2).reshape(-1)
@@ -34,8 +34,7 @@
     return values.astype(np.float32).astype(BF16)
 
 
-def dft_kernel(lev, lat, n_fld, place, grid, table, *refs):
-    outs, (padded, rows) = refs[:n_fld], refs[n_fld:]
+def dft_kernel(lev, lat, n_sec, n_band, n_fld, grid, table, out, padded, rows):
     coeffs = jnp.dot(grid[...], table[...], preferred_element_type=F32)
     group = coeffs.shape[1] // THIRDS
     padded[...] = jnp.zeros_like(padded)
@@ -46,19 +45,10 @@
                 :, third * group : (third + 1) * group
             ]
         rows[pl.ds(level, group, stride=lev), :] = jnp.transpose(padded[...])[:group]
-    size = outs[0].shape[0]
-    for shift in range(n_fld):
-        start = pl.multiple_of((place[0] ^ shift) * size, size)
-        outs[shift][...] = rows[pl.ds(start, size), :].astype(BF16)
-
-
-def regroup_kernel(n_fld, n_band, place, *refs):
-    pieces, outs = refs[:n_fld], refs[n_fld:]
-    size = outs[0].shape[0] // n_fld
-    for shift in range(n_band):
-        start = pl.multiple_of((place[1] ^ shift) * size, size)
-        for piece in range(n_fld):
-            outs[shift][piece * size : (piece + 1) * size, :] = pieces[piece][pl.ds(start, size), :]
+    size = out.shape[1]
+    values = rows[...].astype(BF16).reshape(n_band * n_fld, size, LANES)
+    for sec in range(n_sec):
+        out[sec * n_band * n_fld : (sec + 1) * n_band * n_fld] = values
 
 
 def spread_kernel(lat, n_band, legendre, out, wide):
@@ -80,29 +70,23 @@
             ).astype(BF16)
 
 
-def legendre_kernel(n_sec, n_band, n_fld, lev, place, weights, *refs):
-    pieces, out = refs[: n_sec * n_band], refs[n_sec * n_band]
+def legendre_kernel(n_sec, n_band, n_fld, lev, weights, pieces, out):
     degrees = out.shape[4]
-    size = pieces[0].shape[0] // n_fld
-    half = size // 2
-    first = place[2] == 0
+    half = pieces.shape[1] // 2
     for parity in range(2):
-        basis = jnp.concatenate(
-            [weights[place[1] ^ shift, parity] for shift in range(n_band)], axis=1
-        )
+        rows = slice(parity * half, (parity + 1) * half)
+        basis = jnp.concatenate([weights[band, parity] for band in range(n_band)], axis=1)
         left = jnp.concatenate(
             [
                 jnp.concatenate(
                     [
-                        pieces[sec * n_band + shift][
-                            fld * size + parity * half : fld * size + (parity + 1) * half, :
-                        ]
-                        for shift in range(n_band)
+                        pieces[(sec * n_band + band) * n_fld + fld, rows, :]
+                        for band in range(n_band)
                     ],
                     axis=1,
                 )
+                for fld in range(n_fld)
                 for sec in range(n_sec)
-                for fld in range(n_fld)
             ],
             axis=0,
         )
@@ -111,13 +95,13 @@
             part = result[:, third * degrees : (third + 1) * degrees]
             for fld in range(n_fld):
                 for real in range(2):
-                    near = part[fld * half + real * lev : fld * half + (real + 1) * lev]
-                    base = (n_fld + fld) * half + real * lev
-                    far = part[base : base + lev]
-                    levels = jnp.concatenate(
-                        [jnp.where(first, near, far), jnp.where(first, far, near)], axis=0
+                    levels = [
+                        part[(fld * n_sec + sec) * half + real * lev :][:lev]
+                        for sec in range(n_sec)
+                    ]
+                    out[2 * third + parity, real, fld] = jnp.concatenate(levels, axis=0).astype(
+                        BF16
                     )
-                    out[2 * third + parity, real, place[0] ^ fld] = levels.astype(BF16)
 
 
 def slot_rows(blocks, across, lat_pad):
@@ -161,7 +145,9 @@
         for level in range(lev):
             product = picked[:, level * LANES : (level + 1) * LANES] * weights
             total = jnp.where(lane == level, jnp.sum(product, axis=1, keepdims=True), total)
-        state[:, start : start + chunk] = jnp.transpose(total)[:lev].astype(BF16)
+        values = jnp.transpose(total)[:lev].astype(BF16)
+        for copy in range(state.shape[0]):
+            state[copy, :, start : start + chunk] = values
 
 
 def softplus(x):
@@ -170,15 +156,13 @@
     return jnp.maximum(x, 0.0) + tail
 
 
-def column_kernel(n_sec, n_fld, lat_pad, place, counts, weights, inverses, blocks, interp, *refs):
-    pieces = refs[: n_sec * n_fld]
-    out, state, flux_up, flux_down = refs[n_sec * n_fld :]
-    lev = pieces[0].shape[0]
-    slots = pieces[0].shape[1]
-    for sec in range(n_sec):
-        for fld in range(n_fld):
-            row = ((place[0] ^ fld) * n_sec + (place[2] ^ sec)) * lev
-            state[pl.ds(pl.multiple_of(row, lev), lev), :] = pieces[sec * n_fld + fld][...].astype(F32)
+def column_kernel(n_sec, n_fld, lat_pad, place, counts, weights, inverses, blocks, interp, pieces,
+                  out, state, flux_up, flux_down):
+    lev, slots = pieces.shape[1:]
+    for fld in range(n_fld):
+        for sec in range(n_sec):
+            row = (fld * n_sec + sec) * lev
+            state[row : row + lev, :] = pieces[sec * n_fld + fld].astype(F32)
     column = state[...].astype(BF16)
     flux_rows = inverses.shape[0]
     flux = jnp.zeros((flux_rows, slots), F32)
@@ -234,16 +218,6 @@
     )(*args)
 
 
-def exchange(value, axes, shifts):
-    sizes = [lax.axis_size(axis) for axis in axes]
-    pairs = []
-    for i in range(math.prod(sizes)):
-        at = np.unravel_index(i, sizes)
-        to = tuple(int(a) ^ s for a, s in zip(at, shifts))
-        pairs.append((i, int(np.ravel_multi_index(to, sizes))))
-    return lax.ppermute(value, axes, pairs)
-
-
 def body(grid, legendre, counts, blocks, interp, source_weights, inverses):
     n_sec = lax.axis_size("sec")
     n_band = lax.axis_size("band")
@@ -263,22 +237,21 @@
     table = jnp.asarray(dft_table(lon, wave_dev, n_band, n_fld))
     group = n_fld * n_band * rest
     padded_group = -(-group // LANES) * LANES
+    devices = n_sec * n_band * n_fld
     sent = call(
-        functools.partial(dft_kernel, lev, lat, n_fld),
-        [((n_band * piece, LANES), BF16)] * n_fld,
-        [SMEM, VMEM, VMEM],
+        functools.partial(dft_kernel, lev, lat, n_sec, n_band, n_fld),
+        [((devices, piece, LANES), BF16)],
+        [VMEM, VMEM],
         [pltpu.VMEM((LANES, padded_group), F32), pltpu.VMEM((group * lev, LANES), F32)],
-        (place, grid.reshape(lev * lat, lon), table),
+        (grid.reshape(lev * lat, lon), table),
         2 * lev * lat * lon * THIRDS * group,
         2 * lon * (lev * lat + THIRDS * group),
         "fourier",
     )
-    fields = [sent[0]] + [exchange(sent[d], ("fld",), (d,)) for d in range(1, n_fld)]
-
     depth = -(-across * lat_pad // LANES) * LANES
     state = call(
         functools.partial(pick_kernel, lat_pad),
-        [((lev, slots), BF16)],
+        [((n_sec * n_fld, lev, slots), BF16)],
         [VMEM, VMEM, VMEM],
         [pltpu.VMEM((depth, lev * LANES), BF16), pltpu.VMEM((slots, LANES), jnp.int32)],
         (grid.reshape(lev, lat, lon), block_row, interp),
@@ -286,12 +259,8 @@
         2 * lev * lat * lon + 2 * slots * LANES,
         "pick",
     )
-    columns = [
-        state if sec == 0 and fld == 0 else exchange(state, ("sec", "fld"), (sec, fld))
-        for sec in range(n_sec)
-        for fld in range(n_fld)
-    ]
-
+    columns = lax.all_to_all(state, ("sec", "fld"), 0, 0, tiled=True)
+    pieces = lax.all_to_all(sent, ("sec", "band", "fld"), 0, 0, tiled=True)
     basis = call(
         functools.partial(spread_kernel, lat, n_band),
         [((n_band, 2, THIRDS * degrees, LANES), BF16)],
@@ -302,27 +271,12 @@
         8 * wave_dev * degrees * n_band * LANES,
         "basis",
     )
-    grouped = call(
-        functools.partial(regroup_kernel, n_fld, n_band),
-        [((n_fld * piece, LANES), BF16)] * n_band,
-        [SMEM] + [VMEM] * n_fld,
-        [],
-        (place, *fields),
-        0,
-        4 * n_fld * n_band * piece * LANES,
-        "regroup",
-    )
-    bands = [
-        grouped[0] if sec == 0 and band == 0 else exchange(grouped[band], ("sec", "band"), (sec, band))
-        for sec in range(n_sec)
-        for band in range(n_band)
-    ]
 
     spec_bands, flux_rows, _ = inverses.shape
     heating = call(
         functools.partial(column_kernel, n_sec, n_fld, lat_pad),
         [((n_sec * lev // (n_sec * n_fld), lat, lon), BF16)],
-        [SMEM, SMEM] + [VMEM] * (4 + n_sec * n_fld),
+        [SMEM, SMEM] + [VMEM] * 5,
         [
             pltpu.VMEM((n_sec * n_fld * lev, slots), F32),
             pltpu.VMEM((flux_rows // 2 + 8, slots), F32),
@@ -335,7 +289,7 @@
             jnp.transpose(inverses, (1, 0, 2)).reshape(flux_rows, spec_bands * flux_rows),
             block_row,
             interp,
-            *columns,
+            columns,
         ),
         8 * slots * slots * 1024,
         2 * slots * slots,
@@ -345,9 +299,9 @@
     spectral = call(
         functools.partial(legendre_kernel, n_sec, n_band, n_fld, lev),
         [((wave_dev, 2, n_fld, n_sec * lev, degrees), BF16)],
-        [SMEM] + [VMEM] * (1 + n_sec * n_band),
+        [VMEM, VMEM],
         [],
-        (place, basis, *bands),
+        (basis, pieces),
         4 * n_sec * n_fld * piece * n_band * LANES * degrees * THIRDS,
         2 * n_sec * n_band * n_fld * piece * LANES,
         "legendre",

time: 45.2 us -> 39.5 us (0.87)
  starting transfers between devices: 23.5 us -> 13 us
  local copies, waits for them, and re-layouts: 3.92 us -> 11.1 us
  waiting for transfers between devices: 3.43 us -> 1.4 us
  Pallas kernels: 13.3 us -> 12.7 us
    ppermute x17 -> x0, starting transfers between devices: 23.5 us -> none  [exchange(): return lax.ppermute(value, axes, pairs)]
    all_to_all x0 -> x2, starting transfers between devices: none -> 13 us  [the longest x1 7.39 us: body(): columns = lax.all_to_all(state, ('sec', 'fld'), 0, 0, tiled=True)]
    unnamed x19 -> x27, local copies, waits for them, and re-layouts: 3.1 us -> 7.76 us
    ppermute x17 -> x0, waiting for transfers between devices: 3.43 us -> none  [exchange(): return lax.ppermute(value, axes, pairs)]
    reshape x1, local copies, waits for them, and re-layouts: 0.54 us -> 2.29 us  [body(): jnp.transpose(inverses, (1, 0, 2))]
    all_to_all x0 -> x2, waiting for transfers between devices: none -> 1.4 us  [the longest x1 1 us: body(): pieces = lax.all_to_all(sent, ('sec', 'band', 'fld'), 0, 0, tiled=True)]
    transpose x1, local copies, waits for them, and re-layouts: 0.28 us -> 1.02 us  [body(): jnp.transpose(inverses, (1, 0, 2))]
    pallas_call x6 -> x5, Pallas kernels: 13.3 us -> 12.7 us  [call(): pl.pallas_call(kernel, out_shape=shapes[0] if single else shapes, in_spec...]
  transfers between devices with their start and end apart: 17 -> 2, of which waited for: 3 -> 2; matrix products, arithmetic and copies ran while one was open for 2% -> 14% of each run, Pallas kernels for 23% -> 21%
where the time goes in v2:
time: 39.5 us; the launch traced here: 39 us
  starting transfers between devices  13 us (33%)
  Pallas kernels  12.7 us (32%)
  local copies, waits for them, and re-layouts  11.1 us (28%)
  waiting for transfers between devices  1.4 us (4%)
  between operations  0.76 us (2%)
    pallas_call x5, Pallas kernels, call(): pl.pallas_call(kernel, out_shape=shapes[0] if single else shapes, in_spec...  12.7 us
    unnamed x27, local copies, waits for them, and re-layouts  7.76 us
    all_to_all x1, starting transfers between devices, body(): columns = lax.all_to_all(state, ('sec', 'fld'), 0, 0, tiled=True)  7.39 us
    all_to_all x1, starting transfers between devices, body(): pieces = lax.all_to_all(sent, ('sec', 'band', 'fld'), 0, 0, tiled=True)  5.64 us
    reshape x1, local copies, waits for them, and re-layouts, body(): jnp.transpose(inverses, (1, 0, 2))  2.29 us
    transpose x1, local copies, waits for them, and re-layouts, body(): jnp.transpose(inverses, (1, 0, 2))  1.02 us
    all_to_all x1, waiting for transfers between devices, body(): pieces = lax.all_to_all(sent, ('sec', 'band', 'fld'), 0, 0, tiled=True)  1 us
  transfers between devices with their start and end apart: 2, of which 2 were waited for; matrix products, arithmetic and copies ran while one was open for 14% of the time, Pallas kernels for 21%

profile of v2, /device:TPU:0, one launch (start us, length us, event | category | flops | bytes accessed | tf_op | source)
XLA Modules:
  0.0 39.0 jit_solution(4108853549335731346)
XLA Ops:
  0.6 0.0 copy-start
  0.6 1.5 %copy-done = bf16[1,8,40,2688]{3,2,1,0:T(8,128)(2,1)S(1)} copy-done((bf16[1,8,40,2688]{3,2,1,0:T(8,128)(2,1)S(1)}, bf16[1,8,40,2688]{3,2,1,0:T(8,128)(2,1)}, u32[]{:S(2)}) %copy-start) | copy-done | bytes 1720344
  2.1 0.9 %copy-done.7 = bf16[1024,128]{1,0:T(8,128)(2,1)S(1)} copy-done((bf16[1024,128]{1,0:T(8,128)(2,1)S(1)}, bf16[1024,128]{1,0:T(8,128)(2,1)}, u32[]{:S(2)}) %copy-start.7) | copy-done | bytes 262168
  3.0 0.7 %copy-done.9 = s32[1024]{0:T(1024)S(1)} copy-done((s32[1024]{0:T(1024)S(1)}, s32[1024]{0:T(1024)}, u32[]{:S(2)}) %copy-start.9) | copy-done | bytes 4120
  3.7 3.3 %pick.1 = bf16[8,8,1024]{2,1,0:T(8,128)(2,1)} custom-call(bf16[8,40,2688]{2,1,0:T(8,128)(2,1)S(1)} %bitcast.9, s32[1,1024]{1,0:T(1,128)S(1)} %bitcast.13, bf16[1024,128]{1,0:T(8,128)(2,1)S(1)} %copy-done.7), custom_call_target="tpu_custom_call" | custom-call | flops 2147483648 | bytes 1982464 | tf_op jit(solution)/shard_map/pick/pallas_call | solution.py:209
  7.1 7.4 %all-to-all-start.1 = ((bf16[8,8,1024]{2,1,0:T(8,128)(2,1)}), bf16[8,8,1024]{2,1,0:T(8,128)(2,1)}, u32[]{:S(2)}, u32[]{:S(2)}) async-start(bf16[8,8,1024]{2,1,0:T(8,128)(2,1)} %pick.1), calls=%async_computation.1 | async-start | bytes 262144 | tf_op jit(solution)/shard_map/all_to_all | solution.py:262
  14.5 1.0 %copy.13 = bf16[32,64,32]{2,1,0:T(8,128)(2,1)} copy(bf16[32,64,32]{1,2,0:T(8,128)(2,1)S(1)} %bitcast.15) | data formatting | bytes 262144 | tf_op jit(solution)/shard_map/transpose | solution.py:289
  15.5 2.3 %reshape.17.inverses = bf16[32,2048]{1,0:T(8,128)(2,1)} reshape(bf16[32,64,32]{2,1,0:T(8,128)(2,1)} %copy.13) | data formatting | bytes 262144 | tf_op jit(solution)/shard_map/reshape | solution.py:289
  17.8 2.0 %copy.12 = bf16[64,2048]{0,1:T(8,128)(2,1)} copy(bf16[64,2048]{1,0:T(8,128)(2,1)} %param.13) | data formatting | bytes 524288 | tf_op args[5]
  19.7 0.2 basis.1.weights
  20.0 0.0 copy-start.6
  20.0 0.0 copy-start.10
  20.0 0.0 copy-start.11
  20.0 0.9 %fourier.1 = bf16[32,32,128]{2,1,0:T(8,128)(2,1)S(1)} custom-call(bf16[320,2688]{1,0:T(8,128)(2,1)S(1)} %bitcast.10, bf16[2688,192]{1,0:T(8,128)(2,1)S(1)} %copy-done.2), custom_call_target="tpu_custom_call" | custom-call | flops 330301440 | bytes 2752512 | tf_op jit(solution)/shard_map/fourier/pallas_call | solution.py:209
  20.9 0.0 copy-start.3
  20.9 0.7 %copy-done.3 = bf16[32,32,128]{2,1,0:T(8,128)(2,1)} copy-done((bf16[32,32,128]{2,1,0:T(8,128)(2,1)}, bf16[32,32,128]{2,1,0:T(8,128)(2,1)S(1)}, u32[]{:S(2)}) %copy-start.3) | copy-done | bytes 262168
  21.6 0.1 pad_add_fusion.place
  21.7 0.4 %all-to-all-done.1.pieces = bf16[8,8,1024]{2,1,0:T(8,128)(2,1)} async-done(((bf16[8,8,1024]{2,1,0:T(8,128)(2,1)}), bf16[8,8,1024]{2,1,0:T(8,128)(2,1)}, u32[]{:S(2)}, u32[]{:S(2)}) %all-to-all-start.1) | async-done | bytes 131104 | tf_op jit(solution)/shard_map/all_to_all | solution.py:262
  22.1 5.6 %all-to-all-start = ((bf16[32,32,128]{2,1,0:T(8,128)(2,1)}), bf16[32,32,128]{2,1,0:T(8,128)(2,1)S(1)}, u32[]{:S(2)}, u32[]{:S(2)}) async-start(bf16[32,32,128]{2,1,0:T(8,128)(2,1)} %copy-done.3), calls=%async_computation | async-start | bytes 524288 | tf_op jit(solution)/shard_map/all_to_all | solution.py:263
  27.8 1.0 %copy-done.4 = bf16[64,2048]{0,1:T(8,128)(2,1)S(1)} copy-done((bf16[64,2048]{0,1:T(8,128)(2,1)S(1)}, bf16[64,2048]{0,1:T(8,128)(2,1)}, u32[]{:S(2)}) %copy-start.4) | copy-done | bytes 262168
  28.8 0.9 %copy-done.8 = bf16[1024,128]{1,0:T(8,128)(2,1)S(1)} copy-done((bf16[1024,128]{1,0:T(8,128)(2,1)S(1)}, bf16[1024,128]{1,0:T(8,128)(2,1)}, u32[]{:S(2)}) %copy-start.8) | copy-done | bytes 262168
  29.8 7.2 %columns.1 = bf16[2,40,2688]{2,1,0:T(8,128)(2,1)} custom-call(s32[3]{0:T(128)S(1)} %pad_add_fusion.place, s32[4]{0:T(128)S(1)} %copy-done.11, bf16[2048,64]{1,0:T(8,128)(2,1)S(1)} %bitcast.11, bf16[32,2048]{1,0:T(8,128)(2,1)S(1)} %copy-done.6, s32[1,1024]{1,0:T(1,128)S(1)} %bitcast.14, bf16[1024,128]{1,0:T(8,128)(2,1)S(1)} %copy-done.8, ...), custom_call_target="tpu_custom_call" | custom-call | flops 8589934592 | bytes 2097152 | tf_op jit(solution)/shard_map/columns/pallas_call | solution.py:209
  37.0 1.0 %all-to-all-done.pieces = bf16[32,32,128]{2,1,0:T(8,128)(2,1)S(1)} async-done(((bf16[32,32,128]{2,1,0:T(8,128)(2,1)}), bf16[32,32,128]{2,1,0:T(8,128)(2,1)S(1)}, u32[]{:S(2)}, u32[]{:S(2)}) %all-to-all-start) | async-done | bytes 262176 | tf_op jit(solution)/shard_map/all_to_all | solution.py:263
  38.0 1.0 %legendre.1 = bf16[6,2,4,16,48]{4,3,2,1,0:T(8,128)(2,1)} custom-call(bf16[4,2,144,128]{3,2,1,0:T(8,128)(2,1)S(1)} %basis.1.weights, bf16[32,32,128]{2,1,0:T(8,128)(2,1)S(1)} %all-to-all-done.pieces), custom_call_target="tpu_custom_call" | custom-call | flops 75497472 | bytes 262144 | tf_op jit(solution)/shard_map/legendre/pallas_call | solution.py:209
  (15 shorter events, 0.0 us)
Async XLA Ops:
  0.6 1.5 %copy-start = (bf16[1,8,40,2688]{3,2,1,0:T(8,128)(2,1)S(1)}, bf16[1,8,40,2688]{3,2,1,0:T(8,128)(2,1)}, u32[]{:S(2)}) copy-start(bf16[1,8,40,2688]{3,2,1,0:T(8,128)(2,1)} %param.8) | copy-start | bytes 5160964
  2.1 0.9 %copy-start.7 = (bf16[1024,128]{1,0:T(8,128)(2,1)S(1)}, bf16[1024,128]{1,0:T(8,128)(2,1)}, u32[]{:S(2)}) copy-start(bf16[1024,128]{1,0:T(8,128)(2,1)} %interp.3) | copy-start | bytes 786436
  3.0 0.7 %copy-start.9 = (s32[1024]{0:T(1024)S(1)}, s32[1024]{0:T(1024)}, u32[]{:S(2)}) copy-start(s32[1024]{0:T(1024)} %param.11) | copy-start | bytes 12292
  3.7 10.7 %copy-start.12 = (bf16[64,32,32]{0,2,1:T(8,128)(2,1)S(1)}, bf16[64,32,32]{0,2,1:T(8,128)(2,1)}, u32[]{:S(2)}) copy-start(bf16[64,32,32]{0,2,1:T(8,128)(2,1)} %param.14) | copy-start | bytes 393220
  3.7 16.2 %copy-start.2 = (bf16[2688,192]{1,0:T(8,128)(2,1)S(1)}, bf16[2688,192]{1,0:T(8,128)(2,1)}, u32[]{:S(2)}) copy-start(bf16[2688,192]{1,0:T(8,128)(2,1)} %constant.15.clone.table) | copy-start | bytes 3096580
  7.1 12.7 %copy-start.5 = (bf16[6,160,48]{1,2,0:T(8,128)(2,1)S(1)}, bf16[6,160,48]{1,2,0:T(8,128)(2,1)}, u32[]{:S(2)}) copy-start(bf16[6,160,48]{1,2,0:T(8,128)(2,1)} %param.9) | copy-start | bytes 276484
  7.1 12.9 %copy-start.1 = (bf16[1,8,40,2688]{3,2,1,0:T(8,128)(2,1)S(1)}, bf16[1,8,40,2688]{3,2,1,0:T(8,128)(2,1)}, u32[]{:S(2)}) copy-start(bf16[1,8,40,2688]{3,2,1,0:T(8,128)(2,1)} %param.8) | copy-start | bytes 5160964
  7.1 15.0 %all-to-all-start.1 = ((bf16[8,8,1024]{2,1,0:T(8,128)(2,1)}), bf16[8,8,1024]{2,1,0:T(8,128)(2,1)}, u32[]{:S(2)}, u32[]{:S(2)}) async-start(bf16[8,8,1024]{2,1,0:T(8,128)(2,1)} %pick.1), calls=%async_computation.1 | async-start | bytes 262144 | tf_op jit(solution)/shard_map/all_to_all | solution.py:262
  20.0 7.8 %copy-start.6 = (bf16[32,2048]{1,0:T(8,128)(2,1)S(1)}, bf16[32,2048]{1,0:T(8,128)(2,1)}, u32[]{:S(2)}) copy-start(bf16[32,2048]{1,0:T(8,128)(2,1)} %reshape.17.inverses) | copy-start | bytes 393220
  20.0 7.8 %copy-start.10 = (s32[1024]{0:T(1024)S(1)}, s32[1024]{0:T(1024)}, u32[]{:S(2)}) copy-start(s32[1024]{0:T(1024)} %param.11) | copy-start | bytes 12292
  20.0 7.8 %copy-start.11 = (s32[4]{0:T(128)S(1)}, s32[4]{0:T(128)}, u32[]{:S(2)}) copy-start(s32[4]{0:T(128)} %counts.1) | copy-start | bytes 52
  20.9 0.7 %copy-start.3 = (bf16[32,32,128]{2,1,0:T(8,128)(2,1)}, bf16[32,32,128]{2,1,0:T(8,128)(2,1)S(1)}, u32[]{:S(2)}) copy-start(bf16[32,32,128]{2,1,0:T(8,128)(2,1)S(1)} %fourier.1) | copy-start | bytes 786436
  22.1 15.9 %all-to-all-start = ((bf16[32,32,128]{2,1,0:T(8,128)(2,1)}), bf16[32,32,128]{2,1,0:T(8,128)(2,1)S(1)}, u32[]{:S(2)}, u32[]{:S(2)}) async-start(bf16[32,32,128]{2,1,0:T(8,128)(2,1)} %copy-done.3), calls=%async_computation | async-start | bytes 524288 | tf_op jit(solution)/shard_map/all_to_all | solution.py:263
  27.8 1.0 %copy-start.4 = (bf16[64,2048]{0,1:T(8,128)(2,1)S(1)}, bf16[64,2048]{0,1:T(8,128)(2,1)}, u32[]{:S(2)}) copy-start(bf16[64,2048]{0,1:T(8,128)(2,1)} %copy.12) | copy-start | bytes 786436
  28.8 0.9 %copy-start.8 = (bf16[1024,128]{1,0:T(8,128)(2,1)S(1)}, bf16[1024,128]{1,0:T(8,128)(2,1)}, u32[]{:S(2)}) copy-start(bf16[1024,128]{1,0:T(8,128)(2,1)} %interp.3) | copy-start | bytes 786436

commit v3 on v2

--- a/solution.py
+++ b/solution.py
@@ -145,9 +145,7 @@
         for level in range(lev):
             product = picked[:, level * LANES : (level + 1) * LANES] * weights
             total = jnp.where(lane == level, jnp.sum(product, axis=1, keepdims=True), total)
-        values = jnp.transpose(total)[:lev].astype(BF16)
-        for copy in range(state.shape[0]):
-            state[copy, :, start : start + chunk] = values
+        state[0, :, start : start + chunk] = jnp.transpose(total)[:lev].astype(BF16)
 
 
 def softplus(x):
@@ -251,7 +249,7 @@
     depth = -(-across * lat_pad // LANES) * LANES
     state = call(
         functools.partial(pick_kernel, lat_pad),
-        [((n_sec * n_fld, lev, slots), BF16)],
+        [((1, lev, slots), BF16)],
         [VMEM, VMEM, VMEM],
         [pltpu.VMEM((depth, lev * LANES), BF16), pltpu.VMEM((slots, LANES), jnp.int32)],
         (grid.reshape(lev, lat, lon), block_row, interp),
@@ -259,7 +257,7 @@
         2 * lev * lat * lon + 2 * slots * LANES,
         "pick",
     )
-    columns = lax.all_to_all(state, ("sec", "fld"), 0, 0, tiled=True)
+    columns = lax.all_gather(state, ("sec", "fld"), axis=0, tiled=True)
     pieces = lax.all_to_all(sent, ("sec", "band", "fld"), 0, 0, tiled=True)
     basis = call(
         functools.partial(spread_kernel, lat, n_band),

time: 39.5 us -> 55.7 us (1.41)
  blocking collectives: 0 us -> 31.1 us
  local copies, waits for them, and re-layouts: 11.1 us -> 3.91 us
  starting transfers between devices: 13 us -> 7.3 us
  waiting for transfers between devices: 1.4 us -> 0.01 us
    all_gather x0 -> x1, blocking collectives: none -> 31.1 us  [body(): columns = lax.all_gather(state, ('sec', 'fld'), axis=0, tiled=True)]
    all_to_all x1 -> x0, starting transfers between devices: 7.39 us -> none  [body(): columns = lax.all_to_all(state, ('sec', 'fld'), 0, 0, tiled=True)]
    unnamed x27 -> x19, local copies, waits for them, and re-layouts: 7.76 us -> 3.09 us
    reshape x1, local copies, waits for them, and re-layouts: 2.29 us -> 0.54 us  [body(): jnp.transpose(inverses, (1, 0, 2))]
    all_to_all x1, starting transfers between devices: 5.64 us -> 7.3 us  [body(): pieces = lax.all_to_all(sent, ('sec', 'band', 'fld'), 0, 0, tiled=True)]
    all_to_all x1, waiting for transfers between devices: 1 us -> 0.01 us  [body(): pieces = lax.all_to_all(sent, ('sec', 'band', 'fld'), 0, 0, tiled=True)]
    transpose x1, local copies, waits for them, and re-layouts: 1.02 us -> 0.28 us  [body(): jnp.transpose(inverses, (1, 0, 2))]
  transfers between devices with their start and end apart: 2 -> 1, of which waited for: 2 -> 0; matrix products, arithmetic and copies ran while one was open for 14% -> 2% of each run, Pallas kernels for 21% -> 17%
where the time goes in v3:
time: 55.7 us; the launch traced here: 55.5 us
  blocking collectives  31.1 us (56%)
  Pallas kernels  12.3 us (22%)
  starting transfers between devices  7.3 us (13%)
  local copies, waits for them, and re-layouts  3.91 us (7%)
  between operations  0.74 us (1%)
    all_gather x1, blocking collectives, body(): columns = lax.all_gather(state, ('sec', 'fld'), axis=0, tiled=True)  31.1 us
    pallas_call x5, Pallas kernels, call(): pl.pallas_call(kernel, out_shape=shapes[0] if single else shapes, in_spec...  12.3 us
    all_to_all x1, starting transfers between devices, body(): pieces = lax.all_to_all(sent, ('sec', 'band', 'fld'), 0, 0, tiled=True)  7.3 us
    unnamed x19, local copies, waits for them, and re-layouts  3.09 us
  transfers between devices with their start and end apart: 1, of which 0 were waited for; matrix products, arithmetic and copies ran while one was open for 2% of the time, Pallas kernels for 17%

profile of v3, /device:TPU:0, one launch (start us, length us, event | category | flops | bytes accessed | tf_op | source)
XLA Modules:
  0.0 55.5 jit_solution(7272233332110302795)
XLA Ops:
  0.6 0.0 copy-start
  0.6 1.5 %copy-done = bf16[1,8,40,2688]{3,2,1,0:T(8,128)(2,1)S(1)} copy-done((bf16[1,8,40,2688]{3,2,1,0:T(8,128)(2,1)S(1)}, bf16[1,8,40,2688]{3,2,1,0:T(8,128)(2,1)}, u32[]{:S(2)}) %copy-start) | copy-done | bytes 1720344
  2.1 0.0 copy-start.2
  2.1 1.3 %copy-done.2 = bf16[2688,192]{1,0:T(8,128)(2,1)S(1)} copy-done((bf16[2688,192]{1,0:T(8,128)(2,1)S(1)}, bf16[2688,192]{1,0:T(8,128)(2,1)}, u32[]{:S(2)}) %copy-start.2) | copy-done | bytes 1032216
  3.4 1.6 %fourier.1 = bf16[32,32,128]{2,1,0:T(8,128)(2,1)} custom-call(bf16[320,2688]{1,0:T(8,128)(2,1)S(1)} %bitcast.9, bf16[2688,192]{1,0:T(8,128)(2,1)S(1)} %copy-done.2), custom_call_target="tpu_custom_call" | custom-call | flops 330301440 | bytes 2752512 | tf_op jit(solution)/shard_map/fourier/pallas_call | solution.py:207
  5.1 7.3 %all-to-all-start = ((bf16[32,32,128]{2,1,0:T(8,128)(2,1)}), bf16[32,32,128]{2,1,0:T(8,128)(2,1)S(1)}, u32[]{:S(2)}, u32[]{:S(2)}) async-start(bf16[32,32,128]{2,1,0:T(8,128)(2,1)} %fourier.1), calls=%async_computation | async-start | bytes 524288 | tf_op jit(solution)/shard_map/all_to_all | solution.py:261
  12.4 0.0 copy-done.1
  12.4 0.0 copy-done.4
  12.4 0.0 copy-done.5
  12.4 0.0 copy-start.7
  12.4 2.7 %pick.1 = bf16[1,8,1024]{2,1,0:T(8,128)(2,1)S(1)} custom-call(bf16[8,40,2688]{2,1,0:T(8,128)(2,1)S(1)} %bitcast.10, s32[1,1024]{1,0:T(1,128)S(1)} %bitcast.13, bf16[1024,128]{1,0:T(8,128)(2,1)S(1)} %copy-done.4), custom_call_target="tpu_custom_call" | custom-call | flops 2147483648 | bytes 1982464 | tf_op jit(solution)/shard_map/pick/pallas_call | solution.py:207
  15.1 31.1 %all_gather.3.pieces = bf16[8,8,1024]{2,1,0:T(8,128)(2,1)S(1)} all-gather(bf16[1,8,1024]{2,1,0:T(8,128)(2,1)S(1)} %pick.1), channel_id=1, replica_groups=mesh['sec'=2,'band'=4,'fld'=4] {'sec','fld'}, dimensions={0}, use_global_device_ids=true | all-gather | bytes 147456 | tf_op jit(solution)/shard_map/all_gather | solution.py:260
  46.2 0.0 copy-done.7
  46.2 0.3 copy.15
  46.5 0.5 reshape.17.inverses
  47.0 0.0 copy-done.8
  47.0 0.3 copy.14
  47.3 0.0 copy-done.3
  47.3 0.2 basis.1.weights
  47.5 0.1 pad_add_fusion.place
  47.6 0.0 copy-done.6
  47.6 6.8 %columns.1 = bf16[2,40,2688]{2,1,0:T(8,128)(2,1)} custom-call(s32[3]{0:T(128)S(1)} %pad_add_fusion.place, s32[4]{0:T(128)S(1)} %copy-done.6, bf16[2048,64]{1,0:T(8,128)(2,1)S(1)} %bitcast.11, bf16[32,2048]{1,0:T(8,128)(2,1)S(1)} %reshape.17.inverses, s32[1,1024]{1,0:T(1,128)S(1)} %bitcast.14, bf16[1024,128]{1,0:T(8,128)(2,1)S(1)} %copy-done.4, ...), custom_call_target="tpu_custom_call" | custom-call | flops 8589934592 | bytes 2097152 | tf_op jit(solution)/shard_map/columns/pallas_call | solution.py:207
  54.5 0.0 all-to-all-done.pieces
  54.5 1.0 %legendre.1 = bf16[6,2,4,16,48]{4,3,2,1,0:T(8,128)(2,1)} custom-call(bf16[4,2,144,128]{3,2,1,0:T(8,128)(2,1)S(1)} %basis.1.weights, bf16[32,32,128]{2,1,0:T(8,128)(2,1)S(1)} %all-to-all-done.pieces), custom_call_target="tpu_custom_call" | custom-call | flops 75497472 | bytes 262144 | tf_op jit(solution)/shard_map/legendre/pallas_call | solution.py:207
  (6 shorter events, 0.0 us)
Async XLA Ops:
  0.6 1.5 %copy-start = (bf16[1,8,40,2688]{3,2,1,0:T(8,128)(2,1)S(1)}, bf16[1,8,40,2688]{3,2,1,0:T(8,128)(2,1)}, u32[]{:S(2)}) copy-start(bf16[1,8,40,2688]{3,2,1,0:T(8,128)(2,1)} %param.8) | copy-start | bytes 5160964
  2.1 1.3 %copy-start.2 = (bf16[2688,192]{1,0:T(8,128)(2,1)S(1)}, bf16[2688,192]{1,0:T(8,128)(2,1)}, u32[]{:S(2)}) copy-start(bf16[2688,192]{1,0:T(8,128)(2,1)} %constant.15.clone.table) | copy-start | bytes 3096580
  3.4 8.9 %copy-start.1 = (bf16[1,8,40,2688]{3,2,1,0:T(8,128)(2,1)S(1)}, bf16[1,8,40,2688]{3,2,1,0:T(8,128)(2,1)}, u32[]{:S(2)}) copy-start(bf16[1,8,40,2688]{3,2,1,0:T(8,128)(2,1)} %param.8) | copy-start | bytes 5160964
  3.4 8.9 %copy-start.4 = (bf16[1024,128]{1,0:T(8,128)(2,1)S(1)}, bf16[1024,128]{1,0:T(8,128)(2,1)}, u32[]{:S(2)}) copy-start(bf16[1024,128]{1,0:T(8,128)(2,1)} %interp.3) | copy-start | bytes 786436
  3.4 9.0 %copy-start.5 = (s32[1024]{0:T(1024)S(1)}, s32[1024]{0:T(1024)}, u32[]{:S(2)}) copy-start(s32[1024]{0:T(1024)} %param.11) | copy-start | bytes 12292
  5.1 49.4 %all-to-all-start = ((bf16[32,32,128]{2,1,0:T(8,128)(2,1)}), bf16[32,32,128]{2,1,0:T(8,128)(2,1)S(1)}, u32[]{:S(2)}, u32[]{:S(2)}) async-start(bf16[32,32,128]{2,1,0:T(8,128)(2,1)} %fourier.1), calls=%async_computation | async-start | bytes 524288 | tf_op jit(solution)/shard_map/all_to_all | solution.py:261
  12.4 33.8 %copy-start.7 = (bf16[64,32,32]{0,2,1:T(8,128)(2,1)S(1)}, bf16[64,32,32]{0,2,1:T(8,128)(2,1)}, u32[]{:S(2)}) copy-start(bf16[64,32,32]{0,2,1:T(8,128)(2,1)} %param.14) | copy-start | bytes 393220
  15.1 32.0 %copy-start.8 = (bf16[64,2048]{1,0:T(8,128)(2,1)S(1)}, bf16[64,2048]{1,0:T(8,128)(2,1)}, u32[]{:S(2)}) copy-start(bf16[64,2048]{1,0:T(8,128)(2,1)} %param.13) | copy-start | bytes 786436
  15.1 32.2 %copy-start.3 = (bf16[6,160,48]{1,2,0:T(8,128)(2,1)S(1)}, bf16[6,160,48]{1,2,0:T(8,128)(2,1)}, u32[]{:S(2)}) copy-start(bf16[6,160,48]{1,2,0:T(8,128)(2,1)} %param.9) | copy-start | bytes 276484
  15.1 32.5 %copy-start.6 = (s32[4]{0:T(128)S(1)}, s32[4]{0:T(128)}, u32[]{:S(2)}) copy-start(s32[4]{0:T(128)} %counts.1) | copy-start | bytes 52

commit v4 on v2

--- a/solution.py
+++ b/solution.py
@@ -14,8 +14,10 @@
 LANES = 128
 THIRDS = 3
 VMEM = pl.BlockSpec(memory_space=pltpu.VMEM)
+HBM = pl.BlockSpec(memory_space=pltpu.HBM)
 SMEM = pl.BlockSpec(memory_space=pltpu.SMEM)
 LIMIT = 40 * 1024 * 1024
+WHOLE = 64 * 1024 * 1024
 NT = (((1,), (1,)), ((), ()))
 
 
@@ -34,8 +36,9 @@
     return values.astype(np.float32).astype(BF16)
 
 
-def dft_kernel(lev, lat, n_sec, n_band, n_fld, grid, table, out, padded, rows):
-    coeffs = jnp.dot(grid[...], table[...], preferred_element_type=F32)
+def fourier(lev, lat, grid, table, packed, padded, rows):
+    flat = jnp.concatenate([grid[level] for level in range(lev)], axis=0)
+    coeffs = jnp.dot(flat, table[...], preferred_element_type=F32)
     group = coeffs.shape[1] // THIRDS
     padded[...] = jnp.zeros_like(padded)
     for level in range(lev):
@@ -45,13 +48,28 @@
                 :, third * group : (third + 1) * group
             ]
         rows[pl.ds(level, group, stride=lev), :] = jnp.transpose(padded[...])[:group]
-    size = out.shape[1]
-    values = rows[...].astype(BF16).reshape(n_band * n_fld, size, LANES)
-    for sec in range(n_sec):
-        out[sec * n_band * n_fld : (sec + 1) * n_band * n_fld] = values
-
-
-def spread_kernel(lat, n_band, legendre, out, wide):
+    packed[...] = rows[...].astype(BF16).reshape(packed.shape)
+
+
+def prepare_kernel(lat, n_band, legendre, weights, inverses, out, out_weights, out_inverses,
+                   wide, flipped, rows):
+    states, sources = weights.shape
+    flux_rows, _, spec_bands = inverses.shape
+    for start in range(0, sources, LANES):
+        flipped[start : start + LANES, :] = jnp.transpose(
+            weights[:, start : start + LANES].astype(F32)
+        )
+    for row in range(flux_rows):
+        rows[row * flux_rows : (row + 1) * flux_rows, :] = inverses[row].astype(F32)
+    for row in range(flux_rows):
+        out_weights[row * spec_bands : (row + 1) * spec_bands, :] = flipped[
+            pl.ds(row, spec_bands, stride=flux_rows), :
+        ].astype(BF16)
+    for row in range(0, flux_rows, 2):
+        pair = [rows[pl.ds(row + i, flux_rows, stride=flux_rows), :] for i in range(2)]
+        out_inverses[:, row * spec_bands : (row + 2) * spec_bands] = jnp.concatenate(
+            pair, axis=1
+        ).astype(BF16)
     waves, degrees, _ = legendre.shape
     wide[...] = jnp.zeros_like(wide)
     lane = lax.broadcasted_iota(jnp.int32, (degrees, LANES), 1)
@@ -111,53 +129,92 @@
     return (blocks - lat * across) * lat_pad + lat
 
 
-def pick_kernel(lat_pad, grid, blocks, interp, state, patch, column):
+def local_kernel(lat_pad, parts, grid_hbm, blocks_hbm, interp_hbm, table_hbm, out, out_fourier,
+                 grid, blocks, interp, table, patch, column, selector, state, packed, padded,
+                 rows, sems, sends):
     lev, lat, lon = grid.shape
     across = lon // LANES
     slots = interp.shape[0]
     depth = patch.shape[0]
-    for tile in range(across):
-        patch[tile * lat_pad + lat : (tile + 1) * lat_pad, :] = jnp.zeros(
-            (lat_pad - lat, lev * LANES), BF16
-        )
-        for level in range(lev):
-            patch[
-                tile * lat_pad : tile * lat_pad + lat, level * LANES : (level + 1) * LANES
-            ] = grid[level, :, tile * LANES : (tile + 1) * LANES]
-    if depth > across * lat_pad:
-        patch[across * lat_pad :, :] = jnp.zeros((depth - across * lat_pad, lev * LANES), BF16)
+    step = lon // parts
+    small = [
+        pltpu.make_async_copy(blocks_hbm, blocks, sems.at[parts]),
+        pltpu.make_async_copy(interp_hbm, interp, sems.at[parts + 1]),
+        pltpu.make_async_copy(table_hbm, table, sems.at[parts + 2]),
+    ]
+    loads = [
+        pltpu.make_async_copy(
+            grid_hbm.at[:, :, pl.ds(part * step, step)],
+            grid.at[:, :, pl.ds(part * step, step)],
+            sems.at[part],
+        )
+        for part in range(parts)
+    ]
+    small[0].start()
+    for copy in loads:
+        copy.start()
+    small[1].start()
+    small[2].start()
+    small[0].wait()
     row = slot_rows(blocks[...], across, lat_pad)
     column[...] = jnp.transpose(jnp.broadcast_to(row, (LANES, slots)))
     chunk = 256
     lane = lax.broadcasted_iota(jnp.int32, (chunk, LANES), 1)
     for start in range(0, slots, chunk):
         mine = column[start : start + chunk, :]
-        selector = jnp.concatenate(
-            [
-                jnp.where(mine == lane + base, 1.0, 0.0).astype(BF16)
-                for base in range(0, depth, LANES)
-            ],
-            axis=1,
-        )
-        picked = jnp.dot(selector, patch[...], preferred_element_type=F32)
+        for base in range(0, depth, LANES):
+            selector[start : start + chunk, base : base + LANES] = jnp.where(
+                mine == lane + base, 1.0, 0.0
+            ).astype(BF16)
+    for part in range(parts):
+        loads[part].wait()
+        for tile in range(part * across // parts, (part + 1) * across // parts):
+            patch[tile * lat_pad + lat : (tile + 1) * lat_pad, :] = jnp.zeros(
+                (lat_pad - lat, lev * LANES), BF16
+            )
+            for level in range(lev):
+                patch[
+                    tile * lat_pad : tile * lat_pad + lat, level * LANES : (level + 1) * LANES
+                ] = grid[level, :, tile * LANES : (tile + 1) * LANES]
+    if depth > across * lat_pad:
+        patch[across * lat_pad :, :] = jnp.zeros((depth - across * lat_pad, lev * LANES), BF16)
+    small[1].wait()
+    for start in range(0, slots, chunk):
+        picked = jnp.dot(
+            selector[start : start + chunk, :], patch[...], preferred_element_type=F32
+        )
         weights = interp[start : start + chunk, :].astype(F32)
         total = jnp.zeros((chunk, LANES), F32)
         for level in range(lev):
             product = picked[:, level * LANES : (level + 1) * LANES] * weights
             total = jnp.where(lane == level, jnp.sum(product, axis=1, keepdims=True), total)
-        values = jnp.transpose(total)[:lev].astype(BF16)
-        for copy in range(state.shape[0]):
-            state[copy, :, start : start + chunk] = values
+        state[:, start : start + chunk] = jnp.transpose(total)[:lev].astype(BF16)
+    copies = [pltpu.make_async_copy(state, out.at[i], sends.at[i]) for i in range(out.shape[0])]
+    for copy in copies:
+        copy.start()
+    small[2].wait()
+    fourier(lev, lat, grid, table, packed, padded, rows)
+    targets = packed.shape[0]
+    for part in range(out_fourier.shape[0] // targets):
+        copies.append(
+            pltpu.make_async_copy(
+                packed,
+                out_fourier.at[pl.ds(part * targets, targets)],
+                sends.at[out.shape[0] + part],
+            )
+        )
+        copies[-1].start()
+    for copy in copies:
+        copy.wait()
 
 
 def softplus(x):
-    small = jnp.exp(-jnp.abs(x))
-    tail = jnp.where(small < 2.0**-11, small, jnp.log(1.0 + small))
-    return jnp.maximum(x, 0.0) + tail
-
-
-def column_kernel(n_sec, n_fld, lat_pad, place, counts, weights, inverses, blocks, interp, pieces,
-                  out, state, flux_up, flux_down):
+    power = jnp.exp(jnp.minimum(x, 80.0))
+    return jnp.where(x < -8.0, power, jnp.maximum(x, jnp.log(1.0 + power)))
+
+
+def column_kernel(n_sec, n_fld, lat_pad, counts, weights, inverses, blocks, interp, pieces,
+                  out, state, flux_up, flux_down, spread, result, sems):
     lev, slots = pieces.shape[1:]
     for fld in range(n_fld):
         for sec in range(n_sec):
@@ -178,41 +235,57 @@
     flux_down[:levels, :] = flux[levels:]
     flux_up[levels:, :] = jnp.zeros((8, slots), F32)
     flux_down[levels:, :] = jnp.zeros((8, slots), F32)
-    mine, lat, lon = out.shape
+    mine, lat, lon = result.shape
     across = lon // LANES
-    live = lax.broadcasted_iota(jnp.int32, (1, slots), 1) < counts[place[1]]
-    base = (place[2] * n_fld + place[0]) * mine
-    heats = []
+    live = lax.broadcasted_iota(jnp.int32, (1, slots), 1) < counts[lax.axis_index("band")]
+    base = (lax.axis_index("sec") * n_fld + lax.axis_index("fld")) * mine
     for level in range(mine):
         at = base + level
         heat = (flux_up[pl.ds(at, 1), :] - flux_up[pl.ds(at + 1, 1), :]) - (
             flux_down[pl.ds(at, 1), :] - flux_down[pl.ds(at + 1, 1), :]
         )
-        heats.append(jnp.where(live, heat, 0.0).astype(BF16).astype(F32))
+        heat = jnp.where(live, heat, 0.0).astype(BF16).astype(F32)
+        for start in range(0, slots, LANES):
+            down = jnp.transpose(
+                jnp.broadcast_to(heat[:, start : start + LANES], (LANES, LANES))
+            )
+            spread[start : start + LANES, level * LANES : (level + 1) * LANES] = (
+                down * interp[start : start + LANES, :].astype(F32)
+            ).astype(BF16)
     row = slot_rows(blocks[...], across, lat_pad)
     tiles = max(t for t in range(1, 8) if across % t == 0)
     height = tiles * lat_pad
+    copies = []
     for first in range(0, across, tiles):
         match = row == lax.broadcasted_iota(jnp.int32, (height, slots), 0) + first * lat_pad
+        left = jnp.where(match, 1.0, 0.0).astype(BF16)
+        summed = jnp.dot(left, spread[...], preferred_element_type=F32).astype(BF16)
         for level in range(mine):
-            left = jnp.where(match, heats[level], 0.0).astype(BF16)
-            summed = jnp.dot(left, interp[...], preferred_element_type=F32).astype(BF16)
             for tile in range(tiles):
-                out[level, :, (first + tile) * LANES : (first + tile + 1) * LANES] = summed[
-                    tile * lat_pad : tile * lat_pad + lat
+                result[level, :, (first + tile) * LANES : (first + tile + 1) * LANES] = summed[
+                    tile * lat_pad : tile * lat_pad + lat, level * LANES : (level + 1) * LANES
                 ]
-
-
-def call(kernel, outs, specs, scratch, args, flops, size, name):
+        columns = pl.ds(first * LANES, tiles * LANES)
+        copies.append(
+            pltpu.make_async_copy(
+                result.at[:, :, columns], out.at[:, :, columns], sems.at[first // tiles]
+            )
+        )
+        copies[-1].start()
+    for copy in copies:
+        copy.wait()
+
+
+def call(kernel, outs, specs, scratch, args, flops, size, name, out_spec=VMEM, limit=LIMIT):
     shapes = [jax.ShapeDtypeStruct(shape, dtype) for shape, dtype in outs]
     single = len(outs) == 1
     return pl.pallas_call(
         kernel,
         out_shape=shapes[0] if single else shapes,
         in_specs=specs,
-        out_specs=VMEM if single else [VMEM] * len(outs),
+        out_specs=out_spec if single else [out_spec] * len(outs),
         scratch_shapes=scratch,
-        compiler_params=pltpu.CompilerParams(vmem_limit_bytes=LIMIT),
+        compiler_params=pltpu.CompilerParams(vmem_limit_bytes=limit),
         cost_estimate=pl.CostEstimate(flops=flops, bytes_accessed=size, transcendentals=0),
         name=name,
     )(*args)
@@ -229,71 +302,86 @@
     lat_pad = -(-lat // 16) * 16
     rest = 2 * wave_dev // THIRDS
     piece = rest * lev
-    place = jnp.stack([lax.axis_index("fld"), lax.axis_index("band"), lax.axis_index("sec")]).astype(
-        jnp.int32
-    )
     block_row = blocks.reshape(1, slots)
 
     table = jnp.asarray(dft_table(lon, wave_dev, n_band, n_fld))
     group = n_fld * n_band * rest
     padded_group = -(-group // LANES) * LANES
     devices = n_sec * n_band * n_fld
-    sent = call(
-        functools.partial(dft_kernel, lev, lat, n_sec, n_band, n_fld),
-        [((devices, piece, LANES), BF16)],
-        [VMEM, VMEM],
-        [pltpu.VMEM((LANES, padded_group), F32), pltpu.VMEM((group * lev, LANES), F32)],
-        (grid.reshape(lev * lat, lon), table),
-        2 * lev * lat * lon * THIRDS * group,
-        2 * lon * (lev * lat + THIRDS * group),
-        "fourier",
-    )
+    devices = n_sec * n_band * n_fld
     depth = -(-across * lat_pad // LANES) * LANES
-    state = call(
-        functools.partial(pick_kernel, lat_pad),
-        [((n_sec * n_fld, lev, slots), BF16)],
-        [VMEM, VMEM, VMEM],
-        [pltpu.VMEM((depth, lev * LANES), BF16), pltpu.VMEM((slots, LANES), jnp.int32)],
-        (grid.reshape(lev, lat, lon), block_row, interp),
-        2 * slots * depth * lev * LANES,
+    parts = max(t for t in range(1, 8) if across % t == 0)
+    state, sent = call(
+        functools.partial(local_kernel, lat_pad, parts),
+        [((n_sec * n_fld, lev, slots), BF16), ((devices, piece, LANES), BF16)],
+        [HBM] * 4,
+        [
+            pltpu.VMEM((lev, lat, lon), BF16),
+            pltpu.VMEM((1, slots), jnp.int32),
+            pltpu.VMEM((slots, LANES), BF16),
+            pltpu.VMEM(table.shape, BF16),
+            pltpu.VMEM((depth, lev * LANES), BF16),
+            pltpu.VMEM((slots, LANES), jnp.int32),
+            pltpu.VMEM((slots, depth), BF16),
+            pltpu.VMEM((lev, slots), BF16),
+            pltpu.VMEM((n_band * n_fld, piece, LANES), BF16),
+            pltpu.VMEM((LANES, padded_group), F32),
+            pltpu.VMEM((group * lev, LANES), F32),
+            pltpu.SemaphoreType.DMA((parts + 3,)),
+            pltpu.SemaphoreType.DMA((n_sec * n_fld + n_sec,)),
+        ],
+        (grid.reshape(lev, lat, lon), block_row, interp, table),
+        2 * slots * depth * lev * LANES + 2 * lev * lat * lon * THIRDS * group,
         2 * lev * lat * lon + 2 * slots * LANES,
-        "pick",
+        "local",
+        HBM,
+        WHOLE,
     )
     columns = lax.all_to_all(state, ("sec", "fld"), 0, 0, tiled=True)
     pieces = lax.all_to_all(sent, ("sec", "band", "fld"), 0, 0, tiled=True)
-    basis = call(
-        functools.partial(spread_kernel, lat, n_band),
-        [((n_band, 2, THIRDS * degrees, LANES), BF16)],
-        [VMEM],
-        [pltpu.VMEM((degrees, (n_band * lat // LANES + 2) * LANES), F32)],
-        (jnp.swapaxes(legendre, 1, 2),),
+    spec_bands, flux_rows, _ = inverses.shape
+    sources = spec_bands * flux_rows
+    states = source_weights.shape[0]
+    basis, weights, inverse_rows = call(
+        functools.partial(prepare_kernel, lat, n_band),
+        [
+            ((n_band, 2, THIRDS * degrees, LANES), BF16),
+            ((sources, states), BF16),
+            ((flux_rows, sources), BF16),
+        ],
+        [VMEM, VMEM, VMEM],
+        [
+            pltpu.VMEM((degrees, (n_band * lat // LANES + 2) * LANES), F32),
+            pltpu.VMEM((sources, states), F32),
+            pltpu.VMEM((flux_rows * flux_rows, spec_bands), F32),
+        ],
+        (
+            jnp.swapaxes(legendre, 1, 2),
+            source_weights,
+            jnp.transpose(inverses, (1, 2, 0)),
+        ),
         0,
         8 * wave_dev * degrees * n_band * LANES,
-        "basis",
-    )
-
-    spec_bands, flux_rows, _ = inverses.shape
+        "prepare",
+    )
+    mine = n_sec * lev // (n_sec * n_fld)
     heating = call(
         functools.partial(column_kernel, n_sec, n_fld, lat_pad),
-        [((n_sec * lev // (n_sec * n_fld), lat, lon), BF16)],
-        [SMEM, SMEM] + [VMEM] * 5,
+        [((mine, lat, lon), BF16)],
+        [SMEM] + [VMEM] * 5,
         [
-            pltpu.VMEM((n_sec * n_fld * lev, slots), F32),
+            pltpu.VMEM((states, slots), F32),
             pltpu.VMEM((flux_rows // 2 + 8, slots), F32),
             pltpu.VMEM((flux_rows // 2 + 8, slots), F32),
+            pltpu.VMEM((slots, mine * LANES), BF16),
+            pltpu.VMEM((mine, lat, lon), BF16),
+            pltpu.SemaphoreType.DMA((across,)),
         ],
-        (
-            place,
-            counts,
-            jnp.transpose(source_weights),
-            jnp.transpose(inverses, (1, 0, 2)).reshape(flux_rows, spec_bands * flux_rows),
-            block_row,
-            interp,
-            columns,
-        ),
+        (counts, weights, inverse_rows, block_row, interp, columns),
         8 * slots * slots * 1024,
         2 * slots * slots,
         "columns",
+        HBM,
     )
 
     spectral = call(

time: 39.5 us -> 35.8 us (0.906)
  local copies, waits for them, and re-layouts: 11.1 us -> 5.09 us
  waiting for transfers between devices: 1.4 us -> 4.99 us
  starting transfers between devices: 13 us -> 9.94 us
  Pallas kernels: 12.7 us -> 14.6 us
    all_to_all x1, waiting for transfers between devices: 0.4 us -> 3.38 us  [body(): columns = lax.all_to_all(state, ('sec', 'fld'), 0, 0, tiled=True)]
    all_to_all x1, starting transfers between devices: 5.64 us -> 2.68 us  [body(): pieces = lax.all_to_all(sent, ('sec', 'band', 'fld'), 0, 0, tiled=True)]
    unnamed x27 -> x12, local copies, waits for them, and re-layouts: 7.76 us -> 5.09 us
    reshape x1 -> x0, local copies, waits for them, and re-layouts: 2.29 us -> none  [body(): jnp.transpose(inverses, (1, 0, 2))]
    pallas_call x5 -> x4, Pallas kernels: 12.7 us -> 14.6 us  [call(): pl.pallas_call(kernel, out_shape=shapes[0] if single else shapes, in_spec...]
    transpose x1 -> x0, local copies, waits for them, and re-layouts: 1.02 us -> none  [body(): jnp.transpose(inverses, (1, 0, 2))]
    all_to_all x1, waiting for transfers between devices: 1 us -> 1.61 us  [body(): pieces = lax.all_to_all(sent, ('sec', 'band', 'fld'), 0, 0, tiled=True)]
  transfers between devices with their start and end apart: 2 -> 2, of which waited for: 2 -> 2; matrix products, arithmetic and copies ran while one was open for 14% -> 0% of each run, Pallas kernels for 21% -> 22%
where the time goes in v4:
time: 35.8 us; the launch traced here: 35.3 us
  Pallas kernels  14.6 us (41%)
  starting transfers between devices  9.94 us (28%)
  local copies, waits for them, and re-layouts  5.09 us (14%)
  waiting for transfers between devices  4.99 us (14%)
  between operations  0.68 us (2%)
    pallas_call x4, Pallas kernels, call(): pl.pallas_call(kernel, out_shape=shapes[0] if single else shapes, in_spec...  14.6 us
    all_to_all x1, starting transfers between devices, body(): columns = lax.all_to_all(state, ('sec', 'fld'), 0, 0, tiled=True)  7.26 us
    unnamed x12, local copies, waits for them, and re-layouts  5.09 us
    all_to_all x1, waiting for transfers between devices, body(): columns = lax.all_to_all(state, ('sec', 'fld'), 0, 0, tiled=True)  3.38 us
    all_to_all x1, starting transfers between devices, body(): pieces = lax.all_to_all(sent, ('sec', 'band', 'fld'), 0, 0, tiled=True)  2.68 us
    all_to_all x1, waiting for transfers between devices, body(): pieces = lax.all_to_all(sent, ('sec', 'band', 'fld'), 0, 0, tiled=True)  1.61 us
  transfers between devices with their start and end apart: 2, of which 2 were waited for; matrix products, arithmetic and copies ran while one was open for 0% of the time, Pallas kernels for 22%

profile of v4, /device:TPU:0, one launch (start us, length us, event | category | flops | bytes accessed | tf_op | source)
XLA Modules:
  0.0 35.3 jit_solution(574523981780760680)
XLA Ops:
  0.6 6.0 %local.1 = (bf16[8,8,1024]{2,1,0:T(8,128)(2,1)}, bf16[32,32,128]{2,1,0:T(8,128)(2,1)}) custom-call(bf16[8,40,2688]{2,1,0:T(8,128)(2,1)} %bitcast.8, s32[1,1024]{1,0:T(1,128)} %bitcast.6, bf16[1024,128]{1,0:T(8,128)(2,1)} %interp.1, bf16[2688,192]{1,0:T(8,128)(2,1)} %constant.2.clone.table_hbm), custom_call_target="tpu_custom_call" | custom-call | flops 2477785088 | bytes 1982464 | tf_op jit(solution)/shard_map/local/pallas_call | solution.py:282
  6.6 7.3 %all-to-all-start.1 = ((bf16[8,8,1024]{2,1,0:T(8,128)(2,1)}), bf16[8,8,1024]{2,1,0:T(8,128)(2,1)S(1)}, u32[]{:S(2)}, u32[]{:S(2)}) async-start(bf16[8,8,1024]{2,1,0:T(8,128)(2,1)} %get-tuple-element.11), calls=%async_computation.1 | async-start | bytes 262144 | tf_op jit(solution)/shard_map/all_to_all | solution.py:340
  13.9 0.0 copy-start
  13.9 0.9 %copy-done = bf16[64,2048]{1,0:T(8,128)(2,1)S(1)} copy-done((bf16[64,2048]{1,0:T(8,128)(2,1)S(1)}, bf16[64,2048]{1,0:T(8,128)(2,1)}, u32[]{:S(2)}) %copy-start) | copy-done | bytes 262168
  14.8 0.0 copy-start.1
  14.8 0.9 %copy-done.1 = bf16[64,32,32]{0,2,1:T(8,128)(2,1)S(1)} copy-done((bf16[64,32,32]{0,2,1:T(8,128)(2,1)S(1)}, bf16[64,32,32]{0,2,1:T(8,128)(2,1)}, u32[]{:S(2)}) %copy-start.1) | copy-done | bytes 131096
  15.8 0.0 copy-start.2
  15.8 0.9 %copy-done.2 = bf16[6,160,48]{1,2,0:T(8,128)(2,1)S(1)} copy-done((bf16[6,160,48]{1,2,0:T(8,128)(2,1)S(1)}, bf16[6,160,48]{1,2,0:T(8,128)(2,1)}, u32[]{:S(2)}) %copy-start.2) | copy-done | bytes 92184
  16.7 1.3 %prepare.1 = (bf16[4,2,144,128]{3,2,1,0:T(8,128)(2,1)S(1)}, bf16[2048,64]{1,0:T(8,128)(2,1)S(1)}, bf16[32,2048]{1,0:T(8,128)(2,1)S(1)}) custom-call(bf16[6,48,160]{2,1,0:T(8,128)(2,1)S(1)} %bitcast.5, bf16[64,2048]{1,0:T(8,128)(2,1)S(1)} %copy-done, bf16[32,32,64]{2,1,0:T(8,128)(2,1)S(1)} %bitcast.4), custom_call_target="tpu_custom_call" | custom-call | bytes 1179648 | tf_op jit(solution)/shard_map/prepare/pallas_call | solution.py:282
  18.0 3.4 %all-to-all-done.1.pieces = bf16[8,8,1024]{2,1,0:T(8,128)(2,1)S(1)} async-done(((bf16[8,8,1024]{2,1,0:T(8,128)(2,1)}), bf16[8,8,1024]{2,1,0:T(8,128)(2,1)S(1)}, u32[]{:S(2)}, u32[]{:S(2)}) %all-to-all-start.1) | async-done | bytes 131104 | tf_op jit(solution)/shard_map/all_to_all | solution.py:340
  21.4 2.7 %all-to-all-start = ((bf16[32,32,128]{2,1,0:T(8,128)(2,1)}), bf16[32,32,128]{2,1,0:T(8,128)(2,1)S(1)}, u32[]{:S(2)}, u32[]{:S(2)}) async-start(bf16[32,32,128]{2,1,0:T(8,128)(2,1)} %get-tuple-element.8), calls=%async_computation | async-start | bytes 524288 | tf_op jit(solution)/shard_map/all_to_all | solution.py:341
  24.1 0.0 copy-start.3
  24.1 0.9 %copy-done.3 = bf16[1024,128]{1,0:T(8,128)(2,1)S(1)} copy-done((bf16[1024,128]{1,0:T(8,128)(2,1)S(1)}, bf16[1024,128]{1,0:T(8,128)(2,1)}, u32[]{:S(2)}) %copy-start.3) | copy-done | bytes 262168
  25.0 0.0 copy-start.4
  25.0 0.7 %copy-done.4 = s32[1024]{0:T(1024)S(1)} copy-done((s32[1024]{0:T(1024)S(1)}, s32[1024]{0:T(1024)}, u32[]{:S(2)}) %copy-start.4) | copy-done | bytes 4120
  25.7 0.0 copy-start.5
  25.7 0.7 %copy-done.5 = s32[4]{0:T(128)S(1)} copy-done((s32[4]{0:T(128)S(1)}, s32[4]{0:T(128)}, u32[]{:S(2)}) %copy-start.5) | copy-done | bytes 40
  26.4 6.3 %columns.1 = bf16[2,40,2688]{2,1,0:T(8,128)(2,1)} custom-call(s32[4]{0:T(128)S(1)} %copy-done.5, bf16[2048,64]{1,0:T(8,128)(2,1)S(1)} %get-tuple-element.9.weights, bf16[32,2048]{1,0:T(8,128)(2,1)S(1)} %get-tuple-element.10.inverses, s32[1,1024]{1,0:T(1,128)S(1)} %bitcast.7, bf16[1024,128]{1,0:T(8,128)(2,1)S(1)} %copy-done.3, ...), custom_call_target="tpu_custom_call" | custom-call | flops 8589934592 | bytes 2097152 | tf_op jit(solution)/shard_map/columns/pallas_call | solution.py:282
  32.7 1.6 %all-to-all-done.pieces = bf16[32,32,128]{2,1,0:T(8,128)(2,1)S(1)} async-done(((bf16[32,32,128]{2,1,0:T(8,128)(2,1)}), bf16[32,32,128]{2,1,0:T(8,128)(2,1)S(1)}, u32[]{:S(2)}, u32[]{:S(2)}) %all-to-all-start) | async-done | bytes 262176 | tf_op jit(solution)/shard_map/all_to_all | solution.py:341
  34.3 1.0 %legendre.1 = bf16[6,2,4,16,48]{4,3,2,1,0:T(8,128)(2,1)} custom-call(bf16[4,2,144,128]{3,2,1,0:T(8,128)(2,1)S(1)} %get-tuple-element.7.weights, bf16[32,32,128]{2,1,0:T(8,128)(2,1)S(1)} %all-to-all-done.pieces), custom_call_target="tpu_custom_call" | custom-call | flops 75497472 | bytes 262144 | tf_op jit(solution)/shard_map/legendre/pallas_call | solution.py:282
Async XLA Ops:
  6.6 14.8 %all-to-all-start.1 = ((bf16[8,8,1024]{2,1,0:T(8,128)(2,1)}), bf16[8,8,1024]{2,1,0:T(8,128)(2,1)S(1)}, u32[]{:S(2)}, u32[]{:S(2)}) async-start(bf16[8,8,1024]{2,1,0:T(8,128)(2,1)} %get-tuple-element.11), calls=%async_computation.1 | async-start | bytes 262144 | tf_op jit(solution)/shard_map/all_to_all | solution.py:340
  13.9 0.9 %copy-start = (bf16[64,2048]{1,0:T(8,128)(2,1)S(1)}, bf16[64,2048]{1,0:T(8,128)(2,1)}, u32[]{:S(2)}) copy-start(bf16[64,2048]{1,0:T(8,128)(2,1)} %weights.1) | copy-start | bytes 786436
  14.8 0.9 %copy-start.1 = (bf16[64,32,32]{0,2,1:T(8,128)(2,1)S(1)}, bf16[64,32,32]{0,2,1:T(8,128)(2,1)}, u32[]{:S(2)}) copy-start(bf16[64,32,32]{0,2,1:T(8,128)(2,1)} %param.14) | copy-start | bytes 393220
  15.8 0.9 %copy-start.2 = (bf16[6,160,48]{1,2,0:T(8,128)(2,1)S(1)}, bf16[6,160,48]{1,2,0:T(8,128)(2,1)}, u32[]{:S(2)}) copy-start(bf16[6,160,48]{1,2,0:T(8,128)(2,1)} %param.9) | copy-start | bytes 276484
  21.4 12.9 %all-to-all-start = ((bf16[32,32,128]{2,1,0:T(8,128)(2,1)}), bf16[32,32,128]{2,1,0:T(8,128)(2,1)S(1)}, u32[]{:S(2)}, u32[]{:S(2)}) async-start(bf16[32,32,128]{2,1,0:T(8,128)(2,1)} %get-tuple-element.8), calls=%async_computation | async-start | bytes 524288 | tf_op jit(solution)/shard_map/all_to_all | solution.py:341
  24.1 1.0 %copy-start.3 = (bf16[1024,128]{1,0:T(8,128)(2,1)S(1)}, bf16[1024,128]{1,0:T(8,128)(2,1)}, u32[]{:S(2)}) copy-start(bf16[1024,128]{1,0:T(8,128)(2,1)} %interp.1) | copy-start | bytes 786436
  25.0 0.7 %copy-start.4 = (s32[1024]{0:T(1024)S(1)}, s32[1024]{0:T(1024)}, u32[]{:S(2)}) copy-start(s32[1024]{0:T(1024)} %param.11) | copy-start | bytes 12292
  25.7 0.7 %copy-start.5 = (s32[4]{0:T(128)S(1)}, s32[4]{0:T(128)}, u32[]{:S(2)}) copy-start(s32[4]{0:T(128)} %counts.1) | copy-start | bytes 52

commit v5 on v4

--- a/solution.py
+++ b/solution.py
@@ -17,7 +17,8 @@
 HBM = pl.BlockSpec(memory_space=pltpu.HBM)
 SMEM = pl.BlockSpec(memory_space=pltpu.SMEM)
 LIMIT = 40 * 1024 * 1024
-WHOLE = 64 * 1024 * 1024
+ROOM = 1200 * 1024
+WHOLE = 64 * 1024 * 1024 - ROOM
 NT = (((1,), (1,)), ((), ()))
 
 
@@ -213,13 +214,14 @@
     return jnp.where(x < -8.0, power, jnp.maximum(x, jnp.log(1.0 + power)))
 
 
-def column_kernel(n_sec, n_fld, lat_pad, counts, weights, inverses, blocks, interp, pieces,
+def column_kernel(n_sec, n_fld, lat_pad, counts, weights, inverses, blocks, interp, near, far,
                   out, state, flux_up, flux_down, spread, result, sems):
-    lev, slots = pieces.shape[1:]
+    lev, slots = near.shape[1:]
+    place = lax.axis_index("sec")
     for fld in range(n_fld):
-        for sec in range(n_sec):
-            row = (fld * n_sec + sec) * lev
-            state[row : row + lev, :] = pieces[sec * n_fld + fld].astype(F32)
+        for shift, pieces in enumerate((near, far)):
+            row = (fld * n_sec + (place ^ shift)) * lev
+            state[pl.ds(pl.multiple_of(row, lev), lev), :] = pieces[fld].astype(F32)
     column = state[...].astype(BF16)
     flux_rows = inverses.shape[0]
     flux = jnp.zeros((flux_rows, slots), F32)
@@ -313,7 +315,7 @@
     parts = max(t for t in range(1, 8) if across % t == 0)
     state, sent = call(
         functools.partial(local_kernel, lat_pad, parts),
-        [((n_sec * n_fld, lev, slots), BF16), ((devices, piece, LANES), BF16)],
+        [((n_fld, lev, slots), BF16), ((devices, piece, LANES), BF16)],
         [HBM] * 4,
         [
             pltpu.VMEM((lev, lat, lon), BF16),
@@ -328,7 +330,7 @@
             pltpu.VMEM((LANES, padded_group), F32),
             pltpu.VMEM((group * lev, LANES), F32),
             pltpu.SemaphoreType.DMA((parts + 3,)),
-            pltpu.SemaphoreType.DMA((n_sec * n_fld + n_sec,)),
+            pltpu.SemaphoreType.DMA((n_fld + n_sec,)),
         ],
         (grid.reshape(lev, lat, lon), block_row, interp, table),
         2 * slots * depth * lev * LANES + 2 * lev * lat * lon * THIRDS * group,
@@ -337,8 +339,9 @@
         HBM,
         WHOLE,
     )
-    columns = lax.all_to_all(state, ("sec", "fld"), 0, 0, tiled=True)
+    near = lax.all_to_all(state, "fld", 0, 0, tiled=True)
     pieces = lax.all_to_all(sent, ("sec", "band", "fld"), 0, 0, tiled=True)
+    far = lax.ppermute(near, "sec", [(i, 1 - i) for i in range(n_sec)])
     spec_bands, flux_rows, _ = inverses.shape
     sources = spec_bands * flux_rows
     states = source_weights.shape[0]
@@ -368,7 +371,7 @@
     heating = call(
         functools.partial(column_kernel, n_sec, n_fld, lat_pad),
         [((mine, lat, lon), BF16)],
-        [SMEM] + [VMEM] * 5,
+        [SMEM] + [VMEM] * 6,
         [
             pltpu.VMEM((states, slots), F32),
             pltpu.VMEM((flux_rows // 2 + 8, slots), F32),
@@ -377,7 +380,7 @@
             pltpu.VMEM((mine, lat, lon), BF16),
             pltpu.SemaphoreType.DMA((across,)),
         ],
-        (counts, weights, inverse_rows, block_row, interp, columns),
+        (counts, weights, inverse_rows, block_row, interp, near, far),
         8 * slots * slots * 1024,
         2 * slots * slots,
         "columns",

time: 35.8 us -> 34.4 us (0.961)
  blocking collectives: 0 us -> 12.1 us
  starting transfers between devices: 9.94 us -> 4.08 us
  local copies, waits for them, and re-layouts: 5.09 us -> 0.03 us
  waiting for transfers between devices: 4.99 us -> 2.46 us
    all_to_all x0 -> x1, blocking collectives: none -> 12.1 us  [body(): near = lax.all_to_all(state, 'fld', 0, 0, tiled=True)]
    all_to_all x1 -> x0, starting transfers between devices: 7.26 us -> none  [body(): columns = lax.all_to_all(state, ('sec', 'fld'), 0, 0, tiled=True)]
    unnamed x12, local copies, waits for them, and re-layouts: 5.09 us -> 0.03 us
    all_to_all x1 -> x0, waiting for transfers between devices: 3.38 us -> none  [body(): columns = lax.all_to_all(state, ('sec', 'fld'), 0, 0, tiled=True)]
    ppermute x0 -> x1, starting transfers between devices: none -> 1.49 us  [body(): far = lax.ppermute(near, 'sec', [(i, 1 - i) for i in range(n_sec)])]
    all_to_all x1, waiting for transfers between devices: 1.61 us -> 2.45 us  [body(): pieces = lax.all_to_all(sent, ('sec', 'band', 'fld'), 0, 0, tiled=True)]
  transfers between devices with their start and end apart: 2 -> 2, of which waited for: 2 -> 1; matrix products, arithmetic and copies ran while one was open for 0% -> 0% of each run, Pallas kernels for 22% -> 23%
where the time goes in v5:
time: 34.4 us; the launch traced here: 34.1 us
  Pallas kernels  14.7 us (43%)
  blocking collectives  12.1 us (35%)
  starting transfers between devices  4.08 us (12%)
  waiting for transfers between devices  2.46 us (7%)
  between operations  0.77 us (2%)
    pallas_call x4, Pallas kernels, call(): pl.pallas_call(kernel, out_shape=shapes[0] if single else shapes, in_spec...  14.7 us
    all_to_all x1, blocking collectives, body(): near = lax.all_to_all(state, 'fld', 0, 0, tiled=True)  12.1 us
    all_to_all x1, starting transfers between devices, body(): pieces = lax.all_to_all(sent, ('sec', 'band', 'fld'), 0, 0, tiled=True)  2.58 us
    all_to_all x1, waiting for transfers between devices, body(): pieces = lax.all_to_all(sent, ('sec', 'band', 'fld'), 0, 0, tiled=True)  2.45 us
    ppermute x1, starting transfers between devices, body(): far = lax.ppermute(near, 'sec', [(i, 1 - i) for i in range(n_sec)])  1.49 us
  transfers between devices with their start and end apart: 2, of which 1 were waited for; matrix products, arithmetic and copies ran while one was open for 0% of the time, Pallas kernels for 23%

profile of v5, /device:TPU:0, one launch (start us, length us, event | category | flops | bytes accessed | tf_op | source)
XLA Modules:
  0.0 34.1 jit_solution(11895216995244719032)
XLA Ops:
  0.6 0.0 copy-start
  0.6 0.0 copy-start.1
  0.7 0.0 copy-start.2
  0.7 0.0 copy-start.3
  0.7 0.0 copy-start.4
  0.7 0.0 copy-start.5
  0.7 6.0 %local.1 = (bf16[4,8,1024]{2,1,0:T(8,128)(2,1)}, bf16[32,32,128]{2,1,0:T(8,128)(2,1)}) custom-call(bf16[8,40,2688]{2,1,0:T(8,128)(2,1)} %bitcast.8, s32[1,1024]{1,0:T(1,128)} %bitcast.6, bf16[1024,128]{1,0:T(8,128)(2,1)} %interp.1, bf16[2688,192]{1,0:T(8,128)(2,1)} %constant.2.clone.table_hbm), custom_call_target="tpu_custom_call" | custom-call | flops 2477785088 | bytes 1982464 | tf_op jit(solution)/shard_map/local/pallas_call | solution.py:284
  6.7 12.1 %all_to_all.10.near = bf16[4,8,1024]{2,1,0:T(8,128)(2,1)S(1)} all-to-all(bf16[4,8,1024]{2,1,0:T(8,128)(2,1)} %get-tuple-element.11), channel_id=1, replica_groups=mesh['sec'=2,'band'=4,'fld'=4] {'fld'}, dimensions={0} | all-to-all | bytes 131072 | tf_op jit(solution)/shard_map/all_to_all | solution.py:342
  18.8 1.5 %collective-permute-start = (bf16[4,8,1024]{2,1,0:T(8,128)(2,1)S(1)}, bf16[4,8,1024]{2,1,0:T(8,128)(2,1)S(1)}, u32[]{:S(2)}, u32[]{:S(2)}) collective-permute-start(bf16[4,8,1024]{2,1,0:T(8,128)(2,1)S(1)} %all_to_all.10.near), channel_id=1, source_target_pairs={{0,16},{16,0},{1,17},{17,1},{2,18},{18,2},{3,19},{19,3},{4,20},{20... | collective-permute-start | bytes 196616 | tf_op jit(solution)/shard_map/ppermute | solution.py:344
  20.3 2.6 %all-to-all-start = ((bf16[32,32,128]{2,1,0:T(8,128)(2,1)}), bf16[32,32,128]{2,1,0:T(8,128)(2,1)S(1)}, u32[]{:S(2)}, u32[]{:S(2)}) async-start(bf16[32,32,128]{2,1,0:T(8,128)(2,1)} %get-tuple-element.8), calls=%async_computation | async-start | bytes 524288 | tf_op jit(solution)/shard_map/all_to_all | solution.py:343
  22.8 0.0 copy-done
  22.9 0.0 copy-done.1
  22.9 0.0 copy-done.2
  22.9 1.3 %prepare.1 = (bf16[4,2,144,128]{3,2,1,0:T(8,128)(2,1)S(1)}, bf16[2048,64]{1,0:T(8,128)(2,1)S(1)}, bf16[32,2048]{1,0:T(8,128)(2,1)S(1)}) custom-call(bf16[6,48,160]{2,1,0:T(8,128)(2,1)S(1)} %bitcast.5, bf16[64,2048]{1,0:T(8,128)(2,1)S(1)} %copy-done, bf16[32,32,64]{2,1,0:T(8,128)(2,1)S(1)} %bitcast.4), custom_call_target="tpu_custom_call" | custom-call | bytes 1179648 | tf_op jit(solution)/shard_map/prepare/pallas_call | solution.py:284
  24.2 0.0 collective-permute-done.far
  24.2 0.0 copy-done.3
  24.2 0.0 copy-done.4
  24.2 0.0 copy-done.5
  24.3 6.4 %columns.1 = bf16[2,40,2688]{2,1,0:T(8,128)(2,1)} custom-call(s32[4]{0:T(128)S(1)} %copy-done.5, bf16[2048,64]{1,0:T(8,128)(2,1)S(1)} %get-tuple-element.9.weights, bf16[32,2048]{1,0:T(8,128)(2,1)S(1)} %get-tuple-element.10.inverses, s32[1,1024]{1,0:T(1,128)S(1)} %bitcast.7, bf16[1024,128]{1,0:T(8,128)(2,1)S(1)} %copy-done.3, ...), custom_call_target="tpu_custom_call" | custom-call | flops 8589934592 | bytes 2097152 | tf_op jit(solution)/shard_map/columns/pallas_call | solution.py:284
  30.6 2.5 %all-to-all-done.pieces = bf16[32,32,128]{2,1,0:T(8,128)(2,1)S(1)} async-done(((bf16[32,32,128]{2,1,0:T(8,128)(2,1)}), bf16[32,32,128]{2,1,0:T(8,128)(2,1)S(1)}, u32[]{:S(2)}, u32[]{:S(2)}) %all-to-all-start) | async-done | bytes 262176 | tf_op jit(solution)/shard_map/all_to_all | solution.py:343
  33.1 1.0 %legendre.1 = bf16[6,2,4,16,48]{4,3,2,1,0:T(8,128)(2,1)} custom-call(bf16[4,2,144,128]{3,2,1,0:T(8,128)(2,1)S(1)} %get-tuple-element.7.weights, bf16[32,32,128]{2,1,0:T(8,128)(2,1)S(1)} %all-to-all-done.pieces), custom_call_target="tpu_custom_call" | custom-call | flops 75497472 | bytes 262144 | tf_op jit(solution)/shard_map/legendre/pallas_call | solution.py:284
Async XLA Ops:
  0.6 22.2 %copy-start = (bf16[64,2048]{1,0:T(8,128)(2,1)S(1)}, bf16[64,2048]{1,0:T(8,128)(2,1)}, u32[]{:S(2)}) copy-start(bf16[64,2048]{1,0:T(8,128)(2,1)} %weights.1) | copy-start | bytes 786436
  0.6 22.2 %copy-start.1 = (bf16[64,32,32]{0,2,1:T(8,128)(2,1)S(1)}, bf16[64,32,32]{0,2,1:T(8,128)(2,1)}, u32[]{:S(2)}) copy-start(bf16[64,32,32]{0,2,1:T(8,128)(2,1)} %param.14) | copy-start | bytes 393220
  0.7 22.2 %copy-start.2 = (bf16[6,160,48]{1,2,0:T(8,128)(2,1)S(1)}, bf16[6,160,48]{1,2,0:T(8,128)(2,1)}, u32[]{:S(2)}) copy-start(bf16[6,160,48]{1,2,0:T(8,128)(2,1)} %param.9) | copy-start | bytes 276484
  0.7 23.6 %copy-start.3 = (bf16[1024,128]{1,0:T(8,128)(2,1)S(1)}, bf16[1024,128]{1,0:T(8,128)(2,1)}, u32[]{:S(2)}) copy-start(bf16[1024,128]{1,0:T(8,128)(2,1)} %interp.1) | copy-start | bytes 786436
  0.7 23.6 %copy-start.4 = (s32[1024]{0:T(1024)S(1)}, s32[1024]{0:T(1024)}, u32[]{:S(2)}) copy-start(s32[1024]{0:T(1024)} %param.11) | copy-start | bytes 12292
  0.7 23.6 %copy-start.5 = (s32[4]{0:T(128)S(1)}, s32[4]{0:T(128)}, u32[]{:S(2)}) copy-start(s32[4]{0:T(128)} %counts.1) | copy-start | bytes 52
  18.8 5.5 %collective-permute-start = (bf16[4,8,1024]{2,1,0:T(8,128)(2,1)S(1)}, bf16[4,8,1024]{2,1,0:T(8,128)(2,1)S(1)}, u32[]{:S(2)}, u32[]{:S(2)}) collective-permute-start(bf16[4,8,1024]{2,1,0:T(8,128)(2,1)S(1)} %all_to_all.10.near), channel_id=1, source_target_pairs={{0,16},{16,0},{1,17},{17,1},{2,18},{18,2},{3,19},{19,3},{4,20},{20... | collective-permute-start | bytes 196616 | tf_op jit(solution)/shard_map/ppermute | solution.py:344
  20.3 12.8 %all-to-all-start = ((bf16[32,32,128]{2,1,0:T(8,128)(2,1)}), bf16[32,32,128]{2,1,0:T(8,128)(2,1)S(1)}, u32[]{:S(2)}, u32[]{:S(2)}) async-start(bf16[32,32,128]{2,1,0:T(8,128)(2,1)} %get-tuple-element.8), calls=%async_computation | async-start | bytes 524288 | tf_op jit(solution)/shard_map/all_to_all | solution.py:343

commit v6 on v5

--- a/solution.py
+++ b/solution.py
@@ -25,8 +25,8 @@
 def dft_table(lon, wave_dev, n_band, n_fld):
     values_dev = 2 * wave_dev
     rest = values_dev // THIRDS
-    third, band, fld, low = np.meshgrid(
-        np.arange(THIRDS), np.arange(n_band), np.arange(n_fld), np.arange(rest), indexing="ij"
+    third, fld, band, low = np.meshgrid(
+        np.arange(THIRDS), np.arange(n_fld), np.arange(n_band), np.arange(rest), indexing="ij"
     )
     value = third * rest + low
     wave = ((band * n_fld + fld) * wave_dev + value // 2).reshape(-1)
@@ -37,7 +37,7 @@
     return values.astype(np.float32).astype(BF16)
 
 
-def fourier(lev, lat, grid, table, packed, padded, rows):
+def fourier(lev, lat, grid, table, message, padded, rows):
     flat = jnp.concatenate([grid[level] for level in range(lev)], axis=0)
     coeffs = jnp.dot(flat, table[...], preferred_element_type=F32)
     group = coeffs.shape[1] // THIRDS
@@ -49,7 +49,9 @@
                 :, third * group : (third + 1) * group
             ]
         rows[pl.ds(level, group, stride=lev), :] = jnp.transpose(padded[...])[:group]
-    packed[...] = rows[...].astype(BF16).reshape(packed.shape)
+    targets = message.shape[0]
+    size = rows.shape[0] // targets
+    message[:, :size, :] = rows[...].astype(BF16).reshape(targets, size, LANES)
 
 
 def prepare_kernel(lat, n_band, legendre, weights, inverses, out, out_weights, out_inverses,
@@ -91,7 +93,7 @@
 
 def legendre_kernel(n_sec, n_band, n_fld, lev, weights, pieces, out):
     degrees = out.shape[4]
-    half = pieces.shape[1] // 2
+    half = pieces.shape[2] // 2
     for parity in range(2):
         rows = slice(parity * half, (parity + 1) * half)
         basis = jnp.concatenate([weights[band, parity] for band in range(n_band)], axis=1)
@@ -99,7 +101,7 @@
             [
                 jnp.concatenate(
                     [
-                        pieces[(sec * n_band + band) * n_fld + fld, rows, :]
+                        pieces[sec * n_band + band, fld, rows, :]
                         for band in range(n_band)
                     ],
                     axis=1,
@@ -130,9 +132,9 @@
     return (blocks - lat * across) * lat_pad + lat
 
 
-def local_kernel(lat_pad, parts, grid_hbm, blocks_hbm, interp_hbm, table_hbm, out, out_fourier,
-                 grid, blocks, interp, table, patch, column, selector, state, packed, padded,
-                 rows, sems, sends):
+def local_kernel(lat_pad, parts, grid_hbm, blocks_hbm, interp_hbm, table_hbm, out,
+                 grid, blocks, interp, table, patch, column, selector, message, padded, rows,
+                 sems, send):
     lev, lat, lon = grid.shape
     across = lon // LANES
     slots = interp.shape[0]
@@ -189,22 +191,32 @@
         for level in range(lev):
             product = picked[:, level * LANES : (level + 1) * LANES] * weights
             total = jnp.where(lane == level, jnp.sum(product, axis=1, keepdims=True), total)
-        state[:, start : start + chunk] = jnp.transpose(total)[:lev].astype(BF16)
-    copies = [pltpu.make_async_copy(state, out.at[i], sends.at[i]) for i in range(out.shape[0])]
+        state = jnp.transpose(total)[:lev].astype(BF16)
+        for tile in range(chunk // LANES):
+            row = message.shape[1] - slots // LANES * lev + (start // LANES + tile) * lev
+            for target in range(message.shape[0]):
+                message[target, row : row + lev, :] = state[:, tile * LANES : (tile + 1) * LANES]
+    small[2].wait()
+    fourier(lev, lat, grid, table, message, padded, rows)
+    copy = pltpu.make_async_copy(message, out, send.at[0])
+    copy.start()
+    copy.wait()
+
+
+def regroup_kernel(n_band, arrived, out, out_state, sems):
+    size = out.shape[2]
+    copies = []
+    for target in range(out.shape[0]):
+        rows = pl.ds(target % n_band * size, size)
+        copies.append(
+            pltpu.make_async_copy(arrived.at[:, rows, :], out.at[target], sems.at[target])
+        )
+    rows = pl.ds(n_band * size, out_state.shape[1])
+    copies.append(
+        pltpu.make_async_copy(arrived.at[:, rows, :], out_state, sems.at[out.shape[0]])
+    )
     for copy in copies:
         copy.start()
-    small[2].wait()
-    fourier(lev, lat, grid, table, packed, padded, rows)
-    targets = packed.shape[0]
-    for part in range(out_fourier.shape[0] // targets):
-        copies.append(
-            pltpu.make_async_copy(
-                packed,
-                out_fourier.at[pl.ds(part * targets, targets)],
-                sends.at[out.shape[0] + part],
-            )
-        )
-        copies[-1].start()
     for copy in copies:
         copy.wait()
 
@@ -214,14 +226,17 @@
     return jnp.where(x < -8.0, power, jnp.maximum(x, jnp.log(1.0 + power)))
 
 
-def column_kernel(n_sec, n_fld, lat_pad, counts, weights, inverses, blocks, interp, near, far,
+def column_kernel(n_sec, n_fld, lat_pad, slots, counts, weights, inverses, blocks, interp, near, far,
                   out, state, flux_up, flux_down, spread, result, sems):
-    lev, slots = near.shape[1:]
+    lev = near.shape[1] * LANES // slots
     place = lax.axis_index("sec")
     for fld in range(n_fld):
         for shift, pieces in enumerate((near, far)):
             row = (fld * n_sec + (place ^ shift)) * lev
-            state[pl.ds(pl.multiple_of(row, lev), lev), :] = pieces[fld].astype(F32)
+            for tile in range(slots // LANES):
+                state[
+                    pl.ds(pl.multiple_of(row, lev), lev), tile * LANES : (tile + 1) * LANES
+                ] = pieces[fld, tile * lev : (tile + 1) * lev, :].astype(F32)
     column = state[...].astype(BF16)
     flux_rows = inverses.shape[0]
     flux = jnp.zeros((flux_rows, slots), F32)
@@ -309,13 +324,13 @@
     table = jnp.asarray(dft_table(lon, wave_dev, n_band, n_fld))
     group = n_fld * n_band * rest
     padded_group = -(-group // LANES) * LANES
-    devices = n_sec * n_band * n_fld
-    devices = n_sec * n_band * n_fld
     depth = -(-across * lat_pad // LANES) * LANES
     parts = max(t for t in range(1, 8) if across % t == 0)
-    state, sent = call(
+    state_rows = slots * lev // LANES
+    message_rows = n_band * piece + state_rows
+    message = call(
         functools.partial(local_kernel, lat_pad, parts),
-        [((n_fld, lev, slots), BF16), ((devices, piece, LANES), BF16)],
+        [((n_fld, message_rows, LANES), BF16)],
         [HBM] * 4,
         [
             pltpu.VMEM((lev, lat, lon), BF16),
@@ -325,12 +340,11 @@
             pltpu.VMEM((depth, lev * LANES), BF16),
             pltpu.VMEM((slots, LANES), jnp.int32),
             pltpu.VMEM((slots, depth), BF16),
-            pltpu.VMEM((lev, slots), BF16),
-            pltpu.VMEM((n_band * n_fld, piece, LANES), BF16),
+            pltpu.VMEM((n_fld, message_rows, LANES), BF16),
             pltpu.VMEM((LANES, padded_group), F32),
             pltpu.VMEM((group * lev, LANES), F32),
             pltpu.SemaphoreType.DMA((parts + 3,)),
-            pltpu.SemaphoreType.DMA((n_fld + n_sec,)),
+            pltpu.SemaphoreType.DMA((1,)),
         ],
         (grid.reshape(lev, lat, lon), block_row, interp, table),
         2 * slots * depth * lev * LANES + 2 * lev * lat * lon * THIRDS * group,
@@ -339,9 +353,20 @@
         HBM,
         WHOLE,
     )
-    near = lax.all_to_all(state, "fld", 0, 0, tiled=True)
-    pieces = lax.all_to_all(sent, ("sec", "band", "fld"), 0, 0, tiled=True)
+    arrived = lax.all_to_all(message, "fld", 0, 0, tiled=True)
+    sent, near = call(
+        functools.partial(regroup_kernel, n_band),
+        [((n_sec * n_band, n_fld, piece, LANES), BF16), ((n_fld, state_rows, LANES), BF16)],
+        [HBM],
+        [pltpu.SemaphoreType.DMA((n_sec * n_band + 1,))],
+        (arrived,),
+        0,
+        4 * n_sec * n_band * n_fld * piece * LANES,
+        "regroup",
+        HBM,
+    )
     far = lax.ppermute(near, "sec", [(i, 1 - i) for i in range(n_sec)])
+    pieces = lax.all_to_all(sent, ("sec", "band"), 0, 0, tiled=True)
     spec_bands, flux_rows, _ = inverses.shape
     sources = spec_bands * flux_rows
     states = source_weights.shape[0]
@@ -369,7 +394,7 @@
     )
     mine = n_sec * lev // (n_sec * n_fld)
     heating = call(
-        functools.partial(column_kernel, n_sec, n_fld, lat_pad),
+        functools.partial(column_kernel, n_sec, n_fld, lat_pad, slots),
         [((mine, lat, lon), BF16)],
         [SMEM] + [VMEM] * 6,
         [

time: 34.4 us -> 35.4 us (1.029)
  waiting for transfers between devices: 2.46 us -> 0.01 us
  blocking collectives: 12.1 us -> 13.9 us
  starting transfers between devices: 4.08 us -> 4.98 us
  Pallas kernels: 14.7 us -> 15.4 us
    all_to_all x1, waiting for transfers between devices: 2.45 us -> 0.01 us  [body(): pieces = lax.all_to_all(sent, ('sec', 'band'), 0, 0, tiled=True)]
    all_to_all x1, blocking collectives: 12.1 us -> 13.9 us  [body(): arrived = lax.all_to_all(message, 'fld', 0, 0, tiled=True)]
    all_to_all x1, starting transfers between devices: 2.58 us -> 3.42 us  [body(): pieces = lax.all_to_all(sent, ('sec', 'band'), 0, 0, tiled=True)]
    pallas_call x4 -> x5, Pallas kernels: 14.7 us -> 15.4 us  [call(): pl.pallas_call(kernel, out_shape=shapes[0] if single else shapes, in_spec...]
  transfers between devices with their start and end apart: 2 -> 2, of which waited for: 1 -> 0; matrix products, arithmetic and copies ran while one was open for 0% -> 0% of each run, Pallas kernels for 23% -> 22%
where the time goes in v6:
time: 35.4 us; the launch traced here: 35.1 us
  Pallas kernels  15.4 us (44%)
  blocking collectives  13.9 us (39%)
  starting transfers between devices  4.98 us (14%)
  between operations  0.76 us (2%)
    pallas_call x5, Pallas kernels, call(): pl.pallas_call(kernel, out_shape=shapes[0] if single else shapes, in_spec...  15.4 us
    all_to_all x1, blocking collectives, body(): arrived = lax.all_to_all(message, 'fld', 0, 0, tiled=True)  13.9 us
    all_to_all x1, starting transfers between devices, body(): pieces = lax.all_to_all(sent, ('sec', 'band'), 0, 0, tiled=True)  3.42 us
    ppermute x1, starting transfers between devices, body(): far = lax.ppermute(near, 'sec', [(i, 1 - i) for i in range(n_sec)])  1.56 us
  transfers between devices with their start and end apart: 2, of which 0 were waited for; matrix products, arithmetic and copies ran while one was open for 0% of the time, Pallas kernels for 22%

profile of v6, /device:TPU:0, one launch (start us, length us, event | category | flops | bytes accessed | tf_op | source)
XLA Modules:
  0.0 35.1 jit_solution(2825532027004838517)
XLA Ops:
  0.6 0.0 copy-start
  0.6 0.0 copy-start.1
  0.7 0.0 copy-start.2
  0.7 5.9 %local.1 = bf16[4,192,128]{2,1,0:T(8,128)(2,1)} custom-call(bf16[8,40,2688]{2,1,0:T(8,128)(2,1)} %bitcast.8, s32[1,1024]{1,0:T(1,128)} %bitcast.6, bf16[1024,128]{1,0:T(8,128)(2,1)} %interp.1, bf16[2688,192]{1,0:T(8,128)(2,1)} %constant.2.clone.table_hbm), custom_call_target="tpu_custom_call" | custom-call | flops 2477785088 | bytes 1982464 | tf_op jit(solution)/shard_map/local/pallas_call | solution.py:299
  6.6 0.0 copy-start.3
  6.6 0.0 copy-start.4
  6.6 0.0 copy-start.5
  6.6 13.9 %all_to_all.10.arrived = bf16[4,192,128]{2,1,0:T(8,128)(2,1)S(1)} all-to-all(bf16[4,192,128]{2,1,0:T(8,128)(2,1)} %local.1), channel_id=1, replica_groups=mesh['sec'=2,'band'=4,'fld'=4] {'fld'}, dimensions={0} | all-to-all | bytes 393216 | tf_op jit(solution)/shard_map/all_to_all | solution.py:356
  20.5 0.8 %regroup.1 = (bf16[8,4,32,128]{3,2,1,0:T(8,128)(2,1)}, bf16[4,64,128]{2,1,0:T(8,128)(2,1)S(1)}) custom-call(bf16[4,192,128]{2,1,0:T(8,128)(2,1)S(1)} %all_to_all.10.arrived), custom_call_target="tpu_custom_call" | custom-call | bytes 524288 | tf_op jit(solution)/shard_map/regroup/pallas_call | solution.py:299
  21.3 1.6 %collective-permute-start = (bf16[4,64,128]{2,1,0:T(8,128)(2,1)S(1)}, bf16[4,64,128]{2,1,0:T(8,128)(2,1)S(1)}, u32[]{:S(2)}, u32[]{:S(2)}) collective-permute-start(bf16[4,64,128]{2,1,0:T(8,128)(2,1)S(1)} %get-tuple-element.11.near), channel_id=1, source_target_pairs={{0,16},{16,0},{1,17},{17,1},{2,18},{18,2},{3,19},{19,3},{4,20},{20... | collective-permute-start | bytes 196616 | tf_op jit(solution)/shard_map/ppermute | solution.py:368
  22.9 0.0 copy-done
  22.9 0.0 copy-done.1
  22.9 0.0 copy-done.2
  22.9 1.3 %prepare.1 = (bf16[4,2,144,128]{3,2,1,0:T(8,128)(2,1)S(1)}, bf16[2048,64]{1,0:T(8,128)(2,1)S(1)}, bf16[32,2048]{1,0:T(8,128)(2,1)S(1)}) custom-call(bf16[6,48,160]{2,1,0:T(8,128)(2,1)S(1)} %bitcast.5, bf16[64,2048]{1,0:T(8,128)(2,1)S(1)} %copy-done, bf16[32,32,64]{2,1,0:T(8,128)(2,1)S(1)} %bitcast.4), custom_call_target="tpu_custom_call" | custom-call | bytes 1179648 | tf_op jit(solution)/shard_map/prepare/pallas_call | solution.py:299
  24.2 3.4 %all-to-all-start.1 = ((bf16[8,4,32,128]{3,2,1,0:T(8,128)(2,1)}), bf16[8,4,32,128]{3,2,1,0:T(8,128)(2,1)S(1)}, u32[]{:S(2)}, u32[]{:S(2)}) async-start(bf16[8,4,32,128]{3,2,1,0:T(8,128)(2,1)} %get-tuple-element.8), calls=%async_computation.1 | async-start | bytes 524288 | tf_op jit(solution)/shard_map/all_to_all | solution.py:369
  27.7 0.0 collective-permute-done.far
  27.7 0.0 copy-done.3
  27.7 0.0 copy-done.4
  27.7 0.0 copy-done.5
  27.7 6.4 %columns.1 = bf16[2,40,2688]{2,1,0:T(8,128)(2,1)} custom-call(s32[4]{0:T(128)S(1)} %copy-done.5, bf16[2048,64]{1,0:T(8,128)(2,1)S(1)} %get-tuple-element.9.weights, bf16[32,2048]{1,0:T(8,128)(2,1)S(1)} %get-tuple-element.10.inverses, s32[1,1024]{1,0:T(1,128)S(1)} %bitcast.7, bf16[1024,128]{1,0:T(8,128)(2,1)S(1)} %copy-done.3, ...), custom_call_target="tpu_custom_call" | custom-call | flops 8589934592 | bytes 2097152 | tf_op jit(solution)/shard_map/columns/pallas_call | solution.py:299
  34.1 0.0 all-to-all-done.1.pieces
  34.1 1.0 %legendre.1 = bf16[6,2,4,16,48]{4,3,2,1,0:T(8,128)(2,1)} custom-call(bf16[4,2,144,128]{3,2,1,0:T(8,128)(2,1)S(1)} %get-tuple-element.7.weights, bf16[8,4,32,128]{3,2,1,0:T(8,128)(2,1)S(1)} %all-to-all-done.1.pieces), custom_call_target="tpu_custom_call" | custom-call | flops 75497472 | bytes 262144 | tf_op jit(solution)/shard_map/legendre/pallas_call | solution.py:299
Async XLA Ops:
  0.6 22.3 %copy-start = (bf16[64,2048]{1,0:T(8,128)(2,1)S(1)}, bf16[64,2048]{1,0:T(8,128)(2,1)}, u32[]{:S(2)}) copy-start(bf16[64,2048]{1,0:T(8,128)(2,1)} %weights.1) | copy-start | bytes 786436
  0.6 22.3 %copy-start.1 = (bf16[64,32,32]{0,2,1:T(8,128)(2,1)S(1)}, bf16[64,32,32]{0,2,1:T(8,128)(2,1)}, u32[]{:S(2)}) copy-start(bf16[64,32,32]{0,2,1:T(8,128)(2,1)} %param.14) | copy-start | bytes 393220
  0.7 22.3 %copy-start.2 = (bf16[6,160,48]{1,2,0:T(8,128)(2,1)S(1)}, bf16[6,160,48]{1,2,0:T(8,128)(2,1)}, u32[]{:S(2)}) copy-start(bf16[6,160,48]{1,2,0:T(8,128)(2,1)} %param.9) | copy-start | bytes 276484
  6.6 21.1 %copy-start.3 = (bf16[1024,128]{1,0:T(8,128)(2,1)S(1)}, bf16[1024,128]{1,0:T(8,128)(2,1)}, u32[]{:S(2)}) copy-start(bf16[1024,128]{1,0:T(8,128)(2,1)} %interp.1) | copy-start | bytes 786436
  6.6 21.1 %copy-start.4 = (s32[1024]{0:T(1024)S(1)}, s32[1024]{0:T(1024)}, u32[]{:S(2)}) copy-start(s32[1024]{0:T(1024)} %param.11) | copy-start | bytes 12292
  6.6 21.1 %copy-start.5 = (s32[4]{0:T(128)S(1)}, s32[4]{0:T(128)}, u32[]{:S(2)}) copy-start(s32[4]{0:T(128)} %counts.1) | copy-start | bytes 52
  21.3 6.3 %collective-permute-start = (bf16[4,64,128]{2,1,0:T(8,128)(2,1)S(1)}, bf16[4,64,128]{2,1,0:T(8,128)(2,1)S(1)}, u32[]{:S(2)}, u32[]{:S(2)}) collective-permute-start(bf16[4,64,128]{2,1,0:T(8,128)(2,1)S(1)} %get-tuple-element.11.near), channel_id=1, source_target_pairs={{0,16},{16,0},{1,17},{17,1},{2,18},{18,2},{3,19},{19,3},{4,20},{20... | collective-permute-start | bytes 196616 | tf_op jit(solution)/shard_map/ppermute | solution.py:368
  24.2 9.8 %all-to-all-start.1 = ((bf16[8,4,32,128]{3,2,1,0:T(8,128)(2,1)}), bf16[8,4,32,128]{3,2,1,0:T(8,128)(2,1)S(1)}, u32[]{:S(2)}, u32[]{:S(2)}) async-start(bf16[8,4,32,128]{3,2,1,0:T(8,128)(2,1)} %get-tuple-element.8), calls=%async_computation.1 | async-start | bytes 524288 | tf_op jit(solution)/shard_map/all_to_all | solution.py:369

commit v7 on v6

--- a/solution.py
+++ b/solution.py
@@ -37,16 +37,13 @@
     return values.astype(np.float32).astype(BF16)
 
 
-def fourier(lev, lat, grid, table, message, padded, rows):
-    flat = jnp.concatenate([grid[level] for level in range(lev)], axis=0)
-    coeffs = jnp.dot(flat, table[...], preferred_element_type=F32)
+def pack(lev, lat, coeffs, message, padded, rows):
     group = coeffs.shape[1] // THIRDS
     padded[...] = jnp.zeros_like(padded)
     for level in range(lev):
-        one = coeffs[level * lat : (level + 1) * lat]
         for third in range(THIRDS):
-            padded[third * lat : (third + 1) * lat, :group] = one[
-                :, third * group : (third + 1) * group
+            padded[third * lat : (third + 1) * lat, :group] = coeffs[
+                level * lat : (level + 1) * lat, third * group : (third + 1) * group
             ]
         rows[pl.ds(level, group, stride=lev), :] = jnp.transpose(padded[...])[:group]
     targets = message.shape[0]
@@ -54,25 +51,15 @@
     message[:, :size, :] = rows[...].astype(BF16).reshape(targets, size, LANES)
 
 
-def prepare_kernel(lat, n_band, legendre, weights, inverses, out, out_weights, out_inverses,
-                   wide, flipped, rows):
-    states, sources = weights.shape
+def prepare_kernel(lat, n_band, legendre, inverses, out, out_inverses, wide, rows, turned):
     flux_rows, _, spec_bands = inverses.shape
-    for start in range(0, sources, LANES):
-        flipped[start : start + LANES, :] = jnp.transpose(
-            weights[:, start : start + LANES].astype(F32)
-        )
     for row in range(flux_rows):
         rows[row * flux_rows : (row + 1) * flux_rows, :] = inverses[row].astype(F32)
     for row in range(flux_rows):
-        out_weights[row * spec_bands : (row + 1) * spec_bands, :] = flipped[
-            pl.ds(row, spec_bands, stride=flux_rows), :
-        ].astype(BF16)
-    for row in range(0, flux_rows, 2):
-        pair = [rows[pl.ds(row + i, flux_rows, stride=flux_rows), :] for i in range(2)]
-        out_inverses[:, row * spec_bands : (row + 2) * spec_bands] = jnp.concatenate(
-            pair, axis=1
-        ).astype(BF16)
+        turned[pl.ds(row, spec_bands, stride=flux_rows), :] = jnp.transpose(
+            rows[pl.ds(row, flux_rows, stride=flux_rows), :]
+        )
+    out_inverses[...] = turned[...].astype(BF16)
     waves, degrees, _ = legendre.shape
     wide[...] = jnp.zeros_like(wide)
     lane = lax.broadcasted_iota(jnp.int32, (degrees, LANES), 1)
@@ -143,7 +130,6 @@
     small = [
         pltpu.make_async_copy(blocks_hbm, blocks, sems.at[parts]),
         pltpu.make_async_copy(interp_hbm, interp, sems.at[parts + 1]),
-        pltpu.make_async_copy(table_hbm, table, sems.at[parts + 2]),
     ]
     loads = [
         pltpu.make_async_copy(
@@ -153,11 +139,19 @@
         )
         for part in range(parts)
     ]
+    tables = [
+        pltpu.make_async_copy(
+            table_hbm.at[pl.ds(part * step, step)],
+            table.at[pl.ds(part * step, step)],
+            sems.at[parts + 2 + part],
+        )
+        for part in range(parts)
+    ]
     small[0].start()
-    for copy in loads:
-        copy.start()
+    for part in range(parts):
+        loads[part].start()
+        tables[part].start()
     small[1].start()
-    small[2].start()
     small[0].wait()
     row = slot_rows(blocks[...], across, lat_pad)
     column[...] = jnp.transpose(jnp.broadcast_to(row, (LANES, slots)))
@@ -169,8 +163,16 @@
             selector[start : start + chunk, base : base + LANES] = jnp.where(
                 mine == lane + base, 1.0, 0.0
             ).astype(BF16)
+    coeffs = jnp.zeros((lev * lat, table.shape[1]), F32)
     for part in range(parts):
         loads[part].wait()
+        tables[part].wait()
+        flat = jnp.concatenate(
+            [grid[level, :, part * step : (part + 1) * step] for level in range(lev)], axis=0
+        )
+        coeffs = coeffs + jnp.dot(
+            flat, table[part * step : (part + 1) * step, :], preferred_element_type=F32
+        )
         for tile in range(part * across // parts, (part + 1) * across // parts):
             patch[tile * lat_pad + lat : (tile + 1) * lat_pad, :] = jnp.zeros(
                 (lat_pad - lat, lev * LANES), BF16
@@ -196,14 +198,13 @@
             row = message.shape[1] - slots // LANES * lev + (start // LANES + tile) * lev
             for target in range(message.shape[0]):
                 message[target, row : row + lev, :] = state[:, tile * LANES : (tile + 1) * LANES]
-    small[2].wait()
-    fourier(lev, lat, grid, table, message, padded, rows)
+    pack(lev, lat, coeffs, message, padded, rows)
     copy = pltpu.make_async_copy(message, out, send.at[0])
     copy.start()
     copy.wait()
 
 
-def regroup_kernel(n_band, arrived, out, out_state, sems):
+def regroup_kernel(n_band, arrived, _, out, out_state, sems):
     size = out.shape[2]
     copies = []
     for target in range(out.shape[0]):
@@ -226,8 +227,8 @@
     return jnp.where(x < -8.0, power, jnp.maximum(x, jnp.log(1.0 + power)))
 
 
-def column_kernel(n_sec, n_fld, lat_pad, slots, counts, weights, inverses, blocks, interp, near, far,
-                  out, state, flux_up, flux_down, spread, result, sems):
+def column_kernel(n_sec, n_fld, lat_pad, slots, counts, weights, inverses, blocks, interp,
+                  near, far, out, state, spread, result, sems):
     lev = near.shape[1] * LANES // slots
     place = lax.axis_index("sec")
     for fld in range(n_fld):
@@ -237,37 +238,36 @@
                 state[
                     pl.ds(pl.multiple_of(row, lev), lev), tile * LANES : (tile + 1) * LANES
                 ] = pieces[fld, tile * lev : (tile + 1) * lev, :].astype(F32)
-    column = state[...].astype(BF16)
-    flux_rows = inverses.shape[0]
-    flux = jnp.zeros((flux_rows, slots), F32)
-    chunk = 256
-    for start in range(0, weights.shape[0], chunk):
-        gates = jnp.dot(weights[start : start + chunk, :], column, preferred_element_type=F32)
-        source = softplus(gates).astype(BF16)
-        flux = flux + jnp.dot(
-            inverses[:, start : start + chunk], source, preferred_element_type=F32
-        )
-    levels = flux_rows // 2
-    flux_up[:levels, :] = flux[:levels]
-    flux_down[:levels, :] = flux[levels:]
-    flux_up[levels:, :] = jnp.zeros((8, slots), F32)
-    flux_down[levels:, :] = jnp.zeros((8, slots), F32)
     mine, lat, lon = result.shape
     across = lon // LANES
-    live = lax.broadcasted_iota(jnp.int32, (1, slots), 1) < counts[lax.axis_index("band")]
-    base = (lax.axis_index("sec") * n_fld + lax.axis_index("fld")) * mine
-    for level in range(mine):
-        at = base + level
-        heat = (flux_up[pl.ds(at, 1), :] - flux_up[pl.ds(at + 1, 1), :]) - (
-            flux_down[pl.ds(at, 1), :] - flux_down[pl.ds(at + 1, 1), :]
-        )
-        heat = jnp.where(live, heat, 0.0).astype(BF16).astype(F32)
-        for start in range(0, slots, LANES):
-            down = jnp.transpose(
-                jnp.broadcast_to(heat[:, start : start + LANES], (LANES, LANES))
+    sources, flux_rows = inverses.shape
+    levels = flux_rows // 2
+    count = counts[lax.axis_index("band")]
+    base = (place * n_fld + lax.axis_index("fld")) * mine
+    chunk = 256
+    lane = lax.broadcasted_iota(jnp.int32, (1, flux_rows), 1)
+    slot = lax.broadcasted_iota(jnp.int32, (chunk, 1), 0)
+    for start in range(0, slots, chunk):
+        column = jnp.transpose(state[:, start : start + chunk]).astype(BF16)
+        flux = jnp.zeros((chunk, flux_rows), F32)
+        for source in range(0, sources, chunk):
+            gates = jnp.dot(
+                column, weights[:, source : source + chunk], preferred_element_type=F32
             )
-            spread[start : start + LANES, level * LANES : (level + 1) * LANES] = (
-                down * interp[start : start + LANES, :].astype(F32)
+            flux = flux + jnp.dot(
+                softplus(gates).astype(BF16),
+                inverses[source : source + chunk, :],
+                preferred_element_type=F32,
+            )
+        for level in range(mine):
+            at = base + level
+            plus = (lane == at) | ((lane == at + levels + 1) & (at + 1 < levels))
+            minus = (lane == at + levels) | ((lane == at + 1) & (at + 1 < levels))
+            terms = jnp.where(plus, flux, 0.0) - jnp.where(minus, flux, 0.0)
+            heat = jnp.sum(terms, axis=1, keepdims=True)
+            heat = jnp.where(slot + start < count, heat, 0.0).astype(BF16).astype(F32)
+            spread[start : start + chunk, level * LANES : (level + 1) * LANES] = (
+                heat * interp[start : start + chunk, :].astype(F32)
             ).astype(BF16)
     row = slot_rows(blocks[...], across, lat_pad)
     tiles = max(t for t in range(1, 8) if across % t == 0)
@@ -343,7 +343,7 @@
             pltpu.VMEM((n_fld, message_rows, LANES), BF16),
             pltpu.VMEM((LANES, padded_group), F32),
             pltpu.VMEM((group * lev, LANES), F32),
-            pltpu.SemaphoreType.DMA((parts + 3,)),
+            pltpu.SemaphoreType.DMA((2 * parts + 2,)),
             pltpu.SemaphoreType.DMA((1,)),
         ],
         (grid.reshape(lev, lat, lon), block_row, interp, table),
@@ -354,12 +354,30 @@
         WHOLE,
     )
     arrived = lax.all_to_all(message, "fld", 0, 0, tiled=True)
+    spec_bands, flux_rows, _ = inverses.shape
+    basis, inverse_rows = call(
+        functools.partial(prepare_kernel, lat, n_band),
+        [
+            ((n_band, 2, THIRDS * degrees, LANES), BF16),
+            ((spec_bands * flux_rows, flux_rows), BF16),
+        ],
+        [VMEM, VMEM],
+        [
+            pltpu.VMEM((degrees, (n_band * lat // LANES + 2) * LANES), F32),
+            pltpu.VMEM((flux_rows * flux_rows, spec_bands), F32),
+            pltpu.VMEM((spec_bands * flux_rows, flux_rows), F32),
+        ],
+        (jnp.swapaxes(legendre, 1, 2), jnp.transpose(inverses, (1, 2, 0))),
+        0,
+        8 * wave_dev * degrees * n_band * LANES,
+        "prepare",
+    )
     sent, near = call(
         functools.partial(regroup_kernel, n_band),
         [((n_sec * n_band, n_fld, piece, LANES), BF16), ((n_fld, state_rows, LANES), BF16)],
-        [HBM],
+        [HBM, HBM],
         [pltpu.SemaphoreType.DMA((n_sec * n_band + 1,))],
-        (arrived,),
+        (arrived, basis),
         0,
         4 * n_sec * n_band * n_fld * piece * LANES,
         "regroup",
@@ -367,31 +385,8 @@
     )
     far = lax.ppermute(near, "sec", [(i, 1 - i) for i in range(n_sec)])
     pieces = lax.all_to_all(sent, ("sec", "band"), 0, 0, tiled=True)
-    spec_bands, flux_rows, _ = inverses.shape
     sources = spec_bands * flux_rows
     states = source_weights.shape[0]
-    basis, weights, inverse_rows = call(
-        functools.partial(prepare_kernel, lat, n_band),
-        [
-            ((n_band, 2, THIRDS * degrees, LANES), BF16),
-            ((sources, states), BF16),
-            ((flux_rows, sources), BF16),
-        ],
-        [VMEM, VMEM, VMEM],
-        [
-            pltpu.VMEM((degrees, (n_band * lat // LANES + 2) * LANES), F32),
-            pltpu.VMEM((sources, states), F32),
-            pltpu.VMEM((flux_rows * flux_rows, spec_bands), F32),
-        ],
-        (
-            jnp.swapaxes(legendre, 1, 2),
-            source_weights,
-            jnp.transpose(inverses, (1, 2, 0)),
-        ),
-        0,
-        8 * wave_dev * degrees * n_band * LANES,
-        "prepare",
-    )
     mine = n_sec * lev // (n_sec * n_fld)
     heating = call(
         functools.partial(column_kernel, n_sec, n_fld, lat_pad, slots),
@@ -399,13 +394,11 @@
         [SMEM] + [VMEM] * 6,
         [
             pltpu.VMEM((states, slots), F32),
-            pltpu.VMEM((flux_rows // 2 + 8, slots), F32),
-            pltpu.VMEM((flux_rows // 2 + 8, slots), F32),
             pltpu.VMEM((slots, mine * LANES), BF16),
             pltpu.VMEM((mine, lat, lon), BF16),
             pltpu.SemaphoreType.DMA((across,)),
         ],
-        (counts, weights, inverse_rows, block_row, interp, near, far),
+        (counts, source_weights, inverse_rows, block_row, interp, near, far),
         8 * slots * slots * 1024,
         2 * slots * slots,
         "columns",

time: 35.4 us -> 35.2 us (level)
  blocking collectives: 13.9 us -> 0 us
  starting transfers between devices: 4.98 us -> 11.4 us
  waiting for transfers between devices: 0.01 us -> 6.29 us
  Pallas kernels: 15.4 us -> 16.3 us
    all_to_all x1 -> x0, blocking collectives: 13.9 us -> none  [body(): arrived = lax.all_to_all(message, 'fld', 0, 0, tiled=True)]
    all_to_all x0 -> x1, starting transfers between devices: none -> 6.47 us  [body(): arrived = lax.all_to_all(message, 'fld', 0, 0, tiled=True)]
    all_to_all x0 -> x1, waiting for transfers between devices: none -> 6.28 us  [body(): arrived = lax.all_to_all(message, 'fld', 0, 0, tiled=True)]
    pallas_call x5, Pallas kernels: 15.4 us -> 16.3 us  [call(): pl.pallas_call(kernel, out_shape=shapes[0] if single else shapes, in_spec...]
  transfers between devices with their start and end apart: 2 -> 3, of which waited for: 0 -> 1; matrix products, arithmetic and copies ran while one was open for 0% -> 0% of each run, Pallas kernels for 22% -> 22%
where the time goes in v7:
time: 35.2 us; the launch traced here: 34.9 us
  Pallas kernels  16.3 us (46%)
  starting transfers between devices  11.4 us (32%)
  waiting for transfers between devices  6.29 us (18%)
  between operations  0.76 us (2%)
    pallas_call x5, Pallas kernels, call(): pl.pallas_call(kernel, out_shape=shapes[0] if single else shapes, in_spec...  16.3 us
    all_to_all x1, starting transfers between devices, body(): arrived = lax.all_to_all(message, 'fld', 0, 0, tiled=True)  6.47 us
    all_to_all x1, waiting for transfers between devices, body(): arrived = lax.all_to_all(message, 'fld', 0, 0, tiled=True)  6.28 us
    all_to_all x1, starting transfers between devices, body(): pieces = lax.all_to_all(sent, ('sec', 'band'), 0, 0, tiled=True)  3.41 us
    ppermute x1, starting transfers between devices, body(): far = lax.ppermute(near, 'sec', [(i, 1 - i) for i in range(n_sec)])  1.57 us
  transfers between devices with their start and end apart: 3, of which 1 were waited for; matrix products, arithmetic and copies ran while one was open for 0% of the time, Pallas kernels for 22%

profile of v7, /device:TPU:0, one launch (start us, length us, event | category | flops | bytes accessed | tf_op | source)
XLA Modules:
  0.0 34.9 jit_solution(15974398317998586241)
XLA Ops:
  0.6 0.0 copy-start
  0.6 0.0 copy-start.1
  0.6 7.0 %local.1 = bf16[4,192,128]{2,1,0:T(8,128)(2,1)} custom-call(bf16[8,40,2688]{2,1,0:T(8,128)(2,1)} %bitcast.8, s32[1,1024]{1,0:T(1,128)} %bitcast.6, bf16[1024,128]{1,0:T(8,128)(2,1)} %interp.1, bf16[2688,192]{1,0:T(8,128)(2,1)} %constant.2.clone.table_hbm), custom_call_target="tpu_custom_call" | custom-call | flops 2477785088 | bytes 1982464 | tf_op jit(solution)/shard_map/local/pallas_call | solution.py:299
  7.6 0.0 copy-start.2
  7.6 0.0 copy-start.3
  7.6 0.0 copy-start.4
  7.7 0.0 copy-start.5
  7.7 6.5 %all-to-all-start = ((bf16[4,192,128]{2,1,0:T(8,128)(2,1)}), bf16[4,192,128]{2,1,0:T(8,128)(2,1)S(1)}, u32[]{:S(2)}, u32[]{:S(2)}) async-start(bf16[4,192,128]{2,1,0:T(8,128)(2,1)} %local.1), calls=%async_computation | async-start | bytes 393216 | tf_op jit(solution)/shard_map/all_to_all | solution.py:356
  14.1 0.0 copy-done
  14.1 0.0 copy-done.1
  14.1 1.2 %prepare.1 = (bf16[4,2,144,128]{3,2,1,0:T(8,128)(2,1)S(1)}, bf16[2048,32]{1,0:T(8,128)(2,1)S(1)}) custom-call(bf16[6,48,160]{2,1,0:T(8,128)(2,1)S(1)} %bitcast.5, bf16[32,32,64]{2,1,0:T(8,128)(2,1)S(1)} %bitcast.4), custom_call_target="tpu_custom_call" | custom-call | bytes 1179648 | tf_op jit(solution)/shard_map/prepare/pallas_call | solution.py:299
  15.4 6.3 %all-to-all-done.arrived = bf16[4,192,128]{2,1,0:T(8,128)(2,1)S(1)} async-done(((bf16[4,192,128]{2,1,0:T(8,128)(2,1)}), bf16[4,192,128]{2,1,0:T(8,128)(2,1)S(1)}, u32[]{:S(2)}, u32[]{:S(2)}) %all-to-all-start) | async-done | bytes 196640 | tf_op jit(solution)/shard_map/all_to_all | solution.py:356
  21.6 0.8 %regroup.1 = (bf16[8,4,32,128]{3,2,1,0:T(8,128)(2,1)}, bf16[4,64,128]{2,1,0:T(8,128)(2,1)S(1)}) custom-call(bf16[4,192,128]{2,1,0:T(8,128)(2,1)S(1)} %all-to-all-done.arrived, bf16[4,2,144,128]{3,2,1,0:T(8,128)(2,1)S(1)} %get-tuple-element.6._.weights), custom_call_target="tpu_custom_call" | custom-call | bytes 524288 | tf_op jit(solution)/shard_map/regroup/pallas_call | solution.py:299
  22.4 1.6 %collective-permute-start = (bf16[4,64,128]{2,1,0:T(8,128)(2,1)S(1)}, bf16[4,64,128]{2,1,0:T(8,128)(2,1)S(1)}, u32[]{:S(2)}, u32[]{:S(2)}) collective-permute-start(bf16[4,64,128]{2,1,0:T(8,128)(2,1)S(1)} %get-tuple-element.9.near), channel_id=1, source_target_pairs={{0,16},{16,0},{1,17},{17,1},{2,18},{18,2},{3,19},{19,3},{4,20},{20... | collective-permute-start | bytes 196616 | tf_op jit(solution)/shard_map/ppermute | solution.py:386
  24.0 3.4 %all-to-all-start.1 = ((bf16[8,4,32,128]{3,2,1,0:T(8,128)(2,1)}), bf16[8,4,32,128]{3,2,1,0:T(8,128)(2,1)S(1)}, u32[]{:S(2)}, u32[]{:S(2)}) async-start(bf16[8,4,32,128]{3,2,1,0:T(8,128)(2,1)} %get-tuple-element.7), calls=%async_computation.1 | async-start | bytes 524288 | tf_op jit(solution)/shard_map/all_to_all | solution.py:387
  27.4 0.0 collective-permute-done.far
  27.4 0.0 copy-done.2
  27.4 0.0 copy-done.3
  27.4 0.0 copy-done.4
  27.5 0.0 copy-done.5
  27.5 6.3 %columns.1 = bf16[2,40,2688]{2,1,0:T(8,128)(2,1)} custom-call(s32[4]{0:T(128)S(1)} %copy-done.5, bf16[64,2048]{1,0:T(8,128)(2,1)S(1)} %copy-done.3, bf16[2048,32]{1,0:T(8,128)(2,1)S(1)} %get-tuple-element.8.inverses, s32[1,1024]{1,0:T(1,128)S(1)} %bitcast.7, bf16[1024,128]{1,0:T(8,128)(2,1)S(1)} %copy-done.2, bf16[4,64,128]{2,1,0:T(8,128)(2,1)S(1)} %get-tuple-element.9.near, ...), custom_call_target="tpu_custom_call" | custom-call | flops 8589934592 | bytes 2097152 | tf_op jit(solution)/shard_map/columns/pallas_call | solution.py:299
  33.8 0.0 all-to-all-done.1.pieces
  33.8 1.0 %legendre.1 = bf16[6,2,4,16,48]{4,3,2,1,0:T(8,128)(2,1)} custom-call(bf16[4,2,144,128]{3,2,1,0:T(8,128)(2,1)S(1)} %get-tuple-element.6._.weights, bf16[8,4,32,128]{3,2,1,0:T(8,128)(2,1)S(1)} %all-to-all-done.1.pieces), custom_call_target="tpu_custom_call" | custom-call | flops 75497472 | bytes 262144 | tf_op jit(solution)/shard_map/legendre/pallas_call | solution.py:299
Async XLA Ops:
  0.6 13.5 %copy-start = (bf16[64,32,32]{0,2,1:T(8,128)(2,1)S(1)}, bf16[64,32,32]{0,2,1:T(8,128)(2,1)}, u32[]{:S(2)}) copy-start(bf16[64,32,32]{0,2,1:T(8,128)(2,1)} %param.14) | copy-start | bytes 393220
  0.6 13.5 %copy-start.1 = (bf16[6,160,48]{1,2,0:T(8,128)(2,1)S(1)}, bf16[6,160,48]{1,2,0:T(8,128)(2,1)}, u32[]{:S(2)}) copy-start(bf16[6,160,48]{1,2,0:T(8,128)(2,1)} %param.9) | copy-start | bytes 276484
  7.6 19.8 %copy-start.2 = (bf16[1024,128]{1,0:T(8,128)(2,1)S(1)}, bf16[1024,128]{1,0:T(8,128)(2,1)}, u32[]{:S(2)}) copy-start(bf16[1024,128]{1,0:T(8,128)(2,1)} %interp.1) | copy-start | bytes 786436
  7.6 19.8 %copy-start.3 = (bf16[64,2048]{1,0:T(8,128)(2,1)S(1)}, bf16[64,2048]{1,0:T(8,128)(2,1)}, u32[]{:S(2)}) copy-start(bf16[64,2048]{1,0:T(8,128)(2,1)} %weights.1) | copy-start | bytes 786436
  7.6 19.8 %copy-start.4 = (s32[1024]{0:T(1024)S(1)}, s32[1024]{0:T(1024)}, u32[]{:S(2)}) copy-start(s32[1024]{0:T(1024)} %param.11) | copy-start | bytes 12292
  7.7 19.8 %copy-start.5 = (s32[4]{0:T(128)S(1)}, s32[4]{0:T(128)}, u32[]{:S(2)}) copy-start(s32[4]{0:T(128)} %counts.1) | copy-start | bytes 52
  7.7 14.0 %all-to-all-start = ((bf16[4,192,128]{2,1,0:T(8,128)(2,1)}), bf16[4,192,128]{2,1,0:T(8,128)(2,1)S(1)}, u32[]{:S(2)}, u32[]{:S(2)}) async-start(bf16[4,192,128]{2,1,0:T(8,128)(2,1)} %local.1), calls=%async_computation | async-start | bytes 393216 | tf_op jit(solution)/shard_map/all_to_all | solution.py:356
  22.4 5.0 %collective-permute-start = (bf16[4,64,128]{2,1,0:T(8,128)(2,1)S(1)}, bf16[4,64,128]{2,1,0:T(8,128)(2,1)S(1)}, u32[]{:S(2)}, u32[]{:S(2)}) collective-permute-start(bf16[4,64,128]{2,1,0:T(8,128)(2,1)S(1)} %get-tuple-element.9.near), channel_id=1, source_target_pairs={{0,16},{16,0},{1,17},{17,1},{2,18},{18,2},{3,19},{19,3},{4,20},{20... | collective-permute-start | bytes 196616 | tf_op jit(solution)/shard_map/ppermute | solution.py:386
  24.0 9.8 %all-to-all-start.1 = ((bf16[8,4,32,128]{3,2,1,0:T(8,128)(2,1)}), bf16[8,4,32,128]{3,2,1,0:T(8,128)(2,1)S(1)}, u32[]{:S(2)}, u32[]{:S(2)}) async-start(bf16[8,4,32,128]{3,2,1,0:T(8,128)(2,1)} %get-tuple-element.7), calls=%async_computation.1 | async-start | bytes 524288 | tf_op jit(solution)/shard_map/all_to_all | solution.py:387

commit v8 on v7

--- a/solution.py
+++ b/solution.py
@@ -13,6 +13,7 @@
 F32 = jnp.float32
 LANES = 128
 THIRDS = 3
+LN_2 = math.log(2.0)
 VMEM = pl.BlockSpec(memory_space=pltpu.VMEM)
 HBM = pl.BlockSpec(memory_space=pltpu.HBM)
 SMEM = pl.BlockSpec(memory_space=pltpu.SMEM)
@@ -25,8 +26,8 @@
 def dft_table(lon, wave_dev, n_band, n_fld):
     values_dev = 2 * wave_dev
     rest = values_dev // THIRDS
-    third, fld, band, low = np.meshgrid(
-        np.arange(THIRDS), np.arange(n_fld), np.arange(n_band), np.arange(rest), indexing="ij"
+    third, band, fld, low = np.meshgrid(
+        np.arange(THIRDS), np.arange(n_band), np.arange(n_fld), np.arange(rest), indexing="ij"
     )
     value = third * rest + low
     wave = ((band * n_fld + fld) * wave_dev + value // 2).reshape(-1)
@@ -37,7 +38,7 @@
     return values.astype(np.float32).astype(BF16)
 
 
-def pack(lev, lat, coeffs, message, padded, rows):
+def pack(lev, lat, coeffs, packed, padded, rows):
     group = coeffs.shape[1] // THIRDS
     padded[...] = jnp.zeros_like(padded)
     for level in range(lev):
@@ -46,9 +47,7 @@
                 level * lat : (level + 1) * lat, third * group : (third + 1) * group
             ]
         rows[pl.ds(level, group, stride=lev), :] = jnp.transpose(padded[...])[:group]
-    targets = message.shape[0]
-    size = rows.shape[0] // targets
-    message[:, :size, :] = rows[...].astype(BF16).reshape(targets, size, LANES)
+    packed[...] = rows[...].astype(BF16).reshape(packed.shape)
 
 
 def prepare_kernel(lat, n_band, legendre, inverses, out, out_inverses, wide, rows, turned):
@@ -80,7 +79,7 @@
 
 def legendre_kernel(n_sec, n_band, n_fld, lev, weights, pieces, out):
     degrees = out.shape[4]
-    half = pieces.shape[2] // 2
+    half = pieces.shape[1] // 2
     for parity in range(2):
         rows = slice(parity * half, (parity + 1) * half)
         basis = jnp.concatenate([weights[band, parity] for band in range(n_band)], axis=1)
@@ -88,7 +87,7 @@
             [
                 jnp.concatenate(
                     [
-                        pieces[sec * n_band + band, fld, rows, :]
+                        pieces[(sec * n_band + band) * n_fld + fld, rows, :]
                         for band in range(n_band)
                     ],
                     axis=1,
@@ -120,8 +119,8 @@
 
 
 def local_kernel(lat_pad, parts, grid_hbm, blocks_hbm, interp_hbm, table_hbm, out,
-                 grid, blocks, interp, table, patch, column, selector, message, padded, rows,
-                 sems, send):
+                 out_fourier, grid, blocks, interp, table, patch, column, selector, state, packed,
+                 padded, rows, sems, sends):
     lev, lat, lon = grid.shape
     across = lon // LANES
     slots = interp.shape[0]
@@ -130,6 +129,7 @@
     small = [
         pltpu.make_async_copy(blocks_hbm, blocks, sems.at[parts]),
         pltpu.make_async_copy(interp_hbm, interp, sems.at[parts + 1]),
+        pltpu.make_async_copy(table_hbm, table, sems.at[parts + 2]),
     ]
     loads = [
         pltpu.make_async_copy(
@@ -139,19 +139,11 @@
         )
         for part in range(parts)
     ]
-    tables = [
-        pltpu.make_async_copy(
-            table_hbm.at[pl.ds(part * step, step)],
-            table.at[pl.ds(part * step, step)],
-            sems.at[parts + 2 + part],
-        )
-        for part in range(parts)
-    ]
     small[0].start()
-    for part in range(parts):
-        loads[part].start()
-        tables[part].start()
+    for copy in loads:
+        copy.start()
     small[1].start()
+    small[2].start()
     small[0].wait()
     row = slot_rows(blocks[...], across, lat_pad)
     column[...] = jnp.transpose(jnp.broadcast_to(row, (LANES, slots)))
@@ -163,16 +155,8 @@
             selector[start : start + chunk, base : base + LANES] = jnp.where(
                 mine == lane + base, 1.0, 0.0
             ).astype(BF16)
-    coeffs = jnp.zeros((lev * lat, table.shape[1]), F32)
     for part in range(parts):
         loads[part].wait()
-        tables[part].wait()
-        flat = jnp.concatenate(
-            [grid[level, :, part * step : (part + 1) * step] for level in range(lev)], axis=0
-        )
-        coeffs = coeffs + jnp.dot(
-            flat, table[part * step : (part + 1) * step, :], preferred_element_type=F32
-        )
         for tile in range(part * across // parts, (part + 1) * across // parts):
             patch[tile * lat_pad + lat : (tile + 1) * lat_pad, :] = jnp.zeros(
                 (lat_pad - lat, lev * LANES), BF16
@@ -193,29 +177,29 @@
         for level in range(lev):
             product = picked[:, level * LANES : (level + 1) * LANES] * weights
             total = jnp.where(lane == level, jnp.sum(product, axis=1, keepdims=True), total)
-        state = jnp.transpose(total)[:lev].astype(BF16)
-        for tile in range(chunk // LANES):
-            row = message.shape[1] - slots // LANES * lev + (start // LANES + tile) * lev
-            for target in range(message.shape[0]):
-                message[target, row : row + lev, :] = state[:, tile * LANES : (tile + 1) * LANES]
-    pack(lev, lat, coeffs, message, padded, rows)
-    copy = pltpu.make_async_copy(message, out, send.at[0])
-    copy.start()
-    copy.wait()
-
-
-def regroup_kernel(n_band, arrived, _, out, out_state, sems):
-    size = out.shape[2]
-    copies = []
-    for target in range(out.shape[0]):
-        rows = pl.ds(target % n_band * size, size)
+        state[:, start : start + chunk] = jnp.transpose(total * (1.0 / LN_2))[:lev].astype(BF16)
+    copies = [pltpu.make_async_copy(state, out.at[0], sends.at[0])]
+    copies[0].start()
+    small[2].wait()
+    flat = jnp.concatenate([grid[level] for level in range(lev)], axis=0)
+    coeffs = jnp.dot(flat, table[...], preferred_element_type=F32)
+    pack(lev, lat, coeffs, packed, padded, rows)
+    copies.append(pltpu.make_async_copy(packed, out_fourier, sends.at[1]))
+    copies[1].start()
+    for copy in copies:
+        copy.wait()
+
+
+def merge_kernel(state, other, packed, out_state, out, sems):
+    devices = packed.shape[0]
+    copies = [
+        pltpu.make_async_copy(state, out_state.at[pl.ds(0, 1)], sems.at[0]),
+        pltpu.make_async_copy(other, out_state.at[pl.ds(1, 1)], sems.at[1]),
+    ]
+    for sec in range(out.shape[0] // devices):
         copies.append(
-            pltpu.make_async_copy(arrived.at[:, rows, :], out.at[target], sems.at[target])
-        )
-    rows = pl.ds(n_band * size, out_state.shape[1])
-    copies.append(
-        pltpu.make_async_copy(arrived.at[:, rows, :], out_state, sems.at[out.shape[0]])
-    )
+            pltpu.make_async_copy(packed, out.at[pl.ds(sec * devices, devices)], sems.at[2 + sec])
+        )
     for copy in copies:
         copy.start()
     for copy in copies:
@@ -223,21 +207,18 @@
 
 
 def softplus(x):
-    power = jnp.exp(jnp.minimum(x, 80.0))
-    return jnp.where(x < -8.0, power, jnp.maximum(x, jnp.log(1.0 + power)))
+    power = jnp.exp2(jnp.minimum(x, 120.0))
+    return jnp.where(x < -13.0, power, jnp.maximum(x * LN_2, jnp.log(1.0 + power)))
 
 
 def column_kernel(n_sec, n_fld, lat_pad, slots, counts, weights, inverses, blocks, interp,
                   near, far, out, state, spread, result, sems):
-    lev = near.shape[1] * LANES // slots
+    lev = near.shape[1]
     place = lax.axis_index("sec")
     for fld in range(n_fld):
         for shift, pieces in enumerate((near, far)):
-            row = (fld * n_sec + (place ^ shift)) * lev
-            for tile in range(slots // LANES):
-                state[
-                    pl.ds(pl.multiple_of(row, lev), lev), tile * LANES : (tile + 1) * LANES
-                ] = pieces[fld, tile * lev : (tile + 1) * lev, :].astype(F32)
+            row = ((lax.axis_index("fld") ^ fld) * n_sec + (place ^ shift)) * lev
+            state[pl.ds(pl.multiple_of(row, lev), lev), :] = pieces[fld].astype(F32)
     mine, lat, lon = result.shape
     across = lon // LANES
     sources, flux_rows = inverses.shape
@@ -308,6 +289,10 @@
     )(*args)
 
 
+def exchange(value, axis, shift):
+    return lax.ppermute(value, axis, [(i, i ^ shift) for i in range(lax.axis_size(axis))])
+
+
 def body(grid, legendre, counts, blocks, interp, source_weights, inverses):
     n_sec = lax.axis_size("sec")
     n_band = lax.axis_size("band")
@@ -326,11 +311,9 @@
     padded_group = -(-group // LANES) * LANES
     depth = -(-across * lat_pad // LANES) * LANES
     parts = max(t for t in range(1, 8) if across % t == 0)
-    state_rows = slots * lev // LANES
-    message_rows = n_band * piece + state_rows
-    message = call(
+    state, packed = call(
         functools.partial(local_kernel, lat_pad, parts),
-        [((n_fld, message_rows, LANES), BF16)],
+        [((1, lev, slots), BF16), ((n_band * n_fld, piece, LANES), BF16)],
         [HBM] * 4,
         [
             pltpu.VMEM((lev, lat, lon), BF16),
@@ -340,11 +323,12 @@
             pltpu.VMEM((depth, lev * LANES), BF16),
             pltpu.VMEM((slots, LANES), jnp.int32),
             pltpu.VMEM((slots, depth), BF16),
-            pltpu.VMEM((n_fld, message_rows, LANES), BF16),
+            pltpu.VMEM((lev, slots), BF16),
+            pltpu.VMEM((n_band * n_fld, piece, LANES), BF16),
             pltpu.VMEM((LANES, padded_group), F32),
             pltpu.VMEM((group * lev, LANES), F32),
-            pltpu.SemaphoreType.DMA((2 * parts + 2,)),
-            pltpu.SemaphoreType.DMA((1,)),
+            pltpu.SemaphoreType.DMA((parts + 3,)),
+            pltpu.SemaphoreType.DMA((2,)),
         ],
         (grid.reshape(lev, lat, lon), block_row, interp, table),
         2 * slots * depth * lev * LANES + 2 * lev * lat * lon * THIRDS * group,
@@ -353,7 +337,7 @@
         HBM,
         WHOLE,
     )
-    arrived = lax.all_to_all(message, "fld", 0, 0, tiled=True)
+    other = exchange(state, "fld", 1)
     spec_bands, flux_rows, _ = inverses.shape
     basis, inverse_rows = call(
         functools.partial(prepare_kernel, lat, n_band),
@@ -372,19 +356,23 @@
         8 * wave_dev * degrees * n_band * LANES,
         "prepare",
     )
-    sent, near = call(
-        functools.partial(regroup_kernel, n_band),
-        [((n_sec * n_band, n_fld, piece, LANES), BF16), ((n_fld, state_rows, LANES), BF16)],
-        [HBM, HBM],
-        [pltpu.SemaphoreType.DMA((n_sec * n_band + 1,))],
-        (arrived, basis),
+    near, sent = call(
+        merge_kernel,
+        [((2, lev, slots), BF16), ((n_sec * n_band * n_fld, piece, LANES), BF16)],
+        [HBM] * 3,
+        [pltpu.SemaphoreType.DMA((2 + n_sec,))],
+        (state, other, packed),
         0,
         4 * n_sec * n_band * n_fld * piece * LANES,
-        "regroup",
+        "merge",
         HBM,
     )
-    far = lax.ppermute(near, "sec", [(i, 1 - i) for i in range(n_sec)])
-    pieces = lax.all_to_all(sent, ("sec", "band"), 0, 0, tiled=True)
+    bit = 2
+    while bit < n_fld:
+        near = jnp.concatenate([near, exchange(near, "fld", bit)], axis=0)
+        bit *= 2
+    pieces = lax.all_to_all(sent, ("sec", "band", "fld"), 0, 0, tiled=True)
+    far = exchange(near, "sec", 1)
     sources = spec_bands * flux_rows
     states = source_weights.shape[0]
     mine = n_sec * lev // (n_sec * n_fld)

time: 35.2 us -> 38.8 us (1.10)
  starting transfers between devices: 11.4 us -> 13.2 us
  local copies, waits for them, and re-layouts: 0.03 us -> 1.65 us
  waiting for transfers between devices: 6.29 us -> 7.69 us
  Pallas kernels: 16.3 us -> 15.2 us
    ppermute x1 -> x3, starting transfers between devices: 1.57 us -> 8.01 us  [exchange(): lax.ppermute(value, axis, [(i, i ^ shift) for i in range(lax.axis_size(ax...]
    all_to_all x2 -> x1, starting transfers between devices: 9.88 us -> 5.17 us  [body(): pieces = lax.all_to_all(sent, ('sec', 'band', 'fld'), 0, 0, tiled=True)]
    ppermute x1 -> x3, waiting for transfers between devices: 0.01 us -> 3.82 us  [exchange(): lax.ppermute(value, axis, [(i, i ^ shift) for i in range(lax.axis_size(ax...]
    all_to_all x2 -> x1, waiting for transfers between devices: 6.28 us -> 3.87 us  [body(): pieces = lax.all_to_all(sent, ('sec', 'band', 'fld'), 0, 0, tiled=True)]
    unnamed x12 -> x17, local copies, waits for them, and re-layouts: 0.03 us -> 1.65 us
    pallas_call x5, Pallas kernels: 16.3 us -> 15.2 us  [call(): pl.pallas_call(kernel, out_shape=shapes[0] if single else shapes, in_spec...]
  transfers between devices with their start and end apart: 3 -> 4, of which waited for: 1 -> 3; matrix products, arithmetic and copies ran while one was open for 0% -> 0% of each run, Pallas kernels for 22% -> 20%
where the time goes in v8:
time: 38.8 us; the launch traced here: 38.5 us
  Pallas kernels  15.2 us (39%)
  starting transfers between devices  13.2 us (34%)
  waiting for transfers between devices  7.69 us (20%)
  local copies, waits for them, and re-layouts  1.65 us (4%)
  between operations  0.76 us (2%)
    pallas_call x5, Pallas kernels, call(): pl.pallas_call(kernel, out_shape=shapes[0] if single else shapes, in_spec...  15.2 us
    ppermute x3, starting transfers between devices, exchange(): lax.ppermute(value, axis, [(i, i ^ shift) for i in range(lax.axis_size(ax...  8.01 us
    all_to_all x1, starting transfers between devices, body(): pieces = lax.all_to_all(sent, ('sec', 'band', 'fld'), 0, 0, tiled=True)  5.17 us
    all_to_all x1, waiting for transfers between devices, body(): pieces = lax.all_to_all(sent, ('sec', 'band', 'fld'), 0, 0, tiled=True)  3.87 us
    ppermute x3, waiting for transfers between devices, exchange(): lax.ppermute(value, axis, [(i, i ^ shift) for i in range(lax.axis_size(ax...  3.82 us
    unnamed x17, local copies, waits for them, and re-layouts  1.65 us
  transfers between devices with their start and end apart: 4, of which 3 were waited for; matrix products, arithmetic and copies ran while one was open for 0% of the time, Pallas kernels for 20%

profile of v8, /device:TPU:0, one launch (start us, length us, event | category | flops | bytes accessed | tf_op | source)
XLA Modules:
  0.0 38.5 jit_solution(9384704357569607854)
XLA Ops:
  0.6 0.0 copy-start
  0.6 0.0 copy-start.1
  0.7 0.0 copy-start.4
  0.7 0.0 copy-start.5
  0.7 0.0 copy-start.6
  0.7 0.0 copy-start.7
  0.7 5.9 %local.1 = (bf16[1,8,1024]{2,1,0:T(8,128)(2,1)}, bf16[16,32,128]{2,1,0:T(8,128)(2,1)}) custom-call(bf16[8,40,2688]{2,1,0:T(8,128)(2,1)} %bitcast.8, s32[1,1024]{1,0:T(1,128)} %bitcast.6, bf16[1024,128]{1,0:T(8,128)(2,1)} %interp.1, bf16[2688,192]{1,0:T(8,128)(2,1)} %constant.2.clone.table_hbm), custom_call_target="tpu_custom_call" | custom-call | flops 2477785088 | bytes 1982464 | tf_op jit(solution)/shard_map/local/pallas_call | solution.py:280
  6.6 3.1 %collective-permute-start = (bf16[1,8,1024]{2,1,0:T(8,128)(2,1)}, bf16[1,8,1024]{2,1,0:T(8,128)(2,1)S(1)}, u32[]{:S(2)}, u32[]{:S(2)}) collective-permute-start(bf16[1,8,1024]{2,1,0:T(8,128)(2,1)} %get-tuple-element.9.state), channel_id=1, source_target_pairs={{0,1},{1,0},{2,3},{3,2},{4,5},{5,4},{6,7},{7,6},{8,9},{9,8},{10,11... | collective-permute-start | bytes 49160 | tf_op jit(solution)/shard_map/ppermute | solution.py:293
  9.7 1.9 %collective-permute-done.other = bf16[1,8,1024]{2,1,0:T(8,128)(2,1)S(1)} collective-permute-done((bf16[1,8,1024]{2,1,0:T(8,128)(2,1)}, bf16[1,8,1024]{2,1,0:T(8,128)(2,1)S(1)}, u32[]{:S(2)}, u32[]{:S(2)}) %collective-permute-start) | collective-permute-done | bytes 16416 | tf_op jit(solution)/shard_map/ppermute | solution.py:293
  11.6 0.9 %copy-done.2 = bf16[16,32,128]{2,1,0:T(8,128)(2,1)S(1)} copy-done((bf16[16,32,128]{2,1,0:T(8,128)(2,1)S(1)}, bf16[16,32,128]{2,1,0:T(8,128)(2,1)}, u32[]{:S(2)}) %copy-start.2) | copy-done | bytes 131096
  12.5 0.7 %copy-done.3 = bf16[1,8,1024]{2,1,0:T(8,128)(2,1)S(1)} copy-done((bf16[1,8,1024]{2,1,0:T(8,128)(2,1)S(1)}, bf16[1,8,1024]{2,1,0:T(8,128)(2,1)}, u32[]{:S(2)}) %copy-start.3) | copy-done | bytes 16408
  13.2 0.7 %merge.1 = (bf16[2,8,1024]{2,1,0:T(8,128)(2,1)S(1)}, bf16[32,32,128]{2,1,0:T(8,128)(2,1)}) custom-call(bf16[1,8,1024]{2,1,0:T(8,128)(2,1)S(1)} %copy-done.3, bf16[1,8,1024]{2,1,0:T(8,128)(2,1)S(1)} %collective-permute-done.other, bf16[16,32,128]{2,1,0:T(8,128)(2,1)S(1)} %copy-done.2), custom_call_target="tpu_custom_call" | custom-call | bytes 524288 | tf_op jit(solution)/shard_map/merge/pallas_call | solution.py:280
  14.0 3.1 %collective-permute-start.1 = (bf16[2,8,1024]{2,1,0:T(8,128)(2,1)S(1)}, bf16[2,8,1024]{2,1,0:T(8,128)(2,1)S(1)}, u32[]{:S(2)}, u32[]{:S(2)}) collective-permute-start(bf16[2,8,1024]{2,1,0:T(8,128)(2,1)S(1)} %get-tuple-element.13), channel_id=1, source_target_pairs={{0,2},{1,3},{2,0},{3,1},{4,6},{5,7},{6,4},{7,5},{8,10},{9,11},{10,... | collective-permute-start | bytes 98312 | tf_op jit(solution)/shard_map/ppermute | solution.py:293
  17.1 1.9 %collective-permute-done.1 = bf16[2,8,1024]{2,1,0:T(8,128)(2,1)S(1)} collective-permute-done((bf16[2,8,1024]{2,1,0:T(8,128)(2,1)S(1)}, bf16[2,8,1024]{2,1,0:T(8,128)(2,1)S(1)}, u32[]{:S(2)}, u32[]{:S(2)}) %collective-permute-start.1) | collective-permute-done | bytes 32800 | tf_op jit(solution)/shard_map/ppermute | solution.py:293
  19.0 1.8 %collective-permute-start.2 = (bf16[4,8,1024]{2,1,0:T(8,128)(2,1)S(1)}, bf16[4,8,1024]{2,1,0:T(8,128)(2,1)S(1)}, u32[]{:S(2)}, u32[]{:S(2)}) collective-permute-start(bf16[4,8,1024]{2,1,0:T(8,128)(2,1)S(1)} %constant_dynamic-update-slice_fusion.near), channel_id=1, source_target_pairs={{0,16},{16,0},{1,17},{17,1},{2,18},{18,2},{3,19},{19,3},{4,20},{20... | collective-permute-start | bytes 196616 | tf_op jit(solution)/shard_map/ppermute | solution.py:293
  20.8 0.0 copy-done
  20.8 0.0 copy-done.1
  20.8 1.2 %prepare.1 = (bf16[4,2,144,128]{3,2,1,0:T(8,128)(2,1)S(1)}, bf16[2048,32]{1,0:T(8,128)(2,1)S(1)}) custom-call(bf16[6,48,160]{2,1,0:T(8,128)(2,1)S(1)} %bitcast.5, bf16[32,32,64]{2,1,0:T(8,128)(2,1)S(1)} %bitcast.4), custom_call_target="tpu_custom_call" | custom-call | bytes 1179648 | tf_op jit(solution)/shard_map/prepare/pallas_call | solution.py:280
  22.0 5.2 %all-to-all-start = ((bf16[32,32,128]{2,1,0:T(8,128)(2,1)}), bf16[32,32,128]{2,1,0:T(8,128)(2,1)S(1)}, u32[]{:S(2)}, u32[]{:S(2)}) async-start(bf16[32,32,128]{2,1,0:T(8,128)(2,1)} %get-tuple-element.11), calls=%async_computation | async-start | bytes 524288 | tf_op jit(solution)/shard_map/all_to_all | solution.py:374
  27.2 0.0 collective-permute-done.2.far
  27.2 0.0 copy-done.4
  27.3 6.3 %columns.1 = bf16[2,40,2688]{2,1,0:T(8,128)(2,1)} custom-call(s32[4]{0:T(128)S(1)} %copy-done.7, bf16[64,2048]{1,0:T(8,128)(2,1)S(1)} %copy-done.5, bf16[2048,32]{1,0:T(8,128)(2,1)S(1)} %get-tuple-element.12.inverses, s32[1,1024]{1,0:T(1,128)S(1)} %bitcast.7, bf16[1024,128]{1,0:T(8,128)(2,1)S(1)} %copy-done.4, ...), custom_call_target="tpu_custom_call" | custom-call | flops 8589934592 | bytes 2097152 | tf_op jit(solution)/shard_map/columns/pallas_call | solution.py:280
  33.6 3.9 %all-to-all-done.pieces = bf16[32,32,128]{2,1,0:T(8,128)(2,1)S(1)} async-done(((bf16[32,32,128]{2,1,0:T(8,128)(2,1)}), bf16[32,32,128]{2,1,0:T(8,128)(2,1)S(1)}, u32[]{:S(2)}, u32[]{:S(2)}) %all-to-all-start) | async-done | bytes 262176 | tf_op jit(solution)/shard_map/all_to_all | solution.py:374
  37.4 1.0 %legendre.1 = bf16[6,2,4,16,48]{4,3,2,1,0:T(8,128)(2,1)} custom-call(bf16[4,2,144,128]{3,2,1,0:T(8,128)(2,1)S(1)} %get-tuple-element.8.weights, bf16[32,32,128]{2,1,0:T(8,128)(2,1)S(1)} %all-to-all-done.pieces), custom_call_target="tpu_custom_call" | custom-call | flops 75497472 | bytes 262144 | tf_op jit(solution)/shard_map/legendre/pallas_call | solution.py:280
  (7 shorter events, 0.0 us)
Async XLA Ops:
  0.6 20.2 %copy-start = (bf16[64,32,32]{0,2,1:T(8,128)(2,1)S(1)}, bf16[64,32,32]{0,2,1:T(8,128)(2,1)}, u32[]{:S(2)}) copy-start(bf16[64,32,32]{0,2,1:T(8,128)(2,1)} %param.14) | copy-start | bytes 393220
  0.6 20.2 %copy-start.1 = (bf16[6,160,48]{1,2,0:T(8,128)(2,1)S(1)}, bf16[6,160,48]{1,2,0:T(8,128)(2,1)}, u32[]{:S(2)}) copy-start(bf16[6,160,48]{1,2,0:T(8,128)(2,1)} %param.9) | copy-start | bytes 276484
  0.7 26.6 %copy-start.4 = (bf16[1024,128]{1,0:T(8,128)(2,1)S(1)}, bf16[1024,128]{1,0:T(8,128)(2,1)}, u32[]{:S(2)}) copy-start(bf16[1024,128]{1,0:T(8,128)(2,1)} %interp.1) | copy-start | bytes 786436
  0.7 26.6 %copy-start.5 = (bf16[64,2048]{1,0:T(8,128)(2,1)S(1)}, bf16[64,2048]{1,0:T(8,128)(2,1)}, u32[]{:S(2)}) copy-start(bf16[64,2048]{1,0:T(8,128)(2,1)} %weights.1) | copy-start | bytes 786436
  0.7 26.6 %copy-start.6 = (s32[1024]{0:T(1024)S(1)}, s32[1024]{0:T(1024)}, u32[]{:S(2)}) copy-start(s32[1024]{0:T(1024)} %param.11) | copy-start | bytes 12292
  0.7 26.6 %copy-start.7 = (s32[4]{0:T(128)S(1)}, s32[4]{0:T(128)}, u32[]{:S(2)}) copy-start(s32[4]{0:T(128)} %counts.1) | copy-start | bytes 52
  6.6 5.0 %collective-permute-start = (bf16[1,8,1024]{2,1,0:T(8,128)(2,1)}, bf16[1,8,1024]{2,1,0:T(8,128)(2,1)S(1)}, u32[]{:S(2)}, u32[]{:S(2)}) collective-permute-start(bf16[1,8,1024]{2,1,0:T(8,128)(2,1)} %get-tuple-element.9.state), channel_id=1, source_target_pairs={{0,1},{1,0},{2,3},{3,2},{4,5},{5,4},{6,7},{7,6},{8,9},{9,8},{10,11... | collective-permute-start | bytes 49160 | tf_op jit(solution)/shard_map/ppermute | solution.py:293
  11.6 0.9 %copy-start.2 = (bf16[16,32,128]{2,1,0:T(8,128)(2,1)S(1)}, bf16[16,32,128]{2,1,0:T(8,128)(2,1)}, u32[]{:S(2)}) copy-start(bf16[16,32,128]{2,1,0:T(8,128)(2,1)} %get-tuple-element.10.packed) | copy-start | bytes 393220
  12.5 0.7 %copy-start.3 = (bf16[1,8,1024]{2,1,0:T(8,128)(2,1)S(1)}, bf16[1,8,1024]{2,1,0:T(8,128)(2,1)}, u32[]{:S(2)}) copy-start(bf16[1,8,1024]{2,1,0:T(8,128)(2,1)} %get-tuple-element.9.state) | copy-start | bytes 49156
  14.0 5.0 %collective-permute-start.1 = (bf16[2,8,1024]{2,1,0:T(8,128)(2,1)S(1)}, bf16[2,8,1024]{2,1,0:T(8,128)(2,1)S(1)}, u32[]{:S(2)}, u32[]{:S(2)}) collective-permute-start(bf16[2,8,1024]{2,1,0:T(8,128)(2,1)S(1)} %get-tuple-element.13), channel_id=1, source_target_pairs={{0,2},{1,3},{2,0},{3,1},{4,6},{5,7},{6,4},{7,5},{8,10},{9,11},{10,... | collective-permute-start | bytes 98312 | tf_op jit(solution)/shard_map/ppermute | solution.py:293
  19.0 8.2 %collective-permute-start.2 = (bf16[4,8,1024]{2,1,0:T(8,128)(2,1)S(1)}, bf16[4,8,1024]{2,1,0:T(8,128)(2,1)S(1)}, u32[]{:S(2)}, u32[]{:S(2)}) collective-permute-start(bf16[4,8,1024]{2,1,0:T(8,128)(2,1)S(1)} %constant_dynamic-update-slice_fusion.near), channel_id=1, source_target_pairs={{0,16},{16,0},{1,17},{17,1},{2,18},{18,2},{3,19},{19,3},{4,20},{20... | collective-permute-start | bytes 196616 | tf_op jit(solution)/shard_map/ppermute | solution.py:293
  22.0 15.4 %all-to-all-start = ((bf16[32,32,128]{2,1,0:T(8,128)(2,1)}), bf16[32,32,128]{2,1,0:T(8,128)(2,1)S(1)}, u32[]{:S(2)}, u32[]{:S(2)}) async-start(bf16[32,32,128]{2,1,0:T(8,128)(2,1)} %get-tuple-element.11), calls=%async_computation | async-start | bytes 524288 | tf_op jit(solution)/shard_map/all_to_all | solution.py:374

commit v9 on v7

--- a/solution.py
+++ b/solution.py
@@ -130,6 +130,7 @@
     small = [
         pltpu.make_async_copy(blocks_hbm, blocks, sems.at[parts]),
         pltpu.make_async_copy(interp_hbm, interp, sems.at[parts + 1]),
+        pltpu.make_async_copy(table_hbm, table, sems.at[parts + 2]),
     ]
     loads = [
         pltpu.make_async_copy(
@@ -139,19 +140,11 @@
         )
         for part in range(parts)
     ]
-    tables = [
-        pltpu.make_async_copy(
-            table_hbm.at[pl.ds(part * step, step)],
-            table.at[pl.ds(part * step, step)],
-            sems.at[parts + 2 + part],
-        )
-        for part in range(parts)
-    ]
     small[0].start()
-    for part in range(parts):
-        loads[part].start()
-        tables[part].start()
+    for copy in loads:
+        copy.start()
     small[1].start()
+    small[2].start()
     small[0].wait()
     row = slot_rows(blocks[...], across, lat_pad)
     column[...] = jnp.transpose(jnp.broadcast_to(row, (LANES, slots)))
@@ -163,16 +156,8 @@
             selector[start : start + chunk, base : base + LANES] = jnp.where(
                 mine == lane + base, 1.0, 0.0
             ).astype(BF16)
-    coeffs = jnp.zeros((lev * lat, table.shape[1]), F32)
     for part in range(parts):
         loads[part].wait()
-        tables[part].wait()
-        flat = jnp.concatenate(
-            [grid[level, :, part * step : (part + 1) * step] for level in range(lev)], axis=0
-        )
-        coeffs = coeffs + jnp.dot(
-            flat, table[part * step : (part + 1) * step, :], preferred_element_type=F32
-        )
         for tile in range(part * across // parts, (part + 1) * across // parts):
             patch[tile * lat_pad + lat : (tile + 1) * lat_pad, :] = jnp.zeros(
                 (lat_pad - lat, lev * LANES), BF16
@@ -184,6 +169,13 @@
     if depth > across * lat_pad:
         patch[across * lat_pad :, :] = jnp.zeros((depth - across * lat_pad, lev * LANES), BF16)
     small[1].wait()
+    first_state = message.shape[1] - slots // LANES * lev
+    copies = [
+        pltpu.make_async_copy(message.at[:, rows_of, :], out.at[:, rows_of, :], send.at[i])
+        for i, rows_of in enumerate(
+            (pl.ds(0, first_state), pl.ds(first_state, message.shape[1] - first_state))
+        )
+    ]
     for start in range(0, slots, chunk):
         picked = jnp.dot(
             selector[start : start + chunk, :], patch[...], preferred_element_type=F32
@@ -195,13 +187,18 @@
             total = jnp.where(lane == level, jnp.sum(product, axis=1, keepdims=True), total)
         state = jnp.transpose(total)[:lev].astype(BF16)
         for tile in range(chunk // LANES):
-            row = message.shape[1] - slots // LANES * lev + (start // LANES + tile) * lev
+            row = first_state + (start // LANES + tile) * lev
             for target in range(message.shape[0]):
                 message[target, row : row + lev, :] = state[:, tile * LANES : (tile + 1) * LANES]
-    pack(lev, lat, coeffs, message, padded, rows)
-    copy = pltpu.make_async_copy(message, out, send.at[0])
-    copy.start()
-    copy.wait()
+        if start == chunk:
+            small[2].wait()
+            flat = jnp.concatenate([grid[level] for level in range(lev)], axis=0)
+            coeffs = jnp.dot(flat, table[...], preferred_element_type=F32)
+            pack(lev, lat, coeffs, message, padded, rows)
+            copies[0].start()
+    copies[1].start()
+    for copy in copies:
+        copy.wait()
 
 
 def regroup_kernel(n_band, arrived, _, out, out_state, sems):
@@ -247,23 +244,28 @@
     chunk = 256
     lane = lax.broadcasted_iota(jnp.int32, (1, flux_rows), 1)
     slot = lax.broadcasted_iota(jnp.int32, (chunk, 1), 0)
+    column = jnp.transpose(state[...]).astype(BF16)
+
+    def gates_of(source):
+        return jnp.dot(column, weights[:, source : source + chunk], preferred_element_type=F32)
+
+    flux = jnp.zeros((slots, flux_rows), F32)
+    gates = gates_of(0)
+    for source in range(0, sources, chunk):
+        later = gates_of(source + chunk) if source + chunk < sources else None
+        flux = flux + jnp.dot(
+            softplus(gates).astype(BF16),
+            inverses[source : source + chunk, :],
+            preferred_element_type=F32,
+        )
+        gates = later
     for start in range(0, slots, chunk):
-        column = jnp.transpose(state[:, start : start + chunk]).astype(BF16)
-        flux = jnp.zeros((chunk, flux_rows), F32)
-        for source in range(0, sources, chunk):
-            gates = jnp.dot(
-                column, weights[:, source : source + chunk], preferred_element_type=F32
-            )
-            flux = flux + jnp.dot(
-                softplus(gates).astype(BF16),
-                inverses[source : source + chunk, :],
-                preferred_element_type=F32,
-            )
+        rows = flux[start : start + chunk]
         for level in range(mine):
             at = base + level
             plus = (lane == at) | ((lane == at + levels + 1) & (at + 1 < levels))
             minus = (lane == at + levels) | ((lane == at + 1) & (at + 1 < levels))
-            terms = jnp.where(plus, flux, 0.0) - jnp.where(minus, flux, 0.0)
+            terms = jnp.where(plus, rows, 0.0) - jnp.where(minus, rows, 0.0)
             heat = jnp.sum(terms, axis=1, keepdims=True)
             heat = jnp.where(slot + start < count, heat, 0.0).astype(BF16).astype(F32)
             spread[start : start + chunk, level * LANES : (level + 1) * LANES] = (
@@ -343,8 +345,8 @@
             pltpu.VMEM((n_fld, message_rows, LANES), BF16),
             pltpu.VMEM((LANES, padded_group), F32),
             pltpu.VMEM((group * lev, LANES), F32),
-            pltpu.SemaphoreType.DMA((2 * parts + 2,)),
-            pltpu.SemaphoreType.DMA((1,)),
+            pltpu.SemaphoreType.DMA((parts + 3,)),
+            pltpu.SemaphoreType.DMA((2,)),
         ],
         (grid.reshape(lev, lat, lon), block_row, interp, table),
         2 * slots * depth * lev * LANES + 2 * lev * lat * lon * THIRDS * group,

time: 35.2 us -> 33.6 us (0.955)
  Pallas kernels: 16.3 us -> 14.7 us
    pallas_call x5, Pallas kernels: 16.3 us -> 14.7 us  [call(): pl.pallas_call(kernel, out_shape=shapes[0] if single else shapes, in_spec...]
  transfers between devices with their start and end apart: 3 -> 3, of which waited for: 1 -> 2; matrix products, arithmetic and copies ran while one was open for 0% -> 0% of each run, Pallas kernels for 22% -> 21%
where the time goes in v9:
time: 33.6 us; the launch traced here: 33.3 us
  Pallas kernels  14.7 us (44%)
  starting transfers between devices  11.4 us (34%)
  waiting for transfers between devices  6.39 us (19%)
  between operations  0.76 us (2%)
    pallas_call x5, Pallas kernels, call(): pl.pallas_call(kernel, out_shape=shapes[0] if single else shapes, in_spec...  14.7 us
    all_to_all x1, starting transfers between devices, body(): arrived = lax.all_to_all(message, 'fld', 0, 0, tiled=True)  6.46 us
    all_to_all x1, waiting for transfers between devices, body(): arrived = lax.all_to_all(message, 'fld', 0, 0, tiled=True)  6.3 us
    all_to_all x1, starting transfers between devices, body(): pieces = lax.all_to_all(sent, ('sec', 'band'), 0, 0, tiled=True)  3.41 us
    ppermute x1, starting transfers between devices, body(): far = lax.ppermute(near, 'sec', [(i, 1 - i) for i in range(n_sec)])  1.56 us
  transfers between devices with their start and end apart: 3, of which 2 were waited for; matrix products, arithmetic and copies ran while one was open for 0% of the time, Pallas kernels for 21%

profile of v9, /device:TPU:0, one launch (start us, length us, event | category | flops | bytes accessed | tf_op | source)
XLA Modules:
  0.0 33.3 jit_solution(7894445479826272230)
XLA Ops:
  0.6 0.0 copy-start
  0.6 0.0 copy-start.1
  0.6 5.8 %local.1 = bf16[4,192,128]{2,1,0:T(8,128)(2,1)} custom-call(bf16[8,40,2688]{2,1,0:T(8,128)(2,1)} %bitcast.8, s32[1,1024]{1,0:T(1,128)} %bitcast.6, bf16[1024,128]{1,0:T(8,128)(2,1)} %interp.1, bf16[2688,192]{1,0:T(8,128)(2,1)} %constant.2.clone.table_hbm), custom_call_target="tpu_custom_call" | custom-call | flops 2477785088 | bytes 1982464 | tf_op jit(solution)/shard_map/local/pallas_call | solution.py:301
  6.5 0.0 copy-start.2
  6.5 0.0 copy-start.3
  6.5 0.0 copy-start.4
  6.5 0.0 copy-start.5
  6.5 6.5 %all-to-all-start = ((bf16[4,192,128]{2,1,0:T(8,128)(2,1)}), bf16[4,192,128]{2,1,0:T(8,128)(2,1)S(1)}, u32[]{:S(2)}, u32[]{:S(2)}) async-start(bf16[4,192,128]{2,1,0:T(8,128)(2,1)} %local.1), calls=%async_computation | async-start | bytes 393216 | tf_op jit(solution)/shard_map/all_to_all | solution.py:358
  13.0 0.0 copy-done
  13.0 0.0 copy-done.1
  13.0 1.2 %prepare.1 = (bf16[4,2,144,128]{3,2,1,0:T(8,128)(2,1)S(1)}, bf16[2048,32]{1,0:T(8,128)(2,1)S(1)}) custom-call(bf16[6,48,160]{2,1,0:T(8,128)(2,1)S(1)} %bitcast.5, bf16[32,32,64]{2,1,0:T(8,128)(2,1)S(1)} %bitcast.4), custom_call_target="tpu_custom_call" | custom-call | bytes 1179648 | tf_op jit(solution)/shard_map/prepare/pallas_call | solution.py:301
  14.2 6.3 %all-to-all-done.arrived = bf16[4,192,128]{2,1,0:T(8,128)(2,1)S(1)} async-done(((bf16[4,192,128]{2,1,0:T(8,128)(2,1)}), bf16[4,192,128]{2,1,0:T(8,128)(2,1)S(1)}, u32[]{:S(2)}, u32[]{:S(2)}) %all-to-all-start) | async-done | bytes 196640 | tf_op jit(solution)/shard_map/all_to_all | solution.py:358
  20.5 0.8 %regroup.1 = (bf16[8,4,32,128]{3,2,1,0:T(8,128)(2,1)}, bf16[4,64,128]{2,1,0:T(8,128)(2,1)S(1)}) custom-call(bf16[4,192,128]{2,1,0:T(8,128)(2,1)S(1)} %all-to-all-done.arrived, bf16[4,2,144,128]{3,2,1,0:T(8,128)(2,1)S(1)} %get-tuple-element.6._.weights), custom_call_target="tpu_custom_call" | custom-call | bytes 524288 | tf_op jit(solution)/shard_map/regroup/pallas_call | solution.py:301
  21.3 1.6 %collective-permute-start = (bf16[4,64,128]{2,1,0:T(8,128)(2,1)S(1)}, bf16[4,64,128]{2,1,0:T(8,128)(2,1)S(1)}, u32[]{:S(2)}, u32[]{:S(2)}) collective-permute-start(bf16[4,64,128]{2,1,0:T(8,128)(2,1)S(1)} %get-tuple-element.9.near), channel_id=1, source_target_pairs={{0,16},{16,0},{1,17},{17,1},{2,18},{18,2},{3,19},{19,3},{4,20},{20... | collective-permute-start | bytes 196616 | tf_op jit(solution)/shard_map/ppermute | solution.py:388
  22.9 3.4 %all-to-all-start.1 = ((bf16[8,4,32,128]{3,2,1,0:T(8,128)(2,1)}), bf16[8,4,32,128]{3,2,1,0:T(8,128)(2,1)S(1)}, u32[]{:S(2)}, u32[]{:S(2)}) async-start(bf16[8,4,32,128]{3,2,1,0:T(8,128)(2,1)} %get-tuple-element.7), calls=%async_computation.1 | async-start | bytes 524288 | tf_op jit(solution)/shard_map/all_to_all | solution.py:389
  26.3 0.0 collective-permute-done.far
  26.3 0.0 copy-done.2
  26.3 0.0 copy-done.3
  26.3 0.0 copy-done.4
  26.3 0.0 copy-done.5
  26.3 5.8 %columns.1 = bf16[2,40,2688]{2,1,0:T(8,128)(2,1)} custom-call(s32[4]{0:T(128)S(1)} %copy-done.5, bf16[64,2048]{1,0:T(8,128)(2,1)S(1)} %copy-done.3, bf16[2048,32]{1,0:T(8,128)(2,1)S(1)} %get-tuple-element.8.inverses, s32[1,1024]{1,0:T(1,128)S(1)} %bitcast.7, bf16[1024,128]{1,0:T(8,128)(2,1)S(1)} %copy-done.2, bf16[4,64,128]{2,1,0:T(8,128)(2,1)S(1)} %get-tuple-element.9.near, ...), custom_call_target="tpu_custom_call" | custom-call | flops 8589934592 | bytes 2097152 | tf_op jit(solution)/shard_map/columns/pallas_call | solution.py:301
  32.2 0.1 all-to-all-done.1.pieces
  32.3 1.0 %legendre.1 = bf16[6,2,4,16,48]{4,3,2,1,0:T(8,128)(2,1)} custom-call(bf16[4,2,144,128]{3,2,1,0:T(8,128)(2,1)S(1)} %get-tuple-element.6._.weights, bf16[8,4,32,128]{3,2,1,0:T(8,128)(2,1)S(1)} %all-to-all-done.1.pieces), custom_call_target="tpu_custom_call" | custom-call | flops 75497472 | bytes 262144 | tf_op jit(solution)/shard_map/legendre/pallas_call | solution.py:301
Async XLA Ops:
  0.6 12.4 %copy-start = (bf16[64,32,32]{0,2,1:T(8,128)(2,1)S(1)}, bf16[64,32,32]{0,2,1:T(8,128)(2,1)}, u32[]{:S(2)}) copy-start(bf16[64,32,32]{0,2,1:T(8,128)(2,1)} %param.14) | copy-start | bytes 393220
  0.6 12.4 %copy-start.1 = (bf16[6,160,48]{1,2,0:T(8,128)(2,1)S(1)}, bf16[6,160,48]{1,2,0:T(8,128)(2,1)}, u32[]{:S(2)}) copy-start(bf16[6,160,48]{1,2,0:T(8,128)(2,1)} %param.9) | copy-start | bytes 276484
  6.5 19.8 %copy-start.2 = (bf16[1024,128]{1,0:T(8,128)(2,1)S(1)}, bf16[1024,128]{1,0:T(8,128)(2,1)}, u32[]{:S(2)}) copy-start(bf16[1024,128]{1,0:T(8,128)(2,1)} %interp.1) | copy-start | bytes 786436
  6.5 19.8 %copy-start.3 = (bf16[64,2048]{1,0:T(8,128)(2,1)S(1)}, bf16[64,2048]{1,0:T(8,128)(2,1)}, u32[]{:S(2)}) copy-start(bf16[64,2048]{1,0:T(8,128)(2,1)} %weights.1) | copy-start | bytes 786436
  6.5 19.8 %copy-start.4 = (s32[1024]{0:T(1024)S(1)}, s32[1024]{0:T(1024)}, u32[]{:S(2)}) copy-start(s32[1024]{0:T(1024)} %param.11) | copy-start | bytes 12292
  6.5 19.8 %copy-start.5 = (s32[4]{0:T(128)S(1)}, s32[4]{0:T(128)}, u32[]{:S(2)}) copy-start(s32[4]{0:T(128)} %counts.1) | copy-start | bytes 52
  6.5 14.0 %all-to-all-start = ((bf16[4,192,128]{2,1,0:T(8,128)(2,1)}), bf16[4,192,128]{2,1,0:T(8,128)(2,1)S(1)}, u32[]{:S(2)}, u32[]{:S(2)}) async-start(bf16[4,192,128]{2,1,0:T(8,128)(2,1)} %local.1), calls=%async_computation | async-start | bytes 393216 | tf_op jit(solution)/shard_map/all_to_all | solution.py:358
  21.3 5.0 %collective-permute-start = (bf16[4,64,128]{2,1,0:T(8,128)(2,1)S(1)}, bf16[4,64,128]{2,1,0:T(8,128)(2,1)S(1)}, u32[]{:S(2)}, u32[]{:S(2)}) collective-permute-start(bf16[4,64,128]{2,1,0:T(8,128)(2,1)S(1)} %get-tuple-element.9.near), channel_id=1, source_target_pairs={{0,16},{16,0},{1,17},{17,1},{2,18},{18,2},{3,19},{19,3},{4,20},{20... | collective-permute-start | bytes 196616 | tf_op jit(solution)/shard_map/ppermute | solution.py:388
  22.9 9.4 %all-to-all-start.1 = ((bf16[8,4,32,128]{3,2,1,0:T(8,128)(2,1)}), bf16[8,4,32,128]{3,2,1,0:T(8,128)(2,1)S(1)}, u32[]{:S(2)}, u32[]{:S(2)}) async-start(bf16[8,4,32,128]{3,2,1,0:T(8,128)(2,1)} %get-tuple-element.7), calls=%async_computation.1 | async-start | bytes 524288 | tf_op jit(solution)/shard_map/all_to_all | solution.py:389

commit v10 on v9

--- a/solution.py
+++ b/solution.py
@@ -121,7 +121,7 @@
 
 def local_kernel(lat_pad, parts, grid_hbm, blocks_hbm, interp_hbm, table_hbm, out,
                  grid, blocks, interp, table, patch, column, selector, message, padded, rows,
-                 sems, send):
+                 totals, sems, send):
     lev, lat, lon = grid.shape
     across = lon // LANES
     slots = interp.shape[0]
@@ -176,26 +176,35 @@
             (pl.ds(0, first_state), pl.ds(first_state, message.shape[1] - first_state))
         )
     ]
-    for start in range(0, slots, chunk):
+    pair = 2 * LANES
+    for start in range(0, lev * LANES, pair):
         picked = jnp.dot(
-            selector[start : start + chunk, :], patch[...], preferred_element_type=F32
-        )
-        weights = interp[start : start + chunk, :].astype(F32)
-        total = jnp.zeros((chunk, LANES), F32)
-        for level in range(lev):
-            product = picked[:, level * LANES : (level + 1) * LANES] * weights
-            total = jnp.where(lane == level, jnp.sum(product, axis=1, keepdims=True), total)
-        state = jnp.transpose(total)[:lev].astype(BF16)
-        for tile in range(chunk // LANES):
-            row = first_state + (start // LANES + tile) * lev
-            for target in range(message.shape[0]):
-                message[target, row : row + lev, :] = state[:, tile * LANES : (tile + 1) * LANES]
-        if start == chunk:
+            selector[...], patch[:, start : start + pair], preferred_element_type=F32
+        )
+        for side in range(2):
+            level = start // LANES + side
+            for top in range(0, slots, chunk):
+                product = picked[top : top + chunk, side * LANES : (side + 1) * LANES] * interp[
+                    top : top + chunk, :
+                ].astype(F32)
+                value = jnp.sum(product, axis=1, keepdims=True)
+                if level == 0:
+                    totals[top : top + chunk, :] = jnp.where(lane == level, value, 0.0)
+                else:
+                    totals[top : top + chunk, :] = jnp.where(
+                        lane == level, value, totals[top : top + chunk, :]
+                    )
+        if start == pair:
             small[2].wait()
             flat = jnp.concatenate([grid[level] for level in range(lev)], axis=0)
             coeffs = jnp.dot(flat, table[...], preferred_element_type=F32)
             pack(lev, lat, coeffs, message, padded, rows)
             copies[0].start()
+    for top in range(0, slots, LANES):
+        state = jnp.transpose(totals[top : top + LANES, :])[:lev].astype(BF16)
+        row = first_state + top // LANES * lev
+        for target in range(message.shape[0]):
+            message[target, row : row + lev, :] = state
     copies[1].start()
     for copy in copies:
         copy.wait()
@@ -273,16 +282,16 @@
             ).astype(BF16)
     row = slot_rows(blocks[...], across, lat_pad)
     tiles = max(t for t in range(1, 8) if across % t == 0)
-    height = tiles * lat_pad
+    height = across * lat_pad
+    match = row == lax.broadcasted_iota(jnp.int32, (height, slots), 0)
+    left = jnp.where(match, 1.0, 0.0).astype(BF16)
+    summed = jnp.dot(left, spread[...], preferred_element_type=F32).astype(BF16)
     copies = []
     for first in range(0, across, tiles):
-        match = row == lax.broadcasted_iota(jnp.int32, (height, slots), 0) + first * lat_pad
-        left = jnp.where(match, 1.0, 0.0).astype(BF16)
-        summed = jnp.dot(left, spread[...], preferred_element_type=F32).astype(BF16)
         for level in range(mine):
             for tile in range(tiles):
                 result[level, :, (first + tile) * LANES : (first + tile + 1) * LANES] = summed[
-                    tile * lat_pad : tile * lat_pad + lat, level * LANES : (level + 1) * LANES
+                    (first + tile) * lat_pad : (first + tile) * lat_pad + lat, level * LANES : (level + 1) * LANES
                 ]
         columns = pl.ds(first * LANES, tiles * LANES)
         copies.append(
@@ -345,6 +354,7 @@
             pltpu.VMEM((n_fld, message_rows, LANES), BF16),
             pltpu.VMEM((LANES, padded_group), F32),
             pltpu.VMEM((group * lev, LANES), F32),
+            pltpu.VMEM((slots, LANES), F32),
             pltpu.SemaphoreType.DMA((parts + 3,)),
             pltpu.SemaphoreType.DMA((2,)),
         ],

time: 33.6 us -> 34.9 us (1.039)
  Pallas kernels: 14.7 us -> 16.1 us
    pallas_call x5, Pallas kernels: 14.7 us -> 16.1 us  [call(): pl.pallas_call(kernel, out_shape=shapes[0] if single else shapes, in_spec...]
  transfers between devices with their start and end apart: 3 -> 3, of which waited for: 2 -> 1; matrix products, arithmetic and copies ran while one was open for 0% -> 0% of each run, Pallas kernels for 21% -> 22%
where the time goes in v10:
time: 34.9 us; the launch traced here: 34.6 us
  Pallas kernels  16.1 us (46%)
  starting transfers between devices  11.4 us (33%)
  waiting for transfers between devices  6.29 us (18%)
  between operations  0.76 us (2%)
    pallas_call x5, Pallas kernels, call(): pl.pallas_call(kernel, out_shape=shapes[0] if single else shapes, in_spec...  16.1 us
    all_to_all x1, starting transfers between devices, body(): arrived = lax.all_to_all(message, 'fld', 0, 0, tiled=True)  6.46 us
    all_to_all x1, waiting for transfers between devices, body(): arrived = lax.all_to_all(message, 'fld', 0, 0, tiled=True)  6.29 us
    all_to_all x1, starting transfers between devices, body(): pieces = lax.all_to_all(sent, ('sec', 'band'), 0, 0, tiled=True)  3.41 us
    ppermute x1, starting transfers between devices, body(): far = lax.ppermute(near, 'sec', [(i, 1 - i) for i in range(n_sec)])  1.55 us
  transfers between devices with their start and end apart: 3, of which 1 were waited for; matrix products, arithmetic and copies ran while one was open for 0% of the time, Pallas kernels for 22%

profile of v10, /device:TPU:0, one launch (start us, length us, event | category | flops | bytes accessed | tf_op | source)
XLA Modules:
  0.0 34.6 jit_solution(12399101852371091344)
XLA Ops:
  0.6 0.0 copy-start
  0.6 0.0 copy-start.1
  0.6 6.7 %local.1 = bf16[4,192,128]{2,1,0:T(8,128)(2,1)} custom-call(bf16[8,40,2688]{2,1,0:T(8,128)(2,1)} %bitcast.8, s32[1,1024]{1,0:T(1,128)} %bitcast.6, bf16[1024,128]{1,0:T(8,128)(2,1)} %interp.1, bf16[2688,192]{1,0:T(8,128)(2,1)} %constant.2.clone.table_hbm), custom_call_target="tpu_custom_call" | custom-call | flops 2477785088 | bytes 1982464 | tf_op jit(solution)/shard_map/local/pallas_call | solution.py:310
  7.4 0.0 copy-start.2
  7.4 0.0 copy-start.3
  7.4 0.0 copy-start.4
  7.4 0.0 copy-start.5
  7.4 6.5 %all-to-all-start = ((bf16[4,192,128]{2,1,0:T(8,128)(2,1)}), bf16[4,192,128]{2,1,0:T(8,128)(2,1)S(1)}, u32[]{:S(2)}, u32[]{:S(2)}) async-start(bf16[4,192,128]{2,1,0:T(8,128)(2,1)} %local.1), calls=%async_computation | async-start | bytes 393216 | tf_op jit(solution)/shard_map/all_to_all | solution.py:368
  13.9 0.0 copy-done
  13.9 0.0 copy-done.1
  13.9 1.2 %prepare.1 = (bf16[4,2,144,128]{3,2,1,0:T(8,128)(2,1)S(1)}, bf16[2048,32]{1,0:T(8,128)(2,1)S(1)}) custom-call(bf16[6,48,160]{2,1,0:T(8,128)(2,1)S(1)} %bitcast.5, bf16[32,32,64]{2,1,0:T(8,128)(2,1)S(1)} %bitcast.4), custom_call_target="tpu_custom_call" | custom-call | bytes 1179648 | tf_op jit(solution)/shard_map/prepare/pallas_call | solution.py:310
  15.1 6.3 %all-to-all-done.arrived = bf16[4,192,128]{2,1,0:T(8,128)(2,1)S(1)} async-done(((bf16[4,192,128]{2,1,0:T(8,128)(2,1)}), bf16[4,192,128]{2,1,0:T(8,128)(2,1)S(1)}, u32[]{:S(2)}, u32[]{:S(2)}) %all-to-all-start) | async-done | bytes 196640 | tf_op jit(solution)/shard_map/all_to_all | solution.py:368
  21.4 0.8 %regroup.1 = (bf16[8,4,32,128]{3,2,1,0:T(8,128)(2,1)}, bf16[4,64,128]{2,1,0:T(8,128)(2,1)S(1)}) custom-call(bf16[4,192,128]{2,1,0:T(8,128)(2,1)S(1)} %all-to-all-done.arrived, bf16[4,2,144,128]{3,2,1,0:T(8,128)(2,1)S(1)} %get-tuple-element.6._.weights), custom_call_target="tpu_custom_call" | custom-call | bytes 524288 | tf_op jit(solution)/shard_map/regroup/pallas_call | solution.py:310
  22.2 1.6 %collective-permute-start = (bf16[4,64,128]{2,1,0:T(8,128)(2,1)S(1)}, bf16[4,64,128]{2,1,0:T(8,128)(2,1)S(1)}, u32[]{:S(2)}, u32[]{:S(2)}) collective-permute-start(bf16[4,64,128]{2,1,0:T(8,128)(2,1)S(1)} %get-tuple-element.9.near), channel_id=1, source_target_pairs={{0,16},{16,0},{1,17},{17,1},{2,18},{18,2},{3,19},{19,3},{4,20},{20... | collective-permute-start | bytes 196616 | tf_op jit(solution)/shard_map/ppermute | solution.py:398
  23.7 3.4 %all-to-all-start.1 = ((bf16[8,4,32,128]{3,2,1,0:T(8,128)(2,1)}), bf16[8,4,32,128]{3,2,1,0:T(8,128)(2,1)S(1)}, u32[]{:S(2)}, u32[]{:S(2)}) async-start(bf16[8,4,32,128]{3,2,1,0:T(8,128)(2,1)} %get-tuple-element.7), calls=%async_computation.1 | async-start | bytes 524288 | tf_op jit(solution)/shard_map/all_to_all | solution.py:399
  27.1 0.0 collective-permute-done.far
  27.2 0.0 copy-done.2
  27.2 0.0 copy-done.3
  27.2 0.0 copy-done.4
  27.2 0.0 copy-done.5
  27.2 6.4 %columns.1 = bf16[2,40,2688]{2,1,0:T(8,128)(2,1)} custom-call(s32[4]{0:T(128)S(1)} %copy-done.5, bf16[64,2048]{1,0:T(8,128)(2,1)S(1)} %copy-done.3, bf16[2048,32]{1,0:T(8,128)(2,1)S(1)} %get-tuple-element.8.inverses, s32[1,1024]{1,0:T(1,128)S(1)} %bitcast.7, bf16[1024,128]{1,0:T(8,128)(2,1)S(1)} %copy-done.2, bf16[4,64,128]{2,1,0:T(8,128)(2,1)S(1)} %get-tuple-element.9.near, ...), custom_call_target="tpu_custom_call" | custom-call | flops 8589934592 | bytes 2097152 | tf_op jit(solution)/shard_map/columns/pallas_call | solution.py:310
  33.6 0.0 all-to-all-done.1.pieces
  33.6 1.0 %legendre.1 = bf16[6,2,4,16,48]{4,3,2,1,0:T(8,128)(2,1)} custom-call(bf16[4,2,144,128]{3,2,1,0:T(8,128)(2,1)S(1)} %get-tuple-element.6._.weights, bf16[8,4,32,128]{3,2,1,0:T(8,128)(2,1)S(1)} %all-to-all-done.1.pieces), custom_call_target="tpu_custom_call" | custom-call | flops 75497472 | bytes 262144 | tf_op jit(solution)/shard_map/legendre/pallas_call | solution.py:310
Async XLA Ops:
  0.6 13.2 %copy-start = (bf16[64,32,32]{0,2,1:T(8,128)(2,1)S(1)}, bf16[64,32,32]{0,2,1:T(8,128)(2,1)}, u32[]{:S(2)}) copy-start(bf16[64,32,32]{0,2,1:T(8,128)(2,1)} %param.14) | copy-start | bytes 393220
  0.6 13.2 %copy-start.1 = (bf16[6,160,48]{1,2,0:T(8,128)(2,1)S(1)}, bf16[6,160,48]{1,2,0:T(8,128)(2,1)}, u32[]{:S(2)}) copy-start(bf16[6,160,48]{1,2,0:T(8,128)(2,1)} %param.9) | copy-start | bytes 276484
  7.4 19.8 %copy-start.2 = (bf16[1024,128]{1,0:T(8,128)(2,1)S(1)}, bf16[1024,128]{1,0:T(8,128)(2,1)}, u32[]{:S(2)}) copy-start(bf16[1024,128]{1,0:T(8,128)(2,1)} %interp.1) | copy-start | bytes 786436
  7.4 19.8 %copy-start.3 = (bf16[64,2048]{1,0:T(8,128)(2,1)S(1)}, bf16[64,2048]{1,0:T(8,128)(2,1)}, u32[]{:S(2)}) copy-start(bf16[64,2048]{1,0:T(8,128)(2,1)} %weights.1) | copy-start | bytes 786436
  7.4 19.8 %copy-start.4 = (s32[1024]{0:T(1024)S(1)}, s32[1024]{0:T(1024)}, u32[]{:S(2)}) copy-start(s32[1024]{0:T(1024)} %param.11) | copy-start | bytes 12292
  7.4 19.8 %copy-start.5 = (s32[4]{0:T(128)S(1)}, s32[4]{0:T(128)}, u32[]{:S(2)}) copy-start(s32[4]{0:T(128)} %counts.1) | copy-start | bytes 52
  7.4 14.0 %all-to-all-start = ((bf16[4,192,128]{2,1,0:T(8,128)(2,1)}), bf16[4,192,128]{2,1,0:T(8,128)(2,1)S(1)}, u32[]{:S(2)}, u32[]{:S(2)}) async-start(bf16[4,192,128]{2,1,0:T(8,128)(2,1)} %local.1), calls=%async_computation | async-start | bytes 393216 | tf_op jit(solution)/shard_map/all_to_all | solution.py:368
  22.2 5.0 %collective-permute-start = (bf16[4,64,128]{2,1,0:T(8,128)(2,1)S(1)}, bf16[4,64,128]{2,1,0:T(8,128)(2,1)S(1)}, u32[]{:S(2)}, u32[]{:S(2)}) collective-permute-start(bf16[4,64,128]{2,1,0:T(8,128)(2,1)S(1)} %get-tuple-element.9.near), channel_id=1, source_target_pairs={{0,16},{16,0},{1,17},{17,1},{2,18},{18,2},{3,19},{19,3},{4,20},{20... | collective-permute-start | bytes 196616 | tf_op jit(solution)/shard_map/ppermute | solution.py:398
  23.7 9.9 %all-to-all-start.1 = ((bf16[8,4,32,128]{3,2,1,0:T(8,128)(2,1)}), bf16[8,4,32,128]{3,2,1,0:T(8,128)(2,1)S(1)}, u32[]{:S(2)}, u32[]{:S(2)}) async-start(bf16[8,4,32,128]{3,2,1,0:T(8,128)(2,1)} %get-tuple-element.7), calls=%async_computation.1 | async-start | bytes 524288 | tf_op jit(solution)/shard_map/all_to_all | solution.py:399

commit v11 on v9

--- a/solution.py
+++ b/solution.py
@@ -119,31 +119,29 @@
     return (blocks - lat * across) * lat_pad + lat
 
 
-def local_kernel(lat_pad, parts, grid_hbm, blocks_hbm, interp_hbm, table_hbm, out,
+def local_kernel(lat_pad, grid_hbm, blocks_hbm, interp_hbm, table_hbm, out,
                  grid, blocks, interp, table, patch, column, selector, message, padded, rows,
-                 sems, send):
+                 totals, sems, send):
     lev, lat, lon = grid.shape
     across = lon // LANES
     slots = interp.shape[0]
     depth = patch.shape[0]
-    step = lon // parts
     small = [
-        pltpu.make_async_copy(blocks_hbm, blocks, sems.at[parts]),
-        pltpu.make_async_copy(interp_hbm, interp, sems.at[parts + 1]),
-        pltpu.make_async_copy(table_hbm, table, sems.at[parts + 2]),
+        pltpu.make_async_copy(blocks_hbm, blocks, sems.at[lev]),
+        pltpu.make_async_copy(interp_hbm, interp, sems.at[lev + 1]),
+        pltpu.make_async_copy(table_hbm, table, sems.at[lev + 2]),
     ]
     loads = [
         pltpu.make_async_copy(
-            grid_hbm.at[:, :, pl.ds(part * step, step)],
-            grid.at[:, :, pl.ds(part * step, step)],
-            sems.at[part],
-        )
-        for part in range(parts)
+            grid_hbm.at[pl.ds(level, 1)], grid.at[pl.ds(level, 1)], sems.at[level]
+        )
+        for level in range(lev)
     ]
     small[0].start()
-    for copy in loads:
-        copy.start()
-    small[1].start()
+    for level in range(lev):
+        loads[level].start()
+        if level == 1:
+            small[1].start()
     small[2].start()
     small[0].wait()
     row = slot_rows(blocks[...], across, lat_pad)
@@ -156,19 +154,6 @@
             selector[start : start + chunk, base : base + LANES] = jnp.where(
                 mine == lane + base, 1.0, 0.0
             ).astype(BF16)
-    for part in range(parts):
-        loads[part].wait()
-        for tile in range(part * across // parts, (part + 1) * across // parts):
-            patch[tile * lat_pad + lat : (tile + 1) * lat_pad, :] = jnp.zeros(
-                (lat_pad - lat, lev * LANES), BF16
-            )
-            for level in range(lev):
-                patch[
-                    tile * lat_pad : tile * lat_pad + lat, level * LANES : (level + 1) * LANES
-                ] = grid[level, :, tile * LANES : (tile + 1) * LANES]
-    if depth > across * lat_pad:
-        patch[across * lat_pad :, :] = jnp.zeros((depth - across * lat_pad, lev * LANES), BF16)
-    small[1].wait()
     first_state = message.shape[1] - slots // LANES * lev
     copies = [
         pltpu.make_async_copy(message.at[:, rows_of, :], out.at[:, rows_of, :], send.at[i])
@@ -176,27 +161,47 @@
             (pl.ds(0, first_state), pl.ds(first_state, message.shape[1] - first_state))
         )
     ]
-    for start in range(0, slots, chunk):
-        picked = jnp.dot(
-            selector[start : start + chunk, :], patch[...], preferred_element_type=F32
-        )
-        weights = interp[start : start + chunk, :].astype(F32)
-        total = jnp.zeros((chunk, LANES), F32)
-        for level in range(lev):
-            product = picked[:, level * LANES : (level + 1) * LANES] * weights
-            total = jnp.where(lane == level, jnp.sum(product, axis=1, keepdims=True), total)
-        state = jnp.transpose(total)[:lev].astype(BF16)
-        for tile in range(chunk // LANES):
-            row = first_state + (start // LANES + tile) * lev
-            for target in range(message.shape[0]):
-                message[target, row : row + lev, :] = state[:, tile * LANES : (tile + 1) * LANES]
-        if start == chunk:
-            small[2].wait()
-            flat = jnp.concatenate([grid[level] for level in range(lev)], axis=0)
-            coeffs = jnp.dot(flat, table[...], preferred_element_type=F32)
-            pack(lev, lat, coeffs, message, padded, rows)
-            copies[0].start()
+    for tile in range(across):
+        patch[tile * lat_pad + lat : (tile + 1) * lat_pad, :] = jnp.zeros(
+            (lat_pad - lat, lev * LANES), BF16
+        )
+    if depth > across * lat_pad:
+        patch[across * lat_pad :, :] = jnp.zeros((depth - across * lat_pad, lev * LANES), BF16)
+    pair = 2 * LANES
+    for base in range(0, lev, 2):
+        for level in (base, base + 1):
+            loads[level].wait()
+            for tile in range(across):
+                patch[
+                    tile * lat_pad : tile * lat_pad + lat, level * LANES : (level + 1) * LANES
+                ] = grid[level, :, tile * LANES : (tile + 1) * LANES]
+        if base == 0:
+            small[1].wait()
+        for start in range(0, slots, chunk):
+            top = slice(start, start + chunk)
+            picked = jnp.dot(
+                selector[top, :],
+                patch[:, base * LANES : base * LANES + pair],
+                preferred_element_type=F32,
+            )
+            weights = interp[top, :].astype(F32)
+            values = [
+                jnp.sum(picked[:, i * LANES : (i + 1) * LANES] * weights, axis=1, keepdims=True)
+                for i in range(2)
+            ]
+            both = jnp.where(lane == base, values[0], values[1])
+            totals[top, :] = both if base == 0 else jnp.where(lane < base, totals[top, :], both)
+    small[2].wait()
+    flat = jnp.concatenate([grid[level] for level in range(lev)], axis=0)
+    coeffs = jnp.dot(flat, table[...], preferred_element_type=F32)
+    for top in range(0, slots, LANES):
+        state = jnp.transpose(totals[top : top + LANES, :])[:lev].astype(BF16)
+        row = first_state + top // LANES * lev
+        for target in range(message.shape[0]):
+            message[target, row : row + lev, :] = state
     copies[1].start()
+    pack(lev, lat, coeffs, message, padded, rows)
+    copies[0].start()
     for copy in copies:
         copy.wait()
 
@@ -245,22 +250,31 @@
     lane = lax.broadcasted_iota(jnp.int32, (1, flux_rows), 1)
     slot = lax.broadcasted_iota(jnp.int32, (chunk, 1), 0)
     column = jnp.transpose(state[...]).astype(BF16)
-
-    def gates_of(source):
-        return jnp.dot(column, weights[:, source : source + chunk], preferred_element_type=F32)
-
-    flux = jnp.zeros((slots, flux_rows), F32)
-    gates = gates_of(0)
-    for source in range(0, sources, chunk):
-        later = gates_of(source + chunk) if source + chunk < sources else None
-        flux = flux + jnp.dot(
-            softplus(gates).astype(BF16),
-            inverses[source : source + chunk, :],
-            preferred_element_type=F32,
-        )
-        gates = later
+    tiles = [(top, at) for top in range(0, slots, chunk) for at in range(0, sources, chunk)]
+
+    def gates_of(top, at):
+        return jnp.dot(
+            column[top : top + chunk], weights[:, at : at + chunk], preferred_element_type=F32
+        )
+
+    fluxes = {top: jnp.zeros((chunk, flux_rows), F32) for top in range(0, slots, chunk)}
+
+    def add_flux(top, at, source):
+        fluxes[top] = fluxes[top] + jnp.dot(
+            source, inverses[at : at + chunk, :], preferred_element_type=F32
+        )
+
+    gates = gates_of(*tiles[0])
+    before = None
+    for i, tile in enumerate(tiles):
+        later = gates_of(*tiles[i + 1]) if i + 1 < len(tiles) else None
+        source = softplus(gates).astype(BF16)
+        if before is not None:
+            add_flux(*tiles[i - 1], before)
+        gates, before = later, source
+    add_flux(*tiles[-1], before)
     for start in range(0, slots, chunk):
-        rows = flux[start : start + chunk]
+        rows = fluxes[start]
         for level in range(mine):
             at = base + level
             plus = (lane == at) | ((lane == at + levels + 1) & (at + 1 < levels))
@@ -327,11 +341,10 @@
     group = n_fld * n_band * rest
     padded_group = -(-group // LANES) * LANES
     depth = -(-across * lat_pad // LANES) * LANES
-    parts = max(t for t in range(1, 8) if across % t == 0)
     state_rows = slots * lev // LANES
     message_rows = n_band * piece + state_rows
     message = call(
-        functools.partial(local_kernel, lat_pad, parts),
+        functools.partial(local_kernel, lat_pad),
         [((n_fld, message_rows, LANES), BF16)],
         [HBM] * 4,
         [
@@ -345,7 +358,8 @@
             pltpu.VMEM((n_fld, message_rows, LANES), BF16),
             pltpu.VMEM((LANES, padded_group), F32),
             pltpu.VMEM((group * lev, LANES), F32),
-            pltpu.SemaphoreType.DMA((parts + 3,)),
+            pltpu.VMEM((slots, LANES), F32),
+            pltpu.SemaphoreType.DMA((lev + 3,)),
             pltpu.SemaphoreType.DMA((2,)),
         ],
         (grid.reshape(lev, lat, lon), block_row, interp, table),

time: 33.6 us -> 34.5 us (1.027)
  Pallas kernels: 14.7 us -> 15.5 us
    pallas_call x5, Pallas kernels: 14.7 us -> 15.5 us  [call(): pl.pallas_call(kernel, out_shape=shapes[0] if single else shapes, in_spec...]
  transfers between devices with their start and end apart: 3 -> 3, of which waited for: 2 -> 2; matrix products, arithmetic and copies ran while one was open for 0% -> 0% of each run, Pallas kernels for 21% -> 20%
where the time goes in v11:
time: 34.5 us; the launch traced here: 34.1 us
  Pallas kernels  15.5 us (45%)
  starting transfers between devices  11.4 us (33%)
  waiting for transfers between devices  6.45 us (19%)
  between operations  0.76 us (2%)
    pallas_call x5, Pallas kernels, call(): pl.pallas_call(kernel, out_shape=shapes[0] if single else shapes, in_spec...  15.5 us
    all_to_all x1, starting transfers between devices, body(): arrived = lax.all_to_all(message, 'fld', 0, 0, tiled=True)  6.47 us
    all_to_all x1, waiting for transfers between devices, body(): arrived = lax.all_to_all(message, 'fld', 0, 0, tiled=True)  6.29 us
    all_to_all x1, starting transfers between devices, body(): pieces = lax.all_to_all(sent, ('sec', 'band'), 0, 0, tiled=True)  3.41 us
    ppermute x1, starting transfers between devices, body(): far = lax.ppermute(near, 'sec', [(i, 1 - i) for i in range(n_sec)])  1.56 us
  transfers between devices with their start and end apart: 3, of which 2 were waited for; matrix products, arithmetic and copies ran while one was open for 0% of the time, Pallas kernels for 20%

profile of v11, /device:TPU:0, one launch (start us, length us, event | category | flops | bytes accessed | tf_op | source)
XLA Modules:
  0.0 34.1 jit_solution(8576300539348914483)
XLA Ops:
  0.6 0.0 copy-start
  0.6 0.0 copy-start.1
  0.6 6.7 %local.1 = bf16[4,192,128]{2,1,0:T(8,128)(2,1)} custom-call(bf16[8,40,2688]{2,1,0:T(8,128)(2,1)} %bitcast.8, s32[1,1024]{1,0:T(1,128)} %bitcast.6, bf16[1024,128]{1,0:T(8,128)(2,1)} %interp.1, bf16[2688,192]{1,0:T(8,128)(2,1)} %constant.2.clone.table_hbm), custom_call_target="tpu_custom_call" | custom-call | flops 2477785088 | bytes 1982464 | tf_op jit(solution)/shard_map/local/pallas_call | solution.py:315
  7.3 0.0 copy-start.2
  7.4 0.0 copy-start.3
  7.4 0.0 copy-start.4
  7.4 0.0 copy-start.5
  7.4 6.5 %all-to-all-start = ((bf16[4,192,128]{2,1,0:T(8,128)(2,1)}), bf16[4,192,128]{2,1,0:T(8,128)(2,1)S(1)}, u32[]{:S(2)}, u32[]{:S(2)}) async-start(bf16[4,192,128]{2,1,0:T(8,128)(2,1)} %local.1), calls=%async_computation | async-start | bytes 393216 | tf_op jit(solution)/shard_map/all_to_all | solution.py:372
  13.9 0.0 copy-done
  13.9 0.0 copy-done.1
  13.9 1.2 %prepare.1 = (bf16[4,2,144,128]{3,2,1,0:T(8,128)(2,1)S(1)}, bf16[2048,32]{1,0:T(8,128)(2,1)S(1)}) custom-call(bf16[6,48,160]{2,1,0:T(8,128)(2,1)S(1)} %bitcast.5, bf16[32,32,64]{2,1,0:T(8,128)(2,1)S(1)} %bitcast.4), custom_call_target="tpu_custom_call" | custom-call | bytes 1179648 | tf_op jit(solution)/shard_map/prepare/pallas_call | solution.py:315
  15.1 6.3 %all-to-all-done.arrived = bf16[4,192,128]{2,1,0:T(8,128)(2,1)S(1)} async-done(((bf16[4,192,128]{2,1,0:T(8,128)(2,1)}), bf16[4,192,128]{2,1,0:T(8,128)(2,1)S(1)}, u32[]{:S(2)}, u32[]{:S(2)}) %all-to-all-start) | async-done | bytes 196640 | tf_op jit(solution)/shard_map/all_to_all | solution.py:372
  21.4 0.8 %regroup.1 = (bf16[8,4,32,128]{3,2,1,0:T(8,128)(2,1)}, bf16[4,64,128]{2,1,0:T(8,128)(2,1)S(1)}) custom-call(bf16[4,192,128]{2,1,0:T(8,128)(2,1)S(1)} %all-to-all-done.arrived, bf16[4,2,144,128]{3,2,1,0:T(8,128)(2,1)S(1)} %get-tuple-element.6._.weights), custom_call_target="tpu_custom_call" | custom-call | bytes 524288 | tf_op jit(solution)/shard_map/regroup/pallas_call | solution.py:315
  22.2 1.6 %collective-permute-start = (bf16[4,64,128]{2,1,0:T(8,128)(2,1)S(1)}, bf16[4,64,128]{2,1,0:T(8,128)(2,1)S(1)}, u32[]{:S(2)}, u32[]{:S(2)}) collective-permute-start(bf16[4,64,128]{2,1,0:T(8,128)(2,1)S(1)} %get-tuple-element.9.near), channel_id=1, source_target_pairs={{0,16},{16,0},{1,17},{17,1},{2,18},{18,2},{3,19},{19,3},{4,20},{20... | collective-permute-start | bytes 196616 | tf_op jit(solution)/shard_map/ppermute | solution.py:402
  23.7 3.4 %all-to-all-start.1 = ((bf16[8,4,32,128]{3,2,1,0:T(8,128)(2,1)}), bf16[8,4,32,128]{3,2,1,0:T(8,128)(2,1)S(1)}, u32[]{:S(2)}, u32[]{:S(2)}) async-start(bf16[8,4,32,128]{3,2,1,0:T(8,128)(2,1)} %get-tuple-element.7), calls=%async_computation.1 | async-start | bytes 524288 | tf_op jit(solution)/shard_map/all_to_all | solution.py:403
  27.1 0.0 collective-permute-done.far
  27.2 0.0 copy-done.2
  27.2 0.0 copy-done.3
  27.2 0.0 copy-done.4
  27.2 0.0 copy-done.5
  27.2 5.8 %columns.1 = bf16[2,40,2688]{2,1,0:T(8,128)(2,1)} custom-call(s32[4]{0:T(128)S(1)} %copy-done.5, bf16[64,2048]{1,0:T(8,128)(2,1)S(1)} %copy-done.3, bf16[2048,32]{1,0:T(8,128)(2,1)S(1)} %get-tuple-element.8.inverses, s32[1,1024]{1,0:T(1,128)S(1)} %bitcast.7, bf16[1024,128]{1,0:T(8,128)(2,1)S(1)} %copy-done.2, bf16[4,64,128]{2,1,0:T(8,128)(2,1)S(1)} %get-tuple-element.9.near, ...), custom_call_target="tpu_custom_call" | custom-call | flops 8589934592 | bytes 2097152 | tf_op jit(solution)/shard_map/columns/pallas_call | solution.py:315
  33.0 0.2 all-to-all-done.1.pieces
  33.1 1.0 %legendre.1 = bf16[6,2,4,16,48]{4,3,2,1,0:T(8,128)(2,1)} custom-call(bf16[4,2,144,128]{3,2,1,0:T(8,128)(2,1)S(1)} %get-tuple-element.6._.weights, bf16[8,4,32,128]{3,2,1,0:T(8,128)(2,1)S(1)} %all-to-all-done.1.pieces), custom_call_target="tpu_custom_call" | custom-call | flops 75497472 | bytes 262144 | tf_op jit(solution)/shard_map/legendre/pallas_call | solution.py:315
Async XLA Ops:
  0.6 13.2 %copy-start = (bf16[64,32,32]{0,2,1:T(8,128)(2,1)S(1)}, bf16[64,32,32]{0,2,1:T(8,128)(2,1)}, u32[]{:S(2)}) copy-start(bf16[64,32,32]{0,2,1:T(8,128)(2,1)} %param.14) | copy-start | bytes 393220
  0.6 13.2 %copy-start.1 = (bf16[6,160,48]{1,2,0:T(8,128)(2,1)S(1)}, bf16[6,160,48]{1,2,0:T(8,128)(2,1)}, u32[]{:S(2)}) copy-start(bf16[6,160,48]{1,2,0:T(8,128)(2,1)} %param.9) | copy-start | bytes 276484
  7.3 19.8 %copy-start.2 = (bf16[1024,128]{1,0:T(8,128)(2,1)S(1)}, bf16[1024,128]{1,0:T(8,128)(2,1)}, u32[]{:S(2)}) copy-start(bf16[1024,128]{1,0:T(8,128)(2,1)} %interp.1) | copy-start | bytes 786436
  7.4 19.8 %copy-start.3 = (bf16[64,2048]{1,0:T(8,128)(2,1)S(1)}, bf16[64,2048]{1,0:T(8,128)(2,1)}, u32[]{:S(2)}) copy-start(bf16[64,2048]{1,0:T(8,128)(2,1)} %weights.1) | copy-start | bytes 786436
  7.4 19.8 %copy-start.4 = (s32[1024]{0:T(1024)S(1)}, s32[1024]{0:T(1024)}, u32[]{:S(2)}) copy-start(s32[1024]{0:T(1024)} %param.11) | copy-start | bytes 12292
  7.4 19.8 %copy-start.5 = (s32[4]{0:T(128)S(1)}, s32[4]{0:T(128)}, u32[]{:S(2)}) copy-start(s32[4]{0:T(128)} %counts.1) | copy-start | bytes 52
  7.4 14.0 %all-to-all-start = ((bf16[4,192,128]{2,1,0:T(8,128)(2,1)}), bf16[4,192,128]{2,1,0:T(8,128)(2,1)S(1)}, u32[]{:S(2)}, u32[]{:S(2)}) async-start(bf16[4,192,128]{2,1,0:T(8,128)(2,1)} %local.1), calls=%async_computation | async-start | bytes 393216 | tf_op jit(solution)/shard_map/all_to_all | solution.py:372
  22.2 5.0 %collective-permute-start = (bf16[4,64,128]{2,1,0:T(8,128)(2,1)S(1)}, bf16[4,64,128]{2,1,0:T(8,128)(2,1)S(1)}, u32[]{:S(2)}, u32[]{:S(2)}) collective-permute-start(bf16[4,64,128]{2,1,0:T(8,128)(2,1)S(1)} %get-tuple-element.9.near), channel_id=1, source_target_pairs={{0,16},{16,0},{1,17},{17,1},{2,18},{18,2},{3,19},{19,3},{4,20},{20... | collective-permute-start | bytes 196616 | tf_op jit(solution)/shard_map/ppermute | solution.py:402
  23.7 9.4 %all-to-all-start.1 = ((bf16[8,4,32,128]{3,2,1,0:T(8,128)(2,1)}), bf16[8,4,32,128]{3,2,1,0:T(8,128)(2,1)S(1)}, u32[]{:S(2)}, u32[]{:S(2)}) async-start(bf16[8,4,32,128]{3,2,1,0:T(8,128)(2,1)} %get-tuple-element.7), calls=%async_computation.1 | async-start | bytes 524288 | tf_op jit(solution)/shard_map/all_to_all | solution.py:403

commit v12 on v9

--- a/solution.py
+++ b/solution.py
@@ -119,26 +119,23 @@
     return (blocks - lat * across) * lat_pad + lat
 
 
-def local_kernel(lat_pad, parts, grid_hbm, blocks_hbm, interp_hbm, table_hbm, out,
+def local_kernel(lat_pad, grid_hbm, blocks_hbm, interp_hbm, table_hbm, out,
                  grid, blocks, interp, table, patch, column, selector, message, padded, rows,
                  sems, send):
     lev, lat, lon = grid.shape
     across = lon // LANES
     slots = interp.shape[0]
     depth = patch.shape[0]
-    step = lon // parts
     small = [
-        pltpu.make_async_copy(blocks_hbm, blocks, sems.at[parts]),
-        pltpu.make_async_copy(interp_hbm, interp, sems.at[parts + 1]),
-        pltpu.make_async_copy(table_hbm, table, sems.at[parts + 2]),
+        pltpu.make_async_copy(blocks_hbm, blocks, sems.at[lev]),
+        pltpu.make_async_copy(interp_hbm, interp, sems.at[lev + 1]),
+        pltpu.make_async_copy(table_hbm, table, sems.at[lev + 2]),
     ]
     loads = [
         pltpu.make_async_copy(
-            grid_hbm.at[:, :, pl.ds(part * step, step)],
-            grid.at[:, :, pl.ds(part * step, step)],
-            sems.at[part],
-        )
-        for part in range(parts)
+            grid_hbm.at[pl.ds(level, 1)], grid.at[pl.ds(level, 1)], sems.at[level]
+        )
+        for level in range(lev)
     ]
     small[0].start()
     for copy in loads:
@@ -156,16 +153,20 @@
             selector[start : start + chunk, base : base + LANES] = jnp.where(
                 mine == lane + base, 1.0, 0.0
             ).astype(BF16)
-    for part in range(parts):
-        loads[part].wait()
-        for tile in range(part * across // parts, (part + 1) * across // parts):
-            patch[tile * lat_pad + lat : (tile + 1) * lat_pad, :] = jnp.zeros(
-                (lat_pad - lat, lev * LANES), BF16
-            )
-            for level in range(lev):
-                patch[
-                    tile * lat_pad : tile * lat_pad + lat, level * LANES : (level + 1) * LANES
-                ] = grid[level, :, tile * LANES : (tile + 1) * LANES]
+    for tile in range(across):
+        patch[tile * lat_pad + lat : (tile + 1) * lat_pad, :] = jnp.zeros(
+            (lat_pad - lat, lev * LANES), BF16
+        )
+    ones = (
+        lax.broadcasted_iota(jnp.int32, (lev * LANES, LANES), 0) // LANES
+        == lax.broadcasted_iota(jnp.int32, (lev * LANES, LANES), 1)
+    ).astype(F32).astype(BF16)
+    for level in range(lev):
+        loads[level].wait()
+        for tile in range(across):
+            patch[
+                tile * lat_pad : tile * lat_pad + lat, level * LANES : (level + 1) * LANES
+            ] = grid[level, :, tile * LANES : (tile + 1) * LANES]
     if depth > across * lat_pad:
         patch[across * lat_pad :, :] = jnp.zeros((depth - across * lat_pad, lev * LANES), BF16)
     small[1].wait()
@@ -181,10 +182,14 @@
             selector[start : start + chunk, :], patch[...], preferred_element_type=F32
         )
         weights = interp[start : start + chunk, :].astype(F32)
-        total = jnp.zeros((chunk, LANES), F32)
-        for level in range(lev):
-            product = picked[:, level * LANES : (level + 1) * LANES] * weights
-            total = jnp.where(lane == level, jnp.sum(product, axis=1, keepdims=True), total)
+        products = jnp.concatenate(
+            [
+                (picked[:, level * LANES : (level + 1) * LANES] * weights).astype(BF16)
+                for level in range(lev)
+            ],
+            axis=1,
+        )
+        total = jnp.dot(products, ones, preferred_element_type=F32)
         state = jnp.transpose(total)[:lev].astype(BF16)
         for tile in range(chunk // LANES):
             row = first_state + (start // LANES + tile) * lev
@@ -245,22 +250,31 @@
     lane = lax.broadcasted_iota(jnp.int32, (1, flux_rows), 1)
     slot = lax.broadcasted_iota(jnp.int32, (chunk, 1), 0)
     column = jnp.transpose(state[...]).astype(BF16)
-
-    def gates_of(source):
-        return jnp.dot(column, weights[:, source : source + chunk], preferred_element_type=F32)
-
-    flux = jnp.zeros((slots, flux_rows), F32)
-    gates = gates_of(0)
-    for source in range(0, sources, chunk):
-        later = gates_of(source + chunk) if source + chunk < sources else None
-        flux = flux + jnp.dot(
-            softplus(gates).astype(BF16),
-            inverses[source : source + chunk, :],
-            preferred_element_type=F32,
-        )
-        gates = later
+    tiles = [(top, at) for top in range(0, slots, chunk) for at in range(0, sources, chunk)]
+
+    def gates_of(top, at):
+        return jnp.dot(
+            column[top : top + chunk], weights[:, at : at + chunk], preferred_element_type=F32
+        )
+
+    fluxes = {top: jnp.zeros((chunk, flux_rows), F32) for top in range(0, slots, chunk)}
+
+    def add_flux(top, at, source):
+        fluxes[top] = fluxes[top] + jnp.dot(
+            source, inverses[at : at + chunk, :], preferred_element_type=F32
+        )
+
+    gates = gates_of(*tiles[0])
+    before = None
+    for i, tile in enumerate(tiles):
+        later = gates_of(*tiles[i + 1]) if i + 1 < len(tiles) else None
+        source = softplus(gates).astype(BF16)
+        if before is not None:
+            add_flux(*tiles[i - 1], before)
+        gates, before = later, source
+    add_flux(*tiles[-1], before)
     for start in range(0, slots, chunk):
-        rows = flux[start : start + chunk]
+        rows = fluxes[start]
         for level in range(mine):
             at = base + level
             plus = (lane == at) | ((lane == at + levels + 1) & (at + 1 < levels))
@@ -327,11 +341,10 @@
     group = n_fld * n_band * rest
     padded_group = -(-group // LANES) * LANES
     depth = -(-across * lat_pad // LANES) * LANES
-    parts = max(t for t in range(1, 8) if across % t == 0)
     state_rows = slots * lev // LANES
     message_rows = n_band * piece + state_rows
     message = call(
-        functools.partial(local_kernel, lat_pad, parts),
+        functools.partial(local_kernel, lat_pad),
         [((n_fld, message_rows, LANES), BF16)],
         [HBM] * 4,
         [
@@ -345,7 +358,7 @@
             pltpu.VMEM((n_fld, message_rows, LANES), BF16),
             pltpu.VMEM((LANES, padded_group), F32),
             pltpu.VMEM((group * lev, LANES), F32),
-            pltpu.SemaphoreType.DMA((parts + 3,)),
+            pltpu.SemaphoreType.DMA((lev + 3,)),
             pltpu.SemaphoreType.DMA((2,)),
         ],
         (grid.reshape(lev, lat, lon), block_row, interp, table),

time: 33.6 us -> 34 us (1.012)
    pallas_call x5, Pallas kernels: 14.7 us -> 15 us  [call(): pl.pallas_call(kernel, out_shape=shapes[0] if single else shapes, in_spec...]
where the time goes in v12:
time: 34 us; the launch traced here: 33.7 us
  Pallas kernels  15 us (44%)
  starting transfers between devices  11.4 us (34%)
  waiting for transfers between devices  6.44 us (19%)
  between operations  0.76 us (2%)
    pallas_call x5, Pallas kernels, call(): pl.pallas_call(kernel, out_shape=shapes[0] if single else shapes, in_spec...  15 us
    all_to_all x1, starting transfers between devices, body(): arrived = lax.all_to_all(message, 'fld', 0, 0, tiled=True)  6.46 us
    all_to_all x1, waiting for transfers between devices, body(): arrived = lax.all_to_all(message, 'fld', 0, 0, tiled=True)  6.29 us
    all_to_all x1, starting transfers between devices, body(): pieces = lax.all_to_all(sent, ('sec', 'band'), 0, 0, tiled=True)  3.41 us
    ppermute x1, starting transfers between devices, body(): far = lax.ppermute(near, 'sec', [(i, 1 - i) for i in range(n_sec)])  1.55 us
  transfers between devices with their start and end apart: 3, of which 2 were waited for; matrix products, arithmetic and copies ran while one was open for 0% of the time, Pallas kernels for 21%

profile of v12, /device:TPU:0, one launch (start us, length us, event | category | flops | bytes accessed | tf_op | source)
XLA Modules:
  0.0 33.7 jit_solution(5240726032926992021)
XLA Ops:
  0.6 0.0 copy-start
  0.6 0.0 copy-start.1
  0.6 6.3 %local.1 = bf16[4,192,128]{2,1,0:T(8,128)(2,1)} custom-call(bf16[8,40,2688]{2,1,0:T(8,128)(2,1)} %bitcast.8, s32[1,1024]{1,0:T(1,128)} %bitcast.6, bf16[1024,128]{1,0:T(8,128)(2,1)} %interp.1, bf16[2688,192]{1,0:T(8,128)(2,1)} %constant.2.clone.table_hbm), custom_call_target="tpu_custom_call" | custom-call | flops 2477785088 | bytes 1982464 | tf_op jit(solution)/shard_map/local/pallas_call | solution.py:315
  6.9 0.0 copy-start.2
  6.9 0.0 copy-start.3
  6.9 0.0 copy-start.4
  7.0 0.0 copy-start.5
  7.0 6.5 %all-to-all-start = ((bf16[4,192,128]{2,1,0:T(8,128)(2,1)}), bf16[4,192,128]{2,1,0:T(8,128)(2,1)S(1)}, u32[]{:S(2)}, u32[]{:S(2)}) async-start(bf16[4,192,128]{2,1,0:T(8,128)(2,1)} %local.1), calls=%async_computation | async-start | bytes 393216 | tf_op jit(solution)/shard_map/all_to_all | solution.py:371
  13.4 0.0 copy-done
  13.4 0.0 copy-done.1
  13.4 1.2 %prepare.1 = (bf16[4,2,144,128]{3,2,1,0:T(8,128)(2,1)S(1)}, bf16[2048,32]{1,0:T(8,128)(2,1)S(1)}) custom-call(bf16[6,48,160]{2,1,0:T(8,128)(2,1)S(1)} %bitcast.5, bf16[32,32,64]{2,1,0:T(8,128)(2,1)S(1)} %bitcast.4), custom_call_target="tpu_custom_call" | custom-call | bytes 1179648 | tf_op jit(solution)/shard_map/prepare/pallas_call | solution.py:315
  14.6 6.3 %all-to-all-done.arrived = bf16[4,192,128]{2,1,0:T(8,128)(2,1)S(1)} async-done(((bf16[4,192,128]{2,1,0:T(8,128)(2,1)}), bf16[4,192,128]{2,1,0:T(8,128)(2,1)S(1)}, u32[]{:S(2)}, u32[]{:S(2)}) %all-to-all-start) | async-done | bytes 196640 | tf_op jit(solution)/shard_map/all_to_all | solution.py:371
  20.9 0.8 %regroup.1 = (bf16[8,4,32,128]{3,2,1,0:T(8,128)(2,1)}, bf16[4,64,128]{2,1,0:T(8,128)(2,1)S(1)}) custom-call(bf16[4,192,128]{2,1,0:T(8,128)(2,1)S(1)} %all-to-all-done.arrived, bf16[4,2,144,128]{3,2,1,0:T(8,128)(2,1)S(1)} %get-tuple-element.6._.weights), custom_call_target="tpu_custom_call" | custom-call | bytes 524288 | tf_op jit(solution)/shard_map/regroup/pallas_call | solution.py:315
  21.7 1.5 %collective-permute-start = (bf16[4,64,128]{2,1,0:T(8,128)(2,1)S(1)}, bf16[4,64,128]{2,1,0:T(8,128)(2,1)S(1)}, u32[]{:S(2)}, u32[]{:S(2)}) collective-permute-start(bf16[4,64,128]{2,1,0:T(8,128)(2,1)S(1)} %get-tuple-element.9.near), channel_id=1, source_target_pairs={{0,16},{16,0},{1,17},{17,1},{2,18},{18,2},{3,19},{19,3},{4,20},{20... | collective-permute-start | bytes 196616 | tf_op jit(solution)/shard_map/ppermute | solution.py:401
  23.3 3.4 %all-to-all-start.1 = ((bf16[8,4,32,128]{3,2,1,0:T(8,128)(2,1)}), bf16[8,4,32,128]{3,2,1,0:T(8,128)(2,1)S(1)}, u32[]{:S(2)}, u32[]{:S(2)}) async-start(bf16[8,4,32,128]{3,2,1,0:T(8,128)(2,1)} %get-tuple-element.7), calls=%async_computation.1 | async-start | bytes 524288 | tf_op jit(solution)/shard_map/all_to_all | solution.py:402
  26.7 0.0 collective-permute-done.far
  26.7 0.0 copy-done.2
  26.7 0.0 copy-done.3
  26.7 0.0 copy-done.4
  26.7 0.0 copy-done.5
  26.8 5.8 %columns.1 = bf16[2,40,2688]{2,1,0:T(8,128)(2,1)} custom-call(s32[4]{0:T(128)S(1)} %copy-done.5, bf16[64,2048]{1,0:T(8,128)(2,1)S(1)} %copy-done.3, bf16[2048,32]{1,0:T(8,128)(2,1)S(1)} %get-tuple-element.8.inverses, s32[1,1024]{1,0:T(1,128)S(1)} %bitcast.7, bf16[1024,128]{1,0:T(8,128)(2,1)S(1)} %copy-done.2, bf16[4,64,128]{2,1,0:T(8,128)(2,1)S(1)} %get-tuple-element.9.near, ...), custom_call_target="tpu_custom_call" | custom-call | flops 8589934592 | bytes 2097152 | tf_op jit(solution)/shard_map/columns/pallas_call | solution.py:315
  32.5 0.1 all-to-all-done.1.pieces
  32.7 1.0 %legendre.1 = bf16[6,2,4,16,48]{4,3,2,1,0:T(8,128)(2,1)} custom-call(bf16[4,2,144,128]{3,2,1,0:T(8,128)(2,1)S(1)} %get-tuple-element.6._.weights, bf16[8,4,32,128]{3,2,1,0:T(8,128)(2,1)S(1)} %all-to-all-done.1.pieces), custom_call_target="tpu_custom_call" | custom-call | flops 75497472 | bytes 262144 | tf_op jit(solution)/shard_map/legendre/pallas_call | solution.py:315
Async XLA Ops:
  0.6 12.8 %copy-start = (bf16[64,32,32]{0,2,1:T(8,128)(2,1)S(1)}, bf16[64,32,32]{0,2,1:T(8,128)(2,1)}, u32[]{:S(2)}) copy-start(bf16[64,32,32]{0,2,1:T(8,128)(2,1)} %param.14) | copy-start | bytes 393220
  0.6 12.8 %copy-start.1 = (bf16[6,160,48]{1,2,0:T(8,128)(2,1)S(1)}, bf16[6,160,48]{1,2,0:T(8,128)(2,1)}, u32[]{:S(2)}) copy-start(bf16[6,160,48]{1,2,0:T(8,128)(2,1)} %param.9) | copy-start | bytes 276484
  6.9 19.8 %copy-start.2 = (bf16[1024,128]{1,0:T(8,128)(2,1)S(1)}, bf16[1024,128]{1,0:T(8,128)(2,1)}, u32[]{:S(2)}) copy-start(bf16[1024,128]{1,0:T(8,128)(2,1)} %interp.1) | copy-start | bytes 786436
  6.9 19.8 %copy-start.3 = (bf16[64,2048]{1,0:T(8,128)(2,1)S(1)}, bf16[64,2048]{1,0:T(8,128)(2,1)}, u32[]{:S(2)}) copy-start(bf16[64,2048]{1,0:T(8,128)(2,1)} %weights.1) | copy-start | bytes 786436
  6.9 19.8 %copy-start.4 = (s32[1024]{0:T(1024)S(1)}, s32[1024]{0:T(1024)}, u32[]{:S(2)}) copy-start(s32[1024]{0:T(1024)} %param.11) | copy-start | bytes 12292
  7.0 19.8 %copy-start.5 = (s32[4]{0:T(128)S(1)}, s32[4]{0:T(128)}, u32[]{:S(2)}) copy-start(s32[4]{0:T(128)} %counts.1) | copy-start | bytes 52
  7.0 14.0 %all-to-all-start = ((bf16[4,192,128]{2,1,0:T(8,128)(2,1)}), bf16[4,192,128]{2,1,0:T(8,128)(2,1)S(1)}, u32[]{:S(2)}, u32[]{:S(2)}) async-start(bf16[4,192,128]{2,1,0:T(8,128)(2,1)} %local.1), calls=%async_computation | async-start | bytes 393216 | tf_op jit(solution)/shard_map/all_to_all | solution.py:371
  21.7 5.0 %collective-permute-start = (bf16[4,64,128]{2,1,0:T(8,128)(2,1)S(1)}, bf16[4,64,128]{2,1,0:T(8,128)(2,1)S(1)}, u32[]{:S(2)}, u32[]{:S(2)}) collective-permute-start(bf16[4,64,128]{2,1,0:T(8,128)(2,1)S(1)} %get-tuple-element.9.near), channel_id=1, source_target_pairs={{0,16},{16,0},{1,17},{17,1},{2,18},{18,2},{3,19},{19,3},{4,20},{20... | collective-permute-start | bytes 196616 | tf_op jit(solution)/shard_map/ppermute | solution.py:401
  23.3 9.4 %all-to-all-start.1 = ((bf16[8,4,32,128]{3,2,1,0:T(8,128)(2,1)}), bf16[8,4,32,128]{3,2,1,0:T(8,128)(2,1)S(1)}, u32[]{:S(2)}, u32[]{:S(2)}) async-start(bf16[8,4,32,128]{3,2,1,0:T(8,128)(2,1)} %get-tuple-element.7), calls=%async_computation.1 | async-start | bytes 524288 | tf_op jit(solution)/shard_map/all_to_all | solution.py:402

commit v13 on v9

--- a/solution.py
+++ b/solution.py
@@ -225,7 +225,7 @@
 
 
 def column_kernel(n_sec, n_fld, lat_pad, slots, counts, weights, inverses, blocks, interp,
-                  near, far, out, state, spread, result, sems):
+                  near, far, out, state, total, result, sems):
     lev = near.shape[1] * LANES // slots
     place = lax.axis_index("sec")
     for fld in range(n_fld):
@@ -245,52 +245,81 @@
     lane = lax.broadcasted_iota(jnp.int32, (1, flux_rows), 1)
     slot = lax.broadcasted_iota(jnp.int32, (chunk, 1), 0)
     column = jnp.transpose(state[...]).astype(BF16)
-
-    def gates_of(source):
-        return jnp.dot(column, weights[:, source : source + chunk], preferred_element_type=F32)
-
-    flux = jnp.zeros((slots, flux_rows), F32)
-    gates = gates_of(0)
-    for source in range(0, sources, chunk):
-        later = gates_of(source + chunk) if source + chunk < sources else None
-        flux = flux + jnp.dot(
-            softplus(gates).astype(BF16),
-            inverses[source : source + chunk, :],
-            preferred_element_type=F32,
-        )
-        gates = later
-    for start in range(0, slots, chunk):
-        rows = flux[start : start + chunk]
+    row = slot_rows(blocks[...], across, lat_pad)
+    group = max(t for t in range(1, 4) if across % t == 0)
+    height = group * lat_pad
+    line = lax.broadcasted_iota(jnp.int32, (height, chunk), 0)
+    copies = []
+
+    def gates_of(top, at):
+        return jnp.dot(
+            column[top : top + chunk], weights[:, at : at + chunk], preferred_element_type=F32
+        )
+
+    def spread_of(top, flux):
+        parts = []
         for level in range(mine):
             at = base + level
             plus = (lane == at) | ((lane == at + levels + 1) & (at + 1 < levels))
             minus = (lane == at + levels) | ((lane == at + 1) & (at + 1 < levels))
-            terms = jnp.where(plus, rows, 0.0) - jnp.where(minus, rows, 0.0)
+            terms = jnp.where(plus, flux, 0.0) - jnp.where(minus, flux, 0.0)
             heat = jnp.sum(terms, axis=1, keepdims=True)
-            heat = jnp.where(slot + start < count, heat, 0.0).astype(BF16).astype(F32)
-            spread[start : start + chunk, level * LANES : (level + 1) * LANES] = (
-                heat * interp[start : start + chunk, :].astype(F32)
-            ).astype(BF16)
-    row = slot_rows(blocks[...], across, lat_pad)
-    tiles = max(t for t in range(1, 8) if across % t == 0)
-    height = tiles * lat_pad
-    copies = []
-    for first in range(0, across, tiles):
-        match = row == lax.broadcasted_iota(jnp.int32, (height, slots), 0) + first * lat_pad
-        left = jnp.where(match, 1.0, 0.0).astype(BF16)
-        summed = jnp.dot(left, spread[...], preferred_element_type=F32).astype(BF16)
+            heat = jnp.where(slot + top < count, heat, 0.0).astype(BF16).astype(F32)
+            parts.append((heat * interp[top : top + chunk, :].astype(F32)).astype(BF16))
+        return jnp.concatenate(parts, axis=1)
+
+    def add_spread(top, spread, first):
+        match = row[:, top : top + chunk] == line + first * lat_pad
+        part = jnp.dot(
+            jnp.where(match, 1.0, 0.0).astype(BF16), spread, preferred_element_type=F32
+        )
+        rows = slice(first * lat_pad, first * lat_pad + height)
+        if top > 0:
+            part = part + total[rows, :]
+        if top + chunk < slots:
+            total[rows, :] = part
+            return
+        part = part.astype(BF16)
         for level in range(mine):
-            for tile in range(tiles):
-                result[level, :, (first + tile) * LANES : (first + tile + 1) * LANES] = summed[
+            for tile in range(group):
+                result[level, :, (first + tile) * LANES : (first + tile + 1) * LANES] = part[
                     tile * lat_pad : tile * lat_pad + lat, level * LANES : (level + 1) * LANES
                 ]
-        columns = pl.ds(first * LANES, tiles * LANES)
+        columns = pl.ds(first * LANES, group * LANES)
         copies.append(
             pltpu.make_async_copy(
-                result.at[:, :, columns], out.at[:, :, columns], sems.at[first // tiles]
+                result.at[:, :, columns], out.at[:, :, columns], sems.at[first // group]
             )
         )
         copies[-1].start()
+
+    tiles = [(top, at) for top in range(0, slots, chunk) for at in range(0, sources, chunk)]
+    pending = []
+    flux = jnp.zeros((chunk, flux_rows), F32)
+    gates = gates_of(*tiles[0])
+    before = None
+    for i, (top, at) in enumerate(tiles):
+        later = gates_of(*tiles[i + 1]) if i + 1 < len(tiles) else None
+        source = softplus(gates).astype(BF16)
+        if before is not None:
+            done, place_of = tiles[i - 1]
+            flux = flux + jnp.dot(
+                before, inverses[place_of : place_of + chunk, :], preferred_element_type=F32
+            )
+            if top != done:
+                spread = spread_of(done, flux)
+                pending = [(done, spread, first) for first in range(0, across, group)]
+                flux = jnp.zeros((chunk, flux_rows), F32)
+        if pending:
+            add_spread(*pending.pop(0))
+        gates, before = later, source
+    for one in pending:
+        add_spread(*one)
+    top, at = tiles[-1]
+    flux = flux + jnp.dot(before, inverses[at : at + chunk, :], preferred_element_type=F32)
+    spread = spread_of(top, flux)
+    for first in range(0, across, group):
+        add_spread(top, spread, first)
     for copy in copies:
         copy.wait()
 
@@ -396,7 +425,7 @@
         [SMEM] + [VMEM] * 6,
         [
             pltpu.VMEM((states, slots), F32),
-            pltpu.VMEM((slots, mine * LANES), BF16),
+            pltpu.VMEM((across * lat_pad, mine * LANES), F32),
             pltpu.VMEM((mine, lat, lon), BF16),
             pltpu.SemaphoreType.DMA((across,)),
         ],

time: 33.6 us -> 34 us (1.012)
  Pallas kernels: 14.7 us -> 15.1 us
    pallas_call x5, Pallas kernels: 14.7 us -> 15.1 us  [call(): pl.pallas_call(kernel, out_shape=shapes[0] if single else shapes, in_spec...]
  transfers between devices with their start and end apart: 3 -> 3, of which waited for: 2 -> 1; matrix products, arithmetic and copies ran while one was open for 0% -> 0% of each run, Pallas kernels for 21% -> 22%
where the time goes in v13:
time: 34 us; the launch traced here: 33.6 us
  Pallas kernels  15.1 us (44%)
  starting transfers between devices  11.4 us (34%)
  waiting for transfers between devices  6.3 us (19%)
  between operations  0.76 us (2%)
    pallas_call x5, Pallas kernels, call(): pl.pallas_call(kernel, out_shape=shapes[0] if single else shapes, in_spec...  15.1 us
    all_to_all x1, starting transfers between devices, body(): arrived = lax.all_to_all(message, 'fld', 0, 0, tiled=True)  6.46 us
    all_to_all x1, waiting for transfers between devices, body(): arrived = lax.all_to_all(message, 'fld', 0, 0, tiled=True)  6.3 us
    all_to_all x1, starting transfers between devices, body(): pieces = lax.all_to_all(sent, ('sec', 'band'), 0, 0, tiled=True)  3.41 us
    ppermute x1, starting transfers between devices, body(): far = lax.ppermute(near, 'sec', [(i, 1 - i) for i in range(n_sec)])  1.56 us
  transfers between devices with their start and end apart: 3, of which 1 were waited for; matrix products, arithmetic and copies ran while one was open for 0% of the time, Pallas kernels for 22%

profile of v13, /device:TPU:0, one launch (start us, length us, event | category | flops | bytes accessed | tf_op | source)
XLA Modules:
  0.0 33.6 jit_solution(17628006299004373765)
XLA Ops:
  0.6 0.0 copy-start
  0.6 0.0 copy-start.1
  0.6 5.8 %local.1 = bf16[4,192,128]{2,1,0:T(8,128)(2,1)} custom-call(bf16[8,40,2688]{2,1,0:T(8,128)(2,1)} %bitcast.8, s32[1,1024]{1,0:T(1,128)} %bitcast.6, bf16[1024,128]{1,0:T(8,128)(2,1)} %interp.1, bf16[2688,192]{1,0:T(8,128)(2,1)} %constant.2.clone.table_hbm), custom_call_target="tpu_custom_call" | custom-call | flops 2477785088 | bytes 1982464 | tf_op jit(solution)/shard_map/local/pallas_call | solution.py:330
  6.5 0.0 copy-start.2
  6.5 0.0 copy-start.3
  6.5 0.0 copy-start.4
  6.5 0.0 copy-start.5
  6.5 6.5 %all-to-all-start = ((bf16[4,192,128]{2,1,0:T(8,128)(2,1)}), bf16[4,192,128]{2,1,0:T(8,128)(2,1)S(1)}, u32[]{:S(2)}, u32[]{:S(2)}) async-start(bf16[4,192,128]{2,1,0:T(8,128)(2,1)} %local.1), calls=%async_computation | async-start | bytes 393216 | tf_op jit(solution)/shard_map/all_to_all | solution.py:387
  13.0 0.0 copy-done
  13.0 0.0 copy-done.1
  13.0 1.2 %prepare.1 = (bf16[4,2,144,128]{3,2,1,0:T(8,128)(2,1)S(1)}, bf16[2048,32]{1,0:T(8,128)(2,1)S(1)}) custom-call(bf16[6,48,160]{2,1,0:T(8,128)(2,1)S(1)} %bitcast.5, bf16[32,32,64]{2,1,0:T(8,128)(2,1)S(1)} %bitcast.4), custom_call_target="tpu_custom_call" | custom-call | bytes 1179648 | tf_op jit(solution)/shard_map/prepare/pallas_call | solution.py:330
  14.2 6.3 %all-to-all-done.arrived = bf16[4,192,128]{2,1,0:T(8,128)(2,1)S(1)} async-done(((bf16[4,192,128]{2,1,0:T(8,128)(2,1)}), bf16[4,192,128]{2,1,0:T(8,128)(2,1)S(1)}, u32[]{:S(2)}, u32[]{:S(2)}) %all-to-all-start) | async-done | bytes 196640 | tf_op jit(solution)/shard_map/all_to_all | solution.py:387
  20.5 0.8 %regroup.1 = (bf16[8,4,32,128]{3,2,1,0:T(8,128)(2,1)}, bf16[4,64,128]{2,1,0:T(8,128)(2,1)S(1)}) custom-call(bf16[4,192,128]{2,1,0:T(8,128)(2,1)S(1)} %all-to-all-done.arrived, bf16[4,2,144,128]{3,2,1,0:T(8,128)(2,1)S(1)} %get-tuple-element.6._.weights), custom_call_target="tpu_custom_call" | custom-call | bytes 524288 | tf_op jit(solution)/shard_map/regroup/pallas_call | solution.py:330
  21.3 1.6 %collective-permute-start = (bf16[4,64,128]{2,1,0:T(8,128)(2,1)S(1)}, bf16[4,64,128]{2,1,0:T(8,128)(2,1)S(1)}, u32[]{:S(2)}, u32[]{:S(2)}) collective-permute-start(bf16[4,64,128]{2,1,0:T(8,128)(2,1)S(1)} %get-tuple-element.9.near), channel_id=1, source_target_pairs={{0,16},{16,0},{1,17},{17,1},{2,18},{18,2},{3,19},{19,3},{4,20},{20... | collective-permute-start | bytes 196616 | tf_op jit(solution)/shard_map/ppermute | solution.py:417
  22.9 3.4 %all-to-all-start.1 = ((bf16[8,4,32,128]{3,2,1,0:T(8,128)(2,1)}), bf16[8,4,32,128]{3,2,1,0:T(8,128)(2,1)S(1)}, u32[]{:S(2)}, u32[]{:S(2)}) async-start(bf16[8,4,32,128]{3,2,1,0:T(8,128)(2,1)} %get-tuple-element.7), calls=%async_computation.1 | async-start | bytes 524288 | tf_op jit(solution)/shard_map/all_to_all | solution.py:418
  26.3 0.0 collective-permute-done.far
  26.3 0.0 copy-done.2
  26.3 0.0 copy-done.3
  26.3 0.0 copy-done.4
  26.3 0.0 copy-done.5
  26.3 6.3 %columns.1 = bf16[2,40,2688]{2,1,0:T(8,128)(2,1)} custom-call(s32[4]{0:T(128)S(1)} %copy-done.5, bf16[64,2048]{1,0:T(8,128)(2,1)S(1)} %copy-done.3, bf16[2048,32]{1,0:T(8,128)(2,1)S(1)} %get-tuple-element.8.inverses, s32[1,1024]{1,0:T(1,128)S(1)} %bitcast.7, bf16[1024,128]{1,0:T(8,128)(2,1)S(1)} %copy-done.2, bf16[4,64,128]{2,1,0:T(8,128)(2,1)S(1)} %get-tuple-element.9.near, ...), custom_call_target="tpu_custom_call" | custom-call | flops 8589934592 | bytes 2097152 | tf_op jit(solution)/shard_map/columns/pallas_call | solution.py:330
  32.6 0.0 all-to-all-done.1.pieces
  32.6 1.0 %legendre.1 = bf16[6,2,4,16,48]{4,3,2,1,0:T(8,128)(2,1)} custom-call(bf16[4,2,144,128]{3,2,1,0:T(8,128)(2,1)S(1)} %get-tuple-element.6._.weights, bf16[8,4,32,128]{3,2,1,0:T(8,128)(2,1)S(1)} %all-to-all-done.1.pieces), custom_call_target="tpu_custom_call" | custom-call | flops 75497472 | bytes 262144 | tf_op jit(solution)/shard_map/legendre/pallas_call | solution.py:330
Async XLA Ops:
  0.6 12.4 %copy-start = (bf16[64,32,32]{0,2,1:T(8,128)(2,1)S(1)}, bf16[64,32,32]{0,2,1:T(8,128)(2,1)}, u32[]{:S(2)}) copy-start(bf16[64,32,32]{0,2,1:T(8,128)(2,1)} %param.14) | copy-start | bytes 393220
  0.6 12.4 %copy-start.1 = (bf16[6,160,48]{1,2,0:T(8,128)(2,1)S(1)}, bf16[6,160,48]{1,2,0:T(8,128)(2,1)}, u32[]{:S(2)}) copy-start(bf16[6,160,48]{1,2,0:T(8,128)(2,1)} %param.9) | copy-start | bytes 276484
  6.5 19.8 %copy-start.2 = (bf16[1024,128]{1,0:T(8,128)(2,1)S(1)}, bf16[1024,128]{1,0:T(8,128)(2,1)}, u32[]{:S(2)}) copy-start(bf16[1024,128]{1,0:T(8,128)(2,1)} %interp.1) | copy-start | bytes 786436
  6.5 19.8 %copy-start.3 = (bf16[64,2048]{1,0:T(8,128)(2,1)S(1)}, bf16[64,2048]{1,0:T(8,128)(2,1)}, u32[]{:S(2)}) copy-start(bf16[64,2048]{1,0:T(8,128)(2,1)} %weights.1) | copy-start | bytes 786436
  6.5 19.8 %copy-start.4 = (s32[1024]{0:T(1024)S(1)}, s32[1024]{0:T(1024)}, u32[]{:S(2)}) copy-start(s32[1024]{0:T(1024)} %param.11) | copy-start | bytes 12292
  6.5 19.8 %copy-start.5 = (s32[4]{0:T(128)S(1)}, s32[4]{0:T(128)}, u32[]{:S(2)}) copy-start(s32[4]{0:T(128)} %counts.1) | copy-start | bytes 52
  6.5 14.0 %all-to-all-start = ((bf16[4,192,128]{2,1,0:T(8,128)(2,1)}), bf16[4,192,128]{2,1,0:T(8,128)(2,1)S(1)}, u32[]{:S(2)}, u32[]{:S(2)}) async-start(bf16[4,192,128]{2,1,0:T(8,128)(2,1)} %local.1), calls=%async_computation | async-start | bytes 393216 | tf_op jit(solution)/shard_map/all_to_all | solution.py:387
  21.3 5.0 %collective-permute-start = (bf16[4,64,128]{2,1,0:T(8,128)(2,1)S(1)}, bf16[4,64,128]{2,1,0:T(8,128)(2,1)S(1)}, u32[]{:S(2)}, u32[]{:S(2)}) collective-permute-start(bf16[4,64,128]{2,1,0:T(8,128)(2,1)S(1)} %get-tuple-element.9.near), channel_id=1, source_target_pairs={{0,16},{16,0},{1,17},{17,1},{2,18},{18,2},{3,19},{19,3},{4,20},{20... | collective-permute-start | bytes 196616 | tf_op jit(solution)/shard_map/ppermute | solution.py:417
  22.9 9.7 %all-to-all-start.1 = ((bf16[8,4,32,128]{3,2,1,0:T(8,128)(2,1)}), bf16[8,4,32,128]{3,2,1,0:T(8,128)(2,1)S(1)}, u32[]{:S(2)}, u32[]{:S(2)}) async-start(bf16[8,4,32,128]{3,2,1,0:T(8,128)(2,1)} %get-tuple-element.7), calls=%async_computation.1 | async-start | bytes 524288 | tf_op jit(solution)/shard_map/all_to_all | solution.py:418

commit v14 on v9

--- a/solution.py
+++ b/solution.py
@@ -219,9 +219,15 @@
         copy.wait()
 
 
+TAIL = (0.041015625, -0.1591796875, 0.306640625, -0.49609375, 1.0)
+
+
 def softplus(x):
-    power = jnp.exp(jnp.minimum(x, 80.0))
-    return jnp.where(x < -8.0, power, jnp.maximum(x, jnp.log(1.0 + power)))
+    u = jnp.exp(-jnp.abs(x)).astype(BF16)
+    tail = u * TAIL[0] + TAIL[1]
+    for coefficient in TAIL[2:]:
+        tail = tail * u + coefficient
+    return jnp.maximum(x.astype(BF16), 0.0) + u * tail
 
 
 def column_kernel(n_sec, n_fld, lat_pad, slots, counts, weights, inverses, blocks, interp,
@@ -245,22 +251,31 @@
     lane = lax.broadcasted_iota(jnp.int32, (1, flux_rows), 1)
     slot = lax.broadcasted_iota(jnp.int32, (chunk, 1), 0)
     column = jnp.transpose(state[...]).astype(BF16)
-
-    def gates_of(source):
-        return jnp.dot(column, weights[:, source : source + chunk], preferred_element_type=F32)
-
-    flux = jnp.zeros((slots, flux_rows), F32)
-    gates = gates_of(0)
-    for source in range(0, sources, chunk):
-        later = gates_of(source + chunk) if source + chunk < sources else None
-        flux = flux + jnp.dot(
-            softplus(gates).astype(BF16),
-            inverses[source : source + chunk, :],
-            preferred_element_type=F32,
-        )
-        gates = later
+    tiles = [(top, at) for top in range(0, slots, chunk) for at in range(0, sources, chunk)]
+
+    def gates_of(top, at):
+        return jnp.dot(
+            column[top : top + chunk], weights[:, at : at + chunk], preferred_element_type=F32
+        )
+
+    fluxes = {top: jnp.zeros((chunk, flux_rows), F32) for top in range(0, slots, chunk)}
+
+    def add_flux(top, at, source):
+        fluxes[top] = fluxes[top] + jnp.dot(
+            source, inverses[at : at + chunk, :], preferred_element_type=F32
+        )
+
+    gates = gates_of(*tiles[0])
+    before = None
+    for i, tile in enumerate(tiles):
+        later = gates_of(*tiles[i + 1]) if i + 1 < len(tiles) else None
+        source = softplus(gates)
+        if before is not None:
+            add_flux(*tiles[i - 1], before)
+        gates, before = later, source
+    add_flux(*tiles[-1], before)
     for start in range(0, slots, chunk):
-        rows = flux[start : start + chunk]
+        rows = fluxes[start]
         for level in range(mine):
             at = base + level
             plus = (lane == at) | ((lane == at + levels + 1) & (at + 1 < levels))

time: 33.6 us -> 33.7 us (level)
  transfers between devices with their start and end apart: 3 -> 3, of which waited for: 2 -> 1; matrix products, arithmetic and copies ran while one was open for 0% -> 0% of each run, Pallas kernels for 21% -> 22%
where the time goes in v14:
time: 33.7 us; the launch traced here: 33.4 us
  Pallas kernels  14.8 us (44%)
  starting transfers between devices  11.4 us (34%)
  waiting for transfers between devices  6.3 us (19%)
  between operations  0.76 us (2%)
    pallas_call x5, Pallas kernels, call(): pl.pallas_call(kernel, out_shape=shapes[0] if single else shapes, in_spec...  14.8 us
    all_to_all x1, starting transfers between devices, body(): arrived = lax.all_to_all(message, 'fld', 0, 0, tiled=True)  6.46 us
    all_to_all x1, waiting for transfers between devices, body(): arrived = lax.all_to_all(message, 'fld', 0, 0, tiled=True)  6.3 us
    all_to_all x1, starting transfers between devices, body(): pieces = lax.all_to_all(sent, ('sec', 'band'), 0, 0, tiled=True)  3.41 us
    ppermute x1, starting transfers between devices, body(): far = lax.ppermute(near, 'sec', [(i, 1 - i) for i in range(n_sec)])  1.56 us
  transfers between devices with their start and end apart: 3, of which 1 were waited for; matrix products, arithmetic and copies ran while one was open for 0% of the time, Pallas kernels for 22%

profile of v14, /device:TPU:0, one launch (start us, length us, event | category | flops | bytes accessed | tf_op | source)
XLA Modules:
  0.0 33.4 jit_solution(1608403249865470036)
XLA Ops:
  0.6 0.0 copy-start
  0.6 0.0 copy-start.1
  0.6 5.8 %local.1 = bf16[4,192,128]{2,1,0:T(8,128)(2,1)} custom-call(bf16[8,40,2688]{2,1,0:T(8,128)(2,1)} %bitcast.8, s32[1,1024]{1,0:T(1,128)} %bitcast.6, bf16[1024,128]{1,0:T(8,128)(2,1)} %interp.1, bf16[2688,192]{1,0:T(8,128)(2,1)} %constant.2.clone.table_hbm), custom_call_target="tpu_custom_call" | custom-call | flops 2477785088 | bytes 1982464 | tf_op jit(solution)/shard_map/local/pallas_call | solution.py:316
  6.5 0.0 copy-start.2
  6.5 0.0 copy-start.3
  6.5 0.0 copy-start.4
  6.5 0.0 copy-start.5
  6.5 6.5 %all-to-all-start = ((bf16[4,192,128]{2,1,0:T(8,128)(2,1)}), bf16[4,192,128]{2,1,0:T(8,128)(2,1)S(1)}, u32[]{:S(2)}, u32[]{:S(2)}) async-start(bf16[4,192,128]{2,1,0:T(8,128)(2,1)} %local.1), calls=%async_computation | async-start | bytes 393216 | tf_op jit(solution)/shard_map/all_to_all | solution.py:373
  13.0 0.0 copy-done
  13.0 0.0 copy-done.1
  13.0 1.2 %prepare.1 = (bf16[4,2,144,128]{3,2,1,0:T(8,128)(2,1)S(1)}, bf16[2048,32]{1,0:T(8,128)(2,1)S(1)}) custom-call(bf16[6,48,160]{2,1,0:T(8,128)(2,1)S(1)} %bitcast.5, bf16[32,32,64]{2,1,0:T(8,128)(2,1)S(1)} %bitcast.4), custom_call_target="tpu_custom_call" | custom-call | bytes 1179648 | tf_op jit(solution)/shard_map/prepare/pallas_call | solution.py:316
  14.2 6.3 %all-to-all-done.arrived = bf16[4,192,128]{2,1,0:T(8,128)(2,1)S(1)} async-done(((bf16[4,192,128]{2,1,0:T(8,128)(2,1)}), bf16[4,192,128]{2,1,0:T(8,128)(2,1)S(1)}, u32[]{:S(2)}, u32[]{:S(2)}) %all-to-all-start) | async-done | bytes 196640 | tf_op jit(solution)/shard_map/all_to_all | solution.py:373
  20.5 0.8 %regroup.1 = (bf16[8,4,32,128]{3,2,1,0:T(8,128)(2,1)}, bf16[4,64,128]{2,1,0:T(8,128)(2,1)S(1)}) custom-call(bf16[4,192,128]{2,1,0:T(8,128)(2,1)S(1)} %all-to-all-done.arrived, bf16[4,2,144,128]{3,2,1,0:T(8,128)(2,1)S(1)} %get-tuple-element.6._.weights), custom_call_target="tpu_custom_call" | custom-call | bytes 524288 | tf_op jit(solution)/shard_map/regroup/pallas_call | solution.py:316
  21.3 1.6 %collective-permute-start = (bf16[4,64,128]{2,1,0:T(8,128)(2,1)S(1)}, bf16[4,64,128]{2,1,0:T(8,128)(2,1)S(1)}, u32[]{:S(2)}, u32[]{:S(2)}) collective-permute-start(bf16[4,64,128]{2,1,0:T(8,128)(2,1)S(1)} %get-tuple-element.9.near), channel_id=1, source_target_pairs={{0,16},{16,0},{1,17},{17,1},{2,18},{18,2},{3,19},{19,3},{4,20},{20... | collective-permute-start | bytes 196616 | tf_op jit(solution)/shard_map/ppermute | solution.py:403
  22.9 3.4 %all-to-all-start.1 = ((bf16[8,4,32,128]{3,2,1,0:T(8,128)(2,1)}), bf16[8,4,32,128]{3,2,1,0:T(8,128)(2,1)S(1)}, u32[]{:S(2)}, u32[]{:S(2)}) async-start(bf16[8,4,32,128]{3,2,1,0:T(8,128)(2,1)} %get-tuple-element.7), calls=%async_computation.1 | async-start | bytes 524288 | tf_op jit(solution)/shard_map/all_to_all | solution.py:404
  26.3 0.0 collective-permute-done.far
  26.3 0.0 copy-done.2
  26.3 0.0 copy-done.3
  26.3 0.0 copy-done.4
  26.3 0.0 copy-done.5
  26.3 6.0 %columns.1 = bf16[2,40,2688]{2,1,0:T(8,128)(2,1)} custom-call(s32[4]{0:T(128)S(1)} %copy-done.5, bf16[64,2048]{1,0:T(8,128)(2,1)S(1)} %copy-done.3, bf16[2048,32]{1,0:T(8,128)(2,1)S(1)} %get-tuple-element.8.inverses, s32[1,1024]{1,0:T(1,128)S(1)} %bitcast.7, bf16[1024,128]{1,0:T(8,128)(2,1)S(1)} %copy-done.2, bf16[4,64,128]{2,1,0:T(8,128)(2,1)S(1)} %get-tuple-element.9.near, ...), custom_call_target="tpu_custom_call" | custom-call | flops 8589934592 | bytes 2097152 | tf_op jit(solution)/shard_map/columns/pallas_call | solution.py:316
  32.3 0.0 all-to-all-done.1.pieces
  32.4 1.0 %legendre.1 = bf16[6,2,4,16,48]{4,3,2,1,0:T(8,128)(2,1)} custom-call(bf16[4,2,144,128]{3,2,1,0:T(8,128)(2,1)S(1)} %get-tuple-element.6._.weights, bf16[8,4,32,128]{3,2,1,0:T(8,128)(2,1)S(1)} %all-to-all-done.1.pieces), custom_call_target="tpu_custom_call" | custom-call | flops 75497472 | bytes 262144 | tf_op jit(solution)/shard_map/legendre/pallas_call | solution.py:316
Async XLA Ops:
  0.6 12.4 %copy-start = (bf16[64,32,32]{0,2,1:T(8,128)(2,1)S(1)}, bf16[64,32,32]{0,2,1:T(8,128)(2,1)}, u32[]{:S(2)}) copy-start(bf16[64,32,32]{0,2,1:T(8,128)(2,1)} %param.14) | copy-start | bytes 393220
  0.6 12.4 %copy-start.1 = (bf16[6,160,48]{1,2,0:T(8,128)(2,1)S(1)}, bf16[6,160,48]{1,2,0:T(8,128)(2,1)}, u32[]{:S(2)}) copy-start(bf16[6,160,48]{1,2,0:T(8,128)(2,1)} %param.9) | copy-start | bytes 276484
  6.5 19.8 %copy-start.2 = (bf16[1024,128]{1,0:T(8,128)(2,1)S(1)}, bf16[1024,128]{1,0:T(8,128)(2,1)}, u32[]{:S(2)}) copy-start(bf16[1024,128]{1,0:T(8,128)(2,1)} %interp.1) | copy-start | bytes 786436
  6.5 19.8 %copy-start.3 = (bf16[64,2048]{1,0:T(8,128)(2,1)S(1)}, bf16[64,2048]{1,0:T(8,128)(2,1)}, u32[]{:S(2)}) copy-start(bf16[64,2048]{1,0:T(8,128)(2,1)} %weights.1) | copy-start | bytes 786436
  6.5 19.8 %copy-start.4 = (s32[1024]{0:T(1024)S(1)}, s32[1024]{0:T(1024)}, u32[]{:S(2)}) copy-start(s32[1024]{0:T(1024)} %param.11) | copy-start | bytes 12292
  6.5 19.8 %copy-start.5 = (s32[4]{0:T(128)S(1)}, s32[4]{0:T(128)}, u32[]{:S(2)}) copy-start(s32[4]{0:T(128)} %counts.1) | copy-start | bytes 52
  6.5 14.0 %all-to-all-start = ((bf16[4,192,128]{2,1,0:T(8,128)(2,1)}), bf16[4,192,128]{2,1,0:T(8,128)(2,1)S(1)}, u32[]{:S(2)}, u32[]{:S(2)}) async-start(bf16[4,192,128]{2,1,0:T(8,128)(2,1)} %local.1), calls=%async_computation | async-start | bytes 393216 | tf_op jit(solution)/shard_map/all_to_all | solution.py:373
  21.3 5.0 %collective-permute-start = (bf16[4,64,128]{2,1,0:T(8,128)(2,1)S(1)}, bf16[4,64,128]{2,1,0:T(8,128)(2,1)S(1)}, u32[]{:S(2)}, u32[]{:S(2)}) collective-permute-start(bf16[4,64,128]{2,1,0:T(8,128)(2,1)S(1)} %get-tuple-element.9.near), channel_id=1, source_target_pairs={{0,16},{16,0},{1,17},{17,1},{2,18},{18,2},{3,19},{19,3},{4,20},{20... | collective-permute-start | bytes 196616 | tf_op jit(solution)/shard_map/ppermute | solution.py:403
  22.9 9.5 %all-to-all-start.1 = ((bf16[8,4,32,128]{3,2,1,0:T(8,128)(2,1)}), bf16[8,4,32,128]{3,2,1,0:T(8,128)(2,1)S(1)}, u32[]{:S(2)}, u32[]{:S(2)}) async-start(bf16[8,4,32,128]{3,2,1,0:T(8,128)(2,1)} %get-tuple-element.7), calls=%async_computation.1 | async-start | bytes 524288 | tf_op jit(solution)/shard_map/all_to_all | solution.py:404

commit v15 on v14

--- a/solution.py
+++ b/solution.py
@@ -176,21 +176,23 @@
             (pl.ds(0, first_state), pl.ds(first_state, message.shape[1] - first_state))
         )
     ]
-    for start in range(0, slots, chunk):
+    height = 512
+    lane = lax.broadcasted_iota(jnp.int32, (height, LANES), 1)
+    for start in range(0, slots, height):
         picked = jnp.dot(
-            selector[start : start + chunk, :], patch[...], preferred_element_type=F32
-        )
-        weights = interp[start : start + chunk, :].astype(F32)
-        total = jnp.zeros((chunk, LANES), F32)
+            selector[start : start + height, :], patch[...], preferred_element_type=F32
+        )
+        weights = interp[start : start + height, :].astype(F32)
+        total = jnp.zeros((height, LANES), F32)
         for level in range(lev):
             product = picked[:, level * LANES : (level + 1) * LANES] * weights
             total = jnp.where(lane == level, jnp.sum(product, axis=1, keepdims=True), total)
         state = jnp.transpose(total)[:lev].astype(BF16)
-        for tile in range(chunk // LANES):
+        for tile in range(height // LANES):
             row = first_state + (start // LANES + tile) * lev
             for target in range(message.shape[0]):
                 message[target, row : row + lev, :] = state[:, tile * LANES : (tile + 1) * LANES]
-        if start == chunk:
+        if start == 0:
             small[2].wait()
             flat = jnp.concatenate([grid[level] for level in range(lev)], axis=0)
             coeffs = jnp.dot(flat, table[...], preferred_element_type=F32)
@@ -219,15 +221,9 @@
         copy.wait()
 
 
-TAIL = (0.041015625, -0.1591796875, 0.306640625, -0.49609375, 1.0)
-
-
 def softplus(x):
-    u = jnp.exp(-jnp.abs(x)).astype(BF16)
-    tail = u * TAIL[0] + TAIL[1]
-    for coefficient in TAIL[2:]:
-        tail = tail * u + coefficient
-    return jnp.maximum(x.astype(BF16), 0.0) + u * tail
+    power = jnp.exp(jnp.minimum(x, 80.0))
+    return jnp.where(x < -8.0, power, jnp.maximum(x, jnp.log(1.0 + power)))
 
 
 def column_kernel(n_sec, n_fld, lat_pad, slots, counts, weights, inverses, blocks, interp,
@@ -247,18 +243,18 @@
     levels = flux_rows // 2
     count = counts[lax.axis_index("band")]
     base = (place * n_fld + lax.axis_index("fld")) * mine
-    chunk = 256
+    chunk, height = 256, 512
     lane = lax.broadcasted_iota(jnp.int32, (1, flux_rows), 1)
-    slot = lax.broadcasted_iota(jnp.int32, (chunk, 1), 0)
+    slot = lax.broadcasted_iota(jnp.int32, (height, 1), 0)
     column = jnp.transpose(state[...]).astype(BF16)
-    tiles = [(top, at) for top in range(0, slots, chunk) for at in range(0, sources, chunk)]
+    tiles = [(top, at) for top in range(0, slots, height) for at in range(0, sources, chunk)]
 
     def gates_of(top, at):
         return jnp.dot(
-            column[top : top + chunk], weights[:, at : at + chunk], preferred_element_type=F32
-        )
-
-    fluxes = {top: jnp.zeros((chunk, flux_rows), F32) for top in range(0, slots, chunk)}
+            column[top : top + height], weights[:, at : at + chunk], preferred_element_type=F32
+        )
+
+    fluxes = {top: jnp.zeros((height, flux_rows), F32) for top in range(0, slots, height)}
 
     def add_flux(top, at, source):
         fluxes[top] = fluxes[top] + jnp.dot(
@@ -269,12 +265,12 @@
     before = None
     for i, tile in enumerate(tiles):
         later = gates_of(*tiles[i + 1]) if i + 1 < len(tiles) else None
-        source = softplus(gates)
+        source = softplus(gates).astype(BF16)
         if before is not None:
             add_flux(*tiles[i - 1], before)
         gates, before = later, source
     add_flux(*tiles[-1], before)
-    for start in range(0, slots, chunk):
+    for start in range(0, slots, height):
         rows = fluxes[start]
         for level in range(mine):
             at = base + level
@@ -283,8 +279,8 @@
             terms = jnp.where(plus, rows, 0.0) - jnp.where(minus, rows, 0.0)
             heat = jnp.sum(terms, axis=1, keepdims=True)
             heat = jnp.where(slot + start < count, heat, 0.0).astype(BF16).astype(F32)
-            spread[start : start + chunk, level * LANES : (level + 1) * LANES] = (
-                heat * interp[start : start + chunk, :].astype(F32)
+            spread[start : start + height, level * LANES : (level + 1) * LANES] = (
+                heat * interp[start : start + height, :].astype(F32)
             ).astype(BF16)
     row = slot_rows(blocks[...], across, lat_pad)
     tiles = max(t for t in range(1, 8) if across % t == 0)

time: 33.7 us -> 33.6 us (level)
  transfers between devices with their start and end apart: 3 -> 3, of which waited for: 1 -> 2; matrix products, arithmetic and copies ran while one was open for 0% -> 0% of each run, Pallas kernels for 22% -> 21%
where the time goes in v15:
time: 33.6 us; the launch traced here: 33.3 us
  Pallas kernels  14.6 us (43%)
  starting transfers between devices  11.4 us (34%)
  waiting for transfers between devices  6.48 us (19%)
  between operations  0.76 us (2%)
    pallas_call x5, Pallas kernels, call(): pl.pallas_call(kernel, out_shape=shapes[0] if single else shapes, in_spec...  14.6 us
    all_to_all x1, starting transfers between devices, body(): arrived = lax.all_to_all(message, 'fld', 0, 0, tiled=True)  6.46 us
    all_to_all x1, waiting for transfers between devices, body(): arrived = lax.all_to_all(message, 'fld', 0, 0, tiled=True)  6.29 us
    all_to_all x1, starting transfers between devices, body(): pieces = lax.all_to_all(sent, ('sec', 'band'), 0, 0, tiled=True)  3.41 us
    ppermute x1, starting transfers between devices, body(): far = lax.ppermute(near, 'sec', [(i, 1 - i) for i in range(n_sec)])  1.56 us
  transfers between devices with their start and end apart: 3, of which 2 were waited for; matrix products, arithmetic and copies ran while one was open for 0% of the time, Pallas kernels for 21%

profile of v15, /device:TPU:0, one launch (start us, length us, event | category | flops | bytes accessed | tf_op | source)
XLA Modules:
  0.0 33.3 jit_solution(14531132768030984278)
XLA Ops:
  0.6 0.0 copy-start
  0.6 0.0 copy-start.1
  0.6 5.8 %local.1 = bf16[4,192,128]{2,1,0:T(8,128)(2,1)} custom-call(bf16[8,40,2688]{2,1,0:T(8,128)(2,1)} %bitcast.8, s32[1,1024]{1,0:T(1,128)} %bitcast.6, bf16[1024,128]{1,0:T(8,128)(2,1)} %interp.1, bf16[2688,192]{1,0:T(8,128)(2,1)} %constant.2.clone.table_hbm), custom_call_target="tpu_custom_call" | custom-call | flops 2477785088 | bytes 1982464 | tf_op jit(solution)/shard_map/local/pallas_call | solution.py:312
  6.5 0.0 copy-start.2
  6.5 0.0 copy-start.3
  6.5 0.0 copy-start.4
  6.5 0.0 copy-start.5
  6.6 6.5 %all-to-all-start = ((bf16[4,192,128]{2,1,0:T(8,128)(2,1)}), bf16[4,192,128]{2,1,0:T(8,128)(2,1)S(1)}, u32[]{:S(2)}, u32[]{:S(2)}) async-start(bf16[4,192,128]{2,1,0:T(8,128)(2,1)} %local.1), calls=%async_computation | async-start | bytes 393216 | tf_op jit(solution)/shard_map/all_to_all | solution.py:369
  13.0 0.0 copy-done
  13.0 0.0 copy-done.1
  13.0 1.2 %prepare.1 = (bf16[4,2,144,128]{3,2,1,0:T(8,128)(2,1)S(1)}, bf16[2048,32]{1,0:T(8,128)(2,1)S(1)}) custom-call(bf16[6,48,160]{2,1,0:T(8,128)(2,1)S(1)} %bitcast.5, bf16[32,32,64]{2,1,0:T(8,128)(2,1)S(1)} %bitcast.4), custom_call_target="tpu_custom_call" | custom-call | bytes 1179648 | tf_op jit(solution)/shard_map/prepare/pallas_call | solution.py:312
  14.2 6.3 %all-to-all-done.arrived = bf16[4,192,128]{2,1,0:T(8,128)(2,1)S(1)} async-done(((bf16[4,192,128]{2,1,0:T(8,128)(2,1)}), bf16[4,192,128]{2,1,0:T(8,128)(2,1)S(1)}, u32[]{:S(2)}, u32[]{:S(2)}) %all-to-all-start) | async-done | bytes 196640 | tf_op jit(solution)/shard_map/all_to_all | solution.py:369
  20.5 0.8 %regroup.1 = (bf16[8,4,32,128]{3,2,1,0:T(8,128)(2,1)}, bf16[4,64,128]{2,1,0:T(8,128)(2,1)S(1)}) custom-call(bf16[4,192,128]{2,1,0:T(8,128)(2,1)S(1)} %all-to-all-done.arrived, bf16[4,2,144,128]{3,2,1,0:T(8,128)(2,1)S(1)} %get-tuple-element.6._.weights), custom_call_target="tpu_custom_call" | custom-call | bytes 524288 | tf_op jit(solution)/shard_map/regroup/pallas_call | solution.py:312
  21.3 1.6 %collective-permute-start = (bf16[4,64,128]{2,1,0:T(8,128)(2,1)S(1)}, bf16[4,64,128]{2,1,0:T(8,128)(2,1)S(1)}, u32[]{:S(2)}, u32[]{:S(2)}) collective-permute-start(bf16[4,64,128]{2,1,0:T(8,128)(2,1)S(1)} %get-tuple-element.9.near), channel_id=1, source_target_pairs={{0,16},{16,0},{1,17},{17,1},{2,18},{18,2},{3,19},{19,3},{4,20},{20... | collective-permute-start | bytes 196616 | tf_op jit(solution)/shard_map/ppermute | solution.py:399
  22.9 3.4 %all-to-all-start.1 = ((bf16[8,4,32,128]{3,2,1,0:T(8,128)(2,1)}), bf16[8,4,32,128]{3,2,1,0:T(8,128)(2,1)S(1)}, u32[]{:S(2)}, u32[]{:S(2)}) async-start(bf16[8,4,32,128]{3,2,1,0:T(8,128)(2,1)} %get-tuple-element.7), calls=%async_computation.1 | async-start | bytes 524288 | tf_op jit(solution)/shard_map/all_to_all | solution.py:400
  26.3 0.0 collective-permute-done.far
  26.3 0.0 copy-done.2
  26.3 0.0 copy-done.3
  26.3 0.0 copy-done.4
  26.3 0.0 copy-done.5
  26.3 5.7 %columns.1 = bf16[2,40,2688]{2,1,0:T(8,128)(2,1)} custom-call(s32[4]{0:T(128)S(1)} %copy-done.5, bf16[64,2048]{1,0:T(8,128)(2,1)S(1)} %copy-done.3, bf16[2048,32]{1,0:T(8,128)(2,1)S(1)} %get-tuple-element.8.inverses, s32[1,1024]{1,0:T(1,128)S(1)} %bitcast.7, bf16[1024,128]{1,0:T(8,128)(2,1)S(1)} %copy-done.2, bf16[4,64,128]{2,1,0:T(8,128)(2,1)S(1)} %get-tuple-element.9.near, ...), custom_call_target="tpu_custom_call" | custom-call | flops 8589934592 | bytes 2097152 | tf_op jit(solution)/shard_map/columns/pallas_call | solution.py:312
  32.1 0.2 all-to-all-done.1.pieces
  32.3 1.0 %legendre.1 = bf16[6,2,4,16,48]{4,3,2,1,0:T(8,128)(2,1)} custom-call(bf16[4,2,144,128]{3,2,1,0:T(8,128)(2,1)S(1)} %get-tuple-element.6._.weights, bf16[8,4,32,128]{3,2,1,0:T(8,128)(2,1)S(1)} %all-to-all-done.1.pieces), custom_call_target="tpu_custom_call" | custom-call | flops 75497472 | bytes 262144 | tf_op jit(solution)/shard_map/legendre/pallas_call | solution.py:312
Async XLA Ops:
  0.6 12.4 %copy-start = (bf16[64,32,32]{0,2,1:T(8,128)(2,1)S(1)}, bf16[64,32,32]{0,2,1:T(8,128)(2,1)}, u32[]{:S(2)}) copy-start(bf16[64,32,32]{0,2,1:T(8,128)(2,1)} %param.14) | copy-start | bytes 393220
  0.6 12.4 %copy-start.1 = (bf16[6,160,48]{1,2,0:T(8,128)(2,1)S(1)}, bf16[6,160,48]{1,2,0:T(8,128)(2,1)}, u32[]{:S(2)}) copy-start(bf16[6,160,48]{1,2,0:T(8,128)(2,1)} %param.9) | copy-start | bytes 276484
  6.5 19.8 %copy-start.2 = (bf16[1024,128]{1,0:T(8,128)(2,1)S(1)}, bf16[1024,128]{1,0:T(8,128)(2,1)}, u32[]{:S(2)}) copy-start(bf16[1024,128]{1,0:T(8,128)(2,1)} %interp.1) | copy-start | bytes 786436
  6.5 19.8 %copy-start.3 = (bf16[64,2048]{1,0:T(8,128)(2,1)S(1)}, bf16[64,2048]{1,0:T(8,128)(2,1)}, u32[]{:S(2)}) copy-start(bf16[64,2048]{1,0:T(8,128)(2,1)} %weights.1) | copy-start | bytes 786436
  6.5 19.8 %copy-start.4 = (s32[1024]{0:T(1024)S(1)}, s32[1024]{0:T(1024)}, u32[]{:S(2)}) copy-start(s32[1024]{0:T(1024)} %param.11) | copy-start | bytes 12292
  6.5 19.8 %copy-start.5 = (s32[4]{0:T(128)S(1)}, s32[4]{0:T(128)}, u32[]{:S(2)}) copy-start(s32[4]{0:T(128)} %counts.1) | copy-start | bytes 52
  6.6 14.0 %all-to-all-start = ((bf16[4,192,128]{2,1,0:T(8,128)(2,1)}), bf16[4,192,128]{2,1,0:T(8,128)(2,1)S(1)}, u32[]{:S(2)}, u32[]{:S(2)}) async-start(bf16[4,192,128]{2,1,0:T(8,128)(2,1)} %local.1), calls=%async_computation | async-start | bytes 393216 | tf_op jit(solution)/shard_map/all_to_all | solution.py:369
  21.3 5.0 %collective-permute-start = (bf16[4,64,128]{2,1,0:T(8,128)(2,1)S(1)}, bf16[4,64,128]{2,1,0:T(8,128)(2,1)S(1)}, u32[]{:S(2)}, u32[]{:S(2)}) collective-permute-start(bf16[4,64,128]{2,1,0:T(8,128)(2,1)S(1)} %get-tuple-element.9.near), channel_id=1, source_target_pairs={{0,16},{16,0},{1,17},{17,1},{2,18},{18,2},{3,19},{19,3},{4,20},{20... | collective-permute-start | bytes 196616 | tf_op jit(solution)/shard_map/ppermute | solution.py:399
  22.9 9.4 %all-to-all-start.1 = ((bf16[8,4,32,128]{3,2,1,0:T(8,128)(2,1)}), bf16[8,4,32,128]{3,2,1,0:T(8,128)(2,1)S(1)}, u32[]{:S(2)}, u32[]{:S(2)}) async-start(bf16[8,4,32,128]{3,2,1,0:T(8,128)(2,1)} %get-tuple-element.7), calls=%async_computation.1 | async-start | bytes 524288 | tf_op jit(solution)/shard_map/all_to_all | solution.py:400

commit v16 on v11

--- a/solution.py
+++ b/solution.py
@@ -51,7 +51,15 @@
     message[:, :size, :] = rows[...].astype(BF16).reshape(targets, size, LANES)
 
 
-def prepare_kernel(lat, n_band, legendre, inverses, out, out_inverses, wide, rows, turned):
+def prepare_kernel(lat, n_band, across, legendre, inverses, blocks, out, out_inverses, onehot,
+                   wide, rows, turned):
+    lat_pad = onehot.shape[0] // across
+    row = slot_rows(blocks[...], across, lat_pad)
+    for tile in range(across):
+        line = lax.broadcasted_iota(jnp.int32, (lat_pad, blocks.shape[1]), 0) + tile * lat_pad
+        onehot[tile * lat_pad : (tile + 1) * lat_pad, :] = jnp.where(row == line, 1.0, 0.0).astype(
+            BF16
+        )
     flux_rows, _, spec_bands = inverses.shape
     for row in range(flux_rows):
         rows[row * flux_rows : (row + 1) * flux_rows, :] = inverses[row].astype(F32)
@@ -78,8 +86,9 @@
             ).astype(BF16)
 
 
-def legendre_kernel(n_sec, n_band, n_fld, lev, weights, pieces, out):
+def legendre_kernel(n_sec, n_band, n_fld, lev, weights, pieces, out_hbm, out, sems):
     degrees = out.shape[4]
+    copies = []
     half = pieces.shape[2] // 2
     for parity in range(2):
         rows = slice(parity * half, (parity + 1) * half)
@@ -110,6 +119,13 @@
                     out[2 * third + parity, real, fld] = jnp.concatenate(levels, axis=0).astype(
                         BF16
                     )
+            wave = 2 * third + parity
+            copies.append(
+                pltpu.make_async_copy(out.at[wave], out_hbm.at[wave], sems.at[wave])
+            )
+            copies[-1].start()
+    for copy in copies:
+        copy.wait()
 
 
 def slot_rows(blocks, across, lat_pad):
@@ -137,11 +153,13 @@
         )
         for level in range(lev)
     ]
+    half = lev // 2
     small[0].start()
-    for level in range(lev):
-        loads[level].start()
-        if level == 1:
-            small[1].start()
+    for copy in loads[:half]:
+        copy.start()
+    small[1].start()
+    for copy in loads[half:]:
+        copy.start()
     small[2].start()
     small[0].wait()
     row = slot_rows(blocks[...], across, lat_pad)
@@ -167,9 +185,8 @@
         )
     if depth > across * lat_pad:
         patch[across * lat_pad :, :] = jnp.zeros((depth - across * lat_pad, lev * LANES), BF16)
-    pair = 2 * LANES
-    for base in range(0, lev, 2):
-        for level in (base, base + 1):
+    for base in (0, half):
+        for level in range(base, base + half):
             loads[level].wait()
             for tile in range(across):
                 patch[
@@ -177,31 +194,37 @@
                 ] = grid[level, :, tile * LANES : (tile + 1) * LANES]
         if base == 0:
             small[1].wait()
+        else:
+            small[2].wait()
+            flat = jnp.concatenate([grid[level] for level in range(lev)], axis=0)
+            coeffs = jnp.dot(flat, table[...], preferred_element_type=F32)
+            pack(lev, lat, coeffs, message, padded, rows)
+            copies[0].start()
         for start in range(0, slots, chunk):
             top = slice(start, start + chunk)
             picked = jnp.dot(
                 selector[top, :],
-                patch[:, base * LANES : base * LANES + pair],
+                patch[:, base * LANES : (base + half) * LANES],
                 preferred_element_type=F32,
             )
             weights = interp[top, :].astype(F32)
-            values = [
-                jnp.sum(picked[:, i * LANES : (i + 1) * LANES] * weights, axis=1, keepdims=True)
-                for i in range(2)
-            ]
-            both = jnp.where(lane == base, values[0], values[1])
-            totals[top, :] = both if base == 0 else jnp.where(lane < base, totals[top, :], both)
-    small[2].wait()
-    flat = jnp.concatenate([grid[level] for level in range(lev)], axis=0)
-    coeffs = jnp.dot(flat, table[...], preferred_element_type=F32)
-    for top in range(0, slots, LANES):
-        state = jnp.transpose(totals[top : top + LANES, :])[:lev].astype(BF16)
-        row = first_state + top // LANES * lev
-        for target in range(message.shape[0]):
-            message[target, row : row + lev, :] = state
+            total = jnp.zeros((chunk, LANES), F32) if base == 0 else totals[top, :]
+            for i in range(half):
+                product = picked[:, i * LANES : (i + 1) * LANES] * weights
+                total = jnp.where(
+                    lane == base + i, jnp.sum(product, axis=1, keepdims=True), total
+                )
+            if base == 0:
+                totals[top, :] = total
+                continue
+            state = jnp.transpose(total)[:lev].astype(BF16)
+            for tile in range(chunk // LANES):
+                row = first_state + (start // LANES + tile) * lev
+                for target in range(message.shape[0]):
+                    message[target, row : row + lev, :] = state[
+                        :, tile * LANES : (tile + 1) * LANES
+                    ]
     copies[1].start()
-    pack(lev, lat, coeffs, message, padded, rows)
-    copies[0].start()
     for copy in copies:
         copy.wait()
 
@@ -229,7 +252,7 @@
     return jnp.where(x < -8.0, power, jnp.maximum(x, jnp.log(1.0 + power)))
 
 
-def column_kernel(n_sec, n_fld, lat_pad, slots, counts, weights, inverses, blocks, interp,
+def column_kernel(n_sec, n_fld, lat_pad, slots, counts, weights, inverses, onehot, interp,
                   near, far, out, state, spread, result, sems):
     lev = near.shape[1] * LANES // slots
     place = lax.axis_index("sec")
@@ -285,13 +308,11 @@
             spread[start : start + chunk, level * LANES : (level + 1) * LANES] = (
                 heat * interp[start : start + chunk, :].astype(F32)
             ).astype(BF16)
-    row = slot_rows(blocks[...], across, lat_pad)
     tiles = max(t for t in range(1, 8) if across % t == 0)
     height = tiles * lat_pad
     copies = []
     for first in range(0, across, tiles):
-        match = row == lax.broadcasted_iota(jnp.int32, (height, slots), 0) + first * lat_pad
-        left = jnp.where(match, 1.0, 0.0).astype(BF16)
+        left = onehot[first * lat_pad : first * lat_pad + height, :]
         summed = jnp.dot(left, spread[...], preferred_element_type=F32).astype(BF16)
         for level in range(mine):
             for tile in range(tiles):
@@ -371,19 +392,20 @@
     )
     arrived = lax.all_to_all(message, "fld", 0, 0, tiled=True)
     spec_bands, flux_rows, _ = inverses.shape
-    basis, inverse_rows = call(
-        functools.partial(prepare_kernel, lat, n_band),
+    basis, inverse_rows, onehot = call(
+        functools.partial(prepare_kernel, lat, n_band, across),
         [
             ((n_band, 2, THIRDS * degrees, LANES), BF16),
             ((spec_bands * flux_rows, flux_rows), BF16),
+            ((across * lat_pad, slots), BF16),
         ],
-        [VMEM, VMEM],
+        [VMEM, VMEM, VMEM],
         [
             pltpu.VMEM((degrees, (n_band * lat // LANES + 2) * LANES), F32),
             pltpu.VMEM((flux_rows * flux_rows, spec_bands), F32),
             pltpu.VMEM((spec_bands * flux_rows, flux_rows), F32),
         ],
-        (jnp.swapaxes(legendre, 1, 2), jnp.transpose(inverses, (1, 2, 0))),
+        (jnp.swapaxes(legendre, 1, 2), jnp.transpose(inverses, (1, 2, 0)), block_row),
         0,
         8 * wave_dev * degrees * n_band * LANES,
         "prepare",
@@ -414,7 +436,7 @@
             pltpu.VMEM((mine, lat, lon), BF16),
             pltpu.SemaphoreType.DMA((across,)),
         ],
-        (counts, source_weights, inverse_rows, block_row, interp, near, far),
+        (counts, source_weights, inverse_rows, onehot, interp, near, far),
         8 * slots * slots * 1024,
         2 * slots * slots,
         "columns",
@@ -425,11 +447,15 @@
         functools.partial(legendre_kernel, n_sec, n_band, n_fld, lev),
         [((wave_dev, 2, n_fld, n_sec * lev, degrees), BF16)],
         [VMEM, VMEM],
-        [],
+        [
+            pltpu.VMEM((wave_dev, 2, n_fld, n_sec * lev, degrees), BF16),
+            pltpu.SemaphoreType.DMA((wave_dev,)),
+        ],
         (basis, pieces),
         4 * n_sec * n_fld * piece * n_band * LANES * degrees * THIRDS,
         2 * n_sec * n_band * n_fld * piece * LANES,
         "legendre",
+        HBM,
     )
     return (spectral, heating)
 

time: 34.5 us -> 35.1 us (1.017)
  local copies, waits for them, and re-layouts: 0.03 us -> 2.92 us
  waiting for transfers between devices: 6.45 us -> 4.6 us
  Pallas kernels: 15.5 us -> 15 us
    unnamed x12 -> x16, local copies, waits for them, and re-layouts: 0.03 us -> 2.92 us
    all_to_all x1, waiting for transfers between devices: 6.29 us -> 4.6 us  [body(): arrived = lax.all_to_all(message, 'fld', 0, 0, tiled=True)]
    pallas_call x5, Pallas kernels: 15.5 us -> 15 us  [call(): pl.pallas_call(kernel, out_shape=shapes[0] if single else shapes, in_spec...]
  transfers between devices with their start and end apart: 3 -> 3, of which waited for: 2 -> 1; matrix products, arithmetic and copies ran while one was open for 0% -> 0% of each run, Pallas kernels for 20% -> 21%
where the time goes in v16:
time: 35.1 us; the launch traced here: 34.7 us
  Pallas kernels  15 us (43%)
  starting transfers between devices  11.4 us (32%)
  waiting for transfers between devices  4.6 us (13%)
  local copies, waits for them, and re-layouts  2.92 us (8%)
  between operations  0.78 us (2%)
    pallas_call x5, Pallas kernels, call(): pl.pallas_call(kernel, out_shape=shapes[0] if single else shapes, in_spec...  15 us
    all_to_all x1, starting transfers between devices, body(): arrived = lax.all_to_all(message, 'fld', 0, 0, tiled=True)  6.46 us
    all_to_all x1, waiting for transfers between devices, body(): arrived = lax.all_to_all(message, 'fld', 0, 0, tiled=True)  4.6 us
    all_to_all x1, starting transfers between devices, body(): pieces = lax.all_to_all(sent, ('sec', 'band'), 0, 0, tiled=True)  3.41 us
    unnamed x16, local copies, waits for them, and re-layouts  2.92 us
    ppermute x1, starting transfers between devices, body(): far = lax.ppermute(near, 'sec', [(i, 1 - i) for i in range(n_sec)])  1.55 us
  transfers between devices with their start and end apart: 3, of which 1 were waited for; matrix products, arithmetic and copies ran while one was open for 0% of the time, Pallas kernels for 21%

profile of v16, /device:TPU:0, one launch (start us, length us, event | category | flops | bytes accessed | tf_op | source)
XLA Modules:
  0.0 34.7 jit_solution(11459854348989365304)
XLA Ops:
  0.6 0.0 copy-start
  0.6 0.0 copy-start.1
  0.7 0.0 copy-start.2
  0.7 5.8 %local.1 = bf16[4,192,128]{2,1,0:T(8,128)(2,1)} custom-call(bf16[8,40,2688]{2,1,0:T(8,128)(2,1)} %bitcast.8, s32[1,1024]{1,0:T(1,128)} %bitcast.6, bf16[1024,128]{1,0:T(8,128)(2,1)} %interp.1, bf16[2688,192]{1,0:T(8,128)(2,1)} %constant.2.clone.table_hbm), custom_call_target="tpu_custom_call" | custom-call | flops 2477785088 | bytes 1982464 | tf_op jit(solution)/shard_map/local/pallas_call | solution.py:336
  6.5 0.0 copy-start.5
  6.5 0.0 copy-start.6
  6.5 0.0 copy-start.7
  6.5 6.5 %all-to-all-start = ((bf16[4,192,128]{2,1,0:T(8,128)(2,1)}), bf16[4,192,128]{2,1,0:T(8,128)(2,1)S(1)}, u32[]{:S(2)}, u32[]{:S(2)}) async-start(bf16[4,192,128]{2,1,0:T(8,128)(2,1)} %local.1), calls=%async_computation | async-start | bytes 393216 | tf_op jit(solution)/shard_map/all_to_all | solution.py:393
  13.0 0.0 copy-done
  13.0 0.0 copy-done.1
  13.0 0.0 copy-done.2
  13.0 1.6 %prepare.1 = (bf16[4,2,144,128]{3,2,1,0:T(8,128)(2,1)S(1)}, bf16[2048,32]{1,0:T(8,128)(2,1)S(1)}, bf16[1008,1024]{1,0:T(8,128)(2,1)S(1)}) custom-call(bf16[6,48,160]{2,1,0:T(8,128)(2,1)S(1)} %bitcast.5, bf16[32,32,64]{2,1,0:T(8,128)(2,1)S(1)} %bitcast.4, s32[1,1024]{1,0:T(1,128)S(1)} %bitcast.7), custom_call_target="tpu_custom_call" | custom-call | bytes 1179648 | tf_op jit(solution)/shard_map/prepare/pallas_call | solution.py:336
  14.6 0.0 copy-start.3
  14.6 1.3 %copy-done.3 = bf16[1008,1024]{1,0:T(8,128)(2,1)} copy-done((bf16[1008,1024]{1,0:T(8,128)(2,1)}, bf16[1008,1024]{1,0:T(8,128)(2,1)S(1)}, u32[]{:S(2)}) %copy-start.3) | copy-done | bytes 2064408
  15.9 4.6 %all-to-all-done.arrived = bf16[4,192,128]{2,1,0:T(8,128)(2,1)S(1)} async-done(((bf16[4,192,128]{2,1,0:T(8,128)(2,1)}), bf16[4,192,128]{2,1,0:T(8,128)(2,1)S(1)}, u32[]{:S(2)}, u32[]{:S(2)}) %all-to-all-start) | async-done | bytes 196640 | tf_op jit(solution)/shard_map/all_to_all | solution.py:393
  20.5 0.8 %regroup.1 = (bf16[8,4,32,128]{3,2,1,0:T(8,128)(2,1)}, bf16[4,64,128]{2,1,0:T(8,128)(2,1)S(1)}) custom-call(bf16[4,192,128]{2,1,0:T(8,128)(2,1)S(1)} %all-to-all-done.arrived, bf16[4,2,144,128]{3,2,1,0:T(8,128)(2,1)S(1)} %get-tuple-element.7._.weights), custom_call_target="tpu_custom_call" | custom-call | bytes 524288 | tf_op jit(solution)/shard_map/regroup/pallas_call | solution.py:336
  21.3 1.6 %collective-permute-start = (bf16[4,64,128]{2,1,0:T(8,128)(2,1)S(1)}, bf16[4,64,128]{2,1,0:T(8,128)(2,1)S(1)}, u32[]{:S(2)}, u32[]{:S(2)}) collective-permute-start(bf16[4,64,128]{2,1,0:T(8,128)(2,1)S(1)} %get-tuple-element.11.near), channel_id=1, source_target_pairs={{0,16},{16,0},{1,17},{17,1},{2,18},{18,2},{3,19},{19,3},{4,20},{20... | collective-permute-start | bytes 196616 | tf_op jit(solution)/shard_map/ppermute | solution.py:424
  22.9 3.4 %all-to-all-start.1 = ((bf16[8,4,32,128]{3,2,1,0:T(8,128)(2,1)}), bf16[8,4,32,128]{3,2,1,0:T(8,128)(2,1)S(1)}, u32[]{:S(2)}, u32[]{:S(2)}) async-start(bf16[8,4,32,128]{3,2,1,0:T(8,128)(2,1)} %get-tuple-element.8), calls=%async_computation.1 | async-start | bytes 524288 | tf_op jit(solution)/shard_map/all_to_all | solution.py:425
  26.3 0.0 collective-permute-done.far
  26.3 0.0 copy-done.5
  26.3 1.6 %copy-done.4 = bf16[1008,1024]{1,0:T(8,128)(2,1)S(1)} copy-done((bf16[1008,1024]{1,0:T(8,128)(2,1)S(1)}, bf16[1008,1024]{1,0:T(8,128)(2,1)}, u32[]{:S(2)}) %copy-start.4) | copy-done | bytes 2064408
  27.9 5.8 %columns.1 = bf16[2,40,2688]{2,1,0:T(8,128)(2,1)} custom-call(s32[4]{0:T(128)S(1)} %copy-done.7, bf16[64,2048]{1,0:T(8,128)(2,1)S(1)} %copy-done.6, bf16[2048,32]{1,0:T(8,128)(2,1)S(1)} %get-tuple-element.9.inverses, bf16[1008,1024]{1,0:T(8,128)(2,1)S(1)} %copy-done.4, bf16[1024,128]{1,0:T(8,128)(2,1)S(1)} %copy-done.5, ...), custom_call_target="tpu_custom_call" | custom-call | flops 8589934592 | bytes 2097152 | tf_op jit(solution)/shard_map/columns/pallas_call | solution.py:336
  33.7 0.0 all-to-all-done.1.pieces
  33.7 1.0 %legendre.1 = bf16[6,2,4,16,48]{4,3,2,1,0:T(8,128)(2,1)} custom-call(bf16[4,2,144,128]{3,2,1,0:T(8,128)(2,1)S(1)} %get-tuple-element.7._.weights, bf16[8,4,32,128]{3,2,1,0:T(8,128)(2,1)S(1)} %all-to-all-done.1.pieces), custom_call_target="tpu_custom_call" | custom-call | flops 75497472 | bytes 262144 | tf_op jit(solution)/shard_map/legendre/pallas_call | solution.py:336
  (3 shorter events, 0.0 us)
Async XLA Ops:
  0.6 12.4 %copy-start = (bf16[64,32,32]{0,2,1:T(8,128)(2,1)S(1)}, bf16[64,32,32]{0,2,1:T(8,128)(2,1)}, u32[]{:S(2)}) copy-start(bf16[64,32,32]{0,2,1:T(8,128)(2,1)} %param.14) | copy-start | bytes 393220
  0.6 12.4 %copy-start.1 = (bf16[6,160,48]{1,2,0:T(8,128)(2,1)S(1)}, bf16[6,160,48]{1,2,0:T(8,128)(2,1)}, u32[]{:S(2)}) copy-start(bf16[6,160,48]{1,2,0:T(8,128)(2,1)} %param.9) | copy-start | bytes 276484
  0.7 12.4 %copy-start.2 = (s32[1024]{0:T(1024)S(1)}, s32[1024]{0:T(1024)}, u32[]{:S(2)}) copy-start(s32[1024]{0:T(1024)} %param.11) | copy-start | bytes 12292
  6.5 19.8 %copy-start.5 = (bf16[1024,128]{1,0:T(8,128)(2,1)S(1)}, bf16[1024,128]{1,0:T(8,128)(2,1)}, u32[]{:S(2)}) copy-start(bf16[1024,128]{1,0:T(8,128)(2,1)} %interp.1) | copy-start | bytes 786436
  6.5 19.8 %copy-start.6 = (bf16[64,2048]{1,0:T(8,128)(2,1)S(1)}, bf16[64,2048]{1,0:T(8,128)(2,1)}, u32[]{:S(2)}) copy-start(bf16[64,2048]{1,0:T(8,128)(2,1)} %weights.1) | copy-start | bytes 786436
  6.5 19.8 %copy-start.7 = (s32[4]{0:T(128)S(1)}, s32[4]{0:T(128)}, u32[]{:S(2)}) copy-start(s32[4]{0:T(128)} %counts.1) | copy-start | bytes 52
  6.5 14.0 %all-to-all-start = ((bf16[4,192,128]{2,1,0:T(8,128)(2,1)}), bf16[4,192,128]{2,1,0:T(8,128)(2,1)S(1)}, u32[]{:S(2)}, u32[]{:S(2)}) async-start(bf16[4,192,128]{2,1,0:T(8,128)(2,1)} %local.1), calls=%async_computation | async-start | bytes 393216 | tf_op jit(solution)/shard_map/all_to_all | solution.py:393
  14.6 1.3 %copy-start.3 = (bf16[1008,1024]{1,0:T(8,128)(2,1)}, bf16[1008,1024]{1,0:T(8,128)(2,1)S(1)}, u32[]{:S(2)}) copy-start(bf16[1008,1024]{1,0:T(8,128)(2,1)S(1)} %get-tuple-element.10.onehot) | copy-start | bytes 6193156
  21.3 5.0 %collective-permute-start = (bf16[4,64,128]{2,1,0:T(8,128)(2,1)S(1)}, bf16[4,64,128]{2,1,0:T(8,128)(2,1)S(1)}, u32[]{:S(2)}, u32[]{:S(2)}) collective-permute-start(bf16[4,64,128]{2,1,0:T(8,128)(2,1)S(1)} %get-tuple-element.11.near), channel_id=1, source_target_pairs={{0,16},{16,0},{1,17},{17,1},{2,18},{18,2},{3,19},{19,3},{4,20},{20... | collective-permute-start | bytes 196616 | tf_op jit(solution)/shard_map/ppermute | solution.py:424
  22.9 10.8 %all-to-all-start.1 = ((bf16[8,4,32,128]{3,2,1,0:T(8,128)(2,1)}), bf16[8,4,32,128]{3,2,1,0:T(8,128)(2,1)S(1)}, u32[]{:S(2)}, u32[]{:S(2)}) async-start(bf16[8,4,32,128]{3,2,1,0:T(8,128)(2,1)} %get-tuple-element.8), calls=%async_computation.1 | async-start | bytes 524288 | tf_op jit(solution)/shard_map/all_to_all | solution.py:425
  26.3 1.6 %copy-start.4 = (bf16[1008,1024]{1,0:T(8,128)(2,1)S(1)}, bf16[1008,1024]{1,0:T(8,128)(2,1)}, u32[]{:S(2)}) copy-start(bf16[1008,1024]{1,0:T(8,128)(2,1)} %copy-done.3) | copy-start | bytes 6193156

commit v17 on v16

--- a/solution.py
+++ b/solution.py
@@ -17,6 +17,7 @@
 HBM = pl.BlockSpec(memory_space=pltpu.HBM)
 SMEM = pl.BlockSpec(memory_space=pltpu.SMEM)
 LIMIT = 40 * 1024 * 1024
+SMALL = 4 * 1024 * 1024
 ROOM = 1200 * 1024
 WHOLE = 64 * 1024 * 1024 - ROOM
 NT = (((1,), (1,)), ((), ()))
@@ -46,20 +47,12 @@
                 level * lat : (level + 1) * lat, third * group : (third + 1) * group
             ]
         rows[pl.ds(level, group, stride=lev), :] = jnp.transpose(padded[...])[:group]
-    targets = message.shape[0]
-    size = rows.shape[0] // targets
-    message[:, :size, :] = rows[...].astype(BF16).reshape(targets, size, LANES)
-
-
-def prepare_kernel(lat, n_band, across, legendre, inverses, blocks, out, out_inverses, onehot,
-                   wide, rows, turned):
-    lat_pad = onehot.shape[0] // across
-    row = slot_rows(blocks[...], across, lat_pad)
-    for tile in range(across):
-        line = lax.broadcasted_iota(jnp.int32, (lat_pad, blocks.shape[1]), 0) + tile * lat_pad
-        onehot[tile * lat_pad : (tile + 1) * lat_pad, :] = jnp.where(row == line, 1.0, 0.0).astype(
-            BF16
-        )
+    targets, size = message.shape[0], message.shape[2]
+    bands = rows.shape[0] // targets // size
+    message[:, :bands] = rows[...].astype(BF16).reshape(targets, bands, size, LANES)
+
+
+def prepare_kernel(lat, n_band, legendre, inverses, out, out_inverses, wide, rows, turned):
     flux_rows, _, spec_bands = inverses.shape
     for row in range(flux_rows):
         rows[row * flux_rows : (row + 1) * flux_rows, :] = inverses[row].astype(F32)
@@ -135,9 +128,11 @@
     return (blocks - lat * across) * lat_pad + lat
 
 
-def local_kernel(lat_pad, grid_hbm, blocks_hbm, interp_hbm, table_hbm, out,
-                 grid, blocks, interp, table, patch, column, selector, message, padded, rows,
-                 totals, sems, send):
+def local_kernel(lat_pad, grid_hbm, blocks_hbm, interp_hbm, table_hbm, *refs):
+    targets = len(refs) - 14
+    outs = refs[:targets]
+    (grid, blocks, interp, table, patch, column, selector, message, padded, rows, totals, sems,
+     send_fourier, send_state) = refs[targets:]
     lev, lat, lon = grid.shape
     across = lon // LANES
     slots = interp.shape[0]
@@ -172,13 +167,24 @@
             selector[start : start + chunk, base : base + LANES] = jnp.where(
                 mine == lane + base, 1.0, 0.0
             ).astype(BF16)
-    first_state = message.shape[1] - slots // LANES * lev
-    copies = [
-        pltpu.make_async_copy(message.at[:, rows_of, :], out.at[:, rows_of, :], send.at[i])
-        for i, rows_of in enumerate(
-            (pl.ds(0, first_state), pl.ds(first_state, message.shape[1] - first_state))
-        )
-    ]
+    state_blocks = slots * lev // LANES // message.shape[2]
+    bands = message.shape[1] - state_blocks
+    place = lax.axis_index("fld")
+    fourier_copies, state_copies = [], []
+    for shift in reversed(range(targets)):
+        mine = message.at[place ^ shift]
+        fourier_copies.append(
+            pltpu.make_async_copy(
+                mine.at[pl.ds(0, bands)], outs[shift].at[pl.ds(0, bands)], send_fourier.at[shift]
+            )
+        )
+        state_copies.append(
+            pltpu.make_async_copy(
+                mine.at[pl.ds(bands, state_blocks)],
+                outs[shift].at[pl.ds(bands, state_blocks)],
+                send_state.at[shift],
+            )
+        )
     for tile in range(across):
         patch[tile * lat_pad + lat : (tile + 1) * lat_pad, :] = jnp.zeros(
             (lat_pad - lat, lev * LANES), BF16
@@ -199,7 +205,8 @@
             flat = jnp.concatenate([grid[level] for level in range(lev)], axis=0)
             coeffs = jnp.dot(flat, table[...], preferred_element_type=F32)
             pack(lev, lat, coeffs, message, padded, rows)
-            copies[0].start()
+            for copy in fourier_copies:
+                copy.start()
         for start in range(0, slots, chunk):
             top = slice(start, start + chunk)
             picked = jnp.dot(
@@ -219,28 +226,30 @@
                 continue
             state = jnp.transpose(total)[:lev].astype(BF16)
             for tile in range(chunk // LANES):
-                row = first_state + (start // LANES + tile) * lev
-                for target in range(message.shape[0]):
-                    message[target, row : row + lev, :] = state[
+                block, row = divmod((start // LANES + tile) * lev, message.shape[2])
+                for target in range(targets):
+                    message[target, bands + block, row : row + lev, :] = state[
                         :, tile * LANES : (tile + 1) * LANES
                     ]
-    copies[1].start()
-    for copy in copies:
+    for copy in state_copies:
+        copy.start()
+    for copy in fourier_copies + state_copies:
         copy.wait()
 
 
-def regroup_kernel(n_band, arrived, _, out, out_state, sems):
-    size = out.shape[2]
+def regroup_kernel(n_sec, n_band, *refs):
+    pieces, (_, out, out_state, sems) = refs[:-4], refs[-4:]
+    blocks = out_state.shape[1]
+    place = lax.axis_index("fld")
     copies = []
-    for target in range(out.shape[0]):
-        rows = pl.ds(target % n_band * size, size)
-        copies.append(
-            pltpu.make_async_copy(arrived.at[:, rows, :], out.at[target], sems.at[target])
-        )
-    rows = pl.ds(n_band * size, out_state.shape[1])
-    copies.append(
-        pltpu.make_async_copy(arrived.at[:, rows, :], out_state, sems.at[out.shape[0]])
-    )
+    for shift, piece in enumerate(pieces):
+        fld = place ^ shift
+        copies.append((piece.at[pl.ds(n_band, blocks)], out_state.at[fld]))
+        for sec in range(n_sec):
+            copies.append(
+                (piece.at[pl.ds(0, n_band)], out.at[pl.ds(sec * n_band, n_band), fld])
+            )
+    copies = [pltpu.make_async_copy(*pair, sems.at[i]) for i, pair in enumerate(copies)]
     for copy in copies:
         copy.start()
     for copy in copies:
@@ -252,9 +261,9 @@
     return jnp.where(x < -8.0, power, jnp.maximum(x, jnp.log(1.0 + power)))
 
 
-def column_kernel(n_sec, n_fld, lat_pad, slots, counts, weights, inverses, onehot, interp,
+def column_kernel(n_sec, n_fld, lat_pad, slots, counts, weights, inverses, blocks, interp,
                   near, far, out, state, spread, result, sems):
-    lev = near.shape[1] * LANES // slots
+    lev = near.shape[1] * near.shape[2] * LANES // slots
     place = lax.axis_index("sec")
     for fld in range(n_fld):
         for shift, pieces in enumerate((near, far)):
@@ -262,7 +271,9 @@
             for tile in range(slots // LANES):
                 state[
                     pl.ds(pl.multiple_of(row, lev), lev), tile * LANES : (tile + 1) * LANES
-                ] = pieces[fld, tile * lev : (tile + 1) * lev, :].astype(F32)
+                ] = pieces[fld, tile * lev // near.shape[2]][
+                    tile * lev % near.shape[2] : tile * lev % near.shape[2] + lev
+                ].astype(F32)
     mine, lat, lon = result.shape
     across = lon // LANES
     sources, flux_rows = inverses.shape
@@ -308,11 +319,13 @@
             spread[start : start + chunk, level * LANES : (level + 1) * LANES] = (
                 heat * interp[start : start + chunk, :].astype(F32)
             ).astype(BF16)
+    row = slot_rows(blocks[...], across, lat_pad)
     tiles = max(t for t in range(1, 8) if across % t == 0)
     height = tiles * lat_pad
     copies = []
     for first in range(0, across, tiles):
-        left = onehot[first * lat_pad : first * lat_pad + height, :]
+        match = row == lax.broadcasted_iota(jnp.int32, (height, slots), 0) + first * lat_pad
+        left = jnp.where(match, 1.0, 0.0).astype(BF16)
         summed = jnp.dot(left, spread[...], preferred_element_type=F32).astype(BF16)
         for level in range(mine):
             for tile in range(tiles):
@@ -345,6 +358,10 @@
     )(*args)
 
 
+def exchange(value, axis, shift):
+    return lax.ppermute(value, axis, [(i, i ^ shift) for i in range(lax.axis_size(axis))])
+
+
 def body(grid, legendre, counts, blocks, interp, source_weights, inverses):
     n_sec = lax.axis_size("sec")
     n_band = lax.axis_size("band")
@@ -362,11 +379,11 @@
     group = n_fld * n_band * rest
     padded_group = -(-group // LANES) * LANES
     depth = -(-across * lat_pad // LANES) * LANES
-    state_rows = slots * lev // LANES
-    message_rows = n_band * piece + state_rows
-    message = call(
+    state_blocks = slots * lev // LANES // piece
+    message_blocks = n_band + state_blocks
+    messages = call(
         functools.partial(local_kernel, lat_pad),
-        [((n_fld, message_rows, LANES), BF16)],
+        [((message_blocks, piece, LANES), BF16)] * n_fld,
         [HBM] * 4,
         [
             pltpu.VMEM((lev, lat, lon), BF16),
@@ -376,12 +393,13 @@
             pltpu.VMEM((depth, lev * LANES), BF16),
             pltpu.VMEM((slots, LANES), jnp.int32),
             pltpu.VMEM((slots, depth), BF16),
-            pltpu.VMEM((n_fld, message_rows, LANES), BF16),
+            pltpu.VMEM((n_fld, message_blocks, piece, LANES), BF16),
             pltpu.VMEM((LANES, padded_group), F32),
             pltpu.VMEM((group * lev, LANES), F32),
             pltpu.VMEM((slots, LANES), F32),
             pltpu.SemaphoreType.DMA((lev + 3,)),
-            pltpu.SemaphoreType.DMA((2,)),
+            pltpu.SemaphoreType.DMA((n_fld,)),
+            pltpu.SemaphoreType.DMA((n_fld,)),
         ],
         (grid.reshape(lev, lat, lon), block_row, interp, table),
         2 * slots * depth * lev * LANES + 2 * lev * lat * lon * THIRDS * group,
@@ -390,38 +408,43 @@
         HBM,
         WHOLE,
     )
-    arrived = lax.all_to_all(message, "fld", 0, 0, tiled=True)
+    arrived = [messages[0]] + [None] * (n_fld - 1)
+    for shift in reversed(range(1, n_fld)):
+        arrived[shift] = exchange(messages[shift], "fld", shift)
     spec_bands, flux_rows, _ = inverses.shape
-    basis, inverse_rows, onehot = call(
-        functools.partial(prepare_kernel, lat, n_band, across),
+    basis, inverse_rows = call(
+        functools.partial(prepare_kernel, lat, n_band),
         [
             ((n_band, 2, THIRDS * degrees, LANES), BF16),
             ((spec_bands * flux_rows, flux_rows), BF16),
-            ((across * lat_pad, slots), BF16),
         ],
-        [VMEM, VMEM, VMEM],
+        [VMEM, VMEM],
         [
             pltpu.VMEM((degrees, (n_band * lat // LANES + 2) * LANES), F32),
             pltpu.VMEM((flux_rows * flux_rows, spec_bands), F32),
             pltpu.VMEM((spec_bands * flux_rows, flux_rows), F32),
         ],
-        (jnp.swapaxes(legendre, 1, 2), jnp.transpose(inverses, (1, 2, 0)), block_row),
+        (jnp.swapaxes(legendre, 1, 2), jnp.transpose(inverses, (1, 2, 0))),
         0,
         8 * wave_dev * degrees * n_band * LANES,
         "prepare",
     )
     sent, near = call(
-        functools.partial(regroup_kernel, n_band),
-        [((n_sec * n_band, n_fld, piece, LANES), BF16), ((n_fld, state_rows, LANES), BF16)],
-        [HBM, HBM],
-        [pltpu.SemaphoreType.DMA((n_sec * n_band + 1,))],
-        (arrived, basis),
+        functools.partial(regroup_kernel, n_sec, n_band),
+        [
+            ((n_sec * n_band, n_fld, piece, LANES), BF16),
+            ((n_fld, state_blocks, piece, LANES), BF16),
+        ],
+        [HBM] * (n_fld + 1),
+        [pltpu.SemaphoreType.DMA((n_fld * (1 + n_sec),))],
+        (*arrived, basis),
         0,
         4 * n_sec * n_band * n_fld * piece * LANES,
         "regroup",
         HBM,
-    )
-    far = lax.ppermute(near, "sec", [(i, 1 - i) for i in range(n_sec)])
+        SMALL,
+    )
+    far = exchange(near, "sec", 1)
     pieces = lax.all_to_all(sent, ("sec", "band"), 0, 0, tiled=True)
     sources = spec_bands * flux_rows
     states = source_weights.shape[0]
@@ -436,7 +459,7 @@
             pltpu.VMEM((mine, lat, lon), BF16),
             pltpu.SemaphoreType.DMA((across,)),
         ],
-        (counts, source_weights, inverse_rows, onehot, interp, near, far),
+        (counts, source_weights, inverse_rows, block_row, interp, near, far),
         8 * slots * slots * 1024,
         2 * slots * slots,
         "columns",

time: 35.1 us -> 32.3 us (0.920)
  local copies, waits for them, and re-layouts: 2.92 us -> 0.82 us
  starting transfers between devices: 11.4 us -> 10.6 us
  waiting for transfers between devices: 4.6 us -> 5.07 us
    all_to_all x1 -> x0, starting transfers between devices: 6.46 us -> none  [body(): arrived = lax.all_to_all(message, 'fld', 0, 0, tiled=True)]
    ppermute x1 -> x4, starting transfers between devices: 1.55 us -> 7.24 us  [exchange(): lax.ppermute(value, axis, [(i, i ^ shift) for i in range(lax.axis_size(ax...]
    ppermute x1 -> x4, waiting for transfers between devices: 0.01 us -> 4.87 us  [exchange(): lax.ppermute(value, axis, [(i, i ^ shift) for i in range(lax.axis_size(ax...]
    all_to_all x1 -> x0, waiting for transfers between devices: 4.6 us -> none  [body(): arrived = lax.all_to_all(message, 'fld', 0, 0, tiled=True)]
    unnamed x16 -> x14, local copies, waits for them, and re-layouts: 2.92 us -> 0.82 us
  transfers between devices with their start and end apart: 3 -> 5, of which waited for: 1 -> 3; matrix products, arithmetic and copies ran while one was open for 0% -> 0% of each run, Pallas kernels for 21% -> 22%
where the time goes in v17:
time: 32.3 us; the launch traced here: 32 us
  Pallas kernels  14.7 us (46%)
  starting transfers between devices  10.6 us (33%)
  waiting for transfers between devices  5.07 us (16%)
  local copies, waits for them, and re-layouts  0.82 us (3%)
  between operations  0.77 us (2%)
    pallas_call x5, Pallas kernels, call(): pl.pallas_call(kernel, out_shape=shapes[0] if single else shapes, in_spec...  14.7 us
    ppermute x4, starting transfers between devices, exchange(): lax.ppermute(value, axis, [(i, i ^ shift) for i in range(lax.axis_size(ax...  7.24 us
    ppermute x4, waiting for transfers between devices, exchange(): lax.ppermute(value, axis, [(i, i ^ shift) for i in range(lax.axis_size(ax...  4.87 us
    all_to_all x1, starting transfers between devices, body(): pieces = lax.all_to_all(sent, ('sec', 'band'), 0, 0, tiled=True)  3.41 us
    unnamed x14, local copies, waits for them, and re-layouts  0.82 us
  transfers between devices with their start and end apart: 5, of which 3 were waited for; matrix products, arithmetic and copies ran while one was open for 0% of the time, Pallas kernels for 22%

profile of v17, /device:TPU:0, one launch (start us, length us, event | category | flops | bytes accessed | tf_op | source)
XLA Modules:
  0.0 32.0 jit_solution(14874618871219888423)
XLA Ops:
  0.6 0.0 copy-start
  0.6 0.0 copy-start.1
  0.7 0.0 copy-start.3
  0.7 0.0 copy-start.4
  0.7 0.0 copy-start.5
  0.7 0.0 copy-start.6
  0.7 5.9 %local.1 = (bf16[6,32,128]{2,1,0:T(8,128)(2,1)}, bf16[6,32,128]{2,1,0:T(8,128)(2,1)}, bf16[6,32,128]{2,1,0:T(8,128)(2,1)}, bf16[6,32,128]{2,1,0:T(8,128)(2,1)}) custom-call(bf16[8,40,2688]{2,1,0:T(8,128)(2,1)} %bitcast.8, s32[1,1024]{1,0:T(1,128)} %bitcast.6, bf16[1024,128]{1,0:T(8,128)(2,1)} %interp.1, bf16[2688,192]{1,0:T(8,128)(2,1)} %constant.2.clone.table_hbm), custom_call_target="tpu_custom_call" | custom-call | flops 2477785088 | bytes 1982464 | tf_op jit(solution)/shard_map/local/pallas_call | solution.py:349
  6.6 3.1 %collective-permute-start = (bf16[6,32,128]{2,1,0:T(8,128)(2,1)}, bf16[6,32,128]{2,1,0:T(8,128)(2,1)S(1)}, u32[]{:S(2)}, u32[]{:S(2)}) collective-permute-start(bf16[6,32,128]{2,1,0:T(8,128)(2,1)} %get-tuple-element.12), channel_id=1, source_target_pairs={{0,1},{1,0},{2,3},{3,2},{4,5},{5,4},{6,7},{7,6},{8,9},{9,8},{10,11... | collective-permute-start | bytes 147464 | tf_op jit(solution)/shard_map/ppermute | solution.py:362
  9.7 2.6 %collective-permute-start.1 = (bf16[6,32,128]{2,1,0:T(8,128)(2,1)}, bf16[6,32,128]{2,1,0:T(8,128)(2,1)S(1)}, u32[]{:S(2)}, u32[]{:S(2)}) collective-permute-start(bf16[6,32,128]{2,1,0:T(8,128)(2,1)} %get-tuple-element.13), channel_id=1, source_target_pairs={{0,2},{1,3},{2,0},{3,1},{4,6},{5,7},{6,4},{7,5},{8,10},{9,11},{10,... | collective-permute-start | bytes 147464 | tf_op jit(solution)/shard_map/ppermute | solution.py:362
  12.3 0.0 collective-permute-start.2
  12.3 0.0 copy-done
  12.3 0.0 copy-done.1
  12.3 1.2 %prepare.1 = (bf16[4,2,144,128]{3,2,1,0:T(8,128)(2,1)S(1)}, bf16[2048,32]{1,0:T(8,128)(2,1)S(1)}) custom-call(bf16[6,48,160]{2,1,0:T(8,128)(2,1)S(1)} %bitcast.5, bf16[32,32,64]{2,1,0:T(8,128)(2,1)S(1)} %bitcast.4), custom_call_target="tpu_custom_call" | custom-call | bytes 1179648 | tf_op jit(solution)/shard_map/prepare/pallas_call | solution.py:349
  13.5 0.0 collective-permute-done.refs_1_
  13.5 2.3 %collective-permute-done.1.refs_2_ = bf16[6,32,128]{2,1,0:T(8,128)(2,1)S(1)} collective-permute-done((bf16[6,32,128]{2,1,0:T(8,128)(2,1)}, bf16[6,32,128]{2,1,0:T(8,128)(2,1)S(1)}, u32[]{:S(2)}, u32[]{:S(2)}) %collective-permute-start.1) | collective-permute-done | bytes 49184 | tf_op jit(solution)/shard_map/ppermute | solution.py:362
  15.8 2.6 %collective-permute-done.2.refs_3_ = bf16[6,32,128]{2,1,0:T(8,128)(2,1)S(1)} collective-permute-done((bf16[6,32,128]{2,1,0:T(8,128)(2,1)}, bf16[6,32,128]{2,1,0:T(8,128)(2,1)S(1)}, u32[]{:S(2)}, u32[]{:S(2)}) %collective-permute-start.2) | collective-permute-done | bytes 49184 | tf_op jit(solution)/shard_map/ppermute | solution.py:362
  18.4 0.8 %copy-done.2 = bf16[6,32,128]{2,1,0:T(8,128)(2,1)S(1)} copy-done((bf16[6,32,128]{2,1,0:T(8,128)(2,1)S(1)}, bf16[6,32,128]{2,1,0:T(8,128)(2,1)}, u32[]{:S(2)}) %copy-start.2) | copy-done | bytes 49176
  19.2 0.8 %regroup.1 = (bf16[8,4,32,128]{3,2,1,0:T(8,128)(2,1)}, bf16[4,2,32,128]{3,2,1,0:T(8,128)(2,1)S(1)}) custom-call(bf16[6,32,128]{2,1,0:T(8,128)(2,1)S(1)} %copy-done.2, bf16[6,32,128]{2,1,0:T(8,128)(2,1)S(1)} %collective-permute-done.refs_1_, bf16[6,32,128]{2,1,0:T(8,128)(2,1)S(1)} %collective-permute-done.1.refs_2_, ...), custom_call_target="tpu_custom_call" | custom-call | bytes 524288 | tf_op jit(solution)/shard_map/regroup/pallas_call | solution.py:349
  20.0 1.6 %collective-permute-start.3 = (bf16[4,2,32,128]{3,2,1,0:T(8,128)(2,1)S(1)}, bf16[4,2,32,128]{3,2,1,0:T(8,128)(2,1)S(1)}, u32[]{:S(2)}, u32[]{:S(2)}) collective-permute-start(bf16[4,2,32,128]{3,2,1,0:T(8,128)(2,1)S(1)} %get-tuple-element.17.near), channel_id=1, source_target_pairs={{0,16},{16,0},{1,17},{17,1},{2,18},{18,2},{3,19},{19,3},{4,20},{20... | collective-permute-start | bytes 196616 | tf_op jit(solution)/shard_map/ppermute | solution.py:362
  21.6 3.4 %all-to-all-start = ((bf16[8,4,32,128]{3,2,1,0:T(8,128)(2,1)}), bf16[8,4,32,128]{3,2,1,0:T(8,128)(2,1)S(1)}, u32[]{:S(2)}, u32[]{:S(2)}) async-start(bf16[8,4,32,128]{3,2,1,0:T(8,128)(2,1)} %get-tuple-element.15), calls=%async_computation | async-start | bytes 524288 | tf_op jit(solution)/shard_map/all_to_all | solution.py:448
  25.0 0.0 collective-permute-done.3.far
  25.0 5.7 %columns.1 = bf16[2,40,2688]{2,1,0:T(8,128)(2,1)} custom-call(s32[4]{0:T(128)S(1)} %copy-done.6, bf16[64,2048]{1,0:T(8,128)(2,1)S(1)} %copy-done.4, bf16[2048,32]{1,0:T(8,128)(2,1)S(1)} %get-tuple-element.16.inverses, s32[1,1024]{1,0:T(1,128)S(1)} %bitcast.7, bf16[1024,128]{1,0:T(8,128)(2,1)S(1)} %copy-done.3, ...), custom_call_target="tpu_custom_call" | custom-call | flops 8589934592 | bytes 2097152 | tf_op jit(solution)/shard_map/columns/pallas_call | solution.py:349
  30.7 0.2 all-to-all-done.pieces
  31.0 1.0 %legendre.1 = bf16[6,2,4,16,48]{4,3,2,1,0:T(8,128)(2,1)} custom-call(bf16[4,2,144,128]{3,2,1,0:T(8,128)(2,1)S(1)} %get-tuple-element.10.refs_4_.weights, bf16[8,4,32,128]{3,2,1,0:T(8,128)(2,1)S(1)} %all-to-all-done.pieces), custom_call_target="tpu_custom_call" | custom-call | flops 75497472 | bytes 262144 | tf_op jit(solution)/shard_map/legendre/pallas_call | solution.py:349
  (5 shorter events, 0.0 us)
Async XLA Ops:
  0.6 11.7 %copy-start = (bf16[64,32,32]{0,2,1:T(8,128)(2,1)S(1)}, bf16[64,32,32]{0,2,1:T(8,128)(2,1)}, u32[]{:S(2)}) copy-start(bf16[64,32,32]{0,2,1:T(8,128)(2,1)} %param.14) | copy-start | bytes 393220
  0.6 11.6 %copy-start.1 = (bf16[6,160,48]{1,2,0:T(8,128)(2,1)S(1)}, bf16[6,160,48]{1,2,0:T(8,128)(2,1)}, u32[]{:S(2)}) copy-start(bf16[6,160,48]{1,2,0:T(8,128)(2,1)} %param.9) | copy-start | bytes 276484
  0.7 24.3 %copy-start.3 = (bf16[1024,128]{1,0:T(8,128)(2,1)S(1)}, bf16[1024,128]{1,0:T(8,128)(2,1)}, u32[]{:S(2)}) copy-start(bf16[1024,128]{1,0:T(8,128)(2,1)} %interp.1) | copy-start | bytes 786436
  0.7 24.3 %copy-start.4 = (bf16[64,2048]{1,0:T(8,128)(2,1)S(1)}, bf16[64,2048]{1,0:T(8,128)(2,1)}, u32[]{:S(2)}) copy-start(bf16[64,2048]{1,0:T(8,128)(2,1)} %weights.1) | copy-start | bytes 786436
  0.7 24.3 %copy-start.5 = (s32[1024]{0:T(1024)S(1)}, s32[1024]{0:T(1024)}, u32[]{:S(2)}) copy-start(s32[1024]{0:T(1024)} %param.11) | copy-start | bytes 12292
  0.7 24.3 %copy-start.6 = (s32[4]{0:T(128)S(1)}, s32[4]{0:T(128)}, u32[]{:S(2)}) copy-start(s32[4]{0:T(128)} %counts.1) | copy-start | bytes 52
  6.6 6.9 %collective-permute-start = (bf16[6,32,128]{2,1,0:T(8,128)(2,1)}, bf16[6,32,128]{2,1,0:T(8,128)(2,1)S(1)}, u32[]{:S(2)}, u32[]{:S(2)}) collective-permute-start(bf16[6,32,128]{2,1,0:T(8,128)(2,1)} %get-tuple-element.12), channel_id=1, source_target_pairs={{0,1},{1,0},{2,3},{3,2},{4,5},{5,4},{6,7},{7,6},{8,9},{9,8},{10,11... | collective-permute-start | bytes 147464 | tf_op jit(solution)/shard_map/ppermute | solution.py:362
  9.7 6.1 %collective-permute-start.1 = (bf16[6,32,128]{2,1,0:T(8,128)(2,1)}, bf16[6,32,128]{2,1,0:T(8,128)(2,1)S(1)}, u32[]{:S(2)}, u32[]{:S(2)}) collective-permute-start(bf16[6,32,128]{2,1,0:T(8,128)(2,1)} %get-tuple-element.13), channel_id=1, source_target_pairs={{0,2},{1,3},{2,0},{3,1},{4,6},{5,7},{6,4},{7,5},{8,10},{9,11},{10,... | collective-permute-start | bytes 147464 | tf_op jit(solution)/shard_map/ppermute | solution.py:362
  12.3 6.1 %collective-permute-start.2 = (bf16[6,32,128]{2,1,0:T(8,128)(2,1)}, bf16[6,32,128]{2,1,0:T(8,128)(2,1)S(1)}, u32[]{:S(2)}, u32[]{:S(2)}) collective-permute-start(bf16[6,32,128]{2,1,0:T(8,128)(2,1)} %get-tuple-element.14), channel_id=1, source_target_pairs={{0,3},{1,2},{2,1},{3,0},{4,7},{5,6},{6,5},{7,4},{8,11},{9,10},{10,... | collective-permute-start | bytes 147464 | tf_op jit(solution)/shard_map/ppermute | solution.py:362
  18.4 0.8 %copy-start.2 = (bf16[6,32,128]{2,1,0:T(8,128)(2,1)S(1)}, bf16[6,32,128]{2,1,0:T(8,128)(2,1)}, u32[]{:S(2)}) copy-start(bf16[6,32,128]{2,1,0:T(8,128)(2,1)} %get-tuple-element.11.refs_0_) | copy-start | bytes 147460
  20.0 5.0 %collective-permute-start.3 = (bf16[4,2,32,128]{3,2,1,0:T(8,128)(2,1)S(1)}, bf16[4,2,32,128]{3,2,1,0:T(8,128)(2,1)S(1)}, u32[]{:S(2)}, u32[]{:S(2)}) collective-permute-start(bf16[4,2,32,128]{3,2,1,0:T(8,128)(2,1)S(1)} %get-tuple-element.17.near), channel_id=1, source_target_pairs={{0,16},{16,0},{1,17},{17,1},{2,18},{18,2},{3,19},{19,3},{4,20},{20... | collective-permute-start | bytes 196616 | tf_op jit(solution)/shard_map/ppermute | solution.py:362
  21.6 9.4 %all-to-all-start = ((bf16[8,4,32,128]{3,2,1,0:T(8,128)(2,1)}), bf16[8,4,32,128]{3,2,1,0:T(8,128)(2,1)S(1)}, u32[]{:S(2)}, u32[]{:S(2)}) async-start(bf16[8,4,32,128]{3,2,1,0:T(8,128)(2,1)} %get-tuple-element.15), calls=%async_computation | async-start | bytes 524288 | tf_op jit(solution)/shard_map/all_to_all | solution.py:448

commit v18 on v17

--- a/solution.py
+++ b/solution.py
@@ -129,10 +129,10 @@
 
 
 def local_kernel(lat_pad, grid_hbm, blocks_hbm, interp_hbm, table_hbm, *refs):
-    targets = len(refs) - 14
-    outs = refs[:targets]
     (grid, blocks, interp, table, patch, column, selector, message, padded, rows, totals, sems,
-     send_fourier, send_state) = refs[targets:]
+     send_fourier, send_state) = refs[-14:]
+    *outs, out, out_state = refs[:-14]
+    targets = message.shape[0]
     lev, lat, lon = grid.shape
     across = lon // LANES
     slots = interp.shape[0]
@@ -170,21 +170,22 @@
     state_blocks = slots * lev // LANES // message.shape[2]
     bands = message.shape[1] - state_blocks
     place = lax.axis_index("fld")
-    fourier_copies, state_copies = [], []
-    for shift in reversed(range(targets)):
-        mine = message.at[place ^ shift]
-        fourier_copies.append(
-            pltpu.make_async_copy(
-                mine.at[pl.ds(0, bands)], outs[shift].at[pl.ds(0, bands)], send_fourier.at[shift]
-            )
-        )
-        state_copies.append(
-            pltpu.make_async_copy(
-                mine.at[pl.ds(bands, state_blocks)],
-                outs[shift].at[pl.ds(bands, state_blocks)],
-                send_state.at[shift],
-            )
-        )
+    mine = message.at[place]
+    pairs = [
+        (message.at[place ^ (i + 1)].at[pl.ds(0, bands)], other.at[pl.ds(0, bands)])
+        for i, other in enumerate(outs)
+    ]
+    for first in range(0, out.shape[0], bands):
+        pairs.append((mine.at[pl.ds(0, bands)], out.at[pl.ds(first, bands), place]))
+    fourier_copies = [
+        pltpu.make_async_copy(*pair, send_fourier.at[i]) for i, pair in enumerate(pairs)
+    ]
+    behind = pl.ds(bands, state_blocks)
+    pairs = [
+        (message.at[place ^ (i + 1)].at[behind], other.at[behind]) for i, other in enumerate(outs)
+    ]
+    pairs.append((mine.at[behind], out_state.at[place]))
+    state_copies = [pltpu.make_async_copy(*pair, send_state.at[i]) for i, pair in enumerate(pairs)]
     for tile in range(across):
         patch[tile * lat_pad + lat : (tile + 1) * lat_pad, :] = jnp.zeros(
             (lat_pad - lat, lev * LANES), BF16
@@ -238,12 +239,12 @@
 
 
 def regroup_kernel(n_sec, n_band, *refs):
-    pieces, (_, out, out_state, sems) = refs[:-4], refs[-4:]
+    pieces, (_, _, _, out, out_state, sems) = refs[:-6], refs[-6:]
     blocks = out_state.shape[1]
     place = lax.axis_index("fld")
     copies = []
-    for shift, piece in enumerate(pieces):
-        fld = place ^ shift
+    for i, piece in enumerate(pieces):
+        fld = place ^ (len(pieces) - i)
         copies.append((piece.at[pl.ds(n_band, blocks)], out_state.at[fld]))
         for sec in range(n_sec):
             copies.append(
@@ -343,7 +344,8 @@
         copy.wait()
 
 
-def call(kernel, outs, specs, scratch, args, flops, size, name, out_spec=VMEM, limit=LIMIT):
+def call(kernel, outs, specs, scratch, args, flops, size, name, out_spec=VMEM, limit=LIMIT,
+         aliases={}):
     shapes = [jax.ShapeDtypeStruct(shape, dtype) for shape, dtype in outs]
     single = len(outs) == 1
     return pl.pallas_call(
@@ -355,6 +357,7 @@
         compiler_params=pltpu.CompilerParams(vmem_limit_bytes=limit),
         cost_estimate=pl.CostEstimate(flops=flops, bytes_accessed=size, transcendentals=0),
         name=name,
+        input_output_aliases=aliases,
     )(*args)
 
 
@@ -381,9 +384,13 @@
     depth = -(-across * lat_pad // LANES) * LANES
     state_blocks = slots * lev // LANES // piece
     message_blocks = n_band + state_blocks
-    messages = call(
+    *messages, sent, near = call(
         functools.partial(local_kernel, lat_pad),
-        [((message_blocks, piece, LANES), BF16)] * n_fld,
+        [((message_blocks, piece, LANES), BF16)] * (n_fld - 1)
+        + [
+            ((n_sec * n_band, n_fld, piece, LANES), BF16),
+            ((n_fld, state_blocks, piece, LANES), BF16),
+        ],
         [HBM] * 4,
         [
             pltpu.VMEM((lev, lat, lon), BF16),
@@ -398,7 +405,7 @@
             pltpu.VMEM((group * lev, LANES), F32),
             pltpu.VMEM((slots, LANES), F32),
             pltpu.SemaphoreType.DMA((lev + 3,)),
-            pltpu.SemaphoreType.DMA((n_fld,)),
+            pltpu.SemaphoreType.DMA((n_fld - 1 + n_sec,)),
             pltpu.SemaphoreType.DMA((n_fld,)),
         ],
         (grid.reshape(lev, lat, lon), block_row, interp, table),
@@ -408,9 +415,7 @@
         HBM,
         WHOLE,
     )
-    arrived = [messages[0]] + [None] * (n_fld - 1)
-    for shift in reversed(range(1, n_fld)):
-        arrived[shift] = exchange(messages[shift], "fld", shift)
+    arrived = [exchange(messages[shift - 1], "fld", shift) for shift in reversed(range(1, n_fld))]
     spec_bands, flux_rows, _ = inverses.shape
     basis, inverse_rows = call(
         functools.partial(prepare_kernel, lat, n_band),
@@ -435,14 +440,15 @@
             ((n_sec * n_band, n_fld, piece, LANES), BF16),
             ((n_fld, state_blocks, piece, LANES), BF16),
         ],
-        [HBM] * (n_fld + 1),
-        [pltpu.SemaphoreType.DMA((n_fld * (1 + n_sec),))],
-        (*arrived, basis),
+        [HBM] * (n_fld + 2),
+        [pltpu.SemaphoreType.DMA(((n_fld - 1) * (1 + n_sec),))],
+        (*arrived, basis, sent, near),
         0,
         4 * n_sec * n_band * n_fld * piece * LANES,
         "regroup",
         HBM,
         SMALL,
+        {n_fld: 0, n_fld + 1: 1},
     )
     far = exchange(near, "sec", 1)
     pieces = lax.all_to_all(sent, ("sec", "band"), 0, 0, tiled=True)

time: 32.3 us -> 31.7 us (0.981)
  waiting for transfers between devices: 5.07 us -> 3.35 us
  local copies, waits for them, and re-layouts: 0.82 us -> 1.67 us
    ppermute x4, waiting for transfers between devices: 4.87 us -> 3.35 us  [exchange(): lax.ppermute(value, axis, [(i, i ^ shift) for i in range(lax.axis_size(ax...]
    unnamed x14 -> x16, local copies, waits for them, and re-layouts: 0.82 us -> 1.67 us
  transfers between devices with their start and end apart: 5 -> 5, of which waited for: 3 -> 2; matrix products, arithmetic and copies ran while one was open for 0% -> 0% of each run, Pallas kernels for 22% -> 23%
where the time goes in v18:
time: 31.7 us; the launch traced here: 31.4 us
  Pallas kernels  14.9 us (47%)
  starting transfers between devices  10.7 us (34%)
  waiting for transfers between devices  3.35 us (11%)
  local copies, waits for them, and re-layouts  1.67 us (5%)
  between operations  0.78 us (2%)
    pallas_call x5, Pallas kernels, call(): pl.pallas_call(kernel, out_shape=shapes[0] if single else shapes, in_spec...  14.9 us
    ppermute x4, starting transfers between devices, exchange(): lax.ppermute(value, axis, [(i, i ^ shift) for i in range(lax.axis_size(ax...  7.24 us
    all_to_all x1, starting transfers between devices, body(): pieces = lax.all_to_all(sent, ('sec', 'band'), 0, 0, tiled=True)  3.41 us
    ppermute x4, waiting for transfers between devices, exchange(): lax.ppermute(value, axis, [(i, i ^ shift) for i in range(lax.axis_size(ax...  3.35 us
    unnamed x16, local copies, waits for them, and re-layouts  1.67 us
  transfers between devices with their start and end apart: 5, of which 2 were waited for; matrix products, arithmetic and copies ran while one was open for 0% of the time, Pallas kernels for 23%

profile of v18, /device:TPU:0, one launch (start us, length us, event | category | flops | bytes accessed | tf_op | source)
XLA Modules:
  0.0 31.4 jit_solution(3804595354151927812)
XLA Ops:
  0.7 5.9 %local.1 = (bf16[6,32,128]{2,1,0:T(8,128)(2,1)}, bf16[6,32,128]{2,1,0:T(8,128)(2,1)}, bf16[6,32,128]{2,1,0:T(8,128)(2,1)}, bf16[8,4,32,128]{3,2,1,0:T(8,128)(2,1)}, bf16[4,2,32,128]{3,2,1,0:T(8,128)(2,1)}) custom-call(bf16[8,40,2688]{2,1,0:T(8,128)(2,1)} %bitcast.8, s32[1,1024]{1,0:T(1,128)} %bitcast.6, bf16[1024,128]{1,0:T(8,128)(2,1)} %interp.1, ...), custom_call_target="tpu_custom_call" | custom-call | flops 2477785088 | bytes 1982464 | tf_op jit(solution)/shard_map/local/pallas_call | solution.py:351
  6.6 0.0 copy-start.4
  6.6 0.0 copy-start.6
  6.6 0.0 copy-start.7
  6.6 5.1 %collective-permute-start = (bf16[6,32,128]{2,1,0:T(8,128)(2,1)}, bf16[6,32,128]{2,1,0:T(8,128)(2,1)S(1)}, u32[]{:S(2)}, u32[]{:S(2)}) collective-permute-start(bf16[6,32,128]{2,1,0:T(8,128)(2,1)} %get-tuple-element.12), channel_id=1, source_target_pairs={{0,3},{1,2},{2,1},{3,0},{4,7},{5,6},{6,5},{7,4},{8,11},{9,10},{10,... | collective-permute-start | bytes 147464 | tf_op jit(solution)/shard_map/ppermute | solution.py:365
  11.7 0.0 collective-permute-start.1
  11.7 0.6 %collective-permute-start.2 = (bf16[6,32,128]{2,1,0:T(8,128)(2,1)}, bf16[6,32,128]{2,1,0:T(8,128)(2,1)S(1)}, u32[]{:S(2)}, u32[]{:S(2)}) collective-permute-start(bf16[6,32,128]{2,1,0:T(8,128)(2,1)} %get-tuple-element.14), channel_id=1, source_target_pairs={{0,1},{1,0},{2,3},{3,2},{4,5},{5,4},{6,7},{7,6},{8,9},{9,8},{10,11... | collective-permute-start | bytes 147464 | tf_op jit(solution)/shard_map/ppermute | solution.py:365
  12.4 0.0 copy-done.3
  12.4 1.2 %prepare.1 = (bf16[4,2,144,128]{3,2,1,0:T(8,128)(2,1)S(1)}, bf16[2048,32]{1,0:T(8,128)(2,1)S(1)}) custom-call(bf16[6,48,160]{2,1,0:T(8,128)(2,1)S(1)} %bitcast.5, bf16[32,32,64]{2,1,0:T(8,128)(2,1)S(1)} %bitcast.4), custom_call_target="tpu_custom_call" | custom-call | bytes 1179648 | tf_op jit(solution)/shard_map/prepare/pallas_call | solution.py:351
  13.6 0.6 %collective-permute-done.refs_0_ = bf16[6,32,128]{2,1,0:T(8,128)(2,1)S(1)} collective-permute-done((bf16[6,32,128]{2,1,0:T(8,128)(2,1)}, bf16[6,32,128]{2,1,0:T(8,128)(2,1)S(1)}, u32[]{:S(2)}, u32[]{:S(2)}) %collective-permute-start) | collective-permute-done | bytes 49184 | tf_op jit(solution)/shard_map/ppermute | solution.py:365
  14.2 2.8 %collective-permute-done.1.refs_1_ = bf16[6,32,128]{2,1,0:T(8,128)(2,1)S(1)} collective-permute-done((bf16[6,32,128]{2,1,0:T(8,128)(2,1)}, bf16[6,32,128]{2,1,0:T(8,128)(2,1)S(1)}, u32[]{:S(2)}, u32[]{:S(2)}) %collective-permute-start.1) | collective-permute-done | bytes 49184 | tf_op jit(solution)/shard_map/ppermute | solution.py:365
  16.9 0.0 collective-permute-done.2.refs_2_
  16.9 0.9 %copy-done = bf16[8,4,32,128]{3,2,1,0:T(8,128)(2,1)S(1)} copy-done((bf16[8,4,32,128]{3,2,1,0:T(8,128)(2,1)S(1)}, bf16[8,4,32,128]{3,2,1,0:T(8,128)(2,1)}, u32[]{:S(2)}) %copy-start) | copy-done | bytes 262168
  17.9 0.7 %regroup.1 = (bf16[8,4,32,128]{3,2,1,0:T(8,128)(2,1)S(1)}, bf16[4,2,32,128]{3,2,1,0:T(8,128)(2,1)}) custom-call(bf16[6,32,128]{2,1,0:T(8,128)(2,1)S(1)} %collective-permute-done.refs_0_, bf16[6,32,128]{2,1,0:T(8,128)(2,1)S(1)} %collective-permute-done.1.refs_1_, ...), custom_call_target="tpu_custom_call", output_to_operand_aliasing={{0}: (4, {}), {1}: (5, {})} | custom-call | bytes 524288 | tf_op jit(solution)/shard_map/regroup/pallas_call | solution.py:351
  18.6 0.7 %copy-done.1 = bf16[8,4,32,128]{3,2,1,0:T(8,128)(2,1)} copy-done((bf16[8,4,32,128]{3,2,1,0:T(8,128)(2,1)}, bf16[8,4,32,128]{3,2,1,0:T(8,128)(2,1)S(1)}, u32[]{:S(2)}) %copy-start.1) | copy-done | bytes 262168
  19.3 1.5 %collective-permute-start.3 = (bf16[4,2,32,128]{3,2,1,0:T(8,128)(2,1)}, bf16[4,2,32,128]{3,2,1,0:T(8,128)(2,1)S(1)}, u32[]{:S(2)}, u32[]{:S(2)}) collective-permute-start(bf16[4,2,32,128]{3,2,1,0:T(8,128)(2,1)} %get-tuple-element.19.near), channel_id=1, source_target_pairs={{0,16},{16,0},{1,17},{17,1},{2,18},{18,2},{3,19},{19,3},{4,20},{20... | collective-permute-start | bytes 196616 | tf_op jit(solution)/shard_map/ppermute | solution.py:365
  20.8 3.4 %all-to-all-start = ((bf16[8,4,32,128]{3,2,1,0:T(8,128)(2,1)}), bf16[8,4,32,128]{3,2,1,0:T(8,128)(2,1)S(1)}, u32[]{:S(2)}, u32[]{:S(2)}) async-start(bf16[8,4,32,128]{3,2,1,0:T(8,128)(2,1)} %copy-done.1), calls=%async_computation | async-start | bytes 524288 | tf_op jit(solution)/shard_map/all_to_all | solution.py:454
  24.2 0.0 collective-permute-done.3.far
  24.2 0.0 copy-done.5
  24.2 0.0 copy-done.4
  24.2 0.0 copy-done.6
  24.3 6.0 %columns.1 = bf16[2,40,2688]{2,1,0:T(8,128)(2,1)} custom-call(s32[4]{0:T(128)S(1)} %copy-done.7, bf16[64,2048]{1,0:T(8,128)(2,1)S(1)} %copy-done.5, bf16[2048,32]{1,0:T(8,128)(2,1)S(1)} %get-tuple-element.18.inverses, s32[1,1024]{1,0:T(1,128)S(1)} %bitcast.7, bf16[1024,128]{1,0:T(8,128)(2,1)S(1)} %copy-done.4, ...), custom_call_target="tpu_custom_call" | custom-call | flops 8589934592 | bytes 2097152 | tf_op jit(solution)/shard_map/columns/pallas_call | solution.py:351
  30.3 0.0 all-to-all-done.pieces
  30.3 1.1 %legendre.1 = bf16[6,2,4,16,48]{4,3,2,1,0:T(8,128)(2,1)} custom-call(bf16[4,2,144,128]{3,2,1,0:T(8,128)(2,1)S(1)} %get-tuple-element.11.refs_3_.weights, bf16[8,4,32,128]{3,2,1,0:T(8,128)(2,1)S(1)} %all-to-all-done.pieces), custom_call_target="tpu_custom_call" | custom-call | flops 75497472 | bytes 262144 | tf_op jit(solution)/shard_map/legendre/pallas_call | solution.py:351
  (7 shorter events, 0.0 us)
Async XLA Ops:
  0.6 11.7 %copy-start.2 = (bf16[64,32,32]{0,2,1:T(8,128)(2,1)S(1)}, bf16[64,32,32]{0,2,1:T(8,128)(2,1)}, u32[]{:S(2)}) copy-start(bf16[64,32,32]{0,2,1:T(8,128)(2,1)} %param.14) | copy-start | bytes 393220
  0.6 11.7 %copy-start.3 = (bf16[6,160,48]{1,2,0:T(8,128)(2,1)S(1)}, bf16[6,160,48]{1,2,0:T(8,128)(2,1)}, u32[]{:S(2)}) copy-start(bf16[6,160,48]{1,2,0:T(8,128)(2,1)} %param.9) | copy-start | bytes 276484
  0.7 23.6 %copy-start.5 = (bf16[64,2048]{1,0:T(8,128)(2,1)S(1)}, bf16[64,2048]{1,0:T(8,128)(2,1)}, u32[]{:S(2)}) copy-start(bf16[64,2048]{1,0:T(8,128)(2,1)} %weights.1) | copy-start | bytes 786436
  6.6 17.6 %copy-start.4 = (bf16[1024,128]{1,0:T(8,128)(2,1)S(1)}, bf16[1024,128]{1,0:T(8,128)(2,1)}, u32[]{:S(2)}) copy-start(bf16[1024,128]{1,0:T(8,128)(2,1)} %interp.1) | copy-start | bytes 786436
  6.6 17.6 %copy-start.6 = (s32[1024]{0:T(1024)S(1)}, s32[1024]{0:T(1024)}, u32[]{:S(2)}) copy-start(s32[1024]{0:T(1024)} %param.11) | copy-start | bytes 12292
  6.6 17.6 %copy-start.7 = (s32[4]{0:T(128)S(1)}, s32[4]{0:T(128)}, u32[]{:S(2)}) copy-start(s32[4]{0:T(128)} %counts.1) | copy-start | bytes 52
  6.6 7.5 %collective-permute-start = (bf16[6,32,128]{2,1,0:T(8,128)(2,1)}, bf16[6,32,128]{2,1,0:T(8,128)(2,1)S(1)}, u32[]{:S(2)}, u32[]{:S(2)}) collective-permute-start(bf16[6,32,128]{2,1,0:T(8,128)(2,1)} %get-tuple-element.12), channel_id=1, source_target_pairs={{0,3},{1,2},{2,1},{3,0},{4,7},{5,6},{6,5},{7,4},{8,11},{9,10},{10,... | collective-permute-start | bytes 147464 | tf_op jit(solution)/shard_map/ppermute | solution.py:365
  11.7 5.2 %collective-permute-start.1 = (bf16[6,32,128]{2,1,0:T(8,128)(2,1)}, bf16[6,32,128]{2,1,0:T(8,128)(2,1)S(1)}, u32[]{:S(2)}, u32[]{:S(2)}) collective-permute-start(bf16[6,32,128]{2,1,0:T(8,128)(2,1)} %get-tuple-element.13), channel_id=1, source_target_pairs={{0,2},{1,3},{2,0},{3,1},{4,6},{5,7},{6,4},{7,5},{8,10},{9,11},{10,... | collective-permute-start | bytes 147464 | tf_op jit(solution)/shard_map/ppermute | solution.py:365
  11.7 5.2 %collective-permute-start.2 = (bf16[6,32,128]{2,1,0:T(8,128)(2,1)}, bf16[6,32,128]{2,1,0:T(8,128)(2,1)S(1)}, u32[]{:S(2)}, u32[]{:S(2)}) collective-permute-start(bf16[6,32,128]{2,1,0:T(8,128)(2,1)} %get-tuple-element.14), channel_id=1, source_target_pairs={{0,1},{1,0},{2,3},{3,2},{4,5},{5,4},{6,7},{7,6},{8,9},{9,8},{10,11... | collective-permute-start | bytes 147464 | tf_op jit(solution)/shard_map/ppermute | solution.py:365
  16.9 1.0 %copy-start = (bf16[8,4,32,128]{3,2,1,0:T(8,128)(2,1)S(1)}, bf16[8,4,32,128]{3,2,1,0:T(8,128)(2,1)}, u32[]{:S(2)}) copy-start(bf16[8,4,32,128]{3,2,1,0:T(8,128)(2,1)} %get-tuple-element.15.refs_4_) | copy-start | bytes 786436
  18.6 0.7 %copy-start.1 = (bf16[8,4,32,128]{3,2,1,0:T(8,128)(2,1)}, bf16[8,4,32,128]{3,2,1,0:T(8,128)(2,1)S(1)}, u32[]{:S(2)}) copy-start(bf16[8,4,32,128]{3,2,1,0:T(8,128)(2,1)S(1)} %get-tuple-element.17) | copy-start | bytes 786436
  19.3 4.9 %collective-permute-start.3 = (bf16[4,2,32,128]{3,2,1,0:T(8,128)(2,1)}, bf16[4,2,32,128]{3,2,1,0:T(8,128)(2,1)S(1)}, u32[]{:S(2)}, u32[]{:S(2)}) collective-permute-start(bf16[4,2,32,128]{3,2,1,0:T(8,128)(2,1)} %get-tuple-element.19.near), channel_id=1, source_target_pairs={{0,16},{16,0},{1,17},{17,1},{2,18},{18,2},{3,19},{19,3},{4,20},{20... | collective-permute-start | bytes 196616 | tf_op jit(solution)/shard_map/ppermute | solution.py:365
  20.8 9.5 %all-to-all-start = ((bf16[8,4,32,128]{3,2,1,0:T(8,128)(2,1)}), bf16[8,4,32,128]{3,2,1,0:T(8,128)(2,1)S(1)}, u32[]{:S(2)}, u32[]{:S(2)}) async-start(bf16[8,4,32,128]{3,2,1,0:T(8,128)(2,1)} %copy-done.1), calls=%async_computation | async-start | bytes 524288 | tf_op jit(solution)/shard_map/all_to_all | solution.py:454

commit v19 on v17

--- a/solution.py
+++ b/solution.py
@@ -52,7 +52,7 @@
     message[:, :bands] = rows[...].astype(BF16).reshape(targets, bands, size, LANES)
 
 
-def prepare_kernel(lat, n_band, legendre, inverses, out, out_inverses, wide, rows, turned):
+def prepare_kernel(lat, n_band, legendre, inverses, _, out, out_inverses, wide, rows, turned):
     flux_rows, _, spec_bands = inverses.shape
     for row in range(flux_rows):
         rows[row * flux_rows : (row + 1) * flux_rows, :] = inverses[row].astype(F32)
@@ -242,8 +242,8 @@
     blocks = out_state.shape[1]
     place = lax.axis_index("fld")
     copies = []
-    for shift, piece in enumerate(pieces):
-        fld = place ^ shift
+    for i, piece in enumerate(pieces):
+        fld = place ^ (len(pieces) - 1 - i)
         copies.append((piece.at[pl.ds(n_band, blocks)], out_state.at[fld]))
         for sec in range(n_sec):
             copies.append(
@@ -408,9 +408,8 @@
         HBM,
         WHOLE,
     )
-    arrived = [messages[0]] + [None] * (n_fld - 1)
-    for shift in reversed(range(1, n_fld)):
-        arrived[shift] = exchange(messages[shift], "fld", shift)
+    arrived = [exchange(messages[shift], "fld", shift) for shift in reversed(range(1, n_fld))]
+    arrived.append(messages[0])
     spec_bands, flux_rows, _ = inverses.shape
     basis, inverse_rows = call(
         functools.partial(prepare_kernel, lat, n_band),
@@ -418,13 +417,13 @@
             ((n_band, 2, THIRDS * degrees, LANES), BF16),
             ((spec_bands * flux_rows, flux_rows), BF16),
         ],
-        [VMEM, VMEM],
+        [VMEM, VMEM, VMEM],
         [
             pltpu.VMEM((degrees, (n_band * lat // LANES + 2) * LANES), F32),
             pltpu.VMEM((flux_rows * flux_rows, spec_bands), F32),
             pltpu.VMEM((spec_bands * flux_rows, flux_rows), F32),
         ],
-        (jnp.swapaxes(legendre, 1, 2), jnp.transpose(inverses, (1, 2, 0))),
+        (jnp.swapaxes(legendre, 1, 2), jnp.transpose(inverses, (1, 2, 0)), messages[0]),
         0,
         8 * wave_dev * degrees * n_band * LANES,
         "prepare",

time: 32.3 us -> 30 us (0.929)
  waiting for transfers between devices: 5.07 us -> 2.75 us
    ppermute x4, waiting for transfers between devices: 4.87 us -> 2.54 us  [exchange(): lax.ppermute(value, axis, [(i, i ^ shift) for i in range(lax.axis_size(ax...]
  transfers between devices with their start and end apart: 5 -> 5, of which waited for: 3 -> 2; matrix products, arithmetic and copies ran while one was open for 0% -> 0% of each run, Pallas kernels for 22% -> 23%
where the time goes in v19:
time: 30 us; the launch traced here: 29.8 us
  Pallas kernels  14.7 us (49%)
  starting transfers between devices  10.7 us (36%)
  waiting for transfers between devices  2.75 us (9%)
  local copies, waits for them, and re-layouts  0.82 us (3%)
  between operations  0.77 us (3%)
    pallas_call x5, Pallas kernels, call(): pl.pallas_call(kernel, out_shape=shapes[0] if single else shapes, in_spec...  14.7 us
    ppermute x4, starting transfers between devices, exchange(): lax.ppermute(value, axis, [(i, i ^ shift) for i in range(lax.axis_size(ax...  7.31 us
    all_to_all x1, starting transfers between devices, body(): pieces = lax.all_to_all(sent, ('sec', 'band'), 0, 0, tiled=True)  3.41 us
    ppermute x4, waiting for transfers between devices, exchange(): lax.ppermute(value, axis, [(i, i ^ shift) for i in range(lax.axis_size(ax...  2.54 us
    unnamed x14, local copies, waits for them, and re-layouts  0.82 us
  transfers between devices with their start and end apart: 5, of which 2 were waited for; matrix products, arithmetic and copies ran while one was open for 0% of the time, Pallas kernels for 23%

profile of v19, /device:TPU:0, one launch (start us, length us, event | category | flops | bytes accessed | tf_op | source)
XLA Modules:
  0.0 29.8 jit_solution(14356045229686846038)
XLA Ops:
  0.6 0.0 copy-start
  0.6 0.0 copy-start.2
  0.7 0.0 copy-start.3
  0.7 0.0 copy-start.4
  0.7 0.0 copy-start.5
  0.7 0.0 copy-start.6
  0.7 5.9 %local.1 = (bf16[6,32,128]{2,1,0:T(8,128)(2,1)}, bf16[6,32,128]{2,1,0:T(8,128)(2,1)}, bf16[6,32,128]{2,1,0:T(8,128)(2,1)}, bf16[6,32,128]{2,1,0:T(8,128)(2,1)}) custom-call(bf16[8,40,2688]{2,1,0:T(8,128)(2,1)} %bitcast.8, s32[1,1024]{1,0:T(1,128)} %bitcast.6, bf16[1024,128]{1,0:T(8,128)(2,1)} %interp.1, bf16[2688,192]{1,0:T(8,128)(2,1)} %constant.2.clone.table_hbm), custom_call_target="tpu_custom_call" | custom-call | flops 2477785088 | bytes 1982464 | tf_op jit(solution)/shard_map/local/pallas_call | solution.py:349
  6.6 5.1 %collective-permute-start = (bf16[6,32,128]{2,1,0:T(8,128)(2,1)}, bf16[6,32,128]{2,1,0:T(8,128)(2,1)S(1)}, u32[]{:S(2)}, u32[]{:S(2)}) collective-permute-start(bf16[6,32,128]{2,1,0:T(8,128)(2,1)} %get-tuple-element.12), channel_id=1, source_target_pairs={{0,3},{1,2},{2,1},{3,0},{4,7},{5,6},{6,5},{7,4},{8,11},{9,10},{10,... | collective-permute-start | bytes 147464 | tf_op jit(solution)/shard_map/ppermute | solution.py:362
  11.7 0.0 collective-permute-start.1
  11.7 0.6 %collective-permute-start.2 = (bf16[6,32,128]{2,1,0:T(8,128)(2,1)}, bf16[6,32,128]{2,1,0:T(8,128)(2,1)S(1)}, u32[]{:S(2)}, u32[]{:S(2)}) collective-permute-start(bf16[6,32,128]{2,1,0:T(8,128)(2,1)} %get-tuple-element.14), channel_id=1, source_target_pairs={{0,1},{1,0},{2,3},{3,2},{4,5},{5,4},{6,7},{7,6},{8,9},{9,8},{10,11... | collective-permute-start | bytes 147464 | tf_op jit(solution)/shard_map/ppermute | solution.py:362
  12.4 0.0 copy-done
  12.4 0.0 copy-done.2
  12.4 0.8 %copy-done.1 = bf16[6,32,128]{2,1,0:T(8,128)(2,1)S(1)} copy-done((bf16[6,32,128]{2,1,0:T(8,128)(2,1)S(1)}, bf16[6,32,128]{2,1,0:T(8,128)(2,1)}, u32[]{:S(2)}) %copy-start.1) | copy-done | bytes 49176
  13.2 1.2 %prepare.1 = (bf16[4,2,144,128]{3,2,1,0:T(8,128)(2,1)S(1)}, bf16[2048,32]{1,0:T(8,128)(2,1)S(1)}) custom-call(bf16[6,48,160]{2,1,0:T(8,128)(2,1)S(1)} %bitcast.5, bf16[32,32,64]{2,1,0:T(8,128)(2,1)S(1)} %bitcast.4, bf16[6,32,128]{2,1,0:T(8,128)(2,1)S(1)} %copy-done.1), custom_call_target="tpu_custom_call" | custom-call | bytes 1179648 | tf_op jit(solution)/shard_map/prepare/pallas_call | solution.py:349
  14.4 0.0 collective-permute-done.refs_0_
  14.4 2.5 %collective-permute-done.1.refs_1_ = bf16[6,32,128]{2,1,0:T(8,128)(2,1)S(1)} collective-permute-done((bf16[6,32,128]{2,1,0:T(8,128)(2,1)}, bf16[6,32,128]{2,1,0:T(8,128)(2,1)S(1)}, u32[]{:S(2)}, u32[]{:S(2)}) %collective-permute-start.1) | collective-permute-done | bytes 49184 | tf_op jit(solution)/shard_map/ppermute | solution.py:362
  16.9 0.0 collective-permute-done.2.refs_2_
  16.9 0.8 %regroup.1 = (bf16[8,4,32,128]{3,2,1,0:T(8,128)(2,1)}, bf16[4,2,32,128]{3,2,1,0:T(8,128)(2,1)S(1)}) custom-call(bf16[6,32,128]{2,1,0:T(8,128)(2,1)S(1)} %collective-permute-done.refs_0_, bf16[6,32,128]{2,1,0:T(8,128)(2,1)S(1)} %collective-permute-done.1.refs_1_, bf16[6,32,128]{2,1,0:T(8,128)(2,1)S(1)} %collective-permute-done.2.refs_2_, ...), custom_call_target="tpu_custom_call" | custom-call | bytes 524288 | tf_op jit(solution)/shard_map/regroup/pallas_call | solution.py:349
  17.8 1.6 %collective-permute-start.3 = (bf16[4,2,32,128]{3,2,1,0:T(8,128)(2,1)S(1)}, bf16[4,2,32,128]{3,2,1,0:T(8,128)(2,1)S(1)}, u32[]{:S(2)}, u32[]{:S(2)}) collective-permute-start(bf16[4,2,32,128]{3,2,1,0:T(8,128)(2,1)S(1)} %get-tuple-element.17.near), channel_id=1, source_target_pairs={{0,16},{16,0},{1,17},{17,1},{2,18},{18,2},{3,19},{19,3},{4,20},{20... | collective-permute-start | bytes 196616 | tf_op jit(solution)/shard_map/ppermute | solution.py:362
  19.3 3.4 %all-to-all-start = ((bf16[8,4,32,128]{3,2,1,0:T(8,128)(2,1)}), bf16[8,4,32,128]{3,2,1,0:T(8,128)(2,1)S(1)}, u32[]{:S(2)}, u32[]{:S(2)}) async-start(bf16[8,4,32,128]{3,2,1,0:T(8,128)(2,1)} %get-tuple-element.15), calls=%async_computation | async-start | bytes 524288 | tf_op jit(solution)/shard_map/all_to_all | solution.py:447
  22.7 0.0 collective-permute-done.3.far
  22.8 5.7 %columns.1 = bf16[2,40,2688]{2,1,0:T(8,128)(2,1)} custom-call(s32[4]{0:T(128)S(1)} %copy-done.6, bf16[64,2048]{1,0:T(8,128)(2,1)S(1)} %copy-done.4, bf16[2048,32]{1,0:T(8,128)(2,1)S(1)} %get-tuple-element.16.inverses, s32[1,1024]{1,0:T(1,128)S(1)} %bitcast.7, bf16[1024,128]{1,0:T(8,128)(2,1)S(1)} %copy-done.3, ...), custom_call_target="tpu_custom_call" | custom-call | flops 8589934592 | bytes 2097152 | tf_op jit(solution)/shard_map/columns/pallas_call | solution.py:349
  28.5 0.2 all-to-all-done.pieces
  28.7 1.0 %legendre.1 = bf16[6,2,4,16,48]{4,3,2,1,0:T(8,128)(2,1)} custom-call(bf16[4,2,144,128]{3,2,1,0:T(8,128)(2,1)S(1)} %get-tuple-element.11.refs_4_.weights, bf16[8,4,32,128]{3,2,1,0:T(8,128)(2,1)S(1)} %all-to-all-done.pieces), custom_call_target="tpu_custom_call" | custom-call | flops 75497472 | bytes 262144 | tf_op jit(solution)/shard_map/legendre/pallas_call | solution.py:349
  (5 shorter events, 0.0 us)
Async XLA Ops:
  0.6 11.7 %copy-start = (bf16[64,32,32]{0,2,1:T(8,128)(2,1)S(1)}, bf16[64,32,32]{0,2,1:T(8,128)(2,1)}, u32[]{:S(2)}) copy-start(bf16[64,32,32]{0,2,1:T(8,128)(2,1)} %param.14) | copy-start | bytes 393220
  0.6 11.7 %copy-start.2 = (bf16[6,160,48]{1,2,0:T(8,128)(2,1)S(1)}, bf16[6,160,48]{1,2,0:T(8,128)(2,1)}, u32[]{:S(2)}) copy-start(bf16[6,160,48]{1,2,0:T(8,128)(2,1)} %param.9) | copy-start | bytes 276484
  0.7 22.1 %copy-start.3 = (bf16[1024,128]{1,0:T(8,128)(2,1)S(1)}, bf16[1024,128]{1,0:T(8,128)(2,1)}, u32[]{:S(2)}) copy-start(bf16[1024,128]{1,0:T(8,128)(2,1)} %interp.1) | copy-start | bytes 786436
  0.7 22.1 %copy-start.4 = (bf16[64,2048]{1,0:T(8,128)(2,1)S(1)}, bf16[64,2048]{1,0:T(8,128)(2,1)}, u32[]{:S(2)}) copy-start(bf16[64,2048]{1,0:T(8,128)(2,1)} %weights.1) | copy-start | bytes 786436
  0.7 22.1 %copy-start.5 = (s32[1024]{0:T(1024)S(1)}, s32[1024]{0:T(1024)}, u32[]{:S(2)}) copy-start(s32[1024]{0:T(1024)} %param.11) | copy-start | bytes 12292
  0.7 22.1 %copy-start.6 = (s32[4]{0:T(128)S(1)}, s32[4]{0:T(128)}, u32[]{:S(2)}) copy-start(s32[4]{0:T(128)} %counts.1) | copy-start | bytes 52
  6.6 7.8 %collective-permute-start = (bf16[6,32,128]{2,1,0:T(8,128)(2,1)}, bf16[6,32,128]{2,1,0:T(8,128)(2,1)S(1)}, u32[]{:S(2)}, u32[]{:S(2)}) collective-permute-start(bf16[6,32,128]{2,1,0:T(8,128)(2,1)} %get-tuple-element.12), channel_id=1, source_target_pairs={{0,3},{1,2},{2,1},{3,0},{4,7},{5,6},{6,5},{7,4},{8,11},{9,10},{10,... | collective-permute-start | bytes 147464 | tf_op jit(solution)/shard_map/ppermute | solution.py:362
  11.7 5.2 %collective-permute-start.1 = (bf16[6,32,128]{2,1,0:T(8,128)(2,1)}, bf16[6,32,128]{2,1,0:T(8,128)(2,1)S(1)}, u32[]{:S(2)}, u32[]{:S(2)}) collective-permute-start(bf16[6,32,128]{2,1,0:T(8,128)(2,1)} %get-tuple-element.13), channel_id=1, source_target_pairs={{0,2},{1,3},{2,0},{3,1},{4,6},{5,7},{6,4},{7,5},{8,10},{9,11},{10,... | collective-permute-start | bytes 147464 | tf_op jit(solution)/shard_map/ppermute | solution.py:362
  11.7 5.2 %collective-permute-start.2 = (bf16[6,32,128]{2,1,0:T(8,128)(2,1)}, bf16[6,32,128]{2,1,0:T(8,128)(2,1)S(1)}, u32[]{:S(2)}, u32[]{:S(2)}) collective-permute-start(bf16[6,32,128]{2,1,0:T(8,128)(2,1)} %get-tuple-element.14), channel_id=1, source_target_pairs={{0,1},{1,0},{2,3},{3,2},{4,5},{5,4},{6,7},{7,6},{8,9},{9,8},{10,11... | collective-permute-start | bytes 147464 | tf_op jit(solution)/shard_map/ppermute | solution.py:362
  12.4 0.8 %copy-start.1 = (bf16[6,32,128]{2,1,0:T(8,128)(2,1)S(1)}, bf16[6,32,128]{2,1,0:T(8,128)(2,1)}, u32[]{:S(2)}) copy-start(bf16[6,32,128]{2,1,0:T(8,128)(2,1)} %get-tuple-element.10._.refs_3_) | copy-start | bytes 147460
  17.8 5.0 %collective-permute-start.3 = (bf16[4,2,32,128]{3,2,1,0:T(8,128)(2,1)S(1)}, bf16[4,2,32,128]{3,2,1,0:T(8,128)(2,1)S(1)}, u32[]{:S(2)}, u32[]{:S(2)}) collective-permute-start(bf16[4,2,32,128]{3,2,1,0:T(8,128)(2,1)S(1)} %get-tuple-element.17.near), channel_id=1, source_target_pairs={{0,16},{16,0},{1,17},{17,1},{2,18},{18,2},{3,19},{19,3},{4,20},{20... | collective-permute-start | bytes 196616 | tf_op jit(solution)/shard_map/ppermute | solution.py:362
  19.3 9.4 %all-to-all-start = ((bf16[8,4,32,128]{3,2,1,0:T(8,128)(2,1)}), bf16[8,4,32,128]{3,2,1,0:T(8,128)(2,1)S(1)}, u32[]{:S(2)}, u32[]{:S(2)}) async-start(bf16[8,4,32,128]{3,2,1,0:T(8,128)(2,1)} %get-tuple-element.15), calls=%async_computation | async-start | bytes 524288 | tf_op jit(solution)/shard_map/all_to_all | solution.py:447

commit v20 on v19

--- a/solution.py
+++ b/solution.py
@@ -18,7 +18,7 @@
 SMEM = pl.BlockSpec(memory_space=pltpu.SMEM)
 LIMIT = 40 * 1024 * 1024
 SMALL = 4 * 1024 * 1024
-ROOM = 1200 * 1024
+ROOM = 12000 * 1024
 WHOLE = 64 * 1024 * 1024 - ROOM
 NT = (((1,), (1,)), ((), ()))
 
@@ -38,7 +38,7 @@
     return values.astype(np.float32).astype(BF16)
 
 
-def pack(lev, lat, coeffs, message, padded, rows):
+def pack(lev, lat, coeffs, padded, rows):
     group = coeffs.shape[1] // THIRDS
     padded[...] = jnp.zeros_like(padded)
     for level in range(lev):
@@ -47,12 +47,9 @@
                 level * lat : (level + 1) * lat, third * group : (third + 1) * group
             ]
         rows[pl.ds(level, group, stride=lev), :] = jnp.transpose(padded[...])[:group]
-    targets, size = message.shape[0], message.shape[2]
-    bands = rows.shape[0] // targets // size
-    message[:, :bands] = rows[...].astype(BF16).reshape(targets, bands, size, LANES)
-
-
-def prepare_kernel(lat, n_band, legendre, inverses, _, out, out_inverses, wide, rows, turned):
+
+
+def prepare_kernel(lat, n_band, legendre, inverses, out, out_inverses, wide, rows, turned):
     flux_rows, _, spec_bands = inverses.shape
     for row in range(flux_rows):
         rows[row * flux_rows : (row + 1) * flux_rows, :] = inverses[row].astype(F32)
@@ -129,10 +126,8 @@
 
 
 def local_kernel(lat_pad, grid_hbm, blocks_hbm, interp_hbm, table_hbm, *refs):
-    targets = len(refs) - 14
-    outs = refs[:targets]
-    (grid, blocks, interp, table, patch, column, selector, message, padded, rows, totals, sems,
-     send_fourier, send_state) = refs[targets:]
+    outs = refs[:-11]
+    grid, blocks, interp, table, patch, column, selector, padded, rows, totals, sems = refs[-11:]
     lev, lat, lon = grid.shape
     across = lon // LANES
     slots = interp.shape[0]
@@ -167,24 +162,9 @@
             selector[start : start + chunk, base : base + LANES] = jnp.where(
                 mine == lane + base, 1.0, 0.0
             ).astype(BF16)
-    state_blocks = slots * lev // LANES // message.shape[2]
-    bands = message.shape[1] - state_blocks
+    size = outs[0].shape[1]
+    bands = outs[0].shape[0] - slots * lev // LANES // size
     place = lax.axis_index("fld")
-    fourier_copies, state_copies = [], []
-    for shift in reversed(range(targets)):
-        mine = message.at[place ^ shift]
-        fourier_copies.append(
-            pltpu.make_async_copy(
-                mine.at[pl.ds(0, bands)], outs[shift].at[pl.ds(0, bands)], send_fourier.at[shift]
-            )
-        )
-        state_copies.append(
-            pltpu.make_async_copy(
-                mine.at[pl.ds(bands, state_blocks)],
-                outs[shift].at[pl.ds(bands, state_blocks)],
-                send_state.at[shift],
-            )
-        )
     for tile in range(across):
         patch[tile * lat_pad + lat : (tile + 1) * lat_pad, :] = jnp.zeros(
             (lat_pad - lat, lev * LANES), BF16
@@ -204,9 +184,12 @@
             small[2].wait()
             flat = jnp.concatenate([grid[level] for level in range(lev)], axis=0)
             coeffs = jnp.dot(flat, table[...], preferred_element_type=F32)
-            pack(lev, lat, coeffs, message, padded, rows)
-            for copy in fourier_copies:
-                copy.start()
+            pack(lev, lat, coeffs, padded, rows)
+            height = bands * size
+            for shift, out in enumerate(outs):
+                first = pl.multiple_of((place ^ shift) * height, height)
+                part = rows[pl.ds(first, height), :].astype(BF16)
+                out[:bands] = part.reshape(bands, size, LANES)
         for start in range(0, slots, chunk):
             top = slice(start, start + chunk)
             picked = jnp.dot(
@@ -226,15 +209,11 @@
                 continue
             state = jnp.transpose(total)[:lev].astype(BF16)
             for tile in range(chunk // LANES):
-                block, row = divmod((start // LANES + tile) * lev, message.shape[2])
-                for target in range(targets):
-                    message[target, bands + block, row : row + lev, :] = state[
+                block, row = divmod((start // LANES + tile) * lev, size)
+                for out in outs:
+                    out[bands + block, row : row + lev, :] = state[
                         :, tile * LANES : (tile + 1) * LANES
                     ]
-    for copy in state_copies:
-        copy.start()
-    for copy in fourier_copies + state_copies:
-        copy.wait()
 
 
 def regroup_kernel(n_sec, n_band, *refs):
@@ -393,19 +372,16 @@
             pltpu.VMEM((depth, lev * LANES), BF16),
             pltpu.VMEM((slots, LANES), jnp.int32),
             pltpu.VMEM((slots, depth), BF16),
-            pltpu.VMEM((n_fld, message_blocks, piece, LANES), BF16),
             pltpu.VMEM((LANES, padded_group), F32),
             pltpu.VMEM((group * lev, LANES), F32),
             pltpu.VMEM((slots, LANES), F32),
             pltpu.SemaphoreType.DMA((lev + 3,)),
-            pltpu.SemaphoreType.DMA((n_fld,)),
-            pltpu.SemaphoreType.DMA((n_fld,)),
         ],
         (grid.reshape(lev, lat, lon), block_row, interp, table),
         2 * slots * depth * lev * LANES + 2 * lev * lat * lon * THIRDS * group,
         2 * lev * lat * lon + 2 * slots * LANES,
         "local",
-        HBM,
+        VMEM,
         WHOLE,
     )
     arrived = [exchange(messages[shift], "fld", shift) for shift in reversed(range(1, n_fld))]
@@ -417,13 +393,13 @@
             ((n_band, 2, THIRDS * degrees, LANES), BF16),
             ((spec_bands * flux_rows, flux_rows), BF16),
         ],
-        [VMEM, VMEM, VMEM],
+        [VMEM, VMEM],
         [
             pltpu.VMEM((degrees, (n_band * lat // LANES + 2) * LANES), F32),
             pltpu.VMEM((flux_rows * flux_rows, spec_bands), F32),
             pltpu.VMEM((spec_bands * flux_rows, flux_rows), F32),
         ],
-        (jnp.swapaxes(legendre, 1, 2), jnp.transpose(inverses, (1, 2, 0)), messages[0]),
+        (jnp.swapaxes(legendre, 1, 2), jnp.transpose(inverses, (1, 2, 0))),
         0,
         8 * wave_dev * degrees * n_band * LANES,
         "prepare",

time: 30 us -> 30.6 us (1.020)
  local copies, waits for them, and re-layouts: 0.82 us -> 1.65 us
  Pallas kernels: 14.7 us -> 13.9 us
  waiting for transfers between devices: 2.75 us -> 3.34 us
    unnamed x14 -> x16, local copies, waits for them, and re-layouts: 0.82 us -> 1.65 us
    pallas_call x5, Pallas kernels: 14.7 us -> 13.9 us  [call(): pl.pallas_call(kernel, out_shape=shapes[0] if single else shapes, in_spec...]
    ppermute x4, waiting for transfers between devices: 2.54 us -> 3.13 us  [exchange(): lax.ppermute(value, axis, [(i, i ^ shift) for i in range(lax.axis_size(ax...]
  transfers between devices with their start and end apart: 5 -> 5, of which waited for: 2 -> 3; matrix products, arithmetic and copies ran while one was open for 0% -> 0% of each run, Pallas kernels for 23% -> 23%
where the time goes in v20:
time: 30.6 us; the launch traced here: 30.4 us
  Pallas kernels  13.9 us (45%)
  starting transfers between devices  10.7 us (35%)
  waiting for transfers between devices  3.34 us (11%)
  local copies, waits for them, and re-layouts  1.65 us (5%)
  between operations  0.74 us (2%)
    pallas_call x5, Pallas kernels, call(): pl.pallas_call(kernel, out_shape=shapes[0] if single else shapes, in_spec...  13.9 us
    ppermute x4, starting transfers between devices, exchange(): lax.ppermute(value, axis, [(i, i ^ shift) for i in range(lax.axis_size(ax...  7.31 us
    all_to_all x1, starting transfers between devices, body(): pieces = lax.all_to_all(sent, ('sec', 'band'), 0, 0, tiled=True)  3.41 us
    ppermute x4, waiting for transfers between devices, exchange(): lax.ppermute(value, axis, [(i, i ^ shift) for i in range(lax.axis_size(ax...  3.13 us
    unnamed x16, local copies, waits for them, and re-layouts  1.65 us
  transfers between devices with their start and end apart: 5, of which 3 were waited for; matrix products, arithmetic and copies ran while one was open for 0% of the time, Pallas kernels for 23%

profile of v20, /device:TPU:0, one launch (start us, length us, event | category | flops | bytes accessed | tf_op | source)
XLA Modules:
  0.0 30.4 jit_solution(16136103577371286372)
XLA Ops:
  0.6 0.0 copy-start.2
  0.6 0.9 %copy-done.2 = bf16[1024,128]{1,0:T(8,128)(2,1)S(1)} copy-done((bf16[1024,128]{1,0:T(8,128)(2,1)S(1)}, bf16[1024,128]{1,0:T(8,128)(2,1)}, u32[]{:S(2)}) %copy-start.2) | copy-done | bytes 262168
  1.6 0.7 %copy-done.5 = s32[1024]{0:T(1024)S(1)} copy-done((s32[1024]{0:T(1024)S(1)}, s32[1024]{0:T(1024)}, u32[]{:S(2)}) %copy-start.5) | copy-done | bytes 4120
  2.3 0.0 copy-start.6
  2.3 0.0 copy-start.7
  2.3 5.1 %local.1 = (bf16[6,32,128]{2,1,0:T(8,128)(2,1)S(1)}, bf16[6,32,128]{2,1,0:T(8,128)(2,1)S(1)}, bf16[6,32,128]{2,1,0:T(8,128)(2,1)S(1)}, bf16[6,32,128]{2,1,0:T(8,128)(2,1)S(1)}) custom-call(bf16[8,40,2688]{2,1,0:T(8,128)(2,1)} %bitcast.8, s32[1,1024]{1,0:T(1,128)S(1)} %bitcast.6, bf16[1024,128]{1,0:T(8,128)(2,1)S(1)} %copy-done.2, ...), custom_call_target="tpu_custom_call" | custom-call | flops 2477785088 | bytes 1982464 | tf_op jit(solution)/shard_map/local/pallas_call | solution.py:328
  7.4 5.1 %collective-permute-start = (bf16[6,32,128]{2,1,0:T(8,128)(2,1)S(1)}, bf16[6,32,128]{2,1,0:T(8,128)(2,1)S(1)}, u32[]{:S(2)}, u32[]{:S(2)}) collective-permute-start(bf16[6,32,128]{2,1,0:T(8,128)(2,1)S(1)} %get-tuple-element.11), channel_id=1, source_target_pairs={{0,3},{1,2},{2,1},{3,0},{4,7},{5,6},{6,5},{7,4},{8,11},{9,10},{10,... | collective-permute-start | bytes 147464 | tf_op jit(solution)/shard_map/ppermute | solution.py:341
  12.5 0.0 collective-permute-start.1
  12.5 0.6 %collective-permute-start.2 = (bf16[6,32,128]{2,1,0:T(8,128)(2,1)S(1)}, bf16[6,32,128]{2,1,0:T(8,128)(2,1)S(1)}, u32[]{:S(2)}, u32[]{:S(2)}) collective-permute-start(bf16[6,32,128]{2,1,0:T(8,128)(2,1)S(1)} %get-tuple-element.13), channel_id=1, source_target_pairs={{0,1},{1,0},{2,3},{3,2},{4,5},{5,4},{6,7},{7,6},{8,9},{9,8},{10,11... | collective-permute-start | bytes 147464 | tf_op jit(solution)/shard_map/ppermute | solution.py:341
  13.2 0.0 copy-done
  13.2 0.0 copy-done.1
  13.2 1.2 %prepare.1 = (bf16[4,2,144,128]{3,2,1,0:T(8,128)(2,1)S(1)}, bf16[2048,32]{1,0:T(8,128)(2,1)S(1)}) custom-call(bf16[6,48,160]{2,1,0:T(8,128)(2,1)S(1)} %bitcast.5, bf16[32,32,64]{2,1,0:T(8,128)(2,1)S(1)} %bitcast.4), custom_call_target="tpu_custom_call" | custom-call | bytes 1179648 | tf_op jit(solution)/shard_map/prepare/pallas_call | solution.py:328
  14.4 0.4 %collective-permute-done.refs_0_ = bf16[6,32,128]{2,1,0:T(8,128)(2,1)S(1)} collective-permute-done((bf16[6,32,128]{2,1,0:T(8,128)(2,1)S(1)}, bf16[6,32,128]{2,1,0:T(8,128)(2,1)S(1)}, u32[]{:S(2)}, u32[]{:S(2)}) %collective-permute-start) | collective-permute-done | bytes 49184 | tf_op jit(solution)/shard_map/ppermute | solution.py:341
  14.8 2.8 %collective-permute-done.1.refs_1_ = bf16[6,32,128]{2,1,0:T(8,128)(2,1)S(1)} collective-permute-done((bf16[6,32,128]{2,1,0:T(8,128)(2,1)S(1)}, bf16[6,32,128]{2,1,0:T(8,128)(2,1)S(1)}, u32[]{:S(2)}, u32[]{:S(2)}) %collective-permute-start.1) | collective-permute-done | bytes 49184 | tf_op jit(solution)/shard_map/ppermute | solution.py:341
  17.5 0.0 collective-permute-done.2.refs_2_
  17.5 0.8 %regroup.1 = (bf16[8,4,32,128]{3,2,1,0:T(8,128)(2,1)}, bf16[4,2,32,128]{3,2,1,0:T(8,128)(2,1)S(1)}) custom-call(bf16[6,32,128]{2,1,0:T(8,128)(2,1)S(1)} %collective-permute-done.refs_0_, bf16[6,32,128]{2,1,0:T(8,128)(2,1)S(1)} %collective-permute-done.1.refs_1_, bf16[6,32,128]{2,1,0:T(8,128)(2,1)S(1)} %collective-permute-done.2.refs_2_, ...), custom_call_target="tpu_custom_call" | custom-call | bytes 524288 | tf_op jit(solution)/shard_map/regroup/pallas_call | solution.py:328
  18.4 1.6 %collective-permute-start.3 = (bf16[4,2,32,128]{3,2,1,0:T(8,128)(2,1)S(1)}, bf16[4,2,32,128]{3,2,1,0:T(8,128)(2,1)S(1)}, u32[]{:S(2)}, u32[]{:S(2)}) collective-permute-start(bf16[4,2,32,128]{3,2,1,0:T(8,128)(2,1)S(1)} %get-tuple-element.17.near), channel_id=1, source_target_pairs={{0,16},{16,0},{1,17},{17,1},{2,18},{18,2},{3,19},{19,3},{4,20},{20... | collective-permute-start | bytes 196616 | tf_op jit(solution)/shard_map/ppermute | solution.py:341
  19.9 3.4 %all-to-all-start = ((bf16[8,4,32,128]{3,2,1,0:T(8,128)(2,1)}), bf16[8,4,32,128]{3,2,1,0:T(8,128)(2,1)S(1)}, u32[]{:S(2)}, u32[]{:S(2)}) async-start(bf16[8,4,32,128]{3,2,1,0:T(8,128)(2,1)} %get-tuple-element.15), calls=%async_computation | async-start | bytes 524288 | tf_op jit(solution)/shard_map/all_to_all | solution.py:423
  23.3 0.0 collective-permute-done.3.far
  23.3 0.0 copy-done.3
  23.3 0.0 copy-done.4
  23.4 5.7 %columns.1 = bf16[2,40,2688]{2,1,0:T(8,128)(2,1)} custom-call(s32[4]{0:T(128)S(1)} %copy-done.7, bf16[64,2048]{1,0:T(8,128)(2,1)S(1)} %copy-done.4, bf16[2048,32]{1,0:T(8,128)(2,1)S(1)} %get-tuple-element.16.inverses, s32[1,1024]{1,0:T(1,128)S(1)} %bitcast.7, bf16[1024,128]{1,0:T(8,128)(2,1)S(1)} %copy-done.3, ...), custom_call_target="tpu_custom_call" | custom-call | flops 8589934592 | bytes 2097152 | tf_op jit(solution)/shard_map/columns/pallas_call | solution.py:328
  29.1 0.2 all-to-all-done.pieces
  29.3 1.1 %legendre.1 = bf16[6,2,4,16,48]{4,3,2,1,0:T(8,128)(2,1)} custom-call(bf16[4,2,144,128]{3,2,1,0:T(8,128)(2,1)S(1)} %get-tuple-element.10.refs_4_.weights, bf16[8,4,32,128]{3,2,1,0:T(8,128)(2,1)S(1)} %all-to-all-done.pieces), custom_call_target="tpu_custom_call" | custom-call | flops 75497472 | bytes 262144 | tf_op jit(solution)/shard_map/legendre/pallas_call | solution.py:328
  (7 shorter events, 0.0 us)
Async XLA Ops:
  0.6 1.0 %copy-start.2 = (bf16[1024,128]{1,0:T(8,128)(2,1)S(1)}, bf16[1024,128]{1,0:T(8,128)(2,1)}, u32[]{:S(2)}) copy-start(bf16[1024,128]{1,0:T(8,128)(2,1)} %interp.1) | copy-start | bytes 786436
  1.6 0.7 %copy-start.5 = (s32[1024]{0:T(1024)S(1)}, s32[1024]{0:T(1024)}, u32[]{:S(2)}) copy-start(s32[1024]{0:T(1024)} %param.11) | copy-start | bytes 12292
  2.3 10.9 %copy-start = (bf16[64,32,32]{0,2,1:T(8,128)(2,1)S(1)}, bf16[64,32,32]{0,2,1:T(8,128)(2,1)}, u32[]{:S(2)}) copy-start(bf16[64,32,32]{0,2,1:T(8,128)(2,1)} %param.14) | copy-start | bytes 393220
  2.3 10.9 %copy-start.1 = (bf16[6,160,48]{1,2,0:T(8,128)(2,1)S(1)}, bf16[6,160,48]{1,2,0:T(8,128)(2,1)}, u32[]{:S(2)}) copy-start(bf16[6,160,48]{1,2,0:T(8,128)(2,1)} %param.9) | copy-start | bytes 276484
  2.3 21.1 %copy-start.3 = (bf16[1024,128]{1,0:T(8,128)(2,1)S(1)}, bf16[1024,128]{1,0:T(8,128)(2,1)}, u32[]{:S(2)}) copy-start(bf16[1024,128]{1,0:T(8,128)(2,1)} %interp.1) | copy-start | bytes 786436
  2.3 21.1 %copy-start.4 = (bf16[64,2048]{1,0:T(8,128)(2,1)S(1)}, bf16[64,2048]{1,0:T(8,128)(2,1)}, u32[]{:S(2)}) copy-start(bf16[64,2048]{1,0:T(8,128)(2,1)} %weights.1) | copy-start | bytes 786436
  2.3 21.1 %copy-start.6 = (s32[1024]{0:T(1024)S(1)}, s32[1024]{0:T(1024)}, u32[]{:S(2)}) copy-start(s32[1024]{0:T(1024)} %param.11) | copy-start | bytes 12292
  2.3 21.1 %copy-start.7 = (s32[4]{0:T(128)S(1)}, s32[4]{0:T(128)}, u32[]{:S(2)}) copy-start(s32[4]{0:T(128)} %counts.1) | copy-start | bytes 52
  7.4 7.3 %collective-permute-start = (bf16[6,32,128]{2,1,0:T(8,128)(2,1)S(1)}, bf16[6,32,128]{2,1,0:T(8,128)(2,1)S(1)}, u32[]{:S(2)}, u32[]{:S(2)}) collective-permute-start(bf16[6,32,128]{2,1,0:T(8,128)(2,1)S(1)} %get-tuple-element.11), channel_id=1, source_target_pairs={{0,3},{1,2},{2,1},{3,0},{4,7},{5,6},{6,5},{7,4},{8,11},{9,10},{10,... | collective-permute-start | bytes 147464 | tf_op jit(solution)/shard_map/ppermute | solution.py:341
  12.5 5.0 %collective-permute-start.1 = (bf16[6,32,128]{2,1,0:T(8,128)(2,1)S(1)}, bf16[6,32,128]{2,1,0:T(8,128)(2,1)S(1)}, u32[]{:S(2)}, u32[]{:S(2)}) collective-permute-start(bf16[6,32,128]{2,1,0:T(8,128)(2,1)S(1)} %get-tuple-element.12), channel_id=1, source_target_pairs={{0,2},{1,3},{2,0},{3,1},{4,6},{5,7},{6,4},{7,5},{8,10},{9,11},{10,... | collective-permute-start | bytes 147464 | tf_op jit(solution)/shard_map/ppermute | solution.py:341
  12.5 5.0 %collective-permute-start.2 = (bf16[6,32,128]{2,1,0:T(8,128)(2,1)S(1)}, bf16[6,32,128]{2,1,0:T(8,128)(2,1)S(1)}, u32[]{:S(2)}, u32[]{:S(2)}) collective-permute-start(bf16[6,32,128]{2,1,0:T(8,128)(2,1)S(1)} %get-tuple-element.13), channel_id=1, source_target_pairs={{0,1},{1,0},{2,3},{3,2},{4,5},{5,4},{6,7},{7,6},{8,9},{9,8},{10,11... | collective-permute-start | bytes 147464 | tf_op jit(solution)/shard_map/ppermute | solution.py:341
  18.4 5.0 %collective-permute-start.3 = (bf16[4,2,32,128]{3,2,1,0:T(8,128)(2,1)S(1)}, bf16[4,2,32,128]{3,2,1,0:T(8,128)(2,1)S(1)}, u32[]{:S(2)}, u32[]{:S(2)}) collective-permute-start(bf16[4,2,32,128]{3,2,1,0:T(8,128)(2,1)S(1)} %get-tuple-element.17.near), channel_id=1, source_target_pairs={{0,16},{16,0},{1,17},{17,1},{2,18},{18,2},{3,19},{19,3},{4,20},{20... | collective-permute-start | bytes 196616 | tf_op jit(solution)/shard_map/ppermute | solution.py:341
  19.9 9.4 %all-to-all-start = ((bf16[8,4,32,128]{3,2,1,0:T(8,128)(2,1)}), bf16[8,4,32,128]{3,2,1,0:T(8,128)(2,1)S(1)}, u32[]{:S(2)}, u32[]{:S(2)}) async-start(bf16[8,4,32,128]{3,2,1,0:T(8,128)(2,1)} %get-tuple-element.15), calls=%async_computation | async-start | bytes 524288 | tf_op jit(solution)/shard_map/all_to_all | solution.py:423

commit v21 on v20

--- a/solution.py
+++ b/solution.py
@@ -377,7 +377,12 @@
             pltpu.VMEM((slots, LANES), F32),
             pltpu.SemaphoreType.DMA((lev + 3,)),
         ],
-        (grid.reshape(lev, lat, lon), block_row, interp, table),
+        (
+            pltpu.with_memory_space_constraint(grid.reshape(lev, lat, lon), pltpu.HBM),
+            pltpu.with_memory_space_constraint(block_row, pltpu.HBM),
+            pltpu.with_memory_space_constraint(interp, pltpu.HBM),
+            table,
+        ),
         2 * slots * depth * lev * LANES + 2 * lev * lat * lon * THIRDS * group,
         2 * lev * lat * lon + 2 * slots * LANES,
         "local",

time: 30.6 us -> 30.4 us (level)
    unnamed x16 -> x14, local copies, waits for them, and re-layouts: 1.65 us -> 1.36 us
where the time goes in v21:
time: 30.4 us; the launch traced here: 30.2 us
  Pallas kernels  14 us (46%)
  starting transfers between devices  10.7 us (35%)
  waiting for transfers between devices  3.34 us (11%)
  local copies, waits for them, and re-layouts  1.36 us (4%)
  between operations  0.74 us (2%)
    pallas_call x5, Pallas kernels, call(): pl.pallas_call(kernel, out_shape=shapes[0] if single else shapes, in_spec...  14 us
    ppermute x4, starting transfers between devices, exchange(): lax.ppermute(value, axis, [(i, i ^ shift) for i in range(lax.axis_size(ax...  7.31 us
    all_to_all x1, starting transfers between devices, body(): pieces = lax.all_to_all(sent, ('sec', 'band'), 0, 0, tiled=True)  3.41 us
    ppermute x4, waiting for transfers between devices, exchange(): lax.ppermute(value, axis, [(i, i ^ shift) for i in range(lax.axis_size(ax...  3.14 us
    unnamed x14, local copies, waits for them, and re-layouts  1.36 us
  transfers between devices with their start and end apart: 5, of which 3 were waited for; matrix products, arithmetic and copies ran while one was open for 0% of the time, Pallas kernels for 23%

profile of v21, /device:TPU:0, one launch (start us, length us, event | category | flops | bytes accessed | tf_op | source)
XLA Modules:
  0.0 30.2 jit_solution(9054502109949344048)
XLA Ops:
  0.6 0.0 copy-start.6
  0.6 1.3 %copy-done.6 = bf16[2688,192]{1,0:T(8,128)(2,1)S(1)} copy-done((bf16[2688,192]{1,0:T(8,128)(2,1)S(1)}, bf16[2688,192]{1,0:T(8,128)(2,1)}, u32[]{:S(2)}) %copy-start.6) | copy-done | bytes 1032216
  2.0 0.0 copy-start.4
  2.0 0.0 copy-start.5
  2.0 5.2 %local.1 = (bf16[6,32,128]{2,1,0:T(8,128)(2,1)S(1)}, bf16[6,32,128]{2,1,0:T(8,128)(2,1)S(1)}, bf16[6,32,128]{2,1,0:T(8,128)(2,1)S(1)}, bf16[6,32,128]{2,1,0:T(8,128)(2,1)S(1)}) custom-call(bf16[8,40,2688]{2,1,0:T(8,128)(2,1)} %bitcast.8, s32[1,1024]{1,0:T(1,128)} %bitcast.6, bf16[1024,128]{1,0:T(8,128)(2,1)} %interp.1, bf16[2688,192]{1,0:T(8,128)(2,1)S(1)} %copy-done.6), custom_call_target="tpu_custom_call" | custom-call | flops 2477785088 | bytes 1982464 | tf_op jit(solution)/shard_map/local/pallas_call | solution.py:328
  7.2 5.1 %collective-permute-start = (bf16[6,32,128]{2,1,0:T(8,128)(2,1)S(1)}, bf16[6,32,128]{2,1,0:T(8,128)(2,1)S(1)}, u32[]{:S(2)}, u32[]{:S(2)}) collective-permute-start(bf16[6,32,128]{2,1,0:T(8,128)(2,1)S(1)} %get-tuple-element.11), channel_id=1, source_target_pairs={{0,3},{1,2},{2,1},{3,0},{4,7},{5,6},{6,5},{7,4},{8,11},{9,10},{10,... | collective-permute-start | bytes 147464 | tf_op jit(solution)/shard_map/ppermute | solution.py:341
  12.3 0.0 collective-permute-start.1
  12.3 0.6 %collective-permute-start.2 = (bf16[6,32,128]{2,1,0:T(8,128)(2,1)S(1)}, bf16[6,32,128]{2,1,0:T(8,128)(2,1)S(1)}, u32[]{:S(2)}, u32[]{:S(2)}) collective-permute-start(bf16[6,32,128]{2,1,0:T(8,128)(2,1)S(1)} %get-tuple-element.13), channel_id=1, source_target_pairs={{0,1},{1,0},{2,3},{3,2},{4,5},{5,4},{6,7},{7,6},{8,9},{9,8},{10,11... | collective-permute-start | bytes 147464 | tf_op jit(solution)/shard_map/ppermute | solution.py:341
  13.0 0.0 copy-done
  13.0 0.0 copy-done.1
  13.0 1.2 %prepare.1 = (bf16[4,2,144,128]{3,2,1,0:T(8,128)(2,1)S(1)}, bf16[2048,32]{1,0:T(8,128)(2,1)S(1)}) custom-call(bf16[6,48,160]{2,1,0:T(8,128)(2,1)S(1)} %bitcast.5, bf16[32,32,64]{2,1,0:T(8,128)(2,1)S(1)} %bitcast.4), custom_call_target="tpu_custom_call" | custom-call | bytes 1179648 | tf_op jit(solution)/shard_map/prepare/pallas_call | solution.py:328
  14.2 0.4 %collective-permute-done.refs_0_ = bf16[6,32,128]{2,1,0:T(8,128)(2,1)S(1)} collective-permute-done((bf16[6,32,128]{2,1,0:T(8,128)(2,1)S(1)}, bf16[6,32,128]{2,1,0:T(8,128)(2,1)S(1)}, u32[]{:S(2)}, u32[]{:S(2)}) %collective-permute-start) | collective-permute-done | bytes 49184 | tf_op jit(solution)/shard_map/ppermute | solution.py:341
  14.6 2.8 %collective-permute-done.1.refs_1_ = bf16[6,32,128]{2,1,0:T(8,128)(2,1)S(1)} collective-permute-done((bf16[6,32,128]{2,1,0:T(8,128)(2,1)S(1)}, bf16[6,32,128]{2,1,0:T(8,128)(2,1)S(1)}, u32[]{:S(2)}, u32[]{:S(2)}) %collective-permute-start.1) | collective-permute-done | bytes 49184 | tf_op jit(solution)/shard_map/ppermute | solution.py:341
  17.3 0.0 collective-permute-done.2.refs_2_
  17.3 0.8 %regroup.1 = (bf16[8,4,32,128]{3,2,1,0:T(8,128)(2,1)}, bf16[4,2,32,128]{3,2,1,0:T(8,128)(2,1)S(1)}) custom-call(bf16[6,32,128]{2,1,0:T(8,128)(2,1)S(1)} %collective-permute-done.refs_0_, bf16[6,32,128]{2,1,0:T(8,128)(2,1)S(1)} %collective-permute-done.1.refs_1_, bf16[6,32,128]{2,1,0:T(8,128)(2,1)S(1)} %collective-permute-done.2.refs_2_, ...), custom_call_target="tpu_custom_call" | custom-call | bytes 524288 | tf_op jit(solution)/shard_map/regroup/pallas_call | solution.py:328
  18.2 1.6 %collective-permute-start.3 = (bf16[4,2,32,128]{3,2,1,0:T(8,128)(2,1)S(1)}, bf16[4,2,32,128]{3,2,1,0:T(8,128)(2,1)S(1)}, u32[]{:S(2)}, u32[]{:S(2)}) collective-permute-start(bf16[4,2,32,128]{3,2,1,0:T(8,128)(2,1)S(1)} %get-tuple-element.17.near), channel_id=1, source_target_pairs={{0,16},{16,0},{1,17},{17,1},{2,18},{18,2},{3,19},{19,3},{4,20},{20... | collective-permute-start | bytes 196616 | tf_op jit(solution)/shard_map/ppermute | solution.py:341
  19.7 3.4 %all-to-all-start = ((bf16[8,4,32,128]{3,2,1,0:T(8,128)(2,1)}), bf16[8,4,32,128]{3,2,1,0:T(8,128)(2,1)S(1)}, u32[]{:S(2)}, u32[]{:S(2)}) async-start(bf16[8,4,32,128]{3,2,1,0:T(8,128)(2,1)} %get-tuple-element.15), calls=%async_computation | async-start | bytes 524288 | tf_op jit(solution)/shard_map/all_to_all | solution.py:428
  23.1 0.0 collective-permute-done.3.far
  23.2 0.0 copy-done.2
  23.2 0.0 copy-done.3
  23.2 0.0 copy-done.4
  23.2 5.7 %columns.1 = bf16[2,40,2688]{2,1,0:T(8,128)(2,1)} custom-call(s32[4]{0:T(128)S(1)} %copy-done.5, bf16[64,2048]{1,0:T(8,128)(2,1)S(1)} %copy-done.3, bf16[2048,32]{1,0:T(8,128)(2,1)S(1)} %get-tuple-element.16.inverses, s32[1,1024]{1,0:T(1,128)S(1)} %bitcast.7, bf16[1024,128]{1,0:T(8,128)(2,1)S(1)} %copy-done.2, ...), custom_call_target="tpu_custom_call" | custom-call | flops 8589934592 | bytes 2097152 | tf_op jit(solution)/shard_map/columns/pallas_call | solution.py:328
  28.9 0.2 all-to-all-done.pieces
  29.1 1.0 %legendre.1 = bf16[6,2,4,16,48]{4,3,2,1,0:T(8,128)(2,1)} custom-call(bf16[4,2,144,128]{3,2,1,0:T(8,128)(2,1)S(1)} %get-tuple-element.10.refs_4_.weights, bf16[8,4,32,128]{3,2,1,0:T(8,128)(2,1)S(1)} %all-to-all-done.pieces), custom_call_target="tpu_custom_call" | custom-call | flops 75497472 | bytes 262144 | tf_op jit(solution)/shard_map/legendre/pallas_call | solution.py:328
  (5 shorter events, 0.0 us)
Async XLA Ops:
  0.6 1.3 %copy-start.6 = (bf16[2688,192]{1,0:T(8,128)(2,1)S(1)}, bf16[2688,192]{1,0:T(8,128)(2,1)}, u32[]{:S(2)}) copy-start(bf16[2688,192]{1,0:T(8,128)(2,1)} %constant.2.clone.table_hbm) | copy-start | bytes 3096580
  2.0 11.0 %copy-start = (bf16[64,32,32]{0,2,1:T(8,128)(2,1)S(1)}, bf16[64,32,32]{0,2,1:T(8,128)(2,1)}, u32[]{:S(2)}) copy-start(bf16[64,32,32]{0,2,1:T(8,128)(2,1)} %param.14) | copy-start | bytes 393220
  2.0 11.0 %copy-start.1 = (bf16[6,160,48]{1,2,0:T(8,128)(2,1)S(1)}, bf16[6,160,48]{1,2,0:T(8,128)(2,1)}, u32[]{:S(2)}) copy-start(bf16[6,160,48]{1,2,0:T(8,128)(2,1)} %param.9) | copy-start | bytes 276484
  2.0 21.2 %copy-start.2 = (bf16[1024,128]{1,0:T(8,128)(2,1)S(1)}, bf16[1024,128]{1,0:T(8,128)(2,1)}, u32[]{:S(2)}) copy-start(bf16[1024,128]{1,0:T(8,128)(2,1)} %interp.1) | copy-start | bytes 786436
  2.0 21.2 %copy-start.3 = (bf16[64,2048]{1,0:T(8,128)(2,1)S(1)}, bf16[64,2048]{1,0:T(8,128)(2,1)}, u32[]{:S(2)}) copy-start(bf16[64,2048]{1,0:T(8,128)(2,1)} %weights.1) | copy-start | bytes 786436
  2.0 21.2 %copy-start.4 = (s32[1024]{0:T(1024)S(1)}, s32[1024]{0:T(1024)}, u32[]{:S(2)}) copy-start(s32[1024]{0:T(1024)} %param.11) | copy-start | bytes 12292
  2.0 21.2 %copy-start.5 = (s32[4]{0:T(128)S(1)}, s32[4]{0:T(128)}, u32[]{:S(2)}) copy-start(s32[4]{0:T(128)} %counts.1) | copy-start | bytes 52
  7.2 7.3 %collective-permute-start = (bf16[6,32,128]{2,1,0:T(8,128)(2,1)S(1)}, bf16[6,32,128]{2,1,0:T(8,128)(2,1)S(1)}, u32[]{:S(2)}, u32[]{:S(2)}) collective-permute-start(bf16[6,32,128]{2,1,0:T(8,128)(2,1)S(1)} %get-tuple-element.11), channel_id=1, source_target_pairs={{0,3},{1,2},{2,1},{3,0},{4,7},{5,6},{6,5},{7,4},{8,11},{9,10},{10,... | collective-permute-start | bytes 147464 | tf_op jit(solution)/shard_map/ppermute | solution.py:341
  12.3 5.0 %collective-permute-start.1 = (bf16[6,32,128]{2,1,0:T(8,128)(2,1)S(1)}, bf16[6,32,128]{2,1,0:T(8,128)(2,1)S(1)}, u32[]{:S(2)}, u32[]{:S(2)}) collective-permute-start(bf16[6,32,128]{2,1,0:T(8,128)(2,1)S(1)} %get-tuple-element.12), channel_id=1, source_target_pairs={{0,2},{1,3},{2,0},{3,1},{4,6},{5,7},{6,4},{7,5},{8,10},{9,11},{10,... | collective-permute-start | bytes 147464 | tf_op jit(solution)/shard_map/ppermute | solution.py:341
  12.3 5.0 %collective-permute-start.2 = (bf16[6,32,128]{2,1,0:T(8,128)(2,1)S(1)}, bf16[6,32,128]{2,1,0:T(8,128)(2,1)S(1)}, u32[]{:S(2)}, u32[]{:S(2)}) collective-permute-start(bf16[6,32,128]{2,1,0:T(8,128)(2,1)S(1)} %get-tuple-element.13), channel_id=1, source_target_pairs={{0,1},{1,0},{2,3},{3,2},{4,5},{5,4},{6,7},{7,6},{8,9},{9,8},{10,11... | collective-permute-start | bytes 147464 | tf_op jit(solution)/shard_map/ppermute | solution.py:341
  18.2 5.0 %collective-permute-start.3 = (bf16[4,2,32,128]{3,2,1,0:T(8,128)(2,1)S(1)}, bf16[4,2,32,128]{3,2,1,0:T(8,128)(2,1)S(1)}, u32[]{:S(2)}, u32[]{:S(2)}) collective-permute-start(bf16[4,2,32,128]{3,2,1,0:T(8,128)(2,1)S(1)} %get-tuple-element.17.near), channel_id=1, source_target_pairs={{0,16},{16,0},{1,17},{17,1},{2,18},{18,2},{3,19},{19,3},{4,20},{20... | collective-permute-start | bytes 196616 | tf_op jit(solution)/shard_map/ppermute | solution.py:341
  19.7 9.4 %all-to-all-start = ((bf16[8,4,32,128]{3,2,1,0:T(8,128)(2,1)}), bf16[8,4,32,128]{3,2,1,0:T(8,128)(2,1)S(1)}, u32[]{:S(2)}, u32[]{:S(2)}) async-start(bf16[8,4,32,128]{3,2,1,0:T(8,128)(2,1)} %get-tuple-element.15), calls=%async_computation | async-start | bytes 524288 | tf_op jit(solution)/shard_map/all_to_all | solution.py:428

commit v22 on v20

--- a/solution.py
+++ b/solution.py
@@ -377,7 +377,10 @@
             pltpu.VMEM((slots, LANES), F32),
             pltpu.SemaphoreType.DMA((lev + 3,)),
         ],
-        (grid.reshape(lev, lat, lon), block_row, interp, table),
+        [
+            pltpu.with_memory_space_constraint(value, pltpu.HBM)
+            for value in (grid.reshape(lev, lat, lon), block_row, interp, table)
+        ],
         2 * slots * depth * lev * LANES + 2 * lev * lat * lon * THIRDS * group,
         2 * lev * lat * lon + 2 * slots * LANES,
         "local",

time: 30.6 us -> 29.1 us (0.951)
  local copies, waits for them, and re-layouts: 1.65 us -> 0.03 us
    unnamed x16 -> x12, local copies, waits for them, and re-layouts: 1.65 us -> 0.03 us
  transfers between devices with their start and end apart: 5 -> 5, of which waited for: 3 -> 3; matrix products, arithmetic and copies ran while one was open for 0% -> 0% of each run, Pallas kernels for 23% -> 24%
where the time goes in v22:
time: 29.1 us; the launch traced here: 28.9 us
  Pallas kernels  14 us (48%)
  starting transfers between devices  10.7 us (37%)
  waiting for transfers between devices  3.33 us (11%)
  between operations  0.76 us (3%)
    pallas_call x5, Pallas kernels, call(): pl.pallas_call(kernel, out_shape=shapes[0] if single else shapes, in_spec...  14 us
    ppermute x4, starting transfers between devices, exchange(): lax.ppermute(value, axis, [(i, i ^ shift) for i in range(lax.axis_size(ax...  7.32 us
    all_to_all x1, starting transfers between devices, body(): pieces = lax.all_to_all(sent, ('sec', 'band'), 0, 0, tiled=True)  3.41 us
    ppermute x4, waiting for transfers between devices, exchange(): lax.ppermute(value, axis, [(i, i ^ shift) for i in range(lax.axis_size(ax...  3.14 us
  transfers between devices with their start and end apart: 5, of which 3 were waited for; matrix products, arithmetic and copies ran while one was open for 0% of the time, Pallas kernels for 24%

profile of v22, /device:TPU:0, one launch (start us, length us, event | category | flops | bytes accessed | tf_op | source)
XLA Modules:
  0.0 28.9 jit_solution(3825157314533674475)
XLA Ops:
  0.6 0.0 copy-start
  0.6 0.0 copy-start.1
  0.7 0.0 copy-start.2
  0.7 0.0 copy-start.3
  0.7 0.0 copy-start.4
  0.7 0.0 copy-start.5
  0.7 5.2 %local.1 = (bf16[6,32,128]{2,1,0:T(8,128)(2,1)S(1)}, bf16[6,32,128]{2,1,0:T(8,128)(2,1)S(1)}, bf16[6,32,128]{2,1,0:T(8,128)(2,1)S(1)}, bf16[6,32,128]{2,1,0:T(8,128)(2,1)S(1)}) custom-call(bf16[8,40,2688]{2,1,0:T(8,128)(2,1)} %bitcast.8, s32[1,1024]{1,0:T(1,128)} %bitcast.6, bf16[1024,128]{1,0:T(8,128)(2,1)} %interp.1, bf16[2688,192]{1,0:T(8,128)(2,1)} %constant.2.clone.table_hbm), custom_call_target="tpu_custom_call" | custom-call | flops 2477785088 | bytes 1982464 | tf_op jit(solution)/shard_map/local/pallas_call | solution.py:328
  5.9 5.1 %collective-permute-start = (bf16[6,32,128]{2,1,0:T(8,128)(2,1)S(1)}, bf16[6,32,128]{2,1,0:T(8,128)(2,1)S(1)}, u32[]{:S(2)}, u32[]{:S(2)}) collective-permute-start(bf16[6,32,128]{2,1,0:T(8,128)(2,1)S(1)} %get-tuple-element.11), channel_id=1, source_target_pairs={{0,3},{1,2},{2,1},{3,0},{4,7},{5,6},{6,5},{7,4},{8,11},{9,10},{10,... | collective-permute-start | bytes 147464 | tf_op jit(solution)/shard_map/ppermute | solution.py:341
  11.0 0.0 collective-permute-start.1
  11.0 0.6 %collective-permute-start.2 = (bf16[6,32,128]{2,1,0:T(8,128)(2,1)S(1)}, bf16[6,32,128]{2,1,0:T(8,128)(2,1)S(1)}, u32[]{:S(2)}, u32[]{:S(2)}) collective-permute-start(bf16[6,32,128]{2,1,0:T(8,128)(2,1)S(1)} %get-tuple-element.13), channel_id=1, source_target_pairs={{0,1},{1,0},{2,3},{3,2},{4,5},{5,4},{6,7},{7,6},{8,9},{9,8},{10,11... | collective-permute-start | bytes 147464 | tf_op jit(solution)/shard_map/ppermute | solution.py:341
  11.7 0.0 copy-done
  11.7 0.0 copy-done.1
  11.7 1.2 %prepare.1 = (bf16[4,2,144,128]{3,2,1,0:T(8,128)(2,1)S(1)}, bf16[2048,32]{1,0:T(8,128)(2,1)S(1)}) custom-call(bf16[6,48,160]{2,1,0:T(8,128)(2,1)S(1)} %bitcast.5, bf16[32,32,64]{2,1,0:T(8,128)(2,1)S(1)} %bitcast.4), custom_call_target="tpu_custom_call" | custom-call | bytes 1179648 | tf_op jit(solution)/shard_map/prepare/pallas_call | solution.py:328
  12.9 0.4 %collective-permute-done.refs_0_ = bf16[6,32,128]{2,1,0:T(8,128)(2,1)S(1)} collective-permute-done((bf16[6,32,128]{2,1,0:T(8,128)(2,1)S(1)}, bf16[6,32,128]{2,1,0:T(8,128)(2,1)S(1)}, u32[]{:S(2)}, u32[]{:S(2)}) %collective-permute-start) | collective-permute-done | bytes 49184 | tf_op jit(solution)/shard_map/ppermute | solution.py:341
  13.3 2.8 %collective-permute-done.1.refs_1_ = bf16[6,32,128]{2,1,0:T(8,128)(2,1)S(1)} collective-permute-done((bf16[6,32,128]{2,1,0:T(8,128)(2,1)S(1)}, bf16[6,32,128]{2,1,0:T(8,128)(2,1)S(1)}, u32[]{:S(2)}, u32[]{:S(2)}) %collective-permute-start.1) | collective-permute-done | bytes 49184 | tf_op jit(solution)/shard_map/ppermute | solution.py:341
  16.0 0.0 collective-permute-done.2.refs_2_
  16.0 0.8 %regroup.1 = (bf16[8,4,32,128]{3,2,1,0:T(8,128)(2,1)}, bf16[4,2,32,128]{3,2,1,0:T(8,128)(2,1)S(1)}) custom-call(bf16[6,32,128]{2,1,0:T(8,128)(2,1)S(1)} %collective-permute-done.refs_0_, bf16[6,32,128]{2,1,0:T(8,128)(2,1)S(1)} %collective-permute-done.1.refs_1_, bf16[6,32,128]{2,1,0:T(8,128)(2,1)S(1)} %collective-permute-done.2.refs_2_, ...), custom_call_target="tpu_custom_call" | custom-call | bytes 524288 | tf_op jit(solution)/shard_map/regroup/pallas_call | solution.py:328
  16.9 1.6 %collective-permute-start.3 = (bf16[4,2,32,128]{3,2,1,0:T(8,128)(2,1)S(1)}, bf16[4,2,32,128]{3,2,1,0:T(8,128)(2,1)S(1)}, u32[]{:S(2)}, u32[]{:S(2)}) collective-permute-start(bf16[4,2,32,128]{3,2,1,0:T(8,128)(2,1)S(1)} %get-tuple-element.17.near), channel_id=1, source_target_pairs={{0,16},{16,0},{1,17},{17,1},{2,18},{18,2},{3,19},{19,3},{4,20},{20... | collective-permute-start | bytes 196616 | tf_op jit(solution)/shard_map/ppermute | solution.py:341
  18.4 3.4 %all-to-all-start = ((bf16[8,4,32,128]{3,2,1,0:T(8,128)(2,1)}), bf16[8,4,32,128]{3,2,1,0:T(8,128)(2,1)S(1)}, u32[]{:S(2)}, u32[]{:S(2)}) async-start(bf16[8,4,32,128]{3,2,1,0:T(8,128)(2,1)} %get-tuple-element.15), calls=%async_computation | async-start | bytes 524288 | tf_op jit(solution)/shard_map/all_to_all | solution.py:426
  21.8 0.0 collective-permute-done.3.far
  21.8 0.0 copy-done.2
  21.9 5.7 %columns.1 = bf16[2,40,2688]{2,1,0:T(8,128)(2,1)} custom-call(s32[4]{0:T(128)S(1)} %copy-done.5, bf16[64,2048]{1,0:T(8,128)(2,1)S(1)} %copy-done.3, bf16[2048,32]{1,0:T(8,128)(2,1)S(1)} %get-tuple-element.16.inverses, s32[1,1024]{1,0:T(1,128)S(1)} %bitcast.7, bf16[1024,128]{1,0:T(8,128)(2,1)S(1)} %copy-done.2, ...), custom_call_target="tpu_custom_call" | custom-call | flops 8589934592 | bytes 2097152 | tf_op jit(solution)/shard_map/columns/pallas_call | solution.py:328
  27.6 0.2 all-to-all-done.pieces
  27.8 1.0 %legendre.1 = bf16[6,2,4,16,48]{4,3,2,1,0:T(8,128)(2,1)} custom-call(bf16[4,2,144,128]{3,2,1,0:T(8,128)(2,1)S(1)} %get-tuple-element.10.refs_4_.weights, bf16[8,4,32,128]{3,2,1,0:T(8,128)(2,1)S(1)} %all-to-all-done.pieces), custom_call_target="tpu_custom_call" | custom-call | flops 75497472 | bytes 262144 | tf_op jit(solution)/shard_map/legendre/pallas_call | solution.py:328
  (3 shorter events, 0.0 us)
Async XLA Ops:
  0.6 11.0 %copy-start = (bf16[64,32,32]{0,2,1:T(8,128)(2,1)S(1)}, bf16[64,32,32]{0,2,1:T(8,128)(2,1)}, u32[]{:S(2)}) copy-start(bf16[64,32,32]{0,2,1:T(8,128)(2,1)} %param.14) | copy-start | bytes 393220
  0.6 11.0 %copy-start.1 = (bf16[6,160,48]{1,2,0:T(8,128)(2,1)S(1)}, bf16[6,160,48]{1,2,0:T(8,128)(2,1)}, u32[]{:S(2)}) copy-start(bf16[6,160,48]{1,2,0:T(8,128)(2,1)} %param.9) | copy-start | bytes 276484
  0.7 21.2 %copy-start.2 = (bf16[1024,128]{1,0:T(8,128)(2,1)S(1)}, bf16[1024,128]{1,0:T(8,128)(2,1)}, u32[]{:S(2)}) copy-start(bf16[1024,128]{1,0:T(8,128)(2,1)} %interp.1) | copy-start | bytes 786436
  0.7 21.2 %copy-start.3 = (bf16[64,2048]{1,0:T(8,128)(2,1)S(1)}, bf16[64,2048]{1,0:T(8,128)(2,1)}, u32[]{:S(2)}) copy-start(bf16[64,2048]{1,0:T(8,128)(2,1)} %weights.1) | copy-start | bytes 786436
  0.7 21.2 %copy-start.4 = (s32[1024]{0:T(1024)S(1)}, s32[1024]{0:T(1024)}, u32[]{:S(2)}) copy-start(s32[1024]{0:T(1024)} %param.11) | copy-start | bytes 12292
  0.7 21.2 %copy-start.5 = (s32[4]{0:T(128)S(1)}, s32[4]{0:T(128)}, u32[]{:S(2)}) copy-start(s32[4]{0:T(128)} %counts.1) | copy-start | bytes 52
  5.9 7.3 %collective-permute-start = (bf16[6,32,128]{2,1,0:T(8,128)(2,1)S(1)}, bf16[6,32,128]{2,1,0:T(8,128)(2,1)S(1)}, u32[]{:S(2)}, u32[]{:S(2)}) collective-permute-start(bf16[6,32,128]{2,1,0:T(8,128)(2,1)S(1)} %get-tuple-element.11), channel_id=1, source_target_pairs={{0,3},{1,2},{2,1},{3,0},{4,7},{5,6},{6,5},{7,4},{8,11},{9,10},{10,... | collective-permute-start | bytes 147464 | tf_op jit(solution)/shard_map/ppermute | solution.py:341
  11.0 5.0 %collective-permute-start.1 = (bf16[6,32,128]{2,1,0:T(8,128)(2,1)S(1)}, bf16[6,32,128]{2,1,0:T(8,128)(2,1)S(1)}, u32[]{:S(2)}, u32[]{:S(2)}) collective-permute-start(bf16[6,32,128]{2,1,0:T(8,128)(2,1)S(1)} %get-tuple-element.12), channel_id=1, source_target_pairs={{0,2},{1,3},{2,0},{3,1},{4,6},{5,7},{6,4},{7,5},{8,10},{9,11},{10,... | collective-permute-start | bytes 147464 | tf_op jit(solution)/shard_map/ppermute | solution.py:341
  11.0 5.0 %collective-permute-start.2 = (bf16[6,32,128]{2,1,0:T(8,128)(2,1)S(1)}, bf16[6,32,128]{2,1,0:T(8,128)(2,1)S(1)}, u32[]{:S(2)}, u32[]{:S(2)}) collective-permute-start(bf16[6,32,128]{2,1,0:T(8,128)(2,1)S(1)} %get-tuple-element.13), channel_id=1, source_target_pairs={{0,1},{1,0},{2,3},{3,2},{4,5},{5,4},{6,7},{7,6},{8,9},{9,8},{10,11... | collective-permute-start | bytes 147464 | tf_op jit(solution)/shard_map/ppermute | solution.py:341
  16.9 5.0 %collective-permute-start.3 = (bf16[4,2,32,128]{3,2,1,0:T(8,128)(2,1)S(1)}, bf16[4,2,32,128]{3,2,1,0:T(8,128)(2,1)S(1)}, u32[]{:S(2)}, u32[]{:S(2)}) collective-permute-start(bf16[4,2,32,128]{3,2,1,0:T(8,128)(2,1)S(1)} %get-tuple-element.17.near), channel_id=1, source_target_pairs={{0,16},{16,0},{1,17},{17,1},{2,18},{18,2},{3,19},{19,3},{4,20},{20... | collective-permute-start | bytes 196616 | tf_op jit(solution)/shard_map/ppermute | solution.py:341
  18.4 9.4 %all-to-all-start = ((bf16[8,4,32,128]{3,2,1,0:T(8,128)(2,1)}), bf16[8,4,32,128]{3,2,1,0:T(8,128)(2,1)S(1)}, u32[]{:S(2)}, u32[]{:S(2)}) async-start(bf16[8,4,32,128]{3,2,1,0:T(8,128)(2,1)} %get-tuple-element.15), calls=%async_computation | async-start | bytes 524288 | tf_op jit(solution)/shard_map/all_to_all | solution.py:426

commit v23 on v22

--- a/solution.py
+++ b/solution.py
@@ -216,13 +216,13 @@
                     ]
 
 
-def regroup_kernel(n_sec, n_band, *refs):
+def regroup_kernel(n_sec, n_band, shifts, *refs):
     pieces, (_, out, out_state, sems) = refs[:-4], refs[-4:]
     blocks = out_state.shape[1]
     place = lax.axis_index("fld")
     copies = []
-    for i, piece in enumerate(pieces):
-        fld = place ^ (len(pieces) - 1 - i)
+    for shift, piece in zip(shifts, pieces):
+        fld = place ^ shift
         copies.append((piece.at[pl.ds(n_band, blocks)], out_state.at[fld]))
         for sec in range(n_sec):
             copies.append(
@@ -387,7 +387,9 @@
         VMEM,
         WHOLE,
     )
-    arrived = [exchange(messages[shift], "fld", shift) for shift in reversed(range(1, n_fld))]
+    half = n_fld // 2
+    shifts = [half] + list(range(n_fld - 1, half, -1)) + list(range(half - 1, 0, -1))
+    arrived = [exchange(messages[shift], "fld", shift) for shift in shifts]
     arrived.append(messages[0])
     spec_bands, flux_rows, _ = inverses.shape
     basis, inverse_rows = call(
@@ -408,7 +410,7 @@
         "prepare",
     )
     sent, near = call(
-        functools.partial(regroup_kernel, n_sec, n_band),
+        functools.partial(regroup_kernel, n_sec, n_band, (*shifts, 0)),
         [
             ((n_sec * n_band, n_fld, piece, LANES), BF16),
             ((n_fld, state_blocks, piece, LANES), BF16),

time: 29.1 us -> 29 us (level)
  transfers between devices with their start and end apart: 5 -> 5, of which waited for: 3 -> 2; matrix products, arithmetic and copies ran while one was open for 0% -> 0% of each run, Pallas kernels for 24% -> 24%
where the time goes in v23:
time: 29 us; the launch traced here: 28.8 us
  Pallas kernels  14 us (48%)
  starting transfers between devices  10.6 us (37%)
  waiting for transfers between devices  3.37 us (12%)
  between operations  0.77 us (3%)
    pallas_call x5, Pallas kernels, call(): pl.pallas_call(kernel, out_shape=shapes[0] if single else shapes, in_spec...  14 us
    ppermute x4, starting transfers between devices, exchange(): lax.ppermute(value, axis, [(i, i ^ shift) for i in range(lax.axis_size(ax...  7.24 us
    all_to_all x1, starting transfers between devices, body(): pieces = lax.all_to_all(sent, ('sec', 'band'), 0, 0, tiled=True)  3.41 us
    ppermute x4, waiting for transfers between devices, exchange(): lax.ppermute(value, axis, [(i, i ^ shift) for i in range(lax.axis_size(ax...  3.17 us
  transfers between devices with their start and end apart: 5, of which 2 were waited for; matrix products, arithmetic and copies ran while one was open for 0% of the time, Pallas kernels for 24%

profile of v23, /device:TPU:0, one launch (start us, length us, event | category | flops | bytes accessed | tf_op | source)
XLA Modules:
  0.0 28.8 jit_solution(6571303990045293169)
XLA Ops:
  0.6 0.0 copy-start
  0.6 0.0 copy-start.1
  0.7 0.0 copy-start.2
  0.7 0.0 copy-start.3
  0.7 5.2 %local.1 = (bf16[6,32,128]{2,1,0:T(8,128)(2,1)S(1)}, bf16[6,32,128]{2,1,0:T(8,128)(2,1)S(1)}, bf16[6,32,128]{2,1,0:T(8,128)(2,1)S(1)}, bf16[6,32,128]{2,1,0:T(8,128)(2,1)S(1)}) custom-call(bf16[8,40,2688]{2,1,0:T(8,128)(2,1)} %bitcast.8, s32[1,1024]{1,0:T(1,128)} %bitcast.6, bf16[1024,128]{1,0:T(8,128)(2,1)} %interp.1, bf16[2688,192]{1,0:T(8,128)(2,1)} %constant.2.clone.table_hbm), custom_call_target="tpu_custom_call" | custom-call | flops 2477785088 | bytes 1982464 | tf_op jit(solution)/shard_map/local/pallas_call | solution.py:328
  5.9 4.1 %collective-permute-start = (bf16[6,32,128]{2,1,0:T(8,128)(2,1)S(1)}, bf16[6,32,128]{2,1,0:T(8,128)(2,1)S(1)}, u32[]{:S(2)}, u32[]{:S(2)}) collective-permute-start(bf16[6,32,128]{2,1,0:T(8,128)(2,1)S(1)} %get-tuple-element.11), channel_id=1, source_target_pairs={{0,2},{1,3},{2,0},{3,1},{4,6},{5,7},{6,4},{7,5},{8,10},{9,11},{10,... | collective-permute-start | bytes 147464 | tf_op jit(solution)/shard_map/ppermute | solution.py:341
  10.0 1.3 %collective-permute-start.1 = (bf16[6,32,128]{2,1,0:T(8,128)(2,1)S(1)}, bf16[6,32,128]{2,1,0:T(8,128)(2,1)S(1)}, u32[]{:S(2)}, u32[]{:S(2)}) collective-permute-start(bf16[6,32,128]{2,1,0:T(8,128)(2,1)S(1)} %get-tuple-element.12), channel_id=1, source_target_pairs={{0,3},{1,2},{2,1},{3,0},{4,7},{5,6},{6,5},{7,4},{8,11},{9,10},{10,... | collective-permute-start | bytes 147464 | tf_op jit(solution)/shard_map/ppermute | solution.py:341
  11.4 0.2 collective-permute-start.2
  11.6 0.0 copy-done.1
  11.6 1.2 %prepare.1 = (bf16[4,2,144,128]{3,2,1,0:T(8,128)(2,1)S(1)}, bf16[2048,32]{1,0:T(8,128)(2,1)S(1)}) custom-call(bf16[6,48,160]{2,1,0:T(8,128)(2,1)S(1)} %bitcast.5, bf16[32,32,64]{2,1,0:T(8,128)(2,1)S(1)} %bitcast.4), custom_call_target="tpu_custom_call" | custom-call | bytes 1179648 | tf_op jit(solution)/shard_map/prepare/pallas_call | solution.py:328
  12.8 0.0 collective-permute-done.refs_0_
  12.8 3.2 %collective-permute-done.1.refs_1_ = bf16[6,32,128]{2,1,0:T(8,128)(2,1)S(1)} collective-permute-done((bf16[6,32,128]{2,1,0:T(8,128)(2,1)S(1)}, bf16[6,32,128]{2,1,0:T(8,128)(2,1)S(1)}, u32[]{:S(2)}, u32[]{:S(2)}) %collective-permute-start.1) | collective-permute-done | bytes 49184 | tf_op jit(solution)/shard_map/ppermute | solution.py:341
  16.0 0.0 collective-permute-done.2.refs_2_
  16.0 0.8 %regroup.1 = (bf16[8,4,32,128]{3,2,1,0:T(8,128)(2,1)}, bf16[4,2,32,128]{3,2,1,0:T(8,128)(2,1)S(1)}) custom-call(bf16[6,32,128]{2,1,0:T(8,128)(2,1)S(1)} %collective-permute-done.refs_0_, bf16[6,32,128]{2,1,0:T(8,128)(2,1)S(1)} %collective-permute-done.1.refs_1_, bf16[6,32,128]{2,1,0:T(8,128)(2,1)S(1)} %collective-permute-done.2.refs_2_, ...), custom_call_target="tpu_custom_call" | custom-call | bytes 524288 | tf_op jit(solution)/shard_map/regroup/pallas_call | solution.py:328
  16.8 1.6 %collective-permute-start.3 = (bf16[4,2,32,128]{3,2,1,0:T(8,128)(2,1)S(1)}, bf16[4,2,32,128]{3,2,1,0:T(8,128)(2,1)S(1)}, u32[]{:S(2)}, u32[]{:S(2)}) collective-permute-start(bf16[4,2,32,128]{3,2,1,0:T(8,128)(2,1)S(1)} %get-tuple-element.17.near), channel_id=1, source_target_pairs={{0,16},{16,0},{1,17},{17,1},{2,18},{18,2},{3,19},{19,3},{4,20},{20... | collective-permute-start | bytes 196616 | tf_op jit(solution)/shard_map/ppermute | solution.py:341
  18.4 3.4 %all-to-all-start = ((bf16[8,4,32,128]{3,2,1,0:T(8,128)(2,1)}), bf16[8,4,32,128]{3,2,1,0:T(8,128)(2,1)S(1)}, u32[]{:S(2)}, u32[]{:S(2)}) async-start(bf16[8,4,32,128]{3,2,1,0:T(8,128)(2,1)} %get-tuple-element.15), calls=%async_computation | async-start | bytes 524288 | tf_op jit(solution)/shard_map/all_to_all | solution.py:428
  21.8 0.0 collective-permute-done.3.far
  21.8 0.0 copy-done.2
  21.8 0.0 copy-done.3
  21.8 0.0 copy-done.4
  21.8 0.0 copy-done.5
  21.8 5.7 %columns.1 = bf16[2,40,2688]{2,1,0:T(8,128)(2,1)} custom-call(s32[4]{0:T(128)S(1)} %copy-done.5, bf16[64,2048]{1,0:T(8,128)(2,1)S(1)} %copy-done.3, bf16[2048,32]{1,0:T(8,128)(2,1)S(1)} %get-tuple-element.16.inverses, s32[1,1024]{1,0:T(1,128)S(1)} %bitcast.7, bf16[1024,128]{1,0:T(8,128)(2,1)S(1)} %copy-done.2, ...), custom_call_target="tpu_custom_call" | custom-call | flops 8589934592 | bytes 2097152 | tf_op jit(solution)/shard_map/columns/pallas_call | solution.py:328
  27.6 0.2 all-to-all-done.pieces
  27.8 1.0 %legendre.1 = bf16[6,2,4,16,48]{4,3,2,1,0:T(8,128)(2,1)} custom-call(bf16[4,2,144,128]{3,2,1,0:T(8,128)(2,1)S(1)} %get-tuple-element.10.refs_4_.weights, bf16[8,4,32,128]{3,2,1,0:T(8,128)(2,1)S(1)} %all-to-all-done.pieces), custom_call_target="tpu_custom_call" | custom-call | flops 75497472 | bytes 262144 | tf_op jit(solution)/shard_map/legendre/pallas_call | solution.py:328
  (3 shorter events, 0.0 us)
Async XLA Ops:
  0.6 11.0 %copy-start = (bf16[64,32,32]{0,2,1:T(8,128)(2,1)S(1)}, bf16[64,32,32]{0,2,1:T(8,128)(2,1)}, u32[]{:S(2)}) copy-start(bf16[64,32,32]{0,2,1:T(8,128)(2,1)} %param.14) | copy-start | bytes 393220
  0.6 11.0 %copy-start.1 = (bf16[6,160,48]{1,2,0:T(8,128)(2,1)S(1)}, bf16[6,160,48]{1,2,0:T(8,128)(2,1)}, u32[]{:S(2)}) copy-start(bf16[6,160,48]{1,2,0:T(8,128)(2,1)} %param.9) | copy-start | bytes 276484
  0.7 21.2 %copy-start.2 = (bf16[1024,128]{1,0:T(8,128)(2,1)S(1)}, bf16[1024,128]{1,0:T(8,128)(2,1)}, u32[]{:S(2)}) copy-start(bf16[1024,128]{1,0:T(8,128)(2,1)} %interp.1) | copy-start | bytes 786436
  0.7 21.2 %copy-start.3 = (bf16[64,2048]{1,0:T(8,128)(2,1)S(1)}, bf16[64,2048]{1,0:T(8,128)(2,1)}, u32[]{:S(2)}) copy-start(bf16[64,2048]{1,0:T(8,128)(2,1)} %weights.1) | copy-start | bytes 786436
  0.7 21.2 %copy-start.4 = (s32[1024]{0:T(1024)S(1)}, s32[1024]{0:T(1024)}, u32[]{:S(2)}) copy-start(s32[1024]{0:T(1024)} %param.11) | copy-start | bytes 12292
  0.7 21.2 %copy-start.5 = (s32[4]{0:T(128)S(1)}, s32[4]{0:T(128)}, u32[]{:S(2)}) copy-start(s32[4]{0:T(128)} %counts.1) | copy-start | bytes 52
  5.9 6.9 %collective-permute-start = (bf16[6,32,128]{2,1,0:T(8,128)(2,1)S(1)}, bf16[6,32,128]{2,1,0:T(8,128)(2,1)S(1)}, u32[]{:S(2)}, u32[]{:S(2)}) collective-permute-start(bf16[6,32,128]{2,1,0:T(8,128)(2,1)S(1)} %get-tuple-element.11), channel_id=1, source_target_pairs={{0,2},{1,3},{2,0},{3,1},{4,6},{5,7},{6,4},{7,5},{8,10},{9,11},{10,... | collective-permute-start | bytes 147464 | tf_op jit(solution)/shard_map/ppermute | solution.py:341
  10.0 6.0 %collective-permute-start.1 = (bf16[6,32,128]{2,1,0:T(8,128)(2,1)S(1)}, bf16[6,32,128]{2,1,0:T(8,128)(2,1)S(1)}, u32[]{:S(2)}, u32[]{:S(2)}) collective-permute-start(bf16[6,32,128]{2,1,0:T(8,128)(2,1)S(1)} %get-tuple-element.12), channel_id=1, source_target_pairs={{0,3},{1,2},{2,1},{3,0},{4,7},{5,6},{6,5},{7,4},{8,11},{9,10},{10,... | collective-permute-start | bytes 147464 | tf_op jit(solution)/shard_map/ppermute | solution.py:341
  11.4 4.6 %collective-permute-start.2 = (bf16[6,32,128]{2,1,0:T(8,128)(2,1)S(1)}, bf16[6,32,128]{2,1,0:T(8,128)(2,1)S(1)}, u32[]{:S(2)}, u32[]{:S(2)}) collective-permute-start(bf16[6,32,128]{2,1,0:T(8,128)(2,1)S(1)} %get-tuple-element.13), channel_id=1, source_target_pairs={{0,1},{1,0},{2,3},{3,2},{4,5},{5,4},{6,7},{7,6},{8,9},{9,8},{10,11... | collective-permute-start | bytes 147464 | tf_op jit(solution)/shard_map/ppermute | solution.py:341
  16.8 5.0 %collective-permute-start.3 = (bf16[4,2,32,128]{3,2,1,0:T(8,128)(2,1)S(1)}, bf16[4,2,32,128]{3,2,1,0:T(8,128)(2,1)S(1)}, u32[]{:S(2)}, u32[]{:S(2)}) collective-permute-start(bf16[4,2,32,128]{3,2,1,0:T(8,128)(2,1)S(1)} %get-tuple-element.17.near), channel_id=1, source_target_pairs={{0,16},{16,0},{1,17},{17,1},{2,18},{18,2},{3,19},{19,3},{4,20},{20... | collective-permute-start | bytes 196616 | tf_op jit(solution)/shard_map/ppermute | solution.py:341
  18.4 9.4 %all-to-all-start = ((bf16[8,4,32,128]{3,2,1,0:T(8,128)(2,1)}), bf16[8,4,32,128]{3,2,1,0:T(8,128)(2,1)S(1)}, u32[]{:S(2)}, u32[]{:S(2)}) async-start(bf16[8,4,32,128]{3,2,1,0:T(8,128)(2,1)} %get-tuple-element.15), calls=%async_computation | async-start | bytes 524288 | tf_op jit(solution)/shard_map/all_to_all | solution.py:428

commit v24 on v23

--- a/solution.py
+++ b/solution.py
@@ -49,7 +49,9 @@
         rows[pl.ds(level, group, stride=lev), :] = jnp.transpose(padded[...])[:group]
 
 
-def prepare_kernel(lat, n_band, legendre, inverses, out, out_inverses, wide, rows, turned):
+def prepare_kernel(lat, n_band, legendre, inverses, message, out, out_inverses, out_state, wide,
+                   rows, turned):
+    out_state[...] = message[n_band:]
     flux_rows, _, spec_bands = inverses.shape
     for row in range(flux_rows):
         rows[row * flux_rows : (row + 1) * flux_rows, :] = inverses[row].astype(F32)
@@ -241,17 +243,22 @@
 
 
 def column_kernel(n_sec, n_fld, lat_pad, slots, counts, weights, inverses, blocks, interp,
-                  near, far, out, state, spread, result, sems):
+                  near, *refs):
+    far, (out, state, spread, result, sems) = refs[:n_fld], refs[n_fld:]
     lev = near.shape[1] * near.shape[2] * LANES // slots
+    size = near.shape[2]
     place = lax.axis_index("sec")
     for fld in range(n_fld):
-        for shift, pieces in enumerate((near, far)):
-            row = (fld * n_sec + (place ^ shift)) * lev
+        sources = (
+            (fld * n_sec + place, near.at[fld]),
+            ((lax.axis_index("fld") ^ fld) * n_sec + (place ^ 1), far[fld]),
+        )
+        for at, pieces in sources:
+            row = pl.multiple_of(at * lev, lev)
             for tile in range(slots // LANES):
-                state[
-                    pl.ds(pl.multiple_of(row, lev), lev), tile * LANES : (tile + 1) * LANES
-                ] = pieces[fld, tile * lev // near.shape[2]][
-                    tile * lev % near.shape[2] : tile * lev % near.shape[2] + lev
+                block, line = divmod(tile * lev, size)
+                state[pl.ds(row, lev), tile * LANES : (tile + 1) * LANES] = pieces[
+                    block, line : line + lev
                 ].astype(F32)
     mine, lat, lon = result.shape
     across = lon // LANES
@@ -337,8 +344,14 @@
     )(*args)
 
 
-def exchange(value, axis, shift):
-    return lax.ppermute(value, axis, [(i, i ^ shift) for i in range(lax.axis_size(axis))])
+def exchange(value, axes, shifts):
+    sizes = [lax.axis_size(axis) for axis in axes]
+    pairs = []
+    for i in range(math.prod(sizes)):
+        at = np.unravel_index(i, sizes)
+        to = [int(a) ^ shift for a, shift in zip(at, shifts)]
+        pairs.append((i, int(np.ravel_multi_index(to, sizes))))
+    return lax.ppermute(value, axes, pairs)
 
 
 def body(grid, legendre, counts, blocks, interp, source_weights, inverses):
@@ -389,22 +402,23 @@
     )
     half = n_fld // 2
     shifts = [half] + list(range(n_fld - 1, half, -1)) + list(range(half - 1, 0, -1))
-    arrived = [exchange(messages[shift], "fld", shift) for shift in shifts]
+    arrived = [exchange(messages[shift], ("fld",), (shift,)) for shift in shifts]
     arrived.append(messages[0])
     spec_bands, flux_rows, _ = inverses.shape
-    basis, inverse_rows = call(
+    basis, inverse_rows, state = call(
         functools.partial(prepare_kernel, lat, n_band),
         [
             ((n_band, 2, THIRDS * degrees, LANES), BF16),
             ((spec_bands * flux_rows, flux_rows), BF16),
-        ],
-        [VMEM, VMEM],
+            ((state_blocks, piece, LANES), BF16),
+        ],
+        [VMEM, VMEM, VMEM],
         [
             pltpu.VMEM((degrees, (n_band * lat // LANES + 2) * LANES), F32),
             pltpu.VMEM((flux_rows * flux_rows, spec_bands), F32),
             pltpu.VMEM((spec_bands * flux_rows, flux_rows), F32),
         ],
-        (jnp.swapaxes(legendre, 1, 2), jnp.transpose(inverses, (1, 2, 0))),
+        (jnp.swapaxes(legendre, 1, 2), jnp.transpose(inverses, (1, 2, 0)), messages[0]),
         0,
         8 * wave_dev * degrees * n_band * LANES,
         "prepare",
@@ -424,7 +438,7 @@
         HBM,
         SMALL,
     )
-    far = exchange(near, "sec", 1)
+    far = [exchange(state, ("sec", "fld"), (1, shift)) for shift in range(n_fld)]
     pieces = lax.all_to_all(sent, ("sec", "band"), 0, 0, tiled=True)
     sources = spec_bands * flux_rows
     states = source_weights.shape[0]
@@ -432,14 +446,14 @@
     heating = call(
         functools.partial(column_kernel, n_sec, n_fld, lat_pad, slots),
         [((mine, lat, lon), BF16)],
-        [SMEM] + [VMEM] * 6,
+        [SMEM] + [VMEM] * (5 + n_fld),
         [
             pltpu.VMEM((states, slots), F32),
             pltpu.VMEM((slots, mine * LANES), BF16),
             pltpu.VMEM((mine, lat, lon), BF16),
             pltpu.SemaphoreType.DMA((across,)),
         ],
-        (counts, source_weights, inverse_rows, block_row, interp, near, far),
+        (counts, source_weights, inverse_rows, block_row, interp, near, *far),
         8 * slots * slots * 1024,
         2 * slots * slots,
         "columns",

time: 29 us -> 32.2 us (1.11)
  starting transfers between devices: 10.6 us -> 16.2 us
  waiting for transfers between devices: 3.37 us -> 0.99 us
    ppermute x4 -> x7, starting transfers between devices: 7.24 us -> 12.5 us  [exchange(): return lax.ppermute(value, axes, pairs)]
    ppermute x4 -> x7, waiting for transfers between devices: 3.17 us -> 0.99 us  [exchange(): return lax.ppermute(value, axes, pairs)]
    all_to_all x1, starting transfers between devices: 3.41 us -> 3.73 us  [body(): pieces = lax.all_to_all(sent, ('sec', 'band'), 0, 0, tiled=True)]
  transfers between devices with their start and end apart: 5 -> 8, of which waited for: 2 -> 1; matrix products, arithmetic and copies ran while one was open for 0% -> 0% of each run, Pallas kernels for 24% -> 24%
where the time goes in v24:
time: 32.2 us; the launch traced here: 32 us
  starting transfers between devices  16.2 us (50%)
  Pallas kernels  14 us (43%)
  waiting for transfers between devices  0.99 us (3%)
  between operations  0.76 us (2%)
    pallas_call x5, Pallas kernels, call(): pl.pallas_call(kernel, out_shape=shapes[0] if single else shapes, in_spec...  14 us
    ppermute x7, starting transfers between devices, exchange(): return lax.ppermute(value, axes, pairs)  12.5 us
    all_to_all x1, starting transfers between devices, body(): pieces = lax.all_to_all(sent, ('sec', 'band'), 0, 0, tiled=True)  3.73 us
    ppermute x7, waiting for transfers between devices, exchange(): return lax.ppermute(value, axes, pairs)  0.99 us
  transfers between devices with their start and end apart: 8, of which 1 were waited for; matrix products, arithmetic and copies ran while one was open for 0% of the time, Pallas kernels for 24%

profile of v24, /device:TPU:0, one launch (start us, length us, event | category | flops | bytes accessed | tf_op | source)
XLA Modules:
  0.0 32.0 jit_solution(1545554469651891024)
XLA Ops:
  0.6 0.0 copy-start
  0.6 0.0 copy-start.1
  0.7 0.0 copy-start.2
  0.7 5.2 %local.1 = (bf16[6,32,128]{2,1,0:T(8,128)(2,1)S(1)}, bf16[6,32,128]{2,1,0:T(8,128)(2,1)S(1)}, bf16[6,32,128]{2,1,0:T(8,128)(2,1)S(1)}, bf16[6,32,128]{2,1,0:T(8,128)(2,1)S(1)}) custom-call(bf16[8,40,2688]{2,1,0:T(8,128)(2,1)} %bitcast.8, s32[1,1024]{1,0:T(1,128)} %bitcast.6, bf16[1024,128]{1,0:T(8,128)(2,1)} %interp.1, bf16[2688,192]{1,0:T(8,128)(2,1)} %constant.2.clone.table_hbm), custom_call_target="tpu_custom_call" | custom-call | flops 2477785088 | bytes 1982464 | tf_op jit(solution)/shard_map/local/pallas_call | solution.py:335
  5.9 4.1 %collective-permute-start = (bf16[6,32,128]{2,1,0:T(8,128)(2,1)S(1)}, bf16[6,32,128]{2,1,0:T(8,128)(2,1)S(1)}, u32[]{:S(2)}, u32[]{:S(2)}) collective-permute-start(bf16[6,32,128]{2,1,0:T(8,128)(2,1)S(1)} %get-tuple-element.13), channel_id=1, source_target_pairs={{0,2},{1,3},{2,0},{3,1},{4,6},{5,7},{6,4},{7,5},{8,10},{9,11},{10,... | collective-permute-start | bytes 147464 | tf_op jit(solution)/shard_map/ppermute | solution.py:354
  10.0 1.3 %collective-permute-start.1 = (bf16[6,32,128]{2,1,0:T(8,128)(2,1)S(1)}, bf16[6,32,128]{2,1,0:T(8,128)(2,1)S(1)}, u32[]{:S(2)}, u32[]{:S(2)}) collective-permute-start(bf16[6,32,128]{2,1,0:T(8,128)(2,1)S(1)} %get-tuple-element.14), channel_id=1, source_target_pairs={{0,3},{1,2},{2,1},{3,0},{4,7},{5,6},{6,5},{7,4},{8,11},{9,10},{10,... | collective-permute-start | bytes 147464 | tf_op jit(solution)/shard_map/ppermute | solution.py:354
  11.4 0.2 collective-permute-start.2
  11.6 1.2 %prepare.1 = (bf16[4,2,144,128]{3,2,1,0:T(8,128)(2,1)S(1)}, bf16[2048,32]{1,0:T(8,128)(2,1)S(1)}, bf16[2,32,128]{2,1,0:T(8,128)(2,1)S(1)}) custom-call(bf16[6,48,160]{2,1,0:T(8,128)(2,1)S(1)} %bitcast.5, bf16[32,32,64]{2,1,0:T(8,128)(2,1)S(1)} %bitcast.4, bf16[6,32,128]{2,1,0:T(8,128)(2,1)S(1)} %get-tuple-element.11.message.refs_3_), custom_call_target="tpu_custom_call" | custom-call | bytes 1179648 | tf_op jit(solution)/shard_map/prepare/pallas_call | solution.py:335
  12.8 1.6 %collective-permute-start.3 = (bf16[2,32,128]{2,1,0:T(8,128)(2,1)S(1)}, bf16[2,32,128]{2,1,0:T(8,128)(2,1)S(1)}, u32[]{:S(2)}, u32[]{:S(2)}) collective-permute-start(bf16[2,32,128]{2,1,0:T(8,128)(2,1)S(1)} %get-tuple-element.19), channel_id=1, source_target_pairs={{0,16},{1,17},{2,18},{3,19},{16,0},{17,1},{18,2},{19,3},{4,20},{5,... | collective-permute-start | bytes 49160 | tf_op jit(solution)/shard_map/ppermute | solution.py:354
  14.4 1.8 %collective-permute-start.4 = (bf16[2,32,128]{2,1,0:T(8,128)(2,1)S(1)}, bf16[2,32,128]{2,1,0:T(8,128)(2,1)S(1)}, u32[]{:S(2)}, u32[]{:S(2)}) collective-permute-start(bf16[2,32,128]{2,1,0:T(8,128)(2,1)S(1)} %get-tuple-element.19), channel_id=1, source_target_pairs={{0,17},{1,16},{2,19},{3,18},{16,1},{17,0},{18,3},{19,2},{4,21},{5,... | collective-permute-start | bytes 49160 | tf_op jit(solution)/shard_map/ppermute | solution.py:354
  16.1 0.0 collective-permute-done.refs_0_
  16.1 2.6 %collective-permute-start.5 = (bf16[2,32,128]{2,1,0:T(8,128)(2,1)S(1)}, bf16[2,32,128]{2,1,0:T(8,128)(2,1)S(1)}, u32[]{:S(2)}, u32[]{:S(2)}) collective-permute-start(bf16[2,32,128]{2,1,0:T(8,128)(2,1)S(1)} %get-tuple-element.19), channel_id=1, source_target_pairs={{0,18},{1,19},{2,16},{3,17},{16,2},{17,3},{18,0},{19,1},{4,22},{5,... | collective-permute-start | bytes 49160 | tf_op jit(solution)/shard_map/ppermute | solution.py:354
  18.8 0.0 collective-permute-done.1.refs_1_
  18.8 0.9 %collective-permute-start.6 = (bf16[2,32,128]{2,1,0:T(8,128)(2,1)S(1)}, bf16[2,32,128]{2,1,0:T(8,128)(2,1)S(1)}, u32[]{:S(2)}, u32[]{:S(2)}) collective-permute-start(bf16[2,32,128]{2,1,0:T(8,128)(2,1)S(1)} %get-tuple-element.19), channel_id=1, source_target_pairs={{0,19},{1,18},{2,17},{3,16},{16,3},{17,2},{18,1},{19,0},{4,23},{5,... | collective-permute-start | bytes 49160 | tf_op jit(solution)/shard_map/ppermute | solution.py:354
  19.6 0.0 collective-permute-done.2.refs_2_
  19.6 0.8 %regroup.1 = (bf16[8,4,32,128]{3,2,1,0:T(8,128)(2,1)}, bf16[4,2,32,128]{3,2,1,0:T(8,128)(2,1)S(1)}) custom-call(bf16[6,32,128]{2,1,0:T(8,128)(2,1)S(1)} %collective-permute-done.refs_0_, bf16[6,32,128]{2,1,0:T(8,128)(2,1)S(1)} %collective-permute-done.1.refs_1_, bf16[6,32,128]{2,1,0:T(8,128)(2,1)S(1)} %collective-permute-done.2.refs_2_, ...), custom_call_target="tpu_custom_call" | custom-call | bytes 524288 | tf_op jit(solution)/shard_map/regroup/pallas_call | solution.py:335
  20.5 3.7 %all-to-all-start = ((bf16[8,4,32,128]{3,2,1,0:T(8,128)(2,1)}), bf16[8,4,32,128]{3,2,1,0:T(8,128)(2,1)S(1)}, u32[]{:S(2)}, u32[]{:S(2)}) async-start(bf16[8,4,32,128]{3,2,1,0:T(8,128)(2,1)} %get-tuple-element.16), calls=%async_computation | async-start | bytes 524288 | tf_op jit(solution)/shard_map/all_to_all | solution.py:442
  24.2 0.0 collective-permute-done.3.refs_0_
  24.2 0.0 collective-permute-done.4.refs_1_
  24.2 0.0 collective-permute-done.5.refs_2_
  24.2 1.0 %collective-permute-done.6.refs_3_ = bf16[2,32,128]{2,1,0:T(8,128)(2,1)S(1)} collective-permute-done((bf16[2,32,128]{2,1,0:T(8,128)(2,1)S(1)}, bf16[2,32,128]{2,1,0:T(8,128)(2,1)S(1)}, u32[]{:S(2)}, u32[]{:S(2)}) %collective-permute-start.6) | collective-permute-done | bytes 16416 | tf_op jit(solution)/shard_map/ppermute | solution.py:354
  25.2 5.7 %columns.1 = bf16[2,40,2688]{2,1,0:T(8,128)(2,1)} custom-call(s32[4]{0:T(128)S(1)} %copy-done.5, bf16[64,2048]{1,0:T(8,128)(2,1)S(1)} %copy-done.3, bf16[2048,32]{1,0:T(8,128)(2,1)S(1)} %get-tuple-element.17.inverses, s32[1,1024]{1,0:T(1,128)S(1)} %bitcast.7, bf16[1024,128]{1,0:T(8,128)(2,1)S(1)} %copy-done.2, ...), custom_call_target="tpu_custom_call" | custom-call | flops 8589934592 | bytes 2097152 | tf_op jit(solution)/shard_map/columns/pallas_call | solution.py:335
  30.9 0.0 all-to-all-done.pieces
  30.9 1.0 %legendre.1 = bf16[6,2,4,16,48]{4,3,2,1,0:T(8,128)(2,1)} custom-call(bf16[4,2,144,128]{3,2,1,0:T(8,128)(2,1)S(1)} %get-tuple-element.12.refs_4_.weights, bf16[8,4,32,128]{3,2,1,0:T(8,128)(2,1)S(1)} %all-to-all-done.pieces), custom_call_target="tpu_custom_call" | custom-call | flops 75497472 | bytes 262144 | tf_op jit(solution)/shard_map/legendre/pallas_call | solution.py:335
  (9 shorter events, 0.0 us)
Async XLA Ops:
  0.6 11.0 %copy-start = (bf16[64,32,32]{0,2,1:T(8,128)(2,1)S(1)}, bf16[64,32,32]{0,2,1:T(8,128)(2,1)}, u32[]{:S(2)}) copy-start(bf16[64,32,32]{0,2,1:T(8,128)(2,1)} %param.14) | copy-start | bytes 393220
  0.6 11.0 %copy-start.1 = (bf16[6,160,48]{1,2,0:T(8,128)(2,1)S(1)}, bf16[6,160,48]{1,2,0:T(8,128)(2,1)}, u32[]{:S(2)}) copy-start(bf16[6,160,48]{1,2,0:T(8,128)(2,1)} %param.9) | copy-start | bytes 276484
  0.7 24.6 %copy-start.2 = (bf16[1024,128]{1,0:T(8,128)(2,1)S(1)}, bf16[1024,128]{1,0:T(8,128)(2,1)}, u32[]{:S(2)}) copy-start(bf16[1024,128]{1,0:T(8,128)(2,1)} %interp.1) | copy-start | bytes 786436
  0.7 24.5 %copy-start.3 = (bf16[64,2048]{1,0:T(8,128)(2,1)S(1)}, bf16[64,2048]{1,0:T(8,128)(2,1)}, u32[]{:S(2)}) copy-start(bf16[64,2048]{1,0:T(8,128)(2,1)} %weights.1) | copy-start | bytes 786436
  0.7 24.5 %copy-start.4 = (s32[1024]{0:T(1024)S(1)}, s32[1024]{0:T(1024)}, u32[]{:S(2)}) copy-start(s32[1024]{0:T(1024)} %param.11) | copy-start | bytes 12292
  0.7 24.5 %copy-start.5 = (s32[4]{0:T(128)S(1)}, s32[4]{0:T(128)}, u32[]{:S(2)}) copy-start(s32[4]{0:T(128)} %counts.1) | copy-start | bytes 52
  5.9 10.2 %collective-permute-start = (bf16[6,32,128]{2,1,0:T(8,128)(2,1)S(1)}, bf16[6,32,128]{2,1,0:T(8,128)(2,1)S(1)}, u32[]{:S(2)}, u32[]{:S(2)}) collective-permute-start(bf16[6,32,128]{2,1,0:T(8,128)(2,1)S(1)} %get-tuple-element.13), channel_id=1, source_target_pairs={{0,2},{1,3},{2,0},{3,1},{4,6},{5,7},{6,4},{7,5},{8,10},{9,11},{10,... | collective-permute-start | bytes 147464 | tf_op jit(solution)/shard_map/ppermute | solution.py:354
  10.0 8.7 %collective-permute-start.1 = (bf16[6,32,128]{2,1,0:T(8,128)(2,1)S(1)}, bf16[6,32,128]{2,1,0:T(8,128)(2,1)S(1)}, u32[]{:S(2)}, u32[]{:S(2)}) collective-permute-start(bf16[6,32,128]{2,1,0:T(8,128)(2,1)S(1)} %get-tuple-element.14), channel_id=1, source_target_pairs={{0,3},{1,2},{2,1},{3,0},{4,7},{5,6},{6,5},{7,4},{8,11},{9,10},{10,... | collective-permute-start | bytes 147464 | tf_op jit(solution)/shard_map/ppermute | solution.py:354
  11.4 8.3 %collective-permute-start.2 = (bf16[6,32,128]{2,1,0:T(8,128)(2,1)S(1)}, bf16[6,32,128]{2,1,0:T(8,128)(2,1)S(1)}, u32[]{:S(2)}, u32[]{:S(2)}) collective-permute-start(bf16[6,32,128]{2,1,0:T(8,128)(2,1)S(1)} %get-tuple-element.15), channel_id=1, source_target_pairs={{0,1},{1,0},{2,3},{3,2},{4,5},{5,4},{6,7},{7,6},{8,9},{9,8},{10,11... | collective-permute-start | bytes 147464 | tf_op jit(solution)/shard_map/ppermute | solution.py:354
  12.8 11.4 %collective-permute-start.3 = (bf16[2,32,128]{2,1,0:T(8,128)(2,1)S(1)}, bf16[2,32,128]{2,1,0:T(8,128)(2,1)S(1)}, u32[]{:S(2)}, u32[]{:S(2)}) collective-permute-start(bf16[2,32,128]{2,1,0:T(8,128)(2,1)S(1)} %get-tuple-element.19), channel_id=1, source_target_pairs={{0,16},{1,17},{2,18},{3,19},{16,0},{17,1},{18,2},{19,3},{4,20},{5,... | collective-permute-start | bytes 49160 | tf_op jit(solution)/shard_map/ppermute | solution.py:354
  14.4 9.8 %collective-permute-start.4 = (bf16[2,32,128]{2,1,0:T(8,128)(2,1)S(1)}, bf16[2,32,128]{2,1,0:T(8,128)(2,1)S(1)}, u32[]{:S(2)}, u32[]{:S(2)}) collective-permute-start(bf16[2,32,128]{2,1,0:T(8,128)(2,1)S(1)} %get-tuple-element.19), channel_id=1, source_target_pairs={{0,17},{1,16},{2,19},{3,18},{16,1},{17,0},{18,3},{19,2},{4,21},{5,... | collective-permute-start | bytes 49160 | tf_op jit(solution)/shard_map/ppermute | solution.py:354
  16.1 8.1 %collective-permute-start.5 = (bf16[2,32,128]{2,1,0:T(8,128)(2,1)S(1)}, bf16[2,32,128]{2,1,0:T(8,128)(2,1)S(1)}, u32[]{:S(2)}, u32[]{:S(2)}) collective-permute-start(bf16[2,32,128]{2,1,0:T(8,128)(2,1)S(1)} %get-tuple-element.19), channel_id=1, source_target_pairs={{0,18},{1,19},{2,16},{3,17},{16,2},{17,3},{18,0},{19,1},{4,22},{5,... | collective-permute-start | bytes 49160 | tf_op jit(solution)/shard_map/ppermute | solution.py:354
  18.8 6.4 %collective-permute-start.6 = (bf16[2,32,128]{2,1,0:T(8,128)(2,1)S(1)}, bf16[2,32,128]{2,1,0:T(8,128)(2,1)S(1)}, u32[]{:S(2)}, u32[]{:S(2)}) collective-permute-start(bf16[2,32,128]{2,1,0:T(8,128)(2,1)S(1)} %get-tuple-element.19), channel_id=1, source_target_pairs={{0,19},{1,18},{2,17},{3,16},{16,3},{17,2},{18,1},{19,0},{4,23},{5,... | collective-permute-start | bytes 49160 | tf_op jit(solution)/shard_map/ppermute | solution.py:354
  20.5 10.5 %all-to-all-start = ((bf16[8,4,32,128]{3,2,1,0:T(8,128)(2,1)}), bf16[8,4,32,128]{3,2,1,0:T(8,128)(2,1)S(1)}, u32[]{:S(2)}, u32[]{:S(2)}) async-start(bf16[8,4,32,128]{3,2,1,0:T(8,128)(2,1)} %get-tuple-element.16), calls=%async_computation | async-start | bytes 524288 | tf_op jit(solution)/shard_map/all_to_all | solution.py:442

commit v25 on v23

--- a/solution.py
+++ b/solution.py
@@ -49,7 +49,23 @@
         rows[pl.ds(level, group, stride=lev), :] = jnp.transpose(padded[...])[:group]
 
 
-def prepare_kernel(lat, n_band, legendre, inverses, out, out_inverses, wide, rows, turned):
+def prepare_kernel(lat, n_band, legendre_hbm, inverses_hbm, weights_hbm, interp_hbm, out,
+                   out_inverses, out_weights, out_interp, legendre, inverses, wide, rows, turned,
+                   sems):
+    copies = [
+        pltpu.make_async_copy(*pair, sems.at[i])
+        for i, pair in enumerate(
+            (
+                (inverses_hbm, inverses),
+                (legendre_hbm, legendre),
+                (weights_hbm, out_weights),
+                (interp_hbm, out_interp),
+            )
+        )
+    ]
+    for copy in copies:
+        copy.start()
+    copies[0].wait()
     flux_rows, _, spec_bands = inverses.shape
     for row in range(flux_rows):
         rows[row * flux_rows : (row + 1) * flux_rows, :] = inverses[row].astype(F32)
@@ -60,6 +76,7 @@
     out_inverses[...] = turned[...].astype(BF16)
     waves, degrees, _ = legendre.shape
     wide[...] = jnp.zeros_like(wide)
+    copies[1].wait()
     lane = lax.broadcasted_iota(jnp.int32, (degrees, LANES), 1)
     for wave in range(waves):
         third, parity = wave // 2, wave % 2
@@ -74,6 +91,8 @@
             out[band, parity, third * degrees : (third + 1) * degrees, :] = jnp.where(
                 live, moved[:, :LANES], 0.0
             ).astype(BF16)
+    for copy in copies[2:]:
+        copy.wait()
 
 
 def legendre_kernel(n_sec, n_band, n_fld, lev, weights, pieces, out_hbm, out, sems):
@@ -392,19 +411,32 @@
     arrived = [exchange(messages[shift], "fld", shift) for shift in shifts]
     arrived.append(messages[0])
     spec_bands, flux_rows, _ = inverses.shape
-    basis, inverse_rows = call(
+    basis, inverse_rows, gate_weights, slot_weights = call(
         functools.partial(prepare_kernel, lat, n_band),
         [
             ((n_band, 2, THIRDS * degrees, LANES), BF16),
             ((spec_bands * flux_rows, flux_rows), BF16),
-        ],
-        [VMEM, VMEM],
-        [
+            (source_weights.shape, BF16),
+            (interp.shape, BF16),
+        ],
+        [HBM] * 4,
+        [
+            pltpu.VMEM((wave_dev, degrees, n_band * lat), BF16),
+            pltpu.VMEM((flux_rows, flux_rows, spec_bands), BF16),
             pltpu.VMEM((degrees, (n_band * lat // LANES + 2) * LANES), F32),
             pltpu.VMEM((flux_rows * flux_rows, spec_bands), F32),
             pltpu.VMEM((spec_bands * flux_rows, flux_rows), F32),
-        ],
-        (jnp.swapaxes(legendre, 1, 2), jnp.transpose(inverses, (1, 2, 0))),
+            pltpu.SemaphoreType.DMA((4,)),
+        ],
+        [
+            pltpu.with_memory_space_constraint(value, pltpu.HBM)
+            for value in (
+                jnp.swapaxes(legendre, 1, 2),
+                jnp.transpose(inverses, (1, 2, 0)),
+                source_weights,
+                interp,
+            )
+        ],
         0,
         8 * wave_dev * degrees * n_band * LANES,
         "prepare",
@@ -439,7 +471,7 @@
             pltpu.VMEM((mine, lat, lon), BF16),
             pltpu.SemaphoreType.DMA((across,)),
         ],
-        (counts, source_weights, inverse_rows, block_row, interp, near, far),
+        (counts, gate_weights, inverse_rows, block_row, slot_weights, near, far),
         8 * slots * slots * 1024,
         2 * slots * slots,
         "columns",

time: 29 us -> 29 us (level)
  waiting for transfers between devices: 3.37 us -> 2.36 us
  Pallas kernels: 14 us -> 15 us
    ppermute x4, waiting for transfers between devices: 3.17 us -> 2.13 us  [exchange(): lax.ppermute(value, axis, [(i, i ^ shift) for i in range(lax.axis_size(ax...]
    pallas_call x5, Pallas kernels: 14 us -> 15 us  [call(): pl.pallas_call(kernel, out_shape=shapes[0] if single else shapes, in_spec...]
  transfers between devices with their start and end apart: 5 -> 5, of which waited for: 2 -> 2; matrix products, arithmetic and copies ran while one was open for 0% -> 0% of each run, Pallas kernels for 24% -> 28%
where the time goes in v25:
time: 29 us; the launch traced here: 28.7 us
  Pallas kernels  15 us (52%)
  starting transfers between devices  10.6 us (37%)
  waiting for transfers between devices  2.36 us (8%)
  between operations  0.72 us (2%)
    pallas_call x5, Pallas kernels, call(): pl.pallas_call(kernel, out_shape=shapes[0] if single else shapes, in_spec...  15 us
    ppermute x4, starting transfers between devices, exchange(): lax.ppermute(value, axis, [(i, i ^ shift) for i in range(lax.axis_size(ax...  7.24 us
    all_to_all x1, starting transfers between devices, body(): pieces = lax.all_to_all(sent, ('sec', 'band'), 0, 0, tiled=True)  3.41 us
    ppermute x4, waiting for transfers between devices, exchange(): lax.ppermute(value, axis, [(i, i ^ shift) for i in range(lax.axis_size(ax...  2.13 us
  transfers between devices with their start and end apart: 5, of which 2 were waited for; matrix products, arithmetic and copies ran while one was open for 0% of the time, Pallas kernels for 28%

profile of v25, /device:TPU:0, one launch (start us, length us, event | category | flops | bytes accessed | tf_op | source)
XLA Modules:
  0.0 28.7 jit_solution(8838652052071610552)
XLA Ops:
  0.6 5.1 %local.1 = (bf16[6,32,128]{2,1,0:T(8,128)(2,1)S(1)}, bf16[6,32,128]{2,1,0:T(8,128)(2,1)S(1)}, bf16[6,32,128]{2,1,0:T(8,128)(2,1)S(1)}, bf16[6,32,128]{2,1,0:T(8,128)(2,1)S(1)}) custom-call(bf16[8,40,2688]{2,1,0:T(8,128)(2,1)} %bitcast.8, s32[1,1024]{1,0:T(1,128)} %bitcast.4, bf16[1024,128]{1,0:T(8,128)(2,1)} %interp_hbm.3, ...), custom_call_target="tpu_custom_call" | custom-call | flops 2477785088 | bytes 1982464 | tf_op jit(solution)/shard_map/local/pallas_call | solution.py:347
  5.8 0.0 copy-start
  5.8 0.0 copy-start.1
  5.8 4.1 %collective-permute-start = (bf16[6,32,128]{2,1,0:T(8,128)(2,1)S(1)}, bf16[6,32,128]{2,1,0:T(8,128)(2,1)S(1)}, u32[]{:S(2)}, u32[]{:S(2)}) collective-permute-start(bf16[6,32,128]{2,1,0:T(8,128)(2,1)S(1)} %get-tuple-element.13), channel_id=1, source_target_pairs={{0,2},{1,3},{2,0},{3,1},{4,6},{5,7},{6,4},{7,5},{8,10},{9,11},{10,... | collective-permute-start | bytes 147464 | tf_op jit(solution)/shard_map/ppermute | solution.py:360
  9.9 1.3 %collective-permute-start.1 = (bf16[6,32,128]{2,1,0:T(8,128)(2,1)S(1)}, bf16[6,32,128]{2,1,0:T(8,128)(2,1)S(1)}, u32[]{:S(2)}, u32[]{:S(2)}) collective-permute-start(bf16[6,32,128]{2,1,0:T(8,128)(2,1)S(1)} %get-tuple-element.14), channel_id=1, source_target_pairs={{0,3},{1,2},{2,1},{3,0},{4,7},{5,6},{6,5},{7,4},{8,11},{9,10},{10,... | collective-permute-start | bytes 147464 | tf_op jit(solution)/shard_map/ppermute | solution.py:360
  11.3 0.2 collective-permute-start.2
  11.5 2.2 %prepare.1 = (bf16[4,2,144,128]{3,2,1,0:T(8,128)(2,1)S(1)}, bf16[2048,32]{1,0:T(8,128)(2,1)S(1)}, bf16[64,2048]{1,0:T(8,128)(2,1)S(1)}, bf16[1024,128]{1,0:T(8,128)(2,1)S(1)}) custom-call(bf16[6,48,160]{2,1,0:T(8,128)(2,1)} %bitcast.7, bf16[32,32,64]{2,1,0:T(8,128)(2,1)} %bitcast.6, bf16[64,2048]{1,0:T(8,128)(2,1)} %weights_hbm.1, bf16[1024,128]{1,0:T(8,128)(2,1)} %interp_hbm.3), custom_call_target="tpu_custom_call" | custom-call | bytes 1179648 | tf_op jit(solution)/shard_map/prepare/pallas_call | solution.py:347
  13.7 0.0 collective-permute-done.refs_0_
  13.7 2.1 %collective-permute-done.1.refs_1_ = bf16[6,32,128]{2,1,0:T(8,128)(2,1)S(1)} collective-permute-done((bf16[6,32,128]{2,1,0:T(8,128)(2,1)S(1)}, bf16[6,32,128]{2,1,0:T(8,128)(2,1)S(1)}, u32[]{:S(2)}, u32[]{:S(2)}) %collective-permute-start.1) | collective-permute-done | bytes 49184 | tf_op jit(solution)/shard_map/ppermute | solution.py:360
  15.9 0.0 collective-permute-done.2.refs_2_
  15.9 0.8 %regroup.1 = (bf16[8,4,32,128]{3,2,1,0:T(8,128)(2,1)}, bf16[4,2,32,128]{3,2,1,0:T(8,128)(2,1)S(1)}) custom-call(bf16[6,32,128]{2,1,0:T(8,128)(2,1)S(1)} %collective-permute-done.refs_0_, bf16[6,32,128]{2,1,0:T(8,128)(2,1)S(1)} %collective-permute-done.1.refs_1_, bf16[6,32,128]{2,1,0:T(8,128)(2,1)S(1)} %collective-permute-done.2.refs_2_, ...), custom_call_target="tpu_custom_call" | custom-call | bytes 524288 | tf_op jit(solution)/shard_map/regroup/pallas_call | solution.py:347
  16.7 1.6 %collective-permute-start.3 = (bf16[4,2,32,128]{3,2,1,0:T(8,128)(2,1)S(1)}, bf16[4,2,32,128]{3,2,1,0:T(8,128)(2,1)S(1)}, u32[]{:S(2)}, u32[]{:S(2)}) collective-permute-start(bf16[4,2,32,128]{3,2,1,0:T(8,128)(2,1)S(1)} %get-tuple-element.21.near), channel_id=1, source_target_pairs={{0,16},{16,0},{1,17},{17,1},{2,18},{18,2},{3,19},{19,3},{4,20},{20... | collective-permute-start | bytes 196616 | tf_op jit(solution)/shard_map/ppermute | solution.py:360
  18.3 3.4 %all-to-all-start = ((bf16[8,4,32,128]{3,2,1,0:T(8,128)(2,1)}), bf16[8,4,32,128]{3,2,1,0:T(8,128)(2,1)S(1)}, u32[]{:S(2)}, u32[]{:S(2)}) async-start(bf16[8,4,32,128]{3,2,1,0:T(8,128)(2,1)} %get-tuple-element.17), calls=%async_computation | async-start | bytes 524288 | tf_op jit(solution)/shard_map/all_to_all | solution.py:460
  21.7 0.0 collective-permute-done.3.far
  21.7 0.0 copy-done
  21.7 0.0 copy-done.1
  21.7 5.7 %columns.1 = bf16[2,40,2688]{2,1,0:T(8,128)(2,1)} custom-call(s32[4]{0:T(128)S(1)} %copy-done.1, bf16[64,2048]{1,0:T(8,128)(2,1)S(1)} %get-tuple-element.18.weights, bf16[2048,32]{1,0:T(8,128)(2,1)S(1)} %get-tuple-element.19.inverses, s32[1,1024]{1,0:T(1,128)S(1)} %bitcast.5, bf16[1024,128]{1,0:T(8,128)(2,1)S(1)} %get-tuple-element.20.interp, ...), custom_call_target="tpu_custom_call" | custom-call | flops 8589934592 | bytes 2097152 | tf_op jit(solution)/shard_map/columns/pallas_call | solution.py:347
  27.4 0.2 all-to-all-done.pieces
  27.7 1.0 %legendre.1 = bf16[6,2,4,16,48]{4,3,2,1,0:T(8,128)(2,1)} custom-call(bf16[4,2,144,128]{3,2,1,0:T(8,128)(2,1)S(1)} %get-tuple-element.12.refs_4_.weights, bf16[8,4,32,128]{3,2,1,0:T(8,128)(2,1)S(1)} %all-to-all-done.pieces), custom_call_target="tpu_custom_call" | custom-call | flops 75497472 | bytes 262144 | tf_op jit(solution)/shard_map/legendre/pallas_call | solution.py:347
Async XLA Ops:
  5.8 15.9 %copy-start = (s32[1024]{0:T(1024)S(1)}, s32[1024]{0:T(1024)}, u32[]{:S(2)}) copy-start(s32[1024]{0:T(1024)} %param.11) | copy-start | bytes 12292
  5.8 15.9 %copy-start.1 = (s32[4]{0:T(128)S(1)}, s32[4]{0:T(128)}, u32[]{:S(2)}) copy-start(s32[4]{0:T(128)} %counts.1) | copy-start | bytes 52
  5.8 7.9 %collective-permute-start = (bf16[6,32,128]{2,1,0:T(8,128)(2,1)S(1)}, bf16[6,32,128]{2,1,0:T(8,128)(2,1)S(1)}, u32[]{:S(2)}, u32[]{:S(2)}) collective-permute-start(bf16[6,32,128]{2,1,0:T(8,128)(2,1)S(1)} %get-tuple-element.13), channel_id=1, source_target_pairs={{0,2},{1,3},{2,0},{3,1},{4,6},{5,7},{6,4},{7,5},{8,10},{9,11},{10,... | collective-permute-start | bytes 147464 | tf_op jit(solution)/shard_map/ppermute | solution.py:360
  9.9 6.0 %collective-permute-start.1 = (bf16[6,32,128]{2,1,0:T(8,128)(2,1)S(1)}, bf16[6,32,128]{2,1,0:T(8,128)(2,1)S(1)}, u32[]{:S(2)}, u32[]{:S(2)}) collective-permute-start(bf16[6,32,128]{2,1,0:T(8,128)(2,1)S(1)} %get-tuple-element.14), channel_id=1, source_target_pairs={{0,3},{1,2},{2,1},{3,0},{4,7},{5,6},{6,5},{7,4},{8,11},{9,10},{10,... | collective-permute-start | bytes 147464 | tf_op jit(solution)/shard_map/ppermute | solution.py:360
  11.3 4.6 %collective-permute-start.2 = (bf16[6,32,128]{2,1,0:T(8,128)(2,1)S(1)}, bf16[6,32,128]{2,1,0:T(8,128)(2,1)S(1)}, u32[]{:S(2)}, u32[]{:S(2)}) collective-permute-start(bf16[6,32,128]{2,1,0:T(8,128)(2,1)S(1)} %get-tuple-element.15), channel_id=1, source_target_pairs={{0,1},{1,0},{2,3},{3,2},{4,5},{5,4},{6,7},{7,6},{8,9},{9,8},{10,11... | collective-permute-start | bytes 147464 | tf_op jit(solution)/shard_map/ppermute | solution.py:360
  16.7 5.0 %collective-permute-start.3 = (bf16[4,2,32,128]{3,2,1,0:T(8,128)(2,1)S(1)}, bf16[4,2,32,128]{3,2,1,0:T(8,128)(2,1)S(1)}, u32[]{:S(2)}, u32[]{:S(2)}) collective-permute-start(bf16[4,2,32,128]{3,2,1,0:T(8,128)(2,1)S(1)} %get-tuple-element.21.near), channel_id=1, source_target_pairs={{0,16},{16,0},{1,17},{17,1},{2,18},{18,2},{3,19},{19,3},{4,20},{20... | collective-permute-start | bytes 196616 | tf_op jit(solution)/shard_map/ppermute | solution.py:360
  18.3 9.4 %all-to-all-start = ((bf16[8,4,32,128]{3,2,1,0:T(8,128)(2,1)}), bf16[8,4,32,128]{3,2,1,0:T(8,128)(2,1)S(1)}, u32[]{:S(2)}, u32[]{:S(2)}) async-start(bf16[8,4,32,128]{3,2,1,0:T(8,128)(2,1)} %get-tuple-element.17), calls=%async_computation | async-start | bytes 524288 | tf_op jit(solution)/shard_map/all_to_all | solution.py:460

commit v26 on v23

--- a/solution.py
+++ b/solution.py
@@ -38,15 +38,13 @@
     return values.astype(np.float32).astype(BF16)
 
 
-def pack(lev, lat, coeffs, padded, rows):
+def pack(level, lev, lat, coeffs, padded, rows):
     group = coeffs.shape[1] // THIRDS
-    padded[...] = jnp.zeros_like(padded)
-    for level in range(lev):
-        for third in range(THIRDS):
-            padded[third * lat : (third + 1) * lat, :group] = coeffs[
-                level * lat : (level + 1) * lat, third * group : (third + 1) * group
-            ]
-        rows[pl.ds(level, group, stride=lev), :] = jnp.transpose(padded[...])[:group]
+    for third in range(THIRDS):
+        padded[level, third * lat : (third + 1) * lat, :group] = coeffs[
+            level * lat : (level + 1) * lat, third * group : (third + 1) * group
+        ]
+    rows[pl.ds(level, group, stride=lev), :] = jnp.transpose(padded[level])[:group]
 
 
 def prepare_kernel(lat, n_band, legendre, inverses, out, out_inverses, wide, rows, turned):
@@ -171,6 +169,7 @@
         )
     if depth > across * lat_pad:
         patch[across * lat_pad :, :] = jnp.zeros((depth - across * lat_pad, lev * LANES), BF16)
+    padded[...] = jnp.zeros_like(padded)
     for base in (0, half):
         for level in range(base, base + half):
             loads[level].wait()
@@ -184,12 +183,6 @@
             small[2].wait()
             flat = jnp.concatenate([grid[level] for level in range(lev)], axis=0)
             coeffs = jnp.dot(flat, table[...], preferred_element_type=F32)
-            pack(lev, lat, coeffs, padded, rows)
-            height = bands * size
-            for shift, out in enumerate(outs):
-                first = pl.multiple_of((place ^ shift) * height, height)
-                part = rows[pl.ds(first, height), :].astype(BF16)
-                out[:bands] = part.reshape(bands, size, LANES)
         for start in range(0, slots, chunk):
             top = slice(start, start + chunk)
             picked = jnp.dot(
@@ -197,6 +190,11 @@
                 patch[:, base * LANES : (base + half) * LANES],
                 preferred_element_type=F32,
             )
+            if base > 0:
+                share = -(-lev * chunk // slots)
+                first = start // chunk * share
+                for level in range(first, min(first + share, lev)):
+                    pack(level, lev, lat, coeffs, padded, rows)
             weights = interp[top, :].astype(F32)
             total = jnp.zeros((chunk, LANES), F32) if base == 0 else totals[top, :]
             for i in range(half):
@@ -214,6 +212,11 @@
                     out[bands + block, row : row + lev, :] = state[
                         :, tile * LANES : (tile + 1) * LANES
                     ]
+    height = bands * size
+    for shift, out in enumerate(outs):
+        first = pl.multiple_of((place ^ shift) * height, height)
+        part = rows[pl.ds(first, height), :].astype(BF16)
+        out[:bands] = part.reshape(bands, size, LANES)
 
 
 def regroup_kernel(n_sec, n_band, shifts, *refs):
@@ -372,7 +375,7 @@
             pltpu.VMEM((depth, lev * LANES), BF16),
             pltpu.VMEM((slots, LANES), jnp.int32),
             pltpu.VMEM((slots, depth), BF16),
-            pltpu.VMEM((LANES, padded_group), F32),
+            pltpu.VMEM((lev, LANES, padded_group), F32),
             pltpu.VMEM((group * lev, LANES), F32),
             pltpu.VMEM((slots, LANES), F32),
             pltpu.SemaphoreType.DMA((lev + 3,)),

time: 29 us -> 29 us (level)
  no operation moved by 1% of the time
where the time goes in v26:
time: 29 us; the launch traced here: 28.8 us
  Pallas kernels  14 us (48%)
  starting transfers between devices  10.6 us (37%)
  waiting for transfers between devices  3.37 us (12%)
  between operations  0.77 us (3%)
    pallas_call x5, Pallas kernels, call(): pl.pallas_call(kernel, out_shape=shapes[0] if single else shapes, in_spec...  14 us
    ppermute x4, starting transfers between devices, exchange(): lax.ppermute(value, axis, [(i, i ^ shift) for i in range(lax.axis_size(ax...  7.24 us
    all_to_all x1, starting transfers between devices, body(): pieces = lax.all_to_all(sent, ('sec', 'band'), 0, 0, tiled=True)  3.41 us
    ppermute x4, waiting for transfers between devices, exchange(): lax.ppermute(value, axis, [(i, i ^ shift) for i in range(lax.axis_size(ax...  3.17 us
  transfers between devices with their start and end apart: 5, of which 2 were waited for; matrix products, arithmetic and copies ran while one was open for 0% of the time, Pallas kernels for 24%

profile of v26, /device:TPU:0, one launch (start us, length us, event | category | flops | bytes accessed | tf_op | source)
XLA Modules:
  0.0 28.8 jit_solution(11211379608652674948)
XLA Ops:
  0.6 0.0 copy-start
  0.6 0.0 copy-start.1
  0.7 0.0 copy-start.2
  0.7 0.0 copy-start.3
  0.7 0.0 copy-start.4
  0.7 0.0 copy-start.5
  0.7 5.2 %local.1 = (bf16[6,32,128]{2,1,0:T(8,128)(2,1)S(1)}, bf16[6,32,128]{2,1,0:T(8,128)(2,1)S(1)}, bf16[6,32,128]{2,1,0:T(8,128)(2,1)S(1)}, bf16[6,32,128]{2,1,0:T(8,128)(2,1)S(1)}) custom-call(bf16[8,40,2688]{2,1,0:T(8,128)(2,1)} %bitcast.8, s32[1,1024]{1,0:T(1,128)} %bitcast.6, bf16[1024,128]{1,0:T(8,128)(2,1)} %interp.1, bf16[2688,192]{1,0:T(8,128)(2,1)} %constant.2.clone.table_hbm), custom_call_target="tpu_custom_call" | custom-call | flops 2477785088 | bytes 1982464 | tf_op jit(solution)/shard_map/local/pallas_call | solution.py:331
  5.9 4.1 %collective-permute-start = (bf16[6,32,128]{2,1,0:T(8,128)(2,1)S(1)}, bf16[6,32,128]{2,1,0:T(8,128)(2,1)S(1)}, u32[]{:S(2)}, u32[]{:S(2)}) collective-permute-start(bf16[6,32,128]{2,1,0:T(8,128)(2,1)S(1)} %get-tuple-element.11), channel_id=1, source_target_pairs={{0,2},{1,3},{2,0},{3,1},{4,6},{5,7},{6,4},{7,5},{8,10},{9,11},{10,... | collective-permute-start | bytes 147464 | tf_op jit(solution)/shard_map/ppermute | solution.py:344
  10.0 1.3 %collective-permute-start.1 = (bf16[6,32,128]{2,1,0:T(8,128)(2,1)S(1)}, bf16[6,32,128]{2,1,0:T(8,128)(2,1)S(1)}, u32[]{:S(2)}, u32[]{:S(2)}) collective-permute-start(bf16[6,32,128]{2,1,0:T(8,128)(2,1)S(1)} %get-tuple-element.12), channel_id=1, source_target_pairs={{0,3},{1,2},{2,1},{3,0},{4,7},{5,6},{6,5},{7,4},{8,11},{9,10},{10,... | collective-permute-start | bytes 147464 | tf_op jit(solution)/shard_map/ppermute | solution.py:344
  11.3 0.2 collective-permute-start.2
  11.6 0.0 copy-done
  11.6 0.0 copy-done.1
  11.6 1.2 %prepare.1 = (bf16[4,2,144,128]{3,2,1,0:T(8,128)(2,1)S(1)}, bf16[2048,32]{1,0:T(8,128)(2,1)S(1)}) custom-call(bf16[6,48,160]{2,1,0:T(8,128)(2,1)S(1)} %bitcast.5, bf16[32,32,64]{2,1,0:T(8,128)(2,1)S(1)} %bitcast.4), custom_call_target="tpu_custom_call" | custom-call | bytes 1179648 | tf_op jit(solution)/shard_map/prepare/pallas_call | solution.py:331
  12.8 0.0 collective-permute-done.refs_0_
  12.8 3.2 %collective-permute-done.1.refs_1_ = bf16[6,32,128]{2,1,0:T(8,128)(2,1)S(1)} collective-permute-done((bf16[6,32,128]{2,1,0:T(8,128)(2,1)S(1)}, bf16[6,32,128]{2,1,0:T(8,128)(2,1)S(1)}, u32[]{:S(2)}, u32[]{:S(2)}) %collective-permute-start.1) | collective-permute-done | bytes 49184 | tf_op jit(solution)/shard_map/ppermute | solution.py:344
  16.0 0.0 collective-permute-done.2.refs_2_
  16.0 0.8 %regroup.1 = (bf16[8,4,32,128]{3,2,1,0:T(8,128)(2,1)}, bf16[4,2,32,128]{3,2,1,0:T(8,128)(2,1)S(1)}) custom-call(bf16[6,32,128]{2,1,0:T(8,128)(2,1)S(1)} %collective-permute-done.refs_0_, bf16[6,32,128]{2,1,0:T(8,128)(2,1)S(1)} %collective-permute-done.1.refs_1_, bf16[6,32,128]{2,1,0:T(8,128)(2,1)S(1)} %collective-permute-done.2.refs_2_, ...), custom_call_target="tpu_custom_call" | custom-call | bytes 524288 | tf_op jit(solution)/shard_map/regroup/pallas_call | solution.py:331
  16.8 1.6 %collective-permute-start.3 = (bf16[4,2,32,128]{3,2,1,0:T(8,128)(2,1)S(1)}, bf16[4,2,32,128]{3,2,1,0:T(8,128)(2,1)S(1)}, u32[]{:S(2)}, u32[]{:S(2)}) collective-permute-start(bf16[4,2,32,128]{3,2,1,0:T(8,128)(2,1)S(1)} %get-tuple-element.17.near), channel_id=1, source_target_pairs={{0,16},{16,0},{1,17},{17,1},{2,18},{18,2},{3,19},{19,3},{4,20},{20... | collective-permute-start | bytes 196616 | tf_op jit(solution)/shard_map/ppermute | solution.py:344
  18.4 3.4 %all-to-all-start = ((bf16[8,4,32,128]{3,2,1,0:T(8,128)(2,1)}), bf16[8,4,32,128]{3,2,1,0:T(8,128)(2,1)S(1)}, u32[]{:S(2)}, u32[]{:S(2)}) async-start(bf16[8,4,32,128]{3,2,1,0:T(8,128)(2,1)} %get-tuple-element.15), calls=%async_computation | async-start | bytes 524288 | tf_op jit(solution)/shard_map/all_to_all | solution.py:431
  21.8 0.0 collective-permute-done.3.far
  21.8 0.0 copy-done.2
  21.8 5.7 %columns.1 = bf16[2,40,2688]{2,1,0:T(8,128)(2,1)} custom-call(s32[4]{0:T(128)S(1)} %copy-done.5, bf16[64,2048]{1,0:T(8,128)(2,1)S(1)} %copy-done.3, bf16[2048,32]{1,0:T(8,128)(2,1)S(1)} %get-tuple-element.16.inverses, s32[1,1024]{1,0:T(1,128)S(1)} %bitcast.7, bf16[1024,128]{1,0:T(8,128)(2,1)S(1)} %copy-done.2, ...), custom_call_target="tpu_custom_call" | custom-call | flops 8589934592 | bytes 2097152 | tf_op jit(solution)/shard_map/columns/pallas_call | solution.py:331
  27.5 0.2 all-to-all-done.pieces
  27.7 1.0 %legendre.1 = bf16[6,2,4,16,48]{4,3,2,1,0:T(8,128)(2,1)} custom-call(bf16[4,2,144,128]{3,2,1,0:T(8,128)(2,1)S(1)} %get-tuple-element.10.refs_4_.weights, bf16[8,4,32,128]{3,2,1,0:T(8,128)(2,1)S(1)} %all-to-all-done.pieces), custom_call_target="tpu_custom_call" | custom-call | flops 75497472 | bytes 262144 | tf_op jit(solution)/shard_map/legendre/pallas_call | solution.py:331
  (3 shorter events, 0.0 us)
Async XLA Ops:
  0.6 10.9 %copy-start = (bf16[64,32,32]{0,2,1:T(8,128)(2,1)S(1)}, bf16[64,32,32]{0,2,1:T(8,128)(2,1)}, u32[]{:S(2)}) copy-start(bf16[64,32,32]{0,2,1:T(8,128)(2,1)} %param.14) | copy-start | bytes 393220
  0.6 10.9 %copy-start.1 = (bf16[6,160,48]{1,2,0:T(8,128)(2,1)S(1)}, bf16[6,160,48]{1,2,0:T(8,128)(2,1)}, u32[]{:S(2)}) copy-start(bf16[6,160,48]{1,2,0:T(8,128)(2,1)} %param.9) | copy-start | bytes 276484
  0.7 21.1 %copy-start.2 = (bf16[1024,128]{1,0:T(8,128)(2,1)S(1)}, bf16[1024,128]{1,0:T(8,128)(2,1)}, u32[]{:S(2)}) copy-start(bf16[1024,128]{1,0:T(8,128)(2,1)} %interp.1) | copy-start | bytes 786436
  0.7 21.1 %copy-start.3 = (bf16[64,2048]{1,0:T(8,128)(2,1)S(1)}, bf16[64,2048]{1,0:T(8,128)(2,1)}, u32[]{:S(2)}) copy-start(bf16[64,2048]{1,0:T(8,128)(2,1)} %weights.1) | copy-start | bytes 786436
  0.7 21.1 %copy-start.4 = (s32[1024]{0:T(1024)S(1)}, s32[1024]{0:T(1024)}, u32[]{:S(2)}) copy-start(s32[1024]{0:T(1024)} %param.11) | copy-start | bytes 12292
  0.7 21.1 %copy-start.5 = (s32[4]{0:T(128)S(1)}, s32[4]{0:T(128)}, u32[]{:S(2)}) copy-start(s32[4]{0:T(128)} %counts.1) | copy-start | bytes 52
  5.9 6.9 %collective-permute-start = (bf16[6,32,128]{2,1,0:T(8,128)(2,1)S(1)}, bf16[6,32,128]{2,1,0:T(8,128)(2,1)S(1)}, u32[]{:S(2)}, u32[]{:S(2)}) collective-permute-start(bf16[6,32,128]{2,1,0:T(8,128)(2,1)S(1)} %get-tuple-element.11), channel_id=1, source_target_pairs={{0,2},{1,3},{2,0},{3,1},{4,6},{5,7},{6,4},{7,5},{8,10},{9,11},{10,... | collective-permute-start | bytes 147464 | tf_op jit(solution)/shard_map/ppermute | solution.py:344
  10.0 6.0 %collective-permute-start.1 = (bf16[6,32,128]{2,1,0:T(8,128)(2,1)S(1)}, bf16[6,32,128]{2,1,0:T(8,128)(2,1)S(1)}, u32[]{:S(2)}, u32[]{:S(2)}) collective-permute-start(bf16[6,32,128]{2,1,0:T(8,128)(2,1)S(1)} %get-tuple-element.12), channel_id=1, source_target_pairs={{0,3},{1,2},{2,1},{3,0},{4,7},{5,6},{6,5},{7,4},{8,11},{9,10},{10,... | collective-permute-start | bytes 147464 | tf_op jit(solution)/shard_map/ppermute | solution.py:344
  11.3 4.6 %collective-permute-start.2 = (bf16[6,32,128]{2,1,0:T(8,128)(2,1)S(1)}, bf16[6,32,128]{2,1,0:T(8,128)(2,1)S(1)}, u32[]{:S(2)}, u32[]{:S(2)}) collective-permute-start(bf16[6,32,128]{2,1,0:T(8,128)(2,1)S(1)} %get-tuple-element.13), channel_id=1, source_target_pairs={{0,1},{1,0},{2,3},{3,2},{4,5},{5,4},{6,7},{7,6},{8,9},{9,8},{10,11... | collective-permute-start | bytes 147464 | tf_op jit(solution)/shard_map/ppermute | solution.py:344
  16.8 5.0 %collective-permute-start.3 = (bf16[4,2,32,128]{3,2,1,0:T(8,128)(2,1)S(1)}, bf16[4,2,32,128]{3,2,1,0:T(8,128)(2,1)S(1)}, u32[]{:S(2)}, u32[]{:S(2)}) collective-permute-start(bf16[4,2,32,128]{3,2,1,0:T(8,128)(2,1)S(1)} %get-tuple-element.17.near), channel_id=1, source_target_pairs={{0,16},{16,0},{1,17},{17,1},{2,18},{18,2},{3,19},{19,3},{4,20},{20... | collective-permute-start | bytes 196616 | tf_op jit(solution)/shard_map/ppermute | solution.py:344
  18.4 9.4 %all-to-all-start = ((bf16[8,4,32,128]{3,2,1,0:T(8,128)(2,1)}), bf16[8,4,32,128]{3,2,1,0:T(8,128)(2,1)S(1)}, u32[]{:S(2)}, u32[]{:S(2)}) async-start(bf16[8,4,32,128]{3,2,1,0:T(8,128)(2,1)} %get-tuple-element.15), calls=%async_computation | async-start | bytes 524288 | tf_op jit(solution)/shard_map/all_to_all | solution.py:431

commit v27 on v23

--- a/solution.py
+++ b/solution.py
@@ -171,42 +171,28 @@
         )
     if depth > across * lat_pad:
         patch[across * lat_pad :, :] = jnp.zeros((depth - across * lat_pad, lev * LANES), BF16)
-    for base in (0, half):
-        for level in range(base, base + half):
+    for base in (0,):
+        for level in range(lev):
             loads[level].wait()
             for tile in range(across):
                 patch[
                     tile * lat_pad : tile * lat_pad + lat, level * LANES : (level + 1) * LANES
                 ] = grid[level, :, tile * LANES : (tile + 1) * LANES]
-        if base == 0:
-            small[1].wait()
-        else:
-            small[2].wait()
-            flat = jnp.concatenate([grid[level] for level in range(lev)], axis=0)
-            coeffs = jnp.dot(flat, table[...], preferred_element_type=F32)
-            pack(lev, lat, coeffs, padded, rows)
-            height = bands * size
-            for shift, out in enumerate(outs):
-                first = pl.multiple_of((place ^ shift) * height, height)
-                part = rows[pl.ds(first, height), :].astype(BF16)
-                out[:bands] = part.reshape(bands, size, LANES)
+        small[1].wait()
         for start in range(0, slots, chunk):
             top = slice(start, start + chunk)
             picked = jnp.dot(
                 selector[top, :],
-                patch[:, base * LANES : (base + half) * LANES],
+                patch[...],
                 preferred_element_type=F32,
             )
             weights = interp[top, :].astype(F32)
-            total = jnp.zeros((chunk, LANES), F32) if base == 0 else totals[top, :]
-            for i in range(half):
+            total = jnp.zeros((chunk, LANES), F32)
+            for i in range(lev):
                 product = picked[:, i * LANES : (i + 1) * LANES] * weights
                 total = jnp.where(
-                    lane == base + i, jnp.sum(product, axis=1, keepdims=True), total
+                    lane == i, jnp.sum(product, axis=1, keepdims=True), total
                 )
-            if base == 0:
-                totals[top, :] = total
-                continue
             state = jnp.transpose(total)[:lev].astype(BF16)
             for tile in range(chunk // LANES):
                 block, row = divmod((start // LANES + tile) * lev, size)
@@ -214,6 +200,16 @@
                     out[bands + block, row : row + lev, :] = state[
                         :, tile * LANES : (tile + 1) * LANES
                     ]
+            if start == chunk:
+                small[2].wait()
+                flat = jnp.concatenate([grid[level] for level in range(lev)], axis=0)
+                coeffs = jnp.dot(flat, table[...], preferred_element_type=F32)
+                pack(lev, lat, coeffs, padded, rows)
+                height = bands * size
+                for shift, out in enumerate(outs):
+                    first = pl.multiple_of((place ^ shift) * height, height)
+                    part = rows[pl.ds(first, height), :].astype(BF16)
+                    out[:bands] = part.reshape(bands, size, LANES)
 
 
 def regroup_kernel(n_sec, n_band, shifts, *refs):

time: 29 us -> 29.1 us (level)
  no operation moved by 1% of the time
where the time goes in v27:
time: 29.1 us; the launch traced here: 28.9 us
  Pallas kernels  14.1 us (48%)
  starting transfers between devices  10.7 us (37%)
  waiting for transfers between devices  3.36 us (12%)
  between operations  0.77 us (3%)
    pallas_call x5, Pallas kernels, call(): pl.pallas_call(kernel, out_shape=shapes[0] if single else shapes, in_spec...  14.1 us
    ppermute x4, starting transfers between devices, exchange(): lax.ppermute(value, axis, [(i, i ^ shift) for i in range(lax.axis_size(ax...  7.25 us
    all_to_all x1, starting transfers between devices, body(): pieces = lax.all_to_all(sent, ('sec', 'band'), 0, 0, tiled=True)  3.41 us
    ppermute x4, waiting for transfers between devices, exchange(): lax.ppermute(value, axis, [(i, i ^ shift) for i in range(lax.axis_size(ax...  3.16 us
  transfers between devices with their start and end apart: 5, of which 2 were waited for; matrix products, arithmetic and copies ran while one was open for 0% of the time, Pallas kernels for 24%

profile of v27, /device:TPU:0, one launch (start us, length us, event | category | flops | bytes accessed | tf_op | source)
XLA Modules:
  0.0 28.9 jit_solution(3722505563110727018)
XLA Ops:
  0.6 0.0 copy-start
  0.6 0.0 copy-start.1
  0.7 0.0 copy-start.2
  0.7 0.0 copy-start.3
  0.7 0.0 copy-start.4
  0.7 0.0 copy-start.5
  0.7 5.3 %local.1 = (bf16[6,32,128]{2,1,0:T(8,128)(2,1)S(1)}, bf16[6,32,128]{2,1,0:T(8,128)(2,1)S(1)}, bf16[6,32,128]{2,1,0:T(8,128)(2,1)S(1)}, bf16[6,32,128]{2,1,0:T(8,128)(2,1)S(1)}) custom-call(bf16[8,40,2688]{2,1,0:T(8,128)(2,1)} %bitcast.8, s32[1,1024]{1,0:T(1,128)} %bitcast.6, bf16[1024,128]{1,0:T(8,128)(2,1)} %interp.1, bf16[2688,192]{1,0:T(8,128)(2,1)} %constant.2.clone.table_hbm), custom_call_target="tpu_custom_call" | custom-call | flops 2477785088 | bytes 1982464 | tf_op jit(solution)/shard_map/local/pallas_call | solution.py:324
  6.0 4.1 %collective-permute-start = (bf16[6,32,128]{2,1,0:T(8,128)(2,1)S(1)}, bf16[6,32,128]{2,1,0:T(8,128)(2,1)S(1)}, u32[]{:S(2)}, u32[]{:S(2)}) collective-permute-start(bf16[6,32,128]{2,1,0:T(8,128)(2,1)S(1)} %get-tuple-element.11), channel_id=1, source_target_pairs={{0,2},{1,3},{2,0},{3,1},{4,6},{5,7},{6,4},{7,5},{8,10},{9,11},{10,... | collective-permute-start | bytes 147464 | tf_op jit(solution)/shard_map/ppermute | solution.py:337
  10.1 1.3 %collective-permute-start.1 = (bf16[6,32,128]{2,1,0:T(8,128)(2,1)S(1)}, bf16[6,32,128]{2,1,0:T(8,128)(2,1)S(1)}, u32[]{:S(2)}, u32[]{:S(2)}) collective-permute-start(bf16[6,32,128]{2,1,0:T(8,128)(2,1)S(1)} %get-tuple-element.12), channel_id=1, source_target_pairs={{0,3},{1,2},{2,1},{3,0},{4,7},{5,6},{6,5},{7,4},{8,11},{9,10},{10,... | collective-permute-start | bytes 147464 | tf_op jit(solution)/shard_map/ppermute | solution.py:337
  11.4 0.2 collective-permute-start.2
  11.7 0.0 copy-done
  11.7 0.0 copy-done.1
  11.7 1.2 %prepare.1 = (bf16[4,2,144,128]{3,2,1,0:T(8,128)(2,1)S(1)}, bf16[2048,32]{1,0:T(8,128)(2,1)S(1)}) custom-call(bf16[6,48,160]{2,1,0:T(8,128)(2,1)S(1)} %bitcast.5, bf16[32,32,64]{2,1,0:T(8,128)(2,1)S(1)} %bitcast.4), custom_call_target="tpu_custom_call" | custom-call | bytes 1179648 | tf_op jit(solution)/shard_map/prepare/pallas_call | solution.py:324
  12.9 0.0 collective-permute-done.refs_0_
  12.9 3.1 %collective-permute-done.1.refs_1_ = bf16[6,32,128]{2,1,0:T(8,128)(2,1)S(1)} collective-permute-done((bf16[6,32,128]{2,1,0:T(8,128)(2,1)S(1)}, bf16[6,32,128]{2,1,0:T(8,128)(2,1)S(1)}, u32[]{:S(2)}, u32[]{:S(2)}) %collective-permute-start.1) | collective-permute-done | bytes 49184 | tf_op jit(solution)/shard_map/ppermute | solution.py:337
  16.0 0.0 collective-permute-done.2.refs_2_
  16.0 0.8 %regroup.1 = (bf16[8,4,32,128]{3,2,1,0:T(8,128)(2,1)}, bf16[4,2,32,128]{3,2,1,0:T(8,128)(2,1)S(1)}) custom-call(bf16[6,32,128]{2,1,0:T(8,128)(2,1)S(1)} %collective-permute-done.refs_0_, bf16[6,32,128]{2,1,0:T(8,128)(2,1)S(1)} %collective-permute-done.1.refs_1_, bf16[6,32,128]{2,1,0:T(8,128)(2,1)S(1)} %collective-permute-done.2.refs_2_, ...), custom_call_target="tpu_custom_call" | custom-call | bytes 524288 | tf_op jit(solution)/shard_map/regroup/pallas_call | solution.py:324
  16.9 1.6 %collective-permute-start.3 = (bf16[4,2,32,128]{3,2,1,0:T(8,128)(2,1)S(1)}, bf16[4,2,32,128]{3,2,1,0:T(8,128)(2,1)S(1)}, u32[]{:S(2)}, u32[]{:S(2)}) collective-permute-start(bf16[4,2,32,128]{3,2,1,0:T(8,128)(2,1)S(1)} %get-tuple-element.17.near), channel_id=1, source_target_pairs={{0,16},{16,0},{1,17},{17,1},{2,18},{18,2},{3,19},{19,3},{4,20},{20... | collective-permute-start | bytes 196616 | tf_op jit(solution)/shard_map/ppermute | solution.py:337
  18.4 3.4 %all-to-all-start = ((bf16[8,4,32,128]{3,2,1,0:T(8,128)(2,1)}), bf16[8,4,32,128]{3,2,1,0:T(8,128)(2,1)S(1)}, u32[]{:S(2)}, u32[]{:S(2)}) async-start(bf16[8,4,32,128]{3,2,1,0:T(8,128)(2,1)} %get-tuple-element.15), calls=%async_computation | async-start | bytes 524288 | tf_op jit(solution)/shard_map/all_to_all | solution.py:424
  21.8 0.0 collective-permute-done.3.far
  21.9 0.0 copy-done.2
  21.9 5.7 %columns.1 = bf16[2,40,2688]{2,1,0:T(8,128)(2,1)} custom-call(s32[4]{0:T(128)S(1)} %copy-done.5, bf16[64,2048]{1,0:T(8,128)(2,1)S(1)} %copy-done.3, bf16[2048,32]{1,0:T(8,128)(2,1)S(1)} %get-tuple-element.16.inverses, s32[1,1024]{1,0:T(1,128)S(1)} %bitcast.7, bf16[1024,128]{1,0:T(8,128)(2,1)S(1)} %copy-done.2, ...), custom_call_target="tpu_custom_call" | custom-call | flops 8589934592 | bytes 2097152 | tf_op jit(solution)/shard_map/columns/pallas_call | solution.py:324
  27.6 0.2 all-to-all-done.pieces
  27.8 1.0 %legendre.1 = bf16[6,2,4,16,48]{4,3,2,1,0:T(8,128)(2,1)} custom-call(bf16[4,2,144,128]{3,2,1,0:T(8,128)(2,1)S(1)} %get-tuple-element.10.refs_4_.weights, bf16[8,4,32,128]{3,2,1,0:T(8,128)(2,1)S(1)} %all-to-all-done.pieces), custom_call_target="tpu_custom_call" | custom-call | flops 75497472 | bytes 262144 | tf_op jit(solution)/shard_map/legendre/pallas_call | solution.py:324
  (3 shorter events, 0.0 us)
Async XLA Ops:
  0.6 11.0 %copy-start = (bf16[64,32,32]{0,2,1:T(8,128)(2,1)S(1)}, bf16[64,32,32]{0,2,1:T(8,128)(2,1)}, u32[]{:S(2)}) copy-start(bf16[64,32,32]{0,2,1:T(8,128)(2,1)} %param.14) | copy-start | bytes 393220
  0.6 11.0 %copy-start.1 = (bf16[6,160,48]{1,2,0:T(8,128)(2,1)S(1)}, bf16[6,160,48]{1,2,0:T(8,128)(2,1)}, u32[]{:S(2)}) copy-start(bf16[6,160,48]{1,2,0:T(8,128)(2,1)} %param.9) | copy-start | bytes 276484
  0.7 21.2 %copy-start.2 = (bf16[1024,128]{1,0:T(8,128)(2,1)S(1)}, bf16[1024,128]{1,0:T(8,128)(2,1)}, u32[]{:S(2)}) copy-start(bf16[1024,128]{1,0:T(8,128)(2,1)} %interp.1) | copy-start | bytes 786436
  0.7 21.2 %copy-start.3 = (bf16[64,2048]{1,0:T(8,128)(2,1)S(1)}, bf16[64,2048]{1,0:T(8,128)(2,1)}, u32[]{:S(2)}) copy-start(bf16[64,2048]{1,0:T(8,128)(2,1)} %weights.1) | copy-start | bytes 786436
  0.7 21.2 %copy-start.4 = (s32[1024]{0:T(1024)S(1)}, s32[1024]{0:T(1024)}, u32[]{:S(2)}) copy-start(s32[1024]{0:T(1024)} %param.11) | copy-start | bytes 12292
  0.7 21.2 %copy-start.5 = (s32[4]{0:T(128)S(1)}, s32[4]{0:T(128)}, u32[]{:S(2)}) copy-start(s32[4]{0:T(128)} %counts.1) | copy-start | bytes 52
  6.0 6.9 %collective-permute-start = (bf16[6,32,128]{2,1,0:T(8,128)(2,1)S(1)}, bf16[6,32,128]{2,1,0:T(8,128)(2,1)S(1)}, u32[]{:S(2)}, u32[]{:S(2)}) collective-permute-start(bf16[6,32,128]{2,1,0:T(8,128)(2,1)S(1)} %get-tuple-element.11), channel_id=1, source_target_pairs={{0,2},{1,3},{2,0},{3,1},{4,6},{5,7},{6,4},{7,5},{8,10},{9,11},{10,... | collective-permute-start | bytes 147464 | tf_op jit(solution)/shard_map/ppermute | solution.py:337
  10.1 6.0 %collective-permute-start.1 = (bf16[6,32,128]{2,1,0:T(8,128)(2,1)S(1)}, bf16[6,32,128]{2,1,0:T(8,128)(2,1)S(1)}, u32[]{:S(2)}, u32[]{:S(2)}) collective-permute-start(bf16[6,32,128]{2,1,0:T(8,128)(2,1)S(1)} %get-tuple-element.12), channel_id=1, source_target_pairs={{0,3},{1,2},{2,1},{3,0},{4,7},{5,6},{6,5},{7,4},{8,11},{9,10},{10,... | collective-permute-start | bytes 147464 | tf_op jit(solution)/shard_map/ppermute | solution.py:337
  11.4 4.6 %collective-permute-start.2 = (bf16[6,32,128]{2,1,0:T(8,128)(2,1)S(1)}, bf16[6,32,128]{2,1,0:T(8,128)(2,1)S(1)}, u32[]{:S(2)}, u32[]{:S(2)}) collective-permute-start(bf16[6,32,128]{2,1,0:T(8,128)(2,1)S(1)} %get-tuple-element.13), channel_id=1, source_target_pairs={{0,1},{1,0},{2,3},{3,2},{4,5},{5,4},{6,7},{7,6},{8,9},{9,8},{10,11... | collective-permute-start | bytes 147464 | tf_op jit(solution)/shard_map/ppermute | solution.py:337
  16.9 5.0 %collective-permute-start.3 = (bf16[4,2,32,128]{3,2,1,0:T(8,128)(2,1)S(1)}, bf16[4,2,32,128]{3,2,1,0:T(8,128)(2,1)S(1)}, u32[]{:S(2)}, u32[]{:S(2)}) collective-permute-start(bf16[4,2,32,128]{3,2,1,0:T(8,128)(2,1)S(1)} %get-tuple-element.17.near), channel_id=1, source_target_pairs={{0,16},{16,0},{1,17},{17,1},{2,18},{18,2},{3,19},{19,3},{4,20},{20... | collective-permute-start | bytes 196616 | tf_op jit(solution)/shard_map/ppermute | solution.py:337
  18.4 9.4 %all-to-all-start = ((bf16[8,4,32,128]{3,2,1,0:T(8,128)(2,1)}), bf16[8,4,32,128]{3,2,1,0:T(8,128)(2,1)S(1)}, u32[]{:S(2)}, u32[]{:S(2)}) async-start(bf16[8,4,32,128]{3,2,1,0:T(8,128)(2,1)} %get-tuple-element.15), calls=%async_computation | async-start | bytes 524288 | tf_op jit(solution)/shard_map/all_to_all | solution.py:424
